TPU v7x, 32 devices: a whole 2x2x4 slice. The times are simulated.
32 devices in a mesh: ex: 8 (over y, x, core), tok: 4 (over z).
Axes of the slice: x: 2, y: 2, z: 4, core: 2. Of those that a mesh axis runs over, the one named last changes fastest.
Arguments:
- proj_rows: bfloat16 [65536, 128], P(('ex', 'tok')), may hold values from -6 to 6
- query_features: bfloat16 [512, 4096], P('ex'), may hold values from -0.09375 to 0.09375
- doc_lengths: int32 [8, 32], P('ex'), may hold values from 1 to 4096, 8192 in all within a row
- owner_map: int32 [8, 32], P('ex'), may hold values from 0 to 31, each once within a row
Outputs:
- scores: float32 [512, 256], P('ex', 'tok')
Inputs may be any that keep to these rules, and one draw needn't show every extreme that they name: `owner_map`: each row lists the slots 0 to 31 once each. `doc_lengths`: each row sums to 8192; its largest entry is exactly 4096.
All inputs are finite; a program needn't handle non-finite values.
Results may differ from a plain program's by a relative error of at most 0.0029.
Values may be sent and summed in bfloat16 or wider, within the bound.
No kernel may reach another device: no remote copies, remote signals or barrier semaphores. Data moves between devices by JAX's collectives and lax.ppermute only.
A program may use at most 64 MiB of HBM per device.

v0:
```python
import jax
import jax.numpy as jnp
from jax import lax
from jax.sharding import PartitionSpec as P


def slot_lookup(lengths, owner_slots, positions):
    doc_ends = jnp.cumsum(lengths)
    doc_index = jnp.sum((positions[:, None] >= doc_ends[None, :]).astype(jnp.int32), axis=1)
    doc_match = doc_index[:, None] == jnp.arange(lengths.shape[0], dtype=jnp.int32)[None, :]
    return jnp.sum(jnp.where(doc_match, owner_slots[None, :], 0), axis=1)


def kron_sums(row_data, slots, targets):
    proj_width = row_data.shape[1] // 2
    count = row_data.shape[0]
    input_rows = row_data[:, :proj_width]
    grad_rows = row_data[:, proj_width:]

    def slot_group(slot_set):
        slot_mask = (slots[:, None] == slot_set[None, :]).astype(jnp.bfloat16)
        spread = (slot_mask[:, :, None] * grad_rows[:, None, :]).reshape(count, 4 * proj_width)
        return jnp.einsum("ta,tb->ab", spread, input_rows, preferred_element_type=jnp.float32)

    result = lax.map(slot_group, targets.reshape(-1, 4))
    return result.reshape(targets.shape[0], proj_width * proj_width)


def body(proj_rows, query_features, doc_lengths, owner_map):
    lengths = doc_lengths[0]
    owner_slots = owner_map[0]
    tok_count = lax.axis_size("tok")
    doc_dev = owner_slots.shape[0] // tok_count
    tok_index = lax.axis_index("tok")
    targets = tok_index * doc_dev + jnp.arange(doc_dev, dtype=jnp.int32)
    portion = lax.all_gather(proj_rows, "tok", axis=0, tiled=True)
    positions = jnp.arange(portion.shape[0], dtype=jnp.int32)
    summed = kron_sums(portion, slot_lookup(lengths, owner_slots, positions), targets)
    own_lengths = jnp.sum(
        jnp.where(owner_slots[None, :] == targets[:, None], lengths[None, :], 0), axis=1
    )
    features = (summed / jnp.sqrt(own_lengths.astype(jnp.float32))[:, None]).astype(jnp.bfloat16)
    return jnp.einsum(
        "qf,df->qd",
        query_features,
        lax.all_gather(features, "ex", axis=0, tiled=True),
        preferred_element_type=jnp.float32,
    )


def solution(mesh):
    placed = (P(("ex", "tok"), None), P("ex", None), P("ex", None), P("ex", None))
    return jax.shard_map(
        body, mesh=mesh, in_specs=placed, out_specs=P("ex", "tok"), check_vma=False
    )
```

profile of v0, /device:TPU:0, one launch (start us, length us, event | category | flops | bytes accessed | tf_op | source)
XLA Modules:
  0.0 88.8 jit_solution(14068616613515398700)
XLA Ops:
  6.5 0.0 all-gather.2.cloned.1.call-start
  6.5 0.7 all-gather.2.cloned.1.call-update
  7.3 0.7 copy.11
  8.0 0.1 reduce-window.8
  8.1 0.1 reduce
  8.2 0.9 select_reduce_fusion.1
  9.1 0.2 convert_reduce_fusion
  9.3 0.9 %select_reduce_fusion = s32[8192]{0:T(1024)S(1)} fusion(s32[32]{0:T(128)} %bitcast.28, s32[8192]{0:T(1024)S(1)} %convert_reduce_fusion), kind=kLoop, calls=%fused_computation.7 | loop fusion | flops 778240 | bytes 65664 | tf_op jit(solution)/shard_map/reduce_sum | solution.py:11
  10.2 47.4 %all-gather.2.cloned.1.call-done = bf16[8192,128]{1,0:T(8,128)(2,1)} async-done(((bf16[2048,128]{1,0:T(8,128)(2,1)}), bf16[8192,128]{1,0:T(8,128)(2,1)}) %all-gather.2.cloned.1.call-update) | async-done | bytes 2097168 | tf_op jit(solution)/shard_map/all_gather | solution.py:36
  57.6 4.3 %fusion.2 = (bf16[8192,64]{1,0:T(8,128)(2,1)S(1)}, bf16[8192,64]{1,0:T(8,128)(2,1)}) fusion(bf16[8192,128]{1,0:T(8,128)(2,1)} %all-gather.2.cloned.1.call-done), kind=kLoop, calls=%fused_computation.16 | loop fusion | bytes 4194304 | tf_op jit(solution)/shard_map/slice | solution.py:17
  61.9 2.7 %copy.12 = bf16[8192,64]{0,1:T(8,128)(2,1)} copy(bf16[8192,64]{1,0:T(8,128)(2,1)} %get-tuple-element.63) | data formatting | bytes 2097152 | tf_op jit(solution)/shard_map/while | solution.py:25
  64.5 6.2 %while.10 = (s32[]{:T(128)}, f32[2,256,64]{1,2,0:T(8,128)S(1)}, s32[8192]{0:T(1024)S(1)}, s32[2,4]{1,0:T(2,128)S(1)}, bf16[8192,64]{0,1:T(8,128)(2,1)}, /*index=5*/bf16[8192,64]{1,0:T(8,128)(2,1)S(1)}, s32[]{:T(128)}) while((s32[]{:T(128)}, f32[2,256,64]{1,2,0:T(8,128)S(1)}, s32[8192]{0:T(1024)S(1)}, s32[2,4]{1,0:T(2,128)S(1)}, ...), condition=%wide.region_4.5_spmd, body=%wide.region_3.4_spmd.sunk | while | flops 270598144 | bytes 11763845 | solution.py:25
  64.6 0.1 compare_convert_fusion.2
  64.7 1.6 %broadcast_multiply_fusion.2 = bf16[8192,4,64]{0,2,1:T(8,128)(2,1)S(1)} fusion(bf16[8192,64]{0,1:T(8,128)(2,1)} %get-tuple-element.119, bf16[8192,4]{0,1:T(4,128)(2,1)S(1)} %compare_convert_fusion.2), kind=kLoop, calls=%fused_computation.clone.1 | loop fusion | flops 2097152 | bytes 5308416 | tf_op jit(solution)/shard_map/while/body/eval_jaxpr/mul | solution.py:22
  66.2 1.4 %fusion.14 = f32[2,256,64]{1,2,0:T(8,128)S(1)} fusion(f32[2,256,64]{1,2,0:T(8,128)S(1)} %get-tuple-element.109, s32[]{:T(128)} %get-tuple-element.108, bf16[8192,256]{0,1:T(8,128)(2,1)S(1)} %bitcast.26, bf16[8192,64]{1,0:T(8,128)(2,1)S(1)} %get-tuple-element.120), kind=kOutput, calls=%fused_computation.2.clone.1 | convolution fusion | flops 268435456 | bytes 6356996 | tf_op jit(solution)/shard_map/while/body/eval_jaxpr/ta,tb->ab/dot_general | solution.py:23
  67.7 0.1 compare_convert_fusion.2
  67.8 1.6 %broadcast_multiply_fusion.2 = bf16[8192,4,64]{0,2,1:T(8,128)(2,1)S(1)} fusion(bf16[8192,64]{0,1:T(8,128)(2,1)} %get-tuple-element.119, bf16[8192,4]{0,1:T(4,128)(2,1)S(1)} %compare_convert_fusion.2), kind=kLoop, calls=%fused_computation.clone.1 | loop fusion | flops 2097152 | bytes 5308416 | tf_op jit(solution)/shard_map/while/body/eval_jaxpr/mul | solution.py:22
  69.3 1.4 %fusion.14 = f32[2,256,64]{1,2,0:T(8,128)S(1)} fusion(f32[2,256,64]{1,2,0:T(8,128)S(1)} %get-tuple-element.109, s32[]{:T(128)} %get-tuple-element.108, bf16[8192,256]{0,1:T(8,128)(2,1)S(1)} %bitcast.26, bf16[8192,64]{1,0:T(8,128)(2,1)S(1)} %get-tuple-element.120), kind=kOutput, calls=%fused_computation.2.clone.1 | convolution fusion | flops 268435456 | bytes 6356996 | tf_op jit(solution)/shard_map/while/body/eval_jaxpr/ta,tb->ab/dot_general | solution.py:23
  70.8 0.1 copy.13
  70.9 0.1 reshape.75
  71.0 0.1 divide_convert_fusion
  71.1 9.8 %all_gather.7 = bf16[64,4096]{1,0:T(8,128)(2,1)S(1)} all-gather(bf16[8,4096]{1,0:T(8,128)(2,1)S(1)} %divide_convert_fusion), channel_id=1, replica_groups=mesh['ex'=8,'tok'=4] {'ex'}, dimensions={0}, use_global_device_ids=true | all-gather | bytes 589824 | tf_op jit(solution)/shard_map/all_gather | solution.py:46
  81.0 0.3 convolution_bitcast_fusion.1
  81.3 0.7 copy.14
  (8 shorter events, 0.0 us)
Async XLA Ops:
  6.5 74.4 %copy-start = (bf16[64,4096]{1,0:T(8,128)(2,1)S(1)}, bf16[64,4096]{1,0:T(8,128)(2,1)}, u32[]{:S(2)}) copy-start(bf16[64,4096]{1,0:T(8,128)(2,1)} %param.7) | copy-start | bytes 1572868
  6.5 51.1 %all-gather.2.cloned.1.call-start = ((), (), s32[]{:S(2)}) async-start(), calls=%async_computation | async-start | bytes 2621440 | tf_op jit(solution)/shard_map/all_gather | solution.py:36
Sparse Core Ops, SparseCore 0:
  8.9 48.6 all-gather.1
where the time goes:
time: 89.1 us; the launch traced here: 88.8 us
  waiting for transfers between devices  48.1 us (54%)
  between operations  13.5 us (15%)
  blocking collectives  9.83 us (11%)
  local copies, waits for them, and re-layouts  8.64 us (10%)
  other arithmetic  5.57 us (6%)
  matrix products  3.21 us (4%)
    all_gather x1, waiting for transfers between devices, body(): portion = lax.all_gather(proj_rows, 'tok', axis=0, tiled=True)  47.4 us
    all_gather x1, blocking collectives, body(): lax.all_gather(features, 'ex', axis=0, tiled=True)  9.83 us
    slice x1, local copies, waits for them, and re-layouts, kron_sums(): input_rows = row_data[:, :proj_width]  4.27 us
    mul x2, other arithmetic, slot_group(): slot_mask[:, :, None] * grad_rows[:, None, :]  3.12 us
    dot_general x2, matrix products, slot_group(): jnp.einsum('ta,tb->ab', spread, input_rows, preferred_element_type=jnp.fl...  2.88 us
    while x2, local copies, waits for them, and re-layouts, kron_sums(): result = lax.map(slot_group, targets.reshape(-1, 4))  2.8 us
  transfers between devices with their start and end apart: 1, of which 1 were waited for; matrix products, arithmetic and copies ran while one was open for 3% of the time, Pallas kernels for 0%

commit v1 on v0

v1 whole, which is shorter than its diff:
```python
import jax
import jax.numpy as jnp
from jax import lax
from jax.sharding import PartitionSpec as P

LOW = 4


def partial_features(rows, lengths, owner_slots, first):
    count, width = rows.shape[0], rows.shape[1] // 2
    docs = lengths.shape[0]
    high = docs // LOW
    ends = jnp.cumsum(lengths)
    positions = first + jnp.arange(count, dtype=jnp.int32)
    inside = (positions[:, None] >= (ends - lengths)[None, :]) & (positions[:, None] < ends[None, :])
    slots = jnp.sum(jnp.where(inside, owner_slots[None, :], 0), axis=1)
    by_slot = owner_slots[None, :] == jnp.arange(docs, dtype=jnp.int32)[:, None]
    slot_lengths = jnp.sum(jnp.where(by_slot, lengths[None, :], 0), axis=1)
    high_mask = (slots // LOW)[:, None] == jnp.arange(high, dtype=jnp.int32)[None, :]
    low_mask = (slots % LOW)[:, None] == jnp.arange(LOW, dtype=jnp.int32)[None, :]
    zero = jnp.zeros((), rows.dtype)
    grads = jnp.where(high_mask[:, :, None], rows[:, None, width:], zero).reshape(count, high * width)
    inputs = jnp.where(low_mask[:, :, None], rows[:, None, :width], zero).reshape(count, LOW * width)
    sums = jnp.einsum("ta,tb->ab", grads, inputs, preferred_element_type=jnp.float32)
    sums = sums.reshape(high, width, LOW, width).transpose(0, 2, 1, 3).reshape(docs, width * width)
    return (sums / jnp.sqrt(slot_lengths.astype(jnp.float32))[:, None]).astype(jnp.bfloat16)


def body(proj_rows, query_features, doc_lengths, owner_map):
    tok_count = lax.axis_size("tok")
    tok_index = lax.axis_index("tok")
    parts = partial_features(proj_rows, doc_lengths[0], owner_map[0], tok_index * proj_rows.shape[0])
    doc_dev = parts.shape[0] // tok_count

    def share(shift):
        start = ((tok_index + shift) % tok_count) * doc_dev
        return lax.dynamic_slice_in_dim(parts, start, doc_dev, axis=0)

    total = share(0).astype(jnp.float32)
    for shift in range(1, tok_count):
        pairs = [(i, (i + shift) % tok_count) for i in range(tok_count)]
        total = total + lax.ppermute(share(shift), "tok", pairs).astype(jnp.float32)
    features = total.astype(jnp.bfloat16)
    return jnp.einsum(
        "qf,df->qd",
        query_features,
        lax.all_gather(features, "ex", axis=0, tiled=True),
        preferred_element_type=jnp.float32,
    )


def solution(mesh):
    placed = (P(("ex", "tok"), None), P("ex", None), P("ex", None), P("ex", None))
    return jax.shard_map(
        body, mesh=mesh, in_specs=placed, out_specs=P("ex", "tok"), check_vma=False
    )
```

time: 89.1 us -> 29.3 us (0.33)
  waiting for transfers between devices: 48.1 us -> 5.45 us
  between operations: 13.5 us -> 0.12 us
  starting transfers between devices: 0.01 us -> 6.12 us
  local copies, waits for them, and re-layouts: 8.64 us -> 3.98 us
  other arithmetic: 5.57 us -> 1.93 us
  matrix products: 3.21 us -> 1.59 us
    all_gather x1 -> x0, waiting for transfers between devices: 47.4 us -> none  [body(): portion = lax.all_gather(proj_rows, 'tok', axis=0, tiled=True)]
    ppermute x0 -> x3, starting transfers between devices: none -> 6.12 us  [body(): total = total + lax.ppermute(share(shift), 'tok', pairs).astype(jnp.float32)]
    ppermute x0 -> x3, waiting for transfers between devices: none -> 5.45 us  [body(): total = total + lax.ppermute(share(shift), 'tok', pairs).astype(jnp.float32)]
    mul x2 -> x0, other arithmetic: 3.12 us -> none  [slot_group(): slot_mask[:, :, None] * grad_rows[:, None, :]]
    while x2 -> x0, local copies, waits for them, and re-layouts: 2.8 us -> none  [kron_sums(): result = lax.map(slot_group, targets.reshape(-1, 4))]
    slice x1 -> x3, local copies, waits for them, and re-layouts: 4.27 us -> 1.8 us  [the longest x2 1.61 us: partial_features(): rows[:, None, :width]]
    dot_general x2 -> x1, matrix products: 2.88 us -> 1.26 us  [partial_features(): jnp.einsum('ta,tb->ab', grads, inputs, preferred_element_type=jnp.float32)]
    reduce_sum x3 -> x2, other arithmetic: 1.99 us -> 0.89 us  [the longest x1 0.78 us: partial_features(): slots = jnp.sum(jnp.where(inside, owner_slots[None, :], 0), axis=1)]
  transfers between devices with their start and end apart: 1 -> 3, of which waited for: 1 -> 2; matrix products, arithmetic and copies ran while one was open for 3% -> 0% of each run, Pallas kernels for 0% -> 0%
where the time goes in v1:
time: 29.3 us; the launch traced here: 29.1 us
  blocking collectives  9.87 us (34%)
  starting transfers between devices  6.12 us (21%)
  waiting for transfers between devices  5.45 us (19%)
  local copies, waits for them, and re-layouts  3.98 us (14%)
  other arithmetic  1.93 us (7%)
  matrix products  1.59 us (5%)
    all_gather x1, blocking collectives, body(): lax.all_gather(features, 'ex', axis=0, tiled=True)  9.87 us
    ppermute x3, starting transfers between devices, body(): total = total + lax.ppermute(share(shift), 'tok', pairs).astype(jnp.float32)  6.12 us
    ppermute x3, waiting for transfers between devices, body(): total = total + lax.ppermute(share(shift), 'tok', pairs).astype(jnp.float32)  5.45 us
    slice x2, local copies, waits for them, and re-layouts, partial_features(): rows[:, None, :width]  1.61 us
    dot_general x1, matrix products, partial_features(): jnp.einsum('ta,tb->ab', grads, inputs, preferred_element_type=jnp.float32)  1.26 us
    reshape x1, local copies, waits for them, and re-layouts  0.79 us
    reduce_sum x1, other arithmetic, partial_features(): slots = jnp.sum(jnp.where(inside, owner_slots[None, :], 0), axis=1)  0.78 us
    dot_general x1, local copies, waits for them, and re-layouts, body(): jnp.einsum('qf,df->qd', query_features, lax.all_gather(features, 'ex', ax...  0.7 us
  transfers between devices with their start and end apart: 3, of which 2 were waited for; matrix products, arithmetic and copies ran while one was open for 0% of the time, Pallas kernels for 0%

profile of v1, /device:TPU:0, one launch (start us, length us, event | category | flops | bytes accessed | tf_op | source)
XLA Modules:
  0.0 29.1 jit_solution(16676884839684790110)
XLA Ops:
  0.0 0.8 %copy.13 = s32[32,1]{1,0:T(8,128)S(1)} copy(s32[32,1]{0,1:T(1,128)} %bitcast.41) | data formatting | bytes 256 | tf_op jit(solution)/shard_map/reshape
  0.8 0.1 reduce-window.4
  0.9 0.1 reduce
  1.0 0.7 %fusion.16 = s32[32]{0:T(128)S(1)} fusion(s32[1,32]{1,0:T(1,128)} %param.6, s32[32]{0:T(128)S(1)} %reduce), kind=kLoop, calls=%fused_computation.33 | loop fusion | flops 32 | bytes 384 | tf_op jit(solution)/shard_map/ge | solution.py:15
  1.6 0.8 %select_reduce_fusion = s32[2048]{0:T(1024)S(1)} fusion(s32[32]{0:T(128)} %bitcast.39, s32[2048]{0:T(1024)S(1)} %iota_add_fusion, s32[32]{0:T(128)S(1)} %reduce, s32[32]{0:T(128)S(1)} %fusion.16), kind=kLoop, calls=%fused_computation.14 | loop fusion | flops 325632 | bytes 16768 | tf_op jit(solution)/shard_map/reduce_sum | solution.py:16
  2.5 1.4 %fusion.18 = (bf16[2048,64]{1,0:T(8,128)(2,1)S(1)}, bf16[2048,64]{1,0:T(8,128)(2,1)S(1)}) fusion(bf16[2048,128]{1,0:T(8,128)(2,1)} %param.4), kind=kLoop, calls=%fused_computation.36 | loop fusion | bytes 1048576 | tf_op jit(solution)/shard_map/slice | solution.py:23
  3.9 0.2 copy.14
  4.1 0.2 copy.15
  4.3 1.3 %fusion.4 = f32[8,4,64,64]{3,2,1,0:T(8,128)S(1)} fusion(pred[2048,8]{0,1:T(8,128)(4,1)S(1)} %iota_compare_fusion, bf16[2048,64]{0,1:T(8,128)(2,1)S(1)} %copy.14, pred[2048,4]{0,1:T(4,128)(4,1)S(1)} %iota_compare_fusion.1, bf16[2048,64]{0,1:T(8,128)(2,1)S(1)} %copy.15), kind=kOutput, calls=%fused_computation.4 | convolution fusion | flops 538443776 | bytes 1073152 | tf_op jit(solution)/shard_map/ta,tb->ab/dot_general | solution.py:24
  5.6 0.0 copy-start.1
  5.6 0.0 copy-start.2
  5.6 0.4 %reshape.108 = f32[32,4096]{1,0:T(8,128)S(1)} reshape(f32[8,4,64,64]{3,2,1,0:T(8,128)S(1)} %fusion.4) | data formatting | bytes 1048576 | tf_op jit(solution)/shard_map/reshape | solution.py:25
  6.0 0.3 copy-done.1
  6.2 0.0 copy-done.2
  6.2 0.1 select_reduce_fusion.1
  6.4 0.1 divide_convert_fusion
  6.5 5.1 %collective-permute-start.2 = (bf16[8,4096]{1,0:T(8,128)(2,1)S(1)}, bf16[8,4096]{1,0:T(8,128)(2,1)S(1)}, u32[]{:S(2)}, u32[]{:S(2)}) collective-permute-start(bf16[8,4096]{1,0:T(8,128)(2,1)S(1)} %get-tuple-element.8), channel_id=1, source_target_pairs={{0,3},{1,0},{2,1},{3,2},{4,7},{5,4},{6,5},{7,6},{8,11},{9,8},{10,9... | collective-permute-start | bytes 196616 | tf_op jit(solution)/shard_map/ppermute | solution.py:42
  11.6 1.0 %collective-permute-start = (bf16[8,4096]{1,0:T(8,128)(2,1)S(1)}, bf16[8,4096]{1,0:T(8,128)(2,1)S(1)}, u32[]{:S(2)}, u32[]{:S(2)}) collective-permute-start(bf16[8,4096]{1,0:T(8,128)(2,1)S(1)} %get-tuple-element.7), channel_id=1, source_target_pairs={{0,1},{1,2},{2,3},{3,0},{4,5},{5,6},{6,7},{7,4},{8,9},{9,10},{10,1... | collective-permute-start | bytes 196616 | tf_op jit(solution)/shard_map/ppermute | solution.py:42
  12.7 1.5 %collective-permute-done.2 = bf16[8,4096]{1,0:T(8,128)(2,1)S(1)} collective-permute-done((bf16[8,4096]{1,0:T(8,128)(2,1)S(1)}, bf16[8,4096]{1,0:T(8,128)(2,1)S(1)}, u32[]{:S(2)}, u32[]{:S(2)}) %collective-permute-start.2) | collective-permute-done | bytes 65568 | tf_op jit(solution)/shard_map/ppermute | solution.py:42
  14.1 4.0 %collective-permute-done.1 = bf16[8,4096]{1,0:T(8,128)(2,1)S(1)} collective-permute-done((bf16[8,4096]{1,0:T(8,128)(2,1)S(1)}, bf16[8,4096]{1,0:T(8,128)(2,1)S(1)}, u32[]{:S(2)}, u32[]{:S(2)}) %collective-permute-start.1) | collective-permute-done | bytes 65568 | tf_op jit(solution)/shard_map/ppermute | solution.py:42
  18.1 0.0 collective-permute-done
  18.2 9.9 %all_gather.3 = bf16[64,4096]{1,0:T(8,128)(2,1)S(1)} all-gather(bf16[8,4096]{1,0:T(8,128)(2,1)S(1)} %add_convert_fusion), channel_id=1, replica_groups=mesh['ex'=8,'tok'=4] {'ex'}, dimensions={0}, use_global_device_ids=true | all-gather | bytes 589824 | tf_op jit(solution)/shard_map/all_gather | solution.py:47
  28.0 0.3 %convolution_bitcast_fusion = f32[64,64]{0,1:T(8,128)S(1)} fusion(bf16[64,4096]{1,0:T(8,128)(2,1)S(1)} %all_gather.3, bf16[64,4096]{1,0:T(8,128)(2,1)S(1)} %copy-done), kind=kOutput, calls=%fused_computation.5 | convolution fusion | flops 33554432 | bytes 1064960 | tf_op jit(solution)/shard_map/qf,df->qd/dot_general | solution.py:44
  28.4 0.7 %copy.16 = f32[64,64]{1,0:T(8,128)} copy(f32[64,64]{0,1:T(8,128)S(1)} %convolution_bitcast_fusion) | data formatting | bytes 32768 | tf_op jit(solution)/shard_map/qf,df->qd/dot_general | solution.py:44
  (10 shorter events, 0.1 us)
Async XLA Ops:
  0.0 28.0 %copy-start = (bf16[64,4096]{1,0:T(8,128)(2,1)S(1)}, bf16[64,4096]{1,0:T(8,128)(2,1)}, u32[]{:S(2)}) copy-start(bf16[64,4096]{1,0:T(8,128)(2,1)} %param.5) | copy-start | bytes 1572868
  5.6 0.7 %copy-start.1 = (s32[1,32]{1,0:T(1,128)S(1)}, s32[1,32]{1,0:T(1,128)}, u32[]{:S(2)}) copy-start(s32[1,32]{1,0:T(1,128)} %param.7) | copy-start | bytes 388
  5.6 0.7 %copy-start.2 = (s32[1,32]{1,0:T(1,128)S(1)}, s32[1,32]{1,0:T(1,128)}, u32[]{:S(2)}) copy-start(s32[1,32]{1,0:T(1,128)} %param.6) | copy-start | bytes 388
  6.5 7.6 %collective-permute-start.2 = (bf16[8,4096]{1,0:T(8,128)(2,1)S(1)}, bf16[8,4096]{1,0:T(8,128)(2,1)S(1)}, u32[]{:S(2)}, u32[]{:S(2)}) collective-permute-start(bf16[8,4096]{1,0:T(8,128)(2,1)S(1)} %get-tuple-element.8), channel_id=1, source_target_pairs={{0,3},{1,0},{2,1},{3,2},{4,7},{5,4},{6,5},{7,6},{8,11},{9,8},{10,9... | collective-permute-start | bytes 196616 | tf_op jit(solution)/shard_map/ppermute | solution.py:42
  11.6 6.5 %collective-permute-start.1 = (bf16[8,4096]{1,0:T(8,128)(2,1)S(1)}, bf16[8,4096]{1,0:T(8,128)(2,1)S(1)}, u32[]{:S(2)}, u32[]{:S(2)}) collective-permute-start(bf16[8,4096]{1,0:T(8,128)(2,1)S(1)} %get-tuple-element.9), channel_id=1, source_target_pairs={{0,2},{1,3},{2,0},{3,1},{4,6},{5,7},{6,4},{7,5},{8,10},{9,11},{10,... | collective-permute-start | bytes 196616 | tf_op jit(solution)/shard_map/ppermute | solution.py:42
  11.6 6.5 %collective-permute-start = (bf16[8,4096]{1,0:T(8,128)(2,1)S(1)}, bf16[8,4096]{1,0:T(8,128)(2,1)S(1)}, u32[]{:S(2)}, u32[]{:S(2)}) collective-permute-start(bf16[8,4096]{1,0:T(8,128)(2,1)S(1)} %get-tuple-element.7), channel_id=1, source_target_pairs={{0,1},{1,2},{2,3},{3,0},{4,5},{5,6},{6,7},{7,4},{8,9},{9,10},{10,1... | collective-permute-start | bytes 196616 | tf_op jit(solution)/shard_map/ppermute | solution.py:42

commit v2 on v1

--- a/solution.py
+++ b/solution.py
@@ -30,16 +30,9 @@
     tok_count = lax.axis_size("tok")
     tok_index = lax.axis_index("tok")
     parts = partial_features(proj_rows, doc_lengths[0], owner_map[0], tok_index * proj_rows.shape[0])
-    doc_dev = parts.shape[0] // tok_count
-
-    def share(shift):
-        start = ((tok_index + shift) % tok_count) * doc_dev
-        return lax.dynamic_slice_in_dim(parts, start, doc_dev, axis=0)
-
-    total = share(0).astype(jnp.float32)
-    for shift in range(1, tok_count):
-        pairs = [(i, (i + shift) % tok_count) for i in range(tok_count)]
-        total = total + lax.ppermute(share(shift), "tok", pairs).astype(jnp.float32)
+    shares = parts.reshape(tok_count, -1, parts.shape[1])
+    received = lax.all_to_all(shares, "tok", split_axis=0, concat_axis=0)
+    total = jnp.sum(received.astype(jnp.float32), axis=0)
     features = total.astype(jnp.bfloat16)
     return jnp.einsum(
         "qf,df->qd",

time: 29.3 us -> 32.7 us (1.12)
  blocking collectives: 9.87 us -> 24.9 us
  starting transfers between devices: 6.12 us -> 0 us
  waiting for transfers between devices: 5.45 us -> 0 us
    all_to_all x0 -> x1, blocking collectives: none -> 15 us  [body(): received = lax.all_to_all(shares, 'tok', split_axis=0, concat_axis=0)]
    ppermute x3 -> x0, starting transfers between devices: 6.12 us -> none  [body(): total = total + lax.ppermute(share(shift), 'tok', pairs).astype(jnp.float32)]
    ppermute x3 -> x0, waiting for transfers between devices: 5.45 us -> none  [body(): total = total + lax.ppermute(share(shift), 'tok', pairs).astype(jnp.float32)]
  transfers between devices with their start and end apart: 3 -> 0, of which waited for: 2 -> 0; matrix products, arithmetic and copies ran while one was open for 0% -> 0% of each run, Pallas kernels for 0% -> 0%
where the time goes in v2:
time: 32.7 us; the launch traced here: 32.5 us
  blocking collectives  24.9 us (76%)
  local copies, waits for them, and re-layouts  4.04 us (12%)
  other arithmetic  1.93 us (6%)
  matrix products  1.59 us (5%)
    all_to_all x1, blocking collectives, body(): received = lax.all_to_all(shares, 'tok', split_axis=0, concat_axis=0)  15 us
    all_gather x1, blocking collectives, body(): lax.all_gather(features, 'ex', axis=0, tiled=True)  9.87 us
    slice x2, local copies, waits for them, and re-layouts, partial_features(): rows[:, None, :width]  1.61 us
    dot_general x1, matrix products, partial_features(): jnp.einsum('ta,tb->ab', grads, inputs, preferred_element_type=jnp.float32)  1.26 us
    reshape x1, local copies, waits for them, and re-layouts  0.79 us
    reduce_sum x1, other arithmetic, partial_features(): slots = jnp.sum(jnp.where(inside, owner_slots[None, :], 0), axis=1)  0.78 us
    dot_general x1, local copies, waits for them, and re-layouts, body(): jnp.einsum('qf,df->qd', query_features, lax.all_gather(features, 'ex', ax...  0.7 us
    ge x1, other arithmetic, partial_features(): positions[:, None] >= (ends - lengths)[None, :]  0.66 us

profile of v2, /device:TPU:0, one launch (start us, length us, event | category | flops | bytes accessed | tf_op | source)
XLA Modules:
  0.0 32.5 jit_solution(7322541499041197437)
XLA Ops:
  0.0 0.0 copy-start
  0.0 0.8 %copy.13 = s32[32,1]{1,0:T(8,128)S(1)} copy(s32[32,1]{0,1:T(1,128)} %bitcast.41) | data formatting | bytes 256 | tf_op jit(solution)/shard_map/reshape
  0.8 0.1 reduce-window.4
  0.9 0.1 reduce.1
  1.0 0.7 %fusion.16 = s32[32]{0:T(128)S(1)} fusion(s32[1,32]{1,0:T(1,128)} %param.6, s32[32]{0:T(128)S(1)} %reduce.1), kind=kLoop, calls=%fused_computation.29 | loop fusion | flops 32 | bytes 384 | tf_op jit(solution)/shard_map/ge | solution.py:15
  1.6 0.8 %select_reduce_fusion = s32[2048]{0:T(1024)S(1)} fusion(s32[32]{0:T(128)} %bitcast.39, s32[2048]{0:T(1024)S(1)} %iota_add_fusion, s32[32]{0:T(128)S(1)} %reduce.1, s32[32]{0:T(128)S(1)} %fusion.16), kind=kLoop, calls=%fused_computation.14 | loop fusion | flops 325632 | bytes 16768 | tf_op jit(solution)/shard_map/reduce_sum | solution.py:16
  2.5 1.4 %fusion.18 = (bf16[2048,64]{1,0:T(8,128)(2,1)S(1)}, bf16[2048,64]{1,0:T(8,128)(2,1)S(1)}) fusion(bf16[2048,128]{1,0:T(8,128)(2,1)} %param.4), kind=kLoop, calls=%fused_computation.32 | loop fusion | bytes 1048576 | tf_op jit(solution)/shard_map/slice | solution.py:23
  3.9 0.2 copy.14
  4.1 0.2 copy.15
  4.3 1.3 %fusion.4 = f32[8,4,64,64]{3,2,1,0:T(8,128)S(1)} fusion(pred[2048,8]{0,1:T(8,128)(4,1)S(1)} %iota_compare_fusion, bf16[2048,64]{0,1:T(8,128)(2,1)S(1)} %copy.14, pred[2048,4]{0,1:T(4,128)(4,1)S(1)} %iota_compare_fusion.1, bf16[2048,64]{0,1:T(8,128)(2,1)S(1)} %copy.15), kind=kOutput, calls=%fused_computation.4 | convolution fusion | flops 538443776 | bytes 1073152 | tf_op jit(solution)/shard_map/ta,tb->ab/dot_general | solution.py:24
  5.6 0.0 copy-start.1
  5.6 0.0 copy-start.2
  5.6 0.4 %reshape.118 = f32[4,8,4096]{2,1,0:T(8,128)S(1)} reshape(f32[8,4,64,64]{3,2,1,0:T(8,128)S(1)} %fusion.4) | data formatting | bytes 1048576 | tf_op jit(solution)/shard_map/reshape | solution.py:25
  6.0 0.3 copy-done.1
  6.2 0.0 copy-done.2
  6.2 0.1 select_reduce_fusion.1
  6.4 0.1 sqrt.11
  6.5 0.1 divide_convert_fusion
  6.6 15.0 %all_to_all.5 = bf16[4,8,4096]{2,1,0:T(8,128)(2,1)S(1)} all-to-all(bf16[4,8,4096]{2,1,0:T(8,128)(2,1)S(1)} %divide_convert_fusion), channel_id=1, replica_groups=mesh['ex'=8,'tok'=4] {'tok'}, dimensions={0} | all-to-all | bytes 524288 | tf_op jit(solution)/shard_map/all_to_all | solution.py:34
  21.6 9.9 %all_gather.3 = bf16[64,4096]{1,0:T(8,128)(2,1)S(1)} all-gather(bf16[8,4096]{1,0:T(8,128)(2,1)S(1)} %reduce_sum.32), channel_id=1, replica_groups=mesh['ex'=8,'tok'=4] {'ex'}, dimensions={0}, use_global_device_ids=true | all-gather | bytes 589824 | tf_op jit(solution)/shard_map/all_gather | solution.py:40
  31.5 0.0 copy-done
  31.5 0.3 %convolution_bitcast_fusion = f32[64,64]{0,1:T(8,128)S(1)} fusion(bf16[64,4096]{1,0:T(8,128)(2,1)S(1)} %all_gather.3, bf16[64,4096]{1,0:T(8,128)(2,1)S(1)} %copy-done), kind=kOutput, calls=%fused_computation.5 | convolution fusion | flops 33554432 | bytes 1064960 | tf_op jit(solution)/shard_map/qf,df->qd/dot_general | solution.py:37
  31.8 0.7 %copy.16 = f32[64,64]{1,0:T(8,128)} copy(f32[64,64]{0,1:T(8,128)S(1)} %convolution_bitcast_fusion) | data formatting | bytes 32768 | tf_op jit(solution)/shard_map/qf,df->qd/dot_general | solution.py:37
  (6 shorter events, 0.1 us)
Async XLA Ops:
  0.0 31.5 %copy-start = (bf16[64,4096]{1,0:T(8,128)(2,1)S(1)}, bf16[64,4096]{1,0:T(8,128)(2,1)}, u32[]{:S(2)}) copy-start(bf16[64,4096]{1,0:T(8,128)(2,1)} %param.5) | copy-start | bytes 1572868
  5.6 0.7 %copy-start.1 = (s32[1,32]{1,0:T(1,128)S(1)}, s32[1,32]{1,0:T(1,128)}, u32[]{:S(2)}) copy-start(s32[1,32]{1,0:T(1,128)} %param.7) | copy-start | bytes 388
  5.6 0.7 %copy-start.2 = (s32[1,32]{1,0:T(1,128)S(1)}, s32[1,32]{1,0:T(1,128)}, u32[]{:S(2)}) copy-start(s32[1,32]{1,0:T(1,128)} %param.6) | copy-start | bytes 388

commit v3 on v2

v3 whole, which is shorter than its diff:
```python
import functools

import jax
import jax.numpy as jnp
from jax import lax
from jax.experimental import pallas as pl
from jax.experimental.pallas import tpu as pltpu
from jax.sharding import PartitionSpec as P

LANES = 128
ROW_BY_ROW = (((1,), (1,)), ((), ()))


def feature_kernel(lengths, owners, rows, *refs):
    *shares, grads, inputs, sums = refs
    count, width = rows.shape[0], rows.shape[1] // 2
    docs, tok_count = lengths.shape[1], len(shares)
    doc_dev = docs // tok_count
    tok = lax.axis_index("tok")

    blocks = count // LANES
    token = lax.broadcasted_iota(jnp.int32, (blocks, LANES), 0) * LANES
    token = tok * count + token + lax.broadcasted_iota(jnp.int32, (blocks, LANES), 1)
    share_of = jnp.zeros((blocks, LANES), jnp.int32)
    row_of = jnp.zeros((blocks, LANES), jnp.int32)
    size_row = lax.broadcasted_iota(jnp.int32, (doc_dev, LANES), 0)
    sizes = [jnp.ones((doc_dev, LANES), jnp.int32) for _ in shares]
    start = jnp.int32(0)
    for k in range(docs):
        slot = owners[0, k]
        share = lax.rem(lax.div(slot, doc_dev) - tok + tok_count, tok_count)
        row = lax.rem(slot, doc_dev)
        here = token >= start
        share_of = jnp.where(here, share, share_of)
        row_of = jnp.where(here, row, row_of)
        for s in range(tok_count):
            sizes[s] = jnp.where(size_row == jnp.where(share == s, row, -1), lengths[0, k], sizes[s])
        start = start + lengths[0, k]

    eye = (
        lax.broadcasted_iota(jnp.int32, (2 * width, 2 * width), 0)
        == lax.broadcasted_iota(jnp.int32, (2 * width, 2 * width), 1)
    ).astype(rows.dtype)
    for b in range(blocks):
        part = slice(b * LANES, (b + 1) * LANES)
        turned = lax.dot_general(eye, rows[part, :], ROW_BY_ROW, preferred_element_type=jnp.float32)
        for s in range(tok_count):
            kept = jnp.where(share_of[b : b + 1, :] == s, turned[:width], 0.0)
            inputs[s * width : (s + 1) * width, part] = kept.astype(inputs.dtype)
        for r in range(doc_dev):
            kept = jnp.where(row_of[b : b + 1, :] == r, turned[width:], 0.0)
            grads[r * width : (r + 1) * width, part] = kept.astype(grads.dtype)
    product = lax.dot_general(
        grads[...], inputs[...], ROW_BY_ROW, preferred_element_type=jnp.float32
    )
    for p in range(sums.shape[0]):
        sums[p] = product[:, p * LANES : (p + 1) * LANES]

    scales = [1.0 / jnp.sqrt(size.astype(jnp.float32)) for size in sizes]
    low_half = lax.broadcasted_iota(jnp.int32, (doc_dev, LANES), 1) < width
    for m in range(width // 2):
        out = slice(m * LANES, (m + 1) * LANES)
        for s in range(0, tok_count, 2):
            first = sums[s // 2, pl.ds(2 * m, doc_dev, stride=width), :]
            second = sums[s // 2, pl.ds(2 * m + 1, doc_dev, stride=width), :]
            left = jnp.where(low_half, first, pltpu.roll(second, width, 1))
            right = jnp.where(low_half, pltpu.roll(first, width, 1), second)
            shares[s][:, out] = (left * scales[s]).astype(shares[s].dtype)
            shares[s + 1][:, out] = (right * scales[s + 1]).astype(shares[s + 1].dtype)


def feature_shares(proj_rows, doc_lengths, owner_map, tok_count):
    count, width = proj_rows.shape[0], proj_rows.shape[1] // 2
    doc_dev = doc_lengths.shape[1] // tok_count
    feat = width * width
    small = pl.BlockSpec(memory_space=pltpu.SMEM)
    whole = pl.BlockSpec(memory_space=pltpu.VMEM)
    return pl.pallas_call(
        feature_kernel,
        out_shape=[
            jax.ShapeDtypeStruct((doc_dev, feat), jnp.bfloat16 if s else jnp.float32)
            for s in range(tok_count)
        ],
        in_specs=[small, small, whole],
        out_specs=[whole] * tok_count,
        scratch_shapes=[
            pltpu.VMEM((doc_dev * width, count), jnp.bfloat16),
            pltpu.VMEM((tok_count * width, count), jnp.bfloat16),
            pltpu.VMEM((tok_count // 2, doc_dev * width, LANES), jnp.float32),
        ],
        compiler_params=pltpu.CompilerParams(vmem_limit_bytes=32 * 1024 * 1024),
        name="features",
    )(doc_lengths, owner_map, proj_rows)


def body(proj_rows, query_features, doc_lengths, owner_map):
    tok_count = lax.axis_size("tok")
    shares = feature_shares(proj_rows, doc_lengths, owner_map, tok_count)
    total = shares[0]
    for shift in range(1, tok_count):
        pairs = [(i, (i + shift) % tok_count) for i in range(tok_count)]
        total = total + lax.ppermute(shares[shift], "tok", pairs).astype(jnp.float32)
    features = total.astype(jnp.bfloat16)
    return jnp.einsum(
        "qf,df->qd",
        query_features,
        lax.all_gather(features, "ex", axis=0, tiled=True),
        preferred_element_type=jnp.float32,
    )


def solution(mesh):
    placed = (P(("ex", "tok"), None), P("ex", None), P("ex", None), P("ex", None))
    return jax.shard_map(
        body, mesh=mesh, in_specs=placed, out_specs=P("ex", "tok"), check_vma=False
    )
```

time: 32.7 us -> 26.4 us (0.81)
  blocking collectives: 24.9 us -> 9.92 us
  starting transfers between devices: 0 us -> 7.02 us
  waiting for transfers between devices: 0 us -> 3.36 us
  Pallas kernels: 0 us -> 2.46 us
  other arithmetic: 1.93 us -> 0.04 us
  matrix products: 1.59 us -> 0.33 us
  local copies, waits for them, and re-layouts: 4.04 us -> 3.11 us
    all_to_all x1 -> x0, blocking collectives: 15 us -> none  [body(): received = lax.all_to_all(shares, 'tok', split_axis=0, concat_axis=0)]
    ppermute x0 -> x3, starting transfers between devices: none -> 7.02 us  [body(): lax.ppermute(shares[shift], 'tok', pairs).astype(jnp.float32)]
    ppermute x0 -> x3, waiting for transfers between devices: none -> 3.36 us  [body(): lax.ppermute(shares[shift], 'tok', pairs).astype(jnp.float32)]
    pallas_call x0 -> x1, Pallas kernels: none -> 2.46 us  [feature_shares(): pl.pallas_call(feature_kernel, out_shape=[jax.ShapeDtypeStruct((doc_dev,...]
    unnamed x6 -> x8, local copies, waits for them, and re-layouts: 0.3 us -> 2.41 us
    slice x3 -> x0, local copies, waits for them, and re-layouts: 1.8 us -> none  [the longest x2 1.61 us: partial_features(): rows[:, None, :width]]
    dot_general x1 -> x0, matrix products: 1.26 us -> none  [partial_features(): jnp.einsum('ta,tb->ab', grads, inputs, preferred_element_type=jnp.float32)]
    reshape x2 -> x0, local copies, waits for them, and re-layouts: 1.15 us -> none
  transfers between devices with their start and end apart: 0 -> 3, of which waited for: 0 -> 3; matrix products, arithmetic and copies ran while one was open for 0% -> 0% of each run, Pallas kernels for 0% -> 0%
where the time goes in v3:
time: 26.4 us; the launch traced here: 26.3 us
  blocking collectives  9.92 us (38%)
  starting transfers between devices  7.02 us (27%)
  waiting for transfers between devices  3.36 us (13%)
  local copies, waits for them, and re-layouts  3.11 us (12%)
  Pallas kernels  2.46 us (9%)
  matrix products  0.33 us (1%)
    all_gather x1, blocking collectives, body(): lax.all_gather(features, 'ex', axis=0, tiled=True)  9.92 us
    ppermute x3, starting transfers between devices, body(): lax.ppermute(shares[shift], 'tok', pairs).astype(jnp.float32)  7.02 us
    ppermute x3, waiting for transfers between devices, body(): lax.ppermute(shares[shift], 'tok', pairs).astype(jnp.float32)  3.36 us
    pallas_call x1, Pallas kernels, feature_shares(): pl.pallas_call(feature_kernel, out_shape=[jax.ShapeDtypeStruct((doc_dev,...  2.46 us
    unnamed x8, local copies, waits for them, and re-layouts  2.41 us
    dot_general x1, local copies, waits for them, and re-layouts, body(): jnp.einsum('qf,df->qd', query_features, lax.all_gather(features, 'ex', ax...  0.7 us
  transfers between devices with their start and end apart: 3, of which 3 were waited for; matrix products, arithmetic and copies ran while one was open for 0% of the time, Pallas kernels for 0%

profile of v3, /device:TPU:0, one launch (start us, length us, event | category | flops | bytes accessed | tf_op | source)
XLA Modules:
  0.0 26.3 jit_solution(8910002179904015371)
XLA Ops:
  0.0 0.0 copy-start
  0.0 0.0 copy-start.1
  0.0 1.1 %copy-done.1 = bf16[2048,128]{1,0:T(8,128)(2,1)S(1)} copy-done((bf16[2048,128]{1,0:T(8,128)(2,1)S(1)}, bf16[2048,128]{1,0:T(8,128)(2,1)}, u32[]{:S(2)}) %copy-start.1) | copy-done | bytes 524312
  1.1 0.0 copy-start.2
  1.1 0.7 %copy-done.2 = s32[1,32]{1,0:T(1,128)S(1)} copy-done((s32[1,32]{1,0:T(1,128)S(1)}, s32[1,32]{1,0:T(1,128)}, u32[]{:S(2)}) %copy-start.2) | copy-done | bytes 152
  1.8 0.0 copy-start.3
  1.8 0.7 %copy-done.3 = s32[1,32]{1,0:T(1,128)S(1)} copy-done((s32[1,32]{1,0:T(1,128)S(1)}, s32[1,32]{1,0:T(1,128)}, u32[]{:S(2)}) %copy-start.3) | copy-done | bytes 152
  2.4 2.5 %features.1 = (f32[8,4096]{1,0:T(8,128)S(1)}, bf16[8,4096]{1,0:T(8,128)(2,1)S(1)}, bf16[8,4096]{1,0:T(8,128)(2,1)S(1)}, bf16[8,4096]{1,0:T(8,128)(2,1)S(1)}) custom-call(s32[1,32]{1,0:T(1,128)S(1)} %copy-done.2, s32[1,32]{1,0:T(1,128)S(1)} %copy-done.3, bf16[2048,128]{1,0:T(8,128)(2,1)S(1)} %copy-done.1), custom_call_target="tpu_custom_call" | custom-call | tf_op jit(solution)/shard_map/features/pallas_call | solution.py:78
  4.9 3.1 %collective-permute-start = (bf16[8,4096]{1,0:T(8,128)(2,1)S(1)}, bf16[8,4096]{1,0:T(8,128)(2,1)S(1)}, u32[]{:S(2)}, u32[]{:S(2)}) collective-permute-start(bf16[8,4096]{1,0:T(8,128)(2,1)S(1)} %get-tuple-element.10), channel_id=1, source_target_pairs={{0,1},{1,2},{2,3},{3,0},{4,5},{5,6},{6,7},{7,4},{8,9},{9,10},{10,1... | collective-permute-start | bytes 196616 | tf_op jit(solution)/shard_map/ppermute | solution.py:102
  8.0 2.6 %collective-permute-start.1 = (bf16[8,4096]{1,0:T(8,128)(2,1)S(1)}, bf16[8,4096]{1,0:T(8,128)(2,1)S(1)}, u32[]{:S(2)}, u32[]{:S(2)}) collective-permute-start(bf16[8,4096]{1,0:T(8,128)(2,1)S(1)} %get-tuple-element.11), channel_id=1, source_target_pairs={{0,2},{1,3},{2,0},{3,1},{4,6},{5,7},{6,4},{7,5},{8,10},{9,11},{10,... | collective-permute-start | bytes 196616 | tf_op jit(solution)/shard_map/ppermute | solution.py:102
  10.5 1.4 %collective-permute-start.2 = (bf16[8,4096]{1,0:T(8,128)(2,1)S(1)}, bf16[8,4096]{1,0:T(8,128)(2,1)S(1)}, u32[]{:S(2)}, u32[]{:S(2)}) collective-permute-start(bf16[8,4096]{1,0:T(8,128)(2,1)S(1)} %get-tuple-element.12), channel_id=1, source_target_pairs={{0,3},{1,0},{2,1},{3,2},{4,7},{5,4},{6,5},{7,6},{8,11},{9,8},{10,9... | collective-permute-start | bytes 196616 | tf_op jit(solution)/shard_map/ppermute | solution.py:102
  11.9 0.6 %collective-permute-done = bf16[8,4096]{1,0:T(8,128)(2,1)S(1)} collective-permute-done((bf16[8,4096]{1,0:T(8,128)(2,1)S(1)}, bf16[8,4096]{1,0:T(8,128)(2,1)S(1)}, u32[]{:S(2)}, u32[]{:S(2)}) %collective-permute-start) | collective-permute-done | bytes 65568 | tf_op jit(solution)/shard_map/ppermute | solution.py:102
  12.5 2.5 %collective-permute-done.1 = bf16[8,4096]{1,0:T(8,128)(2,1)S(1)} collective-permute-done((bf16[8,4096]{1,0:T(8,128)(2,1)S(1)}, bf16[8,4096]{1,0:T(8,128)(2,1)S(1)}, u32[]{:S(2)}, u32[]{:S(2)}) %collective-permute-start.1) | collective-permute-done | bytes 65568 | tf_op jit(solution)/shard_map/ppermute | solution.py:102
  15.0 0.2 collective-permute-done.2
  15.3 9.9 %all_gather.3 = bf16[64,4096]{1,0:T(8,128)(2,1)S(1)} all-gather(bf16[8,4096]{1,0:T(8,128)(2,1)S(1)} %add_convert_fusion), channel_id=1, replica_groups=mesh['ex'=8,'tok'=4] {'ex'}, dimensions={0}, use_global_device_ids=true | all-gather | bytes 589824 | tf_op jit(solution)/shard_map/all_gather | solution.py:107
  25.2 0.0 copy-done
  25.2 0.3 %convolution_bitcast_fusion = f32[64,64]{0,1:T(8,128)S(1)} fusion(bf16[64,4096]{1,0:T(8,128)(2,1)S(1)} %all_gather.3, bf16[64,4096]{1,0:T(8,128)(2,1)S(1)} %copy-done), kind=kOutput, calls=%fused_computation | convolution fusion | flops 33554432 | bytes 1064960 | tf_op jit(solution)/shard_map/qf,df->qd/dot_general | solution.py:104
  25.6 0.7 %copy.5 = f32[64,64]{1,0:T(8,128)} copy(f32[64,64]{0,1:T(8,128)S(1)} %convolution_bitcast_fusion) | data formatting | bytes 32768 | tf_op jit(solution)/shard_map/qf,df->qd/dot_general | solution.py:104
  (1 shorter events, 0.0 us)
Async XLA Ops:
  0.0 25.2 %copy-start = (bf16[64,4096]{1,0:T(8,128)(2,1)S(1)}, bf16[64,4096]{1,0:T(8,128)(2,1)}, u32[]{:S(2)}) copy-start(bf16[64,4096]{1,0:T(8,128)(2,1)} %param.5) | copy-start | bytes 1572868
  0.0 1.1 %copy-start.1 = (bf16[2048,128]{1,0:T(8,128)(2,1)S(1)}, bf16[2048,128]{1,0:T(8,128)(2,1)}, u32[]{:S(2)}) copy-start(bf16[2048,128]{1,0:T(8,128)(2,1)} %rows.1) | copy-start | bytes 1572868
  1.1 0.7 %copy-start.2 = (s32[1,32]{1,0:T(1,128)S(1)}, s32[1,32]{1,0:T(1,128)}, u32[]{:S(2)}) copy-start(s32[1,32]{1,0:T(1,128)} %lengths.1) | copy-start | bytes 388
  1.8 0.7 %copy-start.3 = (s32[1,32]{1,0:T(1,128)S(1)}, s32[1,32]{1,0:T(1,128)}, u32[]{:S(2)}) copy-start(s32[1,32]{1,0:T(1,128)} %owners.1) | copy-start | bytes 388
  4.9 7.6 %collective-permute-start = (bf16[8,4096]{1,0:T(8,128)(2,1)S(1)}, bf16[8,4096]{1,0:T(8,128)(2,1)S(1)}, u32[]{:S(2)}, u32[]{:S(2)}) collective-permute-start(bf16[8,4096]{1,0:T(8,128)(2,1)S(1)} %get-tuple-element.10), channel_id=1, source_target_pairs={{0,1},{1,2},{2,3},{3,0},{4,5},{5,6},{6,7},{7,4},{8,9},{9,10},{10,1... | collective-permute-start | bytes 196616 | tf_op jit(solution)/shard_map/ppermute | solution.py:102
  8.0 7.1 %collective-permute-start.1 = (bf16[8,4096]{1,0:T(8,128)(2,1)S(1)}, bf16[8,4096]{1,0:T(8,128)(2,1)S(1)}, u32[]{:S(2)}, u32[]{:S(2)}) collective-permute-start(bf16[8,4096]{1,0:T(8,128)(2,1)S(1)} %get-tuple-element.11), channel_id=1, source_target_pairs={{0,2},{1,3},{2,0},{3,1},{4,6},{5,7},{6,4},{7,5},{8,10},{9,11},{10,... | collective-permute-start | bytes 196616 | tf_op jit(solution)/shard_map/ppermute | solution.py:102
  10.5 4.7 %collective-permute-start.2 = (bf16[8,4096]{1,0:T(8,128)(2,1)S(1)}, bf16[8,4096]{1,0:T(8,128)(2,1)S(1)}, u32[]{:S(2)}, u32[]{:S(2)}) collective-permute-start(bf16[8,4096]{1,0:T(8,128)(2,1)S(1)} %get-tuple-element.12), channel_id=1, source_target_pairs={{0,3},{1,0},{2,1},{3,2},{4,7},{5,4},{6,5},{7,6},{8,11},{9,8},{10,9... | collective-permute-start | bytes 196616 | tf_op jit(solution)/shard_map/ppermute | solution.py:102

commit v4 on v3

--- a/solution.py
+++ b/solution.py
@@ -1,5 +1,3 @@
-import functools
-
 import jax
 import jax.numpy as jnp
 from jax import lax
@@ -11,13 +9,23 @@
 ROW_BY_ROW = (((1,), (1,)), ((), ()))
 
 
-def feature_kernel(lengths, owners, rows, *refs):
-    *shares, grads, inputs, sums = refs
+def feature_kernel(lengths_hbm, owners_hbm, rows_hbm, *refs):
+    *shares, lengths, owners, rows, grads, inputs, sums, arrived = refs
     count, width = rows.shape[0], rows.shape[1] // 2
+    copies = [
+        pltpu.make_async_copy(source, target, arrived.at[i])
+        for i, (source, target) in enumerate(
+            ((lengths_hbm, lengths), (owners_hbm, owners), (rows_hbm, rows))
+        )
+    ]
+    for copy in copies:
+        copy.start()
     docs, tok_count = lengths.shape[1], len(shares)
     doc_dev = docs // tok_count
     tok = lax.axis_index("tok")
 
+    copies[0].wait()
+    copies[1].wait()
     blocks = count // LANES
     token = lax.broadcasted_iota(jnp.int32, (blocks, LANES), 0) * LANES
     token = tok * count + token + lax.broadcasted_iota(jnp.int32, (blocks, LANES), 1)
@@ -41,6 +49,7 @@
         lax.broadcasted_iota(jnp.int32, (2 * width, 2 * width), 0)
         == lax.broadcasted_iota(jnp.int32, (2 * width, 2 * width), 1)
     ).astype(rows.dtype)
+    copies[2].wait()
     for b in range(blocks):
         part = slice(b * LANES, (b + 1) * LANES)
         turned = lax.dot_general(eye, rows[part, :], ROW_BY_ROW, preferred_element_type=jnp.float32)
@@ -73,7 +82,7 @@
     count, width = proj_rows.shape[0], proj_rows.shape[1] // 2
     doc_dev = doc_lengths.shape[1] // tok_count
     feat = width * width
-    small = pl.BlockSpec(memory_space=pltpu.SMEM)
+    far = pl.BlockSpec(memory_space=pltpu.HBM)
     whole = pl.BlockSpec(memory_space=pltpu.VMEM)
     return pl.pallas_call(
         feature_kernel,
@@ -81,16 +90,49 @@
             jax.ShapeDtypeStruct((doc_dev, feat), jnp.bfloat16 if s else jnp.float32)
             for s in range(tok_count)
         ],
-        in_specs=[small, small, whole],
+        in_specs=[far, far, far],
         out_specs=[whole] * tok_count,
         scratch_shapes=[
+            pltpu.SMEM(doc_lengths.shape, jnp.int32),
+            pltpu.SMEM(owner_map.shape, jnp.int32),
+            pltpu.VMEM(proj_rows.shape, proj_rows.dtype),
             pltpu.VMEM((doc_dev * width, count), jnp.bfloat16),
             pltpu.VMEM((tok_count * width, count), jnp.bfloat16),
             pltpu.VMEM((tok_count // 2, doc_dev * width, LANES), jnp.float32),
+            pltpu.SemaphoreType.DMA((3,)),
         ],
         compiler_params=pltpu.CompilerParams(vmem_limit_bytes=32 * 1024 * 1024),
         name="features",
     )(doc_lengths, owner_map, proj_rows)
+
+
+def score_kernel(query, *refs):
+    *blocks, scores = refs
+    doc_dev = blocks[0].shape[0]
+    features = jnp.concatenate([block[...] for block in blocks], axis=0)
+    products = lax.dot_general(
+        features, query[...], ROW_BY_ROW, preferred_element_type=jnp.float32
+    )
+    parts = [products[i * doc_dev : (i + 1) * doc_dev] for i in range(len(blocks))]
+    ex = lax.axis_index("ex")
+    flip = 1
+    while flip < len(blocks):
+        swap = lax.rem(lax.div(ex, flip), 2) == 1
+        parts = [jnp.where(swap, parts[i ^ flip], parts[i]) for i in range(len(parts))]
+        flip *= 2
+    scores[...] = jnp.concatenate(parts, axis=0).T
+
+
+def block_scores(query_features, blocks):
+    whole = pl.BlockSpec(memory_space=pltpu.VMEM)
+    docs = len(blocks) * blocks[0].shape[0]
+    return pl.pallas_call(
+        score_kernel,
+        out_shape=jax.ShapeDtypeStruct((query_features.shape[0], docs), jnp.float32),
+        in_specs=[whole] * (1 + len(blocks)),
+        out_specs=whole,
+        name="scores",
+    )(query_features, *blocks)
 
 
 def body(proj_rows, query_features, doc_lengths, owner_map):
@@ -101,12 +143,14 @@
         pairs = [(i, (i + shift) % tok_count) for i in range(tok_count)]
         total = total + lax.ppermute(shares[shift], "tok", pairs).astype(jnp.float32)
     features = total.astype(jnp.bfloat16)
-    return jnp.einsum(
-        "qf,df->qd",
-        query_features,
-        lax.all_gather(features, "ex", axis=0, tiled=True),
-        preferred_element_type=jnp.float32,
-    )
+    ex_count = lax.axis_size("ex")
+    if ex_count not in (2, 4, 8):
+        gathered = lax.all_gather(features, "ex", axis=0, tiled=True)
+        return jnp.einsum("qf,df->qd", query_features, gathered, preferred_element_type=jnp.float32)
+    blocks = [features] + [None] * (ex_count - 1)
+    for flip in range(ex_count - 1, 0, -1):
+        blocks[flip] = lax.ppermute(features, "ex", [(i, i ^ flip) for i in range(ex_count)])
+    return block_scores(query_features, blocks)
 
 
 def solution(mesh):

time: 26.4 us -> 29.4 us (1.11)
  blocking collectives: 9.92 us -> 0 us
  starting transfers between devices: 7.02 us -> 13.8 us
  waiting for transfers between devices: 3.36 us -> 6.83 us
  Pallas kernels: 2.46 us -> 4.94 us
  local copies, waits for them, and re-layouts: 3.11 us -> 3.55 us
  matrix products: 0.33 us -> 0 us
    all_gather x1 -> x0, blocking collectives: 9.92 us -> none  [body(): lax.all_gather(features, 'ex', axis=0, tiled=True)]
    ppermute x0 -> x7, starting transfers between devices: none -> 6.77 us  [body(): lax.ppermute(features, 'ex', [(i, i ^ flip) for i in range(ex_count)])]
    ppermute x0 -> x7, waiting for transfers between devices: none -> 3.47 us  [body(): lax.ppermute(features, 'ex', [(i, i ^ flip) for i in range(ex_count)])]
    pallas_call x0 -> x1, Pallas kernels: none -> 2.18 us  [block_scores(): pl.pallas_call(score_kernel, out_shape=jax.ShapeDtypeStruct((query_featur...]
    unnamed x8 -> x22, local copies, waits for them, and re-layouts: 2.41 us -> 3.55 us
    dot_general x1 -> x0, local copies, waits for them, and re-layouts: 0.7 us -> none  [body(): jnp.einsum('qf,df->qd', query_features, lax.all_gather(features, 'ex', ax...]
    dot_general x1 -> x0, matrix products: 0.33 us -> none  [body(): jnp.einsum('qf,df->qd', query_features, lax.all_gather(features, 'ex', ax...]
    pallas_call x1, Pallas kernels: 2.46 us -> 2.76 us  [feature_shares(): pl.pallas_call(feature_kernel, out_shape=[jax.ShapeDtypeStruct((doc_dev,...]
  transfers between devices with their start and end apart: 3 -> 10, of which waited for: 3 -> 6; matrix products, arithmetic and copies ran while one was open for 0% -> 0% of each run, Pallas kernels for 0% -> 0%
where the time goes in v4:
time: 29.4 us; the launch traced here: 29.2 us
  starting transfers between devices  13.8 us (47%)
  waiting for transfers between devices  6.83 us (23%)
  Pallas kernels  4.94 us (17%)
  local copies, waits for them, and re-layouts  3.55 us (12%)
    ppermute x3, starting transfers between devices, body(): lax.ppermute(shares[shift], 'tok', pairs).astype(jnp.float32)  7.01 us
    ppermute x7, starting transfers between devices, body(): lax.ppermute(features, 'ex', [(i, i ^ flip) for i in range(ex_count)])  6.77 us
    unnamed x22, local copies, waits for them, and re-layouts  3.55 us
    ppermute x7, waiting for transfers between devices, body(): lax.ppermute(features, 'ex', [(i, i ^ flip) for i in range(ex_count)])  3.47 us
    ppermute x3, waiting for transfers between devices, body(): lax.ppermute(shares[shift], 'tok', pairs).astype(jnp.float32)  3.37 us
    pallas_call x1, Pallas kernels, feature_shares(): pl.pallas_call(feature_kernel, out_shape=[jax.ShapeDtypeStruct((doc_dev,...  2.76 us
    pallas_call x1, Pallas kernels, block_scores(): pl.pallas_call(score_kernel, out_shape=jax.ShapeDtypeStruct((query_featur...  2.18 us
  transfers between devices with their start and end apart: 10, of which 6 were waited for; matrix products, arithmetic and copies ran while one was open for 0% of the time, Pallas kernels for 0%

profile of v4, /device:TPU:0, one launch (start us, length us, event | category | flops | bytes accessed | tf_op | source)
XLA Modules:
  0.0 29.2 jit_solution(3426173120916664744)
XLA Ops:
  0.0 1.0 %copy-done = bf16[2048,128]{1,0:T(8,128)(2,1)S(1)} copy-done((bf16[2048,128]{1,0:T(8,128)(2,1)S(1)}, bf16[2048,128]{1,0:T(8,128)(2,1)}, u32[]{:S(2)}) %copy-start) | copy-done | bytes 524312
  1.0 0.7 %copy-done.1 = s32[1,32]{1,0:T(1,128)S(1)} copy-done((s32[1,32]{1,0:T(1,128)S(1)}, s32[1,32]{1,0:T(1,128)}, u32[]{:S(2)}) %copy-start.1) | copy-done | bytes 152
  1.7 0.7 %copy-done.2 = s32[1,32]{1,0:T(1,128)S(1)} copy-done((s32[1,32]{1,0:T(1,128)S(1)}, s32[1,32]{1,0:T(1,128)}, u32[]{:S(2)}) %copy-start.2) | copy-done | bytes 152
  2.4 2.8 %features.1 = (f32[8,4096]{1,0:T(8,128)S(1)}, bf16[8,4096]{1,0:T(8,128)(2,1)S(1)}, bf16[8,4096]{1,0:T(8,128)(2,1)S(1)}, bf16[8,4096]{1,0:T(8,128)(2,1)S(1)}) custom-call(s32[1,32]{1,0:T(1,128)S(1)} %copy-done.1, s32[1,32]{1,0:T(1,128)S(1)} %copy-done.2, bf16[2048,128]{1,0:T(8,128)(2,1)S(1)} %copy-done), custom_call_target="tpu_custom_call" | custom-call | tf_op jit(solution)/shard_map/features/pallas_call | solution.py:87
  5.1 3.1 %collective-permute-start = (bf16[8,4096]{1,0:T(8,128)(2,1)S(1)}, bf16[8,4096]{1,0:T(8,128)(2,1)S(1)}, u32[]{:S(2)}, u32[]{:S(2)}) collective-permute-start(bf16[8,4096]{1,0:T(8,128)(2,1)S(1)} %get-tuple-element.10), channel_id=1, source_target_pairs={{0,1},{1,2},{2,3},{3,0},{4,5},{5,6},{6,7},{7,4},{8,9},{9,10},{10,1... | collective-permute-start | bytes 196616 | tf_op jit(solution)/shard_map/ppermute | solution.py:144
  8.2 2.6 %collective-permute-start.1 = (bf16[8,4096]{1,0:T(8,128)(2,1)S(1)}, bf16[8,4096]{1,0:T(8,128)(2,1)S(1)}, u32[]{:S(2)}, u32[]{:S(2)}) collective-permute-start(bf16[8,4096]{1,0:T(8,128)(2,1)S(1)} %get-tuple-element.11), channel_id=1, source_target_pairs={{0,2},{1,3},{2,0},{3,1},{4,6},{5,7},{6,4},{7,5},{8,10},{9,11},{10,... | collective-permute-start | bytes 196616 | tf_op jit(solution)/shard_map/ppermute | solution.py:144
  10.8 1.3 %collective-permute-start.2 = (bf16[8,4096]{1,0:T(8,128)(2,1)S(1)}, bf16[8,4096]{1,0:T(8,128)(2,1)S(1)}, u32[]{:S(2)}, u32[]{:S(2)}) collective-permute-start(bf16[8,4096]{1,0:T(8,128)(2,1)S(1)} %get-tuple-element.12), channel_id=1, source_target_pairs={{0,3},{1,0},{2,1},{3,2},{4,7},{5,4},{6,5},{7,6},{8,11},{9,8},{10,9... | collective-permute-start | bytes 196616 | tf_op jit(solution)/shard_map/ppermute | solution.py:144
  12.1 0.6 %collective-permute-done = bf16[8,4096]{1,0:T(8,128)(2,1)S(1)} collective-permute-done((bf16[8,4096]{1,0:T(8,128)(2,1)S(1)}, bf16[8,4096]{1,0:T(8,128)(2,1)S(1)}, u32[]{:S(2)}, u32[]{:S(2)}) %collective-permute-start) | collective-permute-done | bytes 65568 | tf_op jit(solution)/shard_map/ppermute | solution.py:144
  12.8 2.5 %collective-permute-done.1 = bf16[8,4096]{1,0:T(8,128)(2,1)S(1)} collective-permute-done((bf16[8,4096]{1,0:T(8,128)(2,1)S(1)}, bf16[8,4096]{1,0:T(8,128)(2,1)S(1)}, u32[]{:S(2)}, u32[]{:S(2)}) %collective-permute-start.1) | collective-permute-done | bytes 65568 | tf_op jit(solution)/shard_map/ppermute | solution.py:144
  15.3 0.2 collective-permute-done.2
  15.6 1.0 %collective-permute-start.9 = (bf16[8,4096]{1,0:T(8,128)(2,1)S(1)}, bf16[8,4096]{1,0:T(8,128)(2,1)S(1)}, u32[]{:S(2)}, u32[]{:S(2)}) collective-permute-start(bf16[8,4096]{1,0:T(8,128)(2,1)S(1)} %add_convert_fusion.refs_0_), channel_id=1, source_target_pairs={{0,28},{4,24},{8,20},{12,16},{16,12},{20,8},{24,4},{28,0},{1,29},{... | collective-permute-start | bytes 196616 | tf_op jit(solution)/shard_map/ppermute | solution.py:152
  16.5 1.6 %collective-permute-start.8 = (bf16[8,4096]{1,0:T(8,128)(2,1)S(1)}, bf16[8,4096]{1,0:T(8,128)(2,1)S(1)}, u32[]{:S(2)}, u32[]{:S(2)}) collective-permute-start(bf16[8,4096]{1,0:T(8,128)(2,1)S(1)} %add_convert_fusion.refs_0_), channel_id=1, source_target_pairs={{0,24},{4,28},{8,16},{12,20},{16,8},{20,12},{24,0},{28,4},{1,25},{... | collective-permute-start | bytes 196616 | tf_op jit(solution)/shard_map/ppermute | solution.py:152
  18.2 1.4 %collective-permute-start.7 = (bf16[8,4096]{1,0:T(8,128)(2,1)S(1)}, bf16[8,4096]{1,0:T(8,128)(2,1)S(1)}, u32[]{:S(2)}, u32[]{:S(2)}) collective-permute-start(bf16[8,4096]{1,0:T(8,128)(2,1)S(1)} %add_convert_fusion.refs_0_), channel_id=1, source_target_pairs={{0,20},{4,16},{8,28},{12,24},{16,4},{20,0},{24,12},{28,8},{1,21},{... | collective-permute-start | bytes 196616 | tf_op jit(solution)/shard_map/ppermute | solution.py:152
  19.6 0.5 %collective-permute-start.6 = (bf16[8,4096]{1,0:T(8,128)(2,1)S(1)}, bf16[8,4096]{1,0:T(8,128)(2,1)S(1)}, u32[]{:S(2)}, u32[]{:S(2)}) collective-permute-start(bf16[8,4096]{1,0:T(8,128)(2,1)S(1)} %add_convert_fusion.refs_0_), channel_id=1, source_target_pairs={{0,16},{4,20},{8,24},{12,28},{16,0},{20,4},{24,8},{28,12},{1,17},{... | collective-permute-start | bytes 196616 | tf_op jit(solution)/shard_map/ppermute | solution.py:152
  20.0 0.8 %collective-permute-start.5 = (bf16[8,4096]{1,0:T(8,128)(2,1)S(1)}, bf16[8,4096]{1,0:T(8,128)(2,1)S(1)}, u32[]{:S(2)}, u32[]{:S(2)}) collective-permute-start(bf16[8,4096]{1,0:T(8,128)(2,1)S(1)} %add_convert_fusion.refs_0_), channel_id=1, source_target_pairs={{0,12},{4,8},{8,4},{12,0},{16,28},{20,24},{24,20},{28,16},{1,13},{... | collective-permute-start | bytes 196616 | tf_op jit(solution)/shard_map/ppermute | solution.py:152
  20.8 1.0 %collective-permute-start.4 = (bf16[8,4096]{1,0:T(8,128)(2,1)S(1)}, bf16[8,4096]{1,0:T(8,128)(2,1)S(1)}, u32[]{:S(2)}, u32[]{:S(2)}) collective-permute-start(bf16[8,4096]{1,0:T(8,128)(2,1)S(1)} %add_convert_fusion.refs_0_), channel_id=1, source_target_pairs={{0,8},{4,12},{8,0},{12,4},{16,24},{20,28},{24,16},{28,20},{1,9},{5... | collective-permute-start | bytes 196616 | tf_op jit(solution)/shard_map/ppermute | solution.py:152
  21.9 0.5 %collective-permute-start.3 = (bf16[8,4096]{1,0:T(8,128)(2,1)S(1)}, bf16[8,4096]{1,0:T(8,128)(2,1)S(1)}, u32[]{:S(2)}, u32[]{:S(2)}) collective-permute-start(bf16[8,4096]{1,0:T(8,128)(2,1)S(1)} %add_convert_fusion.refs_0_), channel_id=1, source_target_pairs={{0,4},{4,0},{8,12},{12,8},{16,20},{20,16},{24,28},{28,24},{1,5},{5... | collective-permute-start | bytes 196616 | tf_op jit(solution)/shard_map/ppermute | solution.py:152
  22.3 1.4 %collective-permute-done.7.refs_5_ = bf16[8,4096]{1,0:T(8,128)(2,1)S(1)} collective-permute-done((bf16[8,4096]{1,0:T(8,128)(2,1)S(1)}, bf16[8,4096]{1,0:T(8,128)(2,1)S(1)}, u32[]{:S(2)}, u32[]{:S(2)}) %collective-permute-start.7) | collective-permute-done | bytes 65568 | tf_op jit(solution)/shard_map/ppermute | solution.py:152
  23.8 1.4 %collective-permute-done.6.refs_4_ = bf16[8,4096]{1,0:T(8,128)(2,1)S(1)} collective-permute-done((bf16[8,4096]{1,0:T(8,128)(2,1)S(1)}, bf16[8,4096]{1,0:T(8,128)(2,1)S(1)}, u32[]{:S(2)}, u32[]{:S(2)}) %collective-permute-start.6) | collective-permute-done | bytes 65568 | tf_op jit(solution)/shard_map/ppermute | solution.py:152
  25.2 0.6 %collective-permute-done.4.refs_2_ = bf16[8,4096]{1,0:T(8,128)(2,1)S(1)} collective-permute-done((bf16[8,4096]{1,0:T(8,128)(2,1)S(1)}, bf16[8,4096]{1,0:T(8,128)(2,1)S(1)}, u32[]{:S(2)}, u32[]{:S(2)}) %collective-permute-start.4) | collective-permute-done | bytes 65568 | tf_op jit(solution)/shard_map/ppermute | solution.py:152
  25.9 0.0 copy-done.8
  25.9 0.5 %copy-done.9 = bf16[8,4096]{1,0:T(8,128)(2,1)} copy-done((bf16[8,4096]{1,0:T(8,128)(2,1)}, bf16[8,4096]{1,0:T(8,128)(2,1)S(1)}, u32[]{:S(2)}) %copy-start.9) | copy-done | bytes 65560
  26.4 0.6 %copy-done.10 = bf16[8,4096]{1,0:T(8,128)(2,1)} copy-done((bf16[8,4096]{1,0:T(8,128)(2,1)}, bf16[8,4096]{1,0:T(8,128)(2,1)S(1)}, u32[]{:S(2)}) %copy-start.10) | copy-done | bytes 65560
  27.0 2.2 %scores.1 = f32[64,64]{1,0:T(8,128)} custom-call(bf16[64,4096]{1,0:T(8,128)(2,1)} %query.1, bf16[8,4096]{1,0:T(8,128)(2,1)} %copy-done.3, bf16[8,4096]{1,0:T(8,128)(2,1)} %copy-done.10, bf16[8,4096]{1,0:T(8,128)(2,1)} %copy-done.9, bf16[8,4096]{1,0:T(8,128)(2,1)} %copy-done.8, bf16[8,4096]{1,0:T(8,128)(2,1)} %copy-done.7, bf16[8,4096]{1,0:T(8,128)(2,1)} %copy-done.6, ...), custom_call_target="tpu_custom_call" | custom-call | tf_op jit(solution)/shard_map/scores/pallas_call | solution.py:129
  (21 shorter events, 0.1 us)
Async XLA Ops:
  0.0 1.0 %copy-start = (bf16[2048,128]{1,0:T(8,128)(2,1)S(1)}, bf16[2048,128]{1,0:T(8,128)(2,1)}, u32[]{:S(2)}) copy-start(bf16[2048,128]{1,0:T(8,128)(2,1)} %rows_hbm.1) | copy-start | bytes 1572868
  1.0 0.7 %copy-start.1 = (s32[1,32]{1,0:T(1,128)S(1)}, s32[1,32]{1,0:T(1,128)}, u32[]{:S(2)}) copy-start(s32[1,32]{1,0:T(1,128)} %lengths_hbm.1) | copy-start | bytes 388
  1.7 0.7 %copy-start.2 = (s32[1,32]{1,0:T(1,128)S(1)}, s32[1,32]{1,0:T(1,128)}, u32[]{:S(2)}) copy-start(s32[1,32]{1,0:T(1,128)} %owners_hbm.1) | copy-start | bytes 388
  5.1 7.6 %collective-permute-start = (bf16[8,4096]{1,0:T(8,128)(2,1)S(1)}, bf16[8,4096]{1,0:T(8,128)(2,1)S(1)}, u32[]{:S(2)}, u32[]{:S(2)}) collective-permute-start(bf16[8,4096]{1,0:T(8,128)(2,1)S(1)} %get-tuple-element.10), channel_id=1, source_target_pairs={{0,1},{1,2},{2,3},{3,0},{4,5},{5,6},{6,7},{7,4},{8,9},{9,10},{10,1... | collective-permute-start | bytes 196616 | tf_op jit(solution)/shard_map/ppermute | solution.py:144
  8.2 7.1 %collective-permute-start.1 = (bf16[8,4096]{1,0:T(8,128)(2,1)S(1)}, bf16[8,4096]{1,0:T(8,128)(2,1)S(1)}, u32[]{:S(2)}, u32[]{:S(2)}) collective-permute-start(bf16[8,4096]{1,0:T(8,128)(2,1)S(1)} %get-tuple-element.11), channel_id=1, source_target_pairs={{0,2},{1,3},{2,0},{3,1},{4,6},{5,7},{6,4},{7,5},{8,10},{9,11},{10,... | collective-permute-start | bytes 196616 | tf_op jit(solution)/shard_map/ppermute | solution.py:144
  10.8 4.7 %collective-permute-start.2 = (bf16[8,4096]{1,0:T(8,128)(2,1)S(1)}, bf16[8,4096]{1,0:T(8,128)(2,1)S(1)}, u32[]{:S(2)}, u32[]{:S(2)}) collective-permute-start(bf16[8,4096]{1,0:T(8,128)(2,1)S(1)} %get-tuple-element.12), channel_id=1, source_target_pairs={{0,3},{1,0},{2,1},{3,2},{4,7},{5,4},{6,5},{7,6},{8,11},{9,8},{10,9... | collective-permute-start | bytes 196616 | tf_op jit(solution)/shard_map/ppermute | solution.py:144
  15.5 10.3 %copy-start.3 = (bf16[8,4096]{1,0:T(8,128)(2,1)}, bf16[8,4096]{1,0:T(8,128)(2,1)S(1)}, u32[]{:S(2)}) copy-start(bf16[8,4096]{1,0:T(8,128)(2,1)S(1)} %add_convert_fusion.refs_0_) | copy-start | bytes 196612
  15.6 5.2 %collective-permute-start.9 = (bf16[8,4096]{1,0:T(8,128)(2,1)S(1)}, bf16[8,4096]{1,0:T(8,128)(2,1)S(1)}, u32[]{:S(2)}, u32[]{:S(2)}) collective-permute-start(bf16[8,4096]{1,0:T(8,128)(2,1)S(1)} %add_convert_fusion.refs_0_), channel_id=1, source_target_pairs={{0,28},{4,24},{8,20},{12,16},{16,12},{20,8},{24,4},{28,0},{1,29},{... | collective-permute-start | bytes 196616 | tf_op jit(solution)/shard_map/ppermute | solution.py:152
  16.5 5.3 %collective-permute-start.8 = (bf16[8,4096]{1,0:T(8,128)(2,1)S(1)}, bf16[8,4096]{1,0:T(8,128)(2,1)S(1)}, u32[]{:S(2)}, u32[]{:S(2)}) collective-permute-start(bf16[8,4096]{1,0:T(8,128)(2,1)S(1)} %add_convert_fusion.refs_0_), channel_id=1, source_target_pairs={{0,24},{4,28},{8,16},{12,20},{16,8},{20,12},{24,0},{28,4},{1,25},{... | collective-permute-start | bytes 196616 | tf_op jit(solution)/shard_map/ppermute | solution.py:152
  18.2 5.6 %collective-permute-start.7 = (bf16[8,4096]{1,0:T(8,128)(2,1)S(1)}, bf16[8,4096]{1,0:T(8,128)(2,1)S(1)}, u32[]{:S(2)}, u32[]{:S(2)}) collective-permute-start(bf16[8,4096]{1,0:T(8,128)(2,1)S(1)} %add_convert_fusion.refs_0_), channel_id=1, source_target_pairs={{0,20},{4,16},{8,28},{12,24},{16,4},{20,0},{24,12},{28,8},{1,21},{... | collective-permute-start | bytes 196616 | tf_op jit(solution)/shard_map/ppermute | solution.py:152
  19.6 5.7 %collective-permute-start.6 = (bf16[8,4096]{1,0:T(8,128)(2,1)S(1)}, bf16[8,4096]{1,0:T(8,128)(2,1)S(1)}, u32[]{:S(2)}, u32[]{:S(2)}) collective-permute-start(bf16[8,4096]{1,0:T(8,128)(2,1)S(1)} %add_convert_fusion.refs_0_), channel_id=1, source_target_pairs={{0,16},{4,20},{8,24},{12,28},{16,0},{20,4},{24,8},{28,12},{1,17},{... | collective-permute-start | bytes 196616 | tf_op jit(solution)/shard_map/ppermute | solution.py:152
  20.0 5.2 %collective-permute-start.5 = (bf16[8,4096]{1,0:T(8,128)(2,1)S(1)}, bf16[8,4096]{1,0:T(8,128)(2,1)S(1)}, u32[]{:S(2)}, u32[]{:S(2)}) collective-permute-start(bf16[8,4096]{1,0:T(8,128)(2,1)S(1)} %add_convert_fusion.refs_0_), channel_id=1, source_target_pairs={{0,12},{4,8},{8,4},{12,0},{16,28},{20,24},{24,20},{28,16},{1,13},{... | collective-permute-start | bytes 196616 | tf_op jit(solution)/shard_map/ppermute | solution.py:152
  20.8 5.0 %copy-start.4 = (bf16[8,4096]{1,0:T(8,128)(2,1)}, bf16[8,4096]{1,0:T(8,128)(2,1)S(1)}, u32[]{:S(2)}) copy-start(bf16[8,4096]{1,0:T(8,128)(2,1)S(1)} %collective-permute-done.9.refs_7_) | copy-start | bytes 196612
  20.8 5.0 %collective-permute-start.4 = (bf16[8,4096]{1,0:T(8,128)(2,1)S(1)}, bf16[8,4096]{1,0:T(8,128)(2,1)S(1)}, u32[]{:S(2)}, u32[]{:S(2)}) collective-permute-start(bf16[8,4096]{1,0:T(8,128)(2,1)S(1)} %add_convert_fusion.refs_0_), channel_id=1, source_target_pairs={{0,8},{4,12},{8,0},{12,4},{16,24},{20,28},{24,16},{28,20},{1,9},{5... | collective-permute-start | bytes 196616 | tf_op jit(solution)/shard_map/ppermute | solution.py:152
  21.9 4.0 %copy-start.5 = (bf16[8,4096]{1,0:T(8,128)(2,1)}, bf16[8,4096]{1,0:T(8,128)(2,1)S(1)}, u32[]{:S(2)}) copy-start(bf16[8,4096]{1,0:T(8,128)(2,1)S(1)} %collective-permute-done.8.refs_6_) | copy-start | bytes 196612
  21.9 4.0 %collective-permute-start.3 = (bf16[8,4096]{1,0:T(8,128)(2,1)S(1)}, bf16[8,4096]{1,0:T(8,128)(2,1)S(1)}, u32[]{:S(2)}, u32[]{:S(2)}) collective-permute-start(bf16[8,4096]{1,0:T(8,128)(2,1)S(1)} %add_convert_fusion.refs_0_), channel_id=1, source_target_pairs={{0,4},{4,0},{8,12},{12,8},{16,20},{20,16},{24,28},{28,24},{1,5},{5... | collective-permute-start | bytes 196616 | tf_op jit(solution)/shard_map/ppermute | solution.py:152
  23.8 2.1 %copy-start.6 = (bf16[8,4096]{1,0:T(8,128)(2,1)}, bf16[8,4096]{1,0:T(8,128)(2,1)S(1)}, u32[]{:S(2)}) copy-start(bf16[8,4096]{1,0:T(8,128)(2,1)S(1)} %collective-permute-done.7.refs_5_) | copy-start | bytes 196612
  25.2 0.6 %copy-start.7 = (bf16[8,4096]{1,0:T(8,128)(2,1)}, bf16[8,4096]{1,0:T(8,128)(2,1)S(1)}, u32[]{:S(2)}) copy-start(bf16[8,4096]{1,0:T(8,128)(2,1)S(1)} %collective-permute-done.6.refs_4_) | copy-start | bytes 196612
  25.2 0.6 %copy-start.8 = (bf16[8,4096]{1,0:T(8,128)(2,1)}, bf16[8,4096]{1,0:T(8,128)(2,1)S(1)}, u32[]{:S(2)}) copy-start(bf16[8,4096]{1,0:T(8,128)(2,1)S(1)} %collective-permute-done.5.refs_3_) | copy-start | bytes 196612
  25.8 0.6 %copy-start.9 = (bf16[8,4096]{1,0:T(8,128)(2,1)}, bf16[8,4096]{1,0:T(8,128)(2,1)S(1)}, u32[]{:S(2)}) copy-start(bf16[8,4096]{1,0:T(8,128)(2,1)S(1)} %collective-permute-done.4.refs_2_) | copy-start | bytes 196612
  26.4 0.6 %copy-start.10 = (bf16[8,4096]{1,0:T(8,128)(2,1)}, bf16[8,4096]{1,0:T(8,128)(2,1)S(1)}, u32[]{:S(2)}) copy-start(bf16[8,4096]{1,0:T(8,128)(2,1)S(1)} %collective-permute-done.3.refs_1_) | copy-start | bytes 196612

commit v5 on v4

--- a/solution.py
+++ b/solution.py
@@ -36,7 +36,7 @@
     start = jnp.int32(0)
     for k in range(docs):
         slot = owners[0, k]
-        share = lax.rem(lax.div(slot, doc_dev) - tok + tok_count, tok_count)
+        share = lax.div(slot, doc_dev) ^ tok
         row = lax.rem(slot, doc_dev)
         here = token >= start
         share_of = jnp.where(here, share, share_of)
@@ -103,7 +103,7 @@
         ],
         compiler_params=pltpu.CompilerParams(vmem_limit_bytes=32 * 1024 * 1024),
         name="features",
-    )(doc_lengths, owner_map, proj_rows)
+    )(*(pltpu.with_memory_space_constraint(x, pltpu.HBM) for x in (doc_lengths, owner_map, proj_rows)))
 
 
 def score_kernel(query, *refs):
@@ -131,25 +131,31 @@
         out_shape=jax.ShapeDtypeStruct((query_features.shape[0], docs), jnp.float32),
         in_specs=[whole] * (1 + len(blocks)),
         out_specs=whole,
+        compiler_params=pltpu.CompilerParams(vmem_limit_bytes=16 * 1024 * 1024),
         name="scores",
-    )(query_features, *blocks)
+    )(*(pltpu.with_memory_space_constraint(x, pltpu.VMEM) for x in (query_features, *blocks)))
+
+
+def exchange(block, axis, flip):
+    return lax.ppermute(block, axis, [(i, i ^ flip) for i in range(lax.axis_size(axis))])
 
 
 def body(proj_rows, query_features, doc_lengths, owner_map):
     tok_count = lax.axis_size("tok")
     shares = feature_shares(proj_rows, doc_lengths, owner_map, tok_count)
     total = shares[0]
-    for shift in range(1, tok_count):
-        pairs = [(i, (i + shift) % tok_count) for i in range(tok_count)]
-        total = total + lax.ppermute(shares[shift], "tok", pairs).astype(jnp.float32)
+    for shift in range(tok_count - 1, 0, -1):
+        total = total + exchange(shares[shift], "tok", shift).astype(jnp.float32)
     features = total.astype(jnp.bfloat16)
     ex_count = lax.axis_size("ex")
-    if ex_count not in (2, 4, 8):
+    if ex_count != 8:
         gathered = lax.all_gather(features, "ex", axis=0, tiled=True)
         return jnp.einsum("qf,df->qd", query_features, gathered, preferred_element_type=jnp.float32)
     blocks = [features] + [None] * (ex_count - 1)
-    for flip in range(ex_count - 1, 0, -1):
-        blocks[flip] = lax.ppermute(features, "ex", [(i, i ^ flip) for i in range(ex_count)])
+    for flip in (6, 4, 2):
+        blocks[flip] = exchange(features, "ex", flip)
+    for flip in (0, 2, 4, 6):
+        blocks[flip + 1] = exchange(blocks[flip], "ex", 1)
     return block_scores(query_features, blocks)
 
 

time: 29.4 us -> 23.4 us (0.80)
  starting transfers between devices: 13.8 us -> 9.33 us
  local copies, waits for them, and re-layouts: 3.55 us -> 0.01 us
  waiting for transfers between devices: 6.83 us -> 9.93 us
  Pallas kernels: 4.94 us -> 3.93 us
    ppermute x10, starting transfers between devices: 13.8 us -> 9.33 us  [exchange(): lax.ppermute(block, axis, [(i, i ^ flip) for i in range(lax.axis_size(axi...]
    unnamed x22 -> x2, local copies, waits for them, and re-layouts: 3.55 us -> 0.01 us
    ppermute x10, waiting for transfers between devices: 6.83 us -> 9.93 us  [exchange(): lax.ppermute(block, axis, [(i, i ^ flip) for i in range(lax.axis_size(axi...]
    pallas_call x1, Pallas kernels: 2.18 us -> 0.99 us  [block_scores(): pl.pallas_call(score_kernel, out_shape=jax.ShapeDtypeStruct((query_featur...]
  transfers between devices with their start and end apart: 10 -> 10, of which waited for: 6 -> 7; matrix products, arithmetic and copies ran while one was open for 0% -> 0% of each run, Pallas kernels for 0% -> 0%
where the time goes in v5:
time: 23.4 us; the launch traced here: 23.2 us
  waiting for transfers between devices  9.93 us (42%)
  starting transfers between devices  9.33 us (40%)
  Pallas kernels  3.93 us (17%)
    ppermute x10, waiting for transfers between devices, exchange(): lax.ppermute(block, axis, [(i, i ^ flip) for i in range(lax.axis_size(axi...  9.93 us
    ppermute x10, starting transfers between devices, exchange(): lax.ppermute(block, axis, [(i, i ^ flip) for i in range(lax.axis_size(axi...  9.33 us
    pallas_call x1, Pallas kernels, feature_shares(): pl.pallas_call(feature_kernel, out_shape=[jax.ShapeDtypeStruct((doc_dev,...  2.94 us
    pallas_call x1, Pallas kernels, block_scores(): pl.pallas_call(score_kernel, out_shape=jax.ShapeDtypeStruct((query_featur...  0.99 us
  transfers between devices with their start and end apart: 10, of which 7 were waited for; matrix products, arithmetic and copies ran while one was open for 0% of the time, Pallas kernels for 0%

profile of v5, /device:TPU:0, one launch (start us, length us, event | category | flops | bytes accessed | tf_op | source)
XLA Modules:
  0.0 23.2 jit_solution(11802745991104828617)
XLA Ops:
  0.0 0.0 copy-start
  0.0 2.9 %features.1 = (f32[8,4096]{1,0:T(8,128)S(1)}, bf16[8,4096]{1,0:T(8,128)(2,1)S(1)}, bf16[8,4096]{1,0:T(8,128)(2,1)S(1)}, bf16[8,4096]{1,0:T(8,128)(2,1)S(1)}) custom-call(s32[1,32]{1,0:T(1,128)} %lengths_hbm.1, s32[1,32]{1,0:T(1,128)} %owners_hbm.1, bf16[2048,128]{1,0:T(8,128)(2,1)} %rows_hbm.1), custom_call_target="tpu_custom_call" | custom-call | tf_op jit(solution)/shard_map/features/pallas_call | solution.py:87
  2.9 5.1 %collective-permute-start = (bf16[8,4096]{1,0:T(8,128)(2,1)S(1)}, bf16[8,4096]{1,0:T(8,128)(2,1)S(1)}, u32[]{:S(2)}, u32[]{:S(2)}) collective-permute-start(bf16[8,4096]{1,0:T(8,128)(2,1)S(1)} %get-tuple-element.10), channel_id=1, source_target_pairs={{0,3},{1,2},{2,1},{3,0},{4,7},{5,6},{6,5},{7,4},{8,11},{9,10},{10,... | collective-permute-start | bytes 196616 | tf_op jit(solution)/shard_map/ppermute | solution.py:140
  8.1 0.0 collective-permute-start.1
  8.1 0.6 %collective-permute-start.2 = (bf16[8,4096]{1,0:T(8,128)(2,1)S(1)}, bf16[8,4096]{1,0:T(8,128)(2,1)S(1)}, u32[]{:S(2)}, u32[]{:S(2)}) collective-permute-start(bf16[8,4096]{1,0:T(8,128)(2,1)S(1)} %get-tuple-element.12), channel_id=1, source_target_pairs={{0,1},{1,0},{2,3},{3,2},{4,5},{5,4},{6,7},{7,6},{8,9},{9,8},{10,11... | collective-permute-start | bytes 196616 | tf_op jit(solution)/shard_map/ppermute | solution.py:140
  8.7 1.9 %collective-permute-done = bf16[8,4096]{1,0:T(8,128)(2,1)S(1)} collective-permute-done((bf16[8,4096]{1,0:T(8,128)(2,1)S(1)}, bf16[8,4096]{1,0:T(8,128)(2,1)S(1)}, u32[]{:S(2)}, u32[]{:S(2)}) %collective-permute-start) | collective-permute-done | bytes 65568 | tf_op jit(solution)/shard_map/ppermute | solution.py:140
  10.6 3.0 %collective-permute-done.1 = bf16[8,4096]{1,0:T(8,128)(2,1)S(1)} collective-permute-done((bf16[8,4096]{1,0:T(8,128)(2,1)S(1)}, bf16[8,4096]{1,0:T(8,128)(2,1)S(1)}, u32[]{:S(2)}, u32[]{:S(2)}) %collective-permute-start.1) | collective-permute-done | bytes 65568 | tf_op jit(solution)/shard_map/ppermute | solution.py:140
  13.7 0.0 collective-permute-done.2
  13.7 2.5 %collective-permute-start.8 = (bf16[8,4096]{1,0:T(8,128)(2,1)S(1)}, bf16[8,4096]{1,0:T(8,128)(2,1)S(1)}, u32[]{:S(2)}, u32[]{:S(2)}) collective-permute-start(bf16[8,4096]{1,0:T(8,128)(2,1)S(1)} %add_convert_fusion.refs_0_), channel_id=1, source_target_pairs={{0,24},{4,28},{8,16},{12,20},{16,8},{20,12},{24,0},{28,4},{1,25},{... | collective-permute-start | bytes 196616 | tf_op jit(solution)/shard_map/ppermute | solution.py:140
  16.2 0.5 %collective-permute-start.6 = (bf16[8,4096]{1,0:T(8,128)(2,1)S(1)}, bf16[8,4096]{1,0:T(8,128)(2,1)S(1)}, u32[]{:S(2)}, u32[]{:S(2)}) collective-permute-start(bf16[8,4096]{1,0:T(8,128)(2,1)S(1)} %add_convert_fusion.refs_0_), channel_id=1, source_target_pairs={{0,16},{4,20},{8,24},{12,28},{16,0},{20,4},{24,8},{28,12},{1,17},{... | collective-permute-start | bytes 196616 | tf_op jit(solution)/shard_map/ppermute | solution.py:140
  16.7 0.5 %collective-permute-start.4 = (bf16[8,4096]{1,0:T(8,128)(2,1)S(1)}, bf16[8,4096]{1,0:T(8,128)(2,1)S(1)}, u32[]{:S(2)}, u32[]{:S(2)}) collective-permute-start(bf16[8,4096]{1,0:T(8,128)(2,1)S(1)} %add_convert_fusion.refs_0_), channel_id=1, source_target_pairs={{0,8},{4,12},{8,0},{12,4},{16,24},{20,28},{24,16},{28,20},{1,9},{5... | collective-permute-start | bytes 196616 | tf_op jit(solution)/shard_map/ppermute | solution.py:140
  17.3 0.0 collective-permute-start.3
  17.3 1.7 %collective-permute-done.8.refs_6_ = bf16[8,4096]{1,0:T(8,128)(2,1)S(1)} collective-permute-done((bf16[8,4096]{1,0:T(8,128)(2,1)S(1)}, bf16[8,4096]{1,0:T(8,128)(2,1)S(1)}, u32[]{:S(2)}, u32[]{:S(2)}) %collective-permute-start.8) | collective-permute-done | bytes 65568 | tf_op jit(solution)/shard_map/ppermute | solution.py:140
  19.0 0.0 collective-permute-start.9
  19.0 1.5 %collective-permute-done.6.refs_4_ = bf16[8,4096]{1,0:T(8,128)(2,1)S(1)} collective-permute-done((bf16[8,4096]{1,0:T(8,128)(2,1)S(1)}, bf16[8,4096]{1,0:T(8,128)(2,1)S(1)}, u32[]{:S(2)}, u32[]{:S(2)}) %collective-permute-start.6) | collective-permute-done | bytes 65568 | tf_op jit(solution)/shard_map/ppermute | solution.py:140
  20.5 0.0 collective-permute-start.7
  20.5 0.5 %collective-permute-done.4.refs_2_ = bf16[8,4096]{1,0:T(8,128)(2,1)S(1)} collective-permute-done((bf16[8,4096]{1,0:T(8,128)(2,1)S(1)}, bf16[8,4096]{1,0:T(8,128)(2,1)S(1)}, u32[]{:S(2)}, u32[]{:S(2)}) %collective-permute-start.4) | collective-permute-done | bytes 65568 | tf_op jit(solution)/shard_map/ppermute | solution.py:140
  21.0 0.0 collective-permute-start.5
  21.0 0.0 collective-permute-done.3.refs_1_
  21.0 0.0 collective-permute-done.9.refs_7_
  21.0 0.7 %collective-permute-done.7.refs_5_ = bf16[8,4096]{1,0:T(8,128)(2,1)S(1)} collective-permute-done((bf16[8,4096]{1,0:T(8,128)(2,1)S(1)}, bf16[8,4096]{1,0:T(8,128)(2,1)S(1)}, u32[]{:S(2)}, u32[]{:S(2)}) %collective-permute-start.7) | collective-permute-done | bytes 65568 | tf_op jit(solution)/shard_map/ppermute | solution.py:140
  21.7 0.5 %collective-permute-done.5.refs_3_ = bf16[8,4096]{1,0:T(8,128)(2,1)S(1)} collective-permute-done((bf16[8,4096]{1,0:T(8,128)(2,1)S(1)}, bf16[8,4096]{1,0:T(8,128)(2,1)S(1)}, u32[]{:S(2)}, u32[]{:S(2)}) %collective-permute-start.5) | collective-permute-done | bytes 65568 | tf_op jit(solution)/shard_map/ppermute | solution.py:140
  22.3 0.0 copy-done
  22.3 1.0 %scores.1 = f32[64,64]{1,0:T(8,128)} custom-call(bf16[64,4096]{1,0:T(8,128)(2,1)S(1)} %copy-done, bf16[8,4096]{1,0:T(8,128)(2,1)S(1)} %add_convert_fusion.refs_0_, bf16[8,4096]{1,0:T(8,128)(2,1)S(1)} %collective-permute-done.3.refs_1_, bf16[8,4096]{1,0:T(8,128)(2,1)S(1)} %collective-permute-done.4.refs_2_, ...), custom_call_target="tpu_custom_call" | custom-call | tf_op jit(solution)/shard_map/scores/pallas_call | solution.py:129
  (1 shorter events, 0.0 us)
Async XLA Ops:
  0.0 22.3 %copy-start = (bf16[64,4096]{1,0:T(8,128)(2,1)S(1)}, bf16[64,4096]{1,0:T(8,128)(2,1)}, u32[]{:S(2)}) copy-start(bf16[64,4096]{1,0:T(8,128)(2,1)} %query.1) | copy-start | bytes 1572868
  2.9 7.7 %collective-permute-start = (bf16[8,4096]{1,0:T(8,128)(2,1)S(1)}, bf16[8,4096]{1,0:T(8,128)(2,1)S(1)}, u32[]{:S(2)}, u32[]{:S(2)}) collective-permute-start(bf16[8,4096]{1,0:T(8,128)(2,1)S(1)} %get-tuple-element.10), channel_id=1, source_target_pairs={{0,3},{1,2},{2,1},{3,0},{4,7},{5,6},{6,5},{7,4},{8,11},{9,10},{10,... | collective-permute-start | bytes 196616 | tf_op jit(solution)/shard_map/ppermute | solution.py:140
  8.1 5.6 %collective-permute-start.1 = (bf16[8,4096]{1,0:T(8,128)(2,1)S(1)}, bf16[8,4096]{1,0:T(8,128)(2,1)S(1)}, u32[]{:S(2)}, u32[]{:S(2)}) collective-permute-start(bf16[8,4096]{1,0:T(8,128)(2,1)S(1)} %get-tuple-element.11), channel_id=1, source_target_pairs={{0,2},{1,3},{2,0},{3,1},{4,6},{5,7},{6,4},{7,5},{8,10},{9,11},{10,... | collective-permute-start | bytes 196616 | tf_op jit(solution)/shard_map/ppermute | solution.py:140
  8.1 5.6 %collective-permute-start.2 = (bf16[8,4096]{1,0:T(8,128)(2,1)S(1)}, bf16[8,4096]{1,0:T(8,128)(2,1)S(1)}, u32[]{:S(2)}, u32[]{:S(2)}) collective-permute-start(bf16[8,4096]{1,0:T(8,128)(2,1)S(1)} %get-tuple-element.12), channel_id=1, source_target_pairs={{0,1},{1,0},{2,3},{3,2},{4,5},{5,4},{6,7},{7,6},{8,9},{9,8},{10,11... | collective-permute-start | bytes 196616 | tf_op jit(solution)/shard_map/ppermute | solution.py:140
  13.7 5.3 %collective-permute-start.8 = (bf16[8,4096]{1,0:T(8,128)(2,1)S(1)}, bf16[8,4096]{1,0:T(8,128)(2,1)S(1)}, u32[]{:S(2)}, u32[]{:S(2)}) collective-permute-start(bf16[8,4096]{1,0:T(8,128)(2,1)S(1)} %add_convert_fusion.refs_0_), channel_id=1, source_target_pairs={{0,24},{4,28},{8,16},{12,20},{16,8},{20,12},{24,0},{28,4},{1,25},{... | collective-permute-start | bytes 196616 | tf_op jit(solution)/shard_map/ppermute | solution.py:140
  16.2 4.3 %collective-permute-start.6 = (bf16[8,4096]{1,0:T(8,128)(2,1)S(1)}, bf16[8,4096]{1,0:T(8,128)(2,1)S(1)}, u32[]{:S(2)}, u32[]{:S(2)}) collective-permute-start(bf16[8,4096]{1,0:T(8,128)(2,1)S(1)} %add_convert_fusion.refs_0_), channel_id=1, source_target_pairs={{0,16},{4,20},{8,24},{12,28},{16,0},{20,4},{24,8},{28,12},{1,17},{... | collective-permute-start | bytes 196616 | tf_op jit(solution)/shard_map/ppermute | solution.py:140
  16.7 4.3 %collective-permute-start.4 = (bf16[8,4096]{1,0:T(8,128)(2,1)S(1)}, bf16[8,4096]{1,0:T(8,128)(2,1)S(1)}, u32[]{:S(2)}, u32[]{:S(2)}) collective-permute-start(bf16[8,4096]{1,0:T(8,128)(2,1)S(1)} %add_convert_fusion.refs_0_), channel_id=1, source_target_pairs={{0,8},{4,12},{8,0},{12,4},{16,24},{20,28},{24,16},{28,20},{1,9},{5... | collective-permute-start | bytes 196616 | tf_op jit(solution)/shard_map/ppermute | solution.py:140
  17.3 3.7 %collective-permute-start.3 = (bf16[8,4096]{1,0:T(8,128)(2,1)S(1)}, bf16[8,4096]{1,0:T(8,128)(2,1)S(1)}, u32[]{:S(2)}, u32[]{:S(2)}) collective-permute-start(bf16[8,4096]{1,0:T(8,128)(2,1)S(1)} %add_convert_fusion.refs_0_), channel_id=1, source_target_pairs={{0,4},{4,0},{8,12},{12,8},{16,20},{20,16},{24,28},{28,24},{1,5},{5... | collective-permute-start | bytes 196616 | tf_op jit(solution)/shard_map/ppermute | solution.py:140
  19.0 2.0 %collective-permute-start.9 = (bf16[8,4096]{1,0:T(8,128)(2,1)S(1)}, bf16[8,4096]{1,0:T(8,128)(2,1)S(1)}, u32[]{:S(2)}, u32[]{:S(2)}) collective-permute-start(bf16[8,4096]{1,0:T(8,128)(2,1)S(1)} %collective-permute-done.8.refs_6_), channel_id=1, source_target_pairs={{0,4},{4,0},{8,12},{12,8},{16,20},{20,16},{24,28},{28,24},{1,5},{5... | collective-permute-start | bytes 196616 | tf_op jit(solution)/shard_map/ppermute | solution.py:140
  20.5 1.3 %collective-permute-start.7 = (bf16[8,4096]{1,0:T(8,128)(2,1)S(1)}, bf16[8,4096]{1,0:T(8,128)(2,1)S(1)}, u32[]{:S(2)}, u32[]{:S(2)}) collective-permute-start(bf16[8,4096]{1,0:T(8,128)(2,1)S(1)} %collective-permute-done.6.refs_4_), channel_id=1, source_target_pairs={{0,4},{4,0},{8,12},{12,8},{16,20},{20,16},{24,28},{28,24},{1,5},{5... | collective-permute-start | bytes 196616 | tf_op jit(solution)/shard_map/ppermute | solution.py:140
  21.0 1.3 %collective-permute-start.5 = (bf16[8,4096]{1,0:T(8,128)(2,1)S(1)}, bf16[8,4096]{1,0:T(8,128)(2,1)S(1)}, u32[]{:S(2)}, u32[]{:S(2)}) collective-permute-start(bf16[8,4096]{1,0:T(8,128)(2,1)S(1)} %collective-permute-done.4.refs_2_), channel_id=1, source_target_pairs={{0,4},{4,0},{8,12},{12,8},{16,20},{20,16},{24,28},{28,24},{1,5},{5... | collective-permute-start | bytes 196616 | tf_op jit(solution)/shard_map/ppermute | solution.py:140

commit v6 on v5

--- a/solution.py
+++ b/solution.py
@@ -144,7 +144,7 @@
     tok_count = lax.axis_size("tok")
     shares = feature_shares(proj_rows, doc_lengths, owner_map, tok_count)
     total = shares[0]
-    for shift in range(tok_count - 1, 0, -1):
+    for shift in sorted(range(1, tok_count), key=lambda flip: (flip < 2, flip)):
         total = total + exchange(shares[shift], "tok", shift).astype(jnp.float32)
     features = total.astype(jnp.bfloat16)
     ex_count = lax.axis_size("ex")
@@ -152,9 +152,9 @@
         gathered = lax.all_gather(features, "ex", axis=0, tiled=True)
         return jnp.einsum("qf,df->qd", query_features, gathered, preferred_element_type=jnp.float32)
     blocks = [features] + [None] * (ex_count - 1)
-    for flip in (6, 4, 2):
+    for flip in (4, 2, 6):
         blocks[flip] = exchange(features, "ex", flip)
-    for flip in (0, 2, 4, 6):
+    for flip in (0, 4, 2, 6):
         blocks[flip + 1] = exchange(blocks[flip], "ex", 1)
     return block_scores(query_features, blocks)
 

time: 23.4 us -> 23.1 us (0.987)
  transfers between devices with their start and end apart: 10 -> 10, of which waited for: 7 -> 8; matrix products, arithmetic and copies ran while one was open for 0% -> 0% of each run, Pallas kernels for 0% -> 0%
where the time goes in v6:
time: 23.1 us; the launch traced here: 22.9 us
  waiting for transfers between devices  9.7 us (42%)
  starting transfers between devices  9.25 us (40%)
  Pallas kernels  3.93 us (17%)
    ppermute x10, waiting for transfers between devices, exchange(): lax.ppermute(block, axis, [(i, i ^ flip) for i in range(lax.axis_size(axi...  9.7 us
    ppermute x10, starting transfers between devices, exchange(): lax.ppermute(block, axis, [(i, i ^ flip) for i in range(lax.axis_size(axi...  9.25 us
    pallas_call x1, Pallas kernels, feature_shares(): pl.pallas_call(feature_kernel, out_shape=[jax.ShapeDtypeStruct((doc_dev,...  2.94 us
    pallas_call x1, Pallas kernels, block_scores(): pl.pallas_call(score_kernel, out_shape=jax.ShapeDtypeStruct((query_featur...  0.99 us
  transfers between devices with their start and end apart: 10, of which 8 were waited for; matrix products, arithmetic and copies ran while one was open for 0% of the time, Pallas kernels for 0%

profile of v6, /device:TPU:0, one launch (start us, length us, event | category | flops | bytes accessed | tf_op | source)
XLA Modules:
  0.0 22.9 jit_solution(1225300948061615512)
XLA Ops:
  0.0 0.0 copy-start
  0.0 2.9 %features.1 = (f32[8,4096]{1,0:T(8,128)S(1)}, bf16[8,4096]{1,0:T(8,128)(2,1)S(1)}, bf16[8,4096]{1,0:T(8,128)(2,1)S(1)}, bf16[8,4096]{1,0:T(8,128)(2,1)S(1)}) custom-call(s32[1,32]{1,0:T(1,128)} %lengths_hbm.1, s32[1,32]{1,0:T(1,128)} %owners_hbm.1, bf16[2048,128]{1,0:T(8,128)(2,1)} %rows_hbm.1), custom_call_target="tpu_custom_call" | custom-call | tf_op jit(solution)/shard_map/features/pallas_call | solution.py:87
  2.9 4.1 %collective-permute-start = (bf16[8,4096]{1,0:T(8,128)(2,1)S(1)}, bf16[8,4096]{1,0:T(8,128)(2,1)S(1)}, u32[]{:S(2)}, u32[]{:S(2)}) collective-permute-start(bf16[8,4096]{1,0:T(8,128)(2,1)S(1)} %get-tuple-element.10), channel_id=1, source_target_pairs={{0,2},{1,3},{2,0},{3,1},{4,6},{5,7},{6,4},{7,5},{8,10},{9,11},{10,... | collective-permute-start | bytes 196616 | tf_op jit(solution)/shard_map/ppermute | solution.py:140
  7.1 1.3 %collective-permute-start.1 = (bf16[8,4096]{1,0:T(8,128)(2,1)S(1)}, bf16[8,4096]{1,0:T(8,128)(2,1)S(1)}, u32[]{:S(2)}, u32[]{:S(2)}) collective-permute-start(bf16[8,4096]{1,0:T(8,128)(2,1)S(1)} %get-tuple-element.11), channel_id=1, source_target_pairs={{0,3},{1,2},{2,1},{3,0},{4,7},{5,6},{6,5},{7,4},{8,11},{9,10},{10,... | collective-permute-start | bytes 196616 | tf_op jit(solution)/shard_map/ppermute | solution.py:140
  8.4 0.2 %collective-permute-start.2 = (bf16[8,4096]{1,0:T(8,128)(2,1)S(1)}, bf16[8,4096]{1,0:T(8,128)(2,1)S(1)}, u32[]{:S(2)}, u32[]{:S(2)}) collective-permute-start(bf16[8,4096]{1,0:T(8,128)(2,1)S(1)} %get-tuple-element.12), channel_id=1, source_target_pairs={{0,1},{1,0},{2,3},{3,2},{4,5},{5,4},{6,7},{7,6},{8,9},{9,8},{10,11... | collective-permute-start | bytes 196616 | tf_op jit(solution)/shard_map/ppermute | solution.py:140
  8.6 2.2 %collective-permute-done = bf16[8,4096]{1,0:T(8,128)(2,1)S(1)} collective-permute-done((bf16[8,4096]{1,0:T(8,128)(2,1)S(1)}, bf16[8,4096]{1,0:T(8,128)(2,1)S(1)}, u32[]{:S(2)}, u32[]{:S(2)}) %collective-permute-start) | collective-permute-done | bytes 65568 | tf_op jit(solution)/shard_map/ppermute | solution.py:140
  10.8 2.5 %collective-permute-done.1 = bf16[8,4096]{1,0:T(8,128)(2,1)S(1)} collective-permute-done((bf16[8,4096]{1,0:T(8,128)(2,1)S(1)}, bf16[8,4096]{1,0:T(8,128)(2,1)S(1)}, u32[]{:S(2)}, u32[]{:S(2)}) %collective-permute-start.1) | collective-permute-done | bytes 65568 | tf_op jit(solution)/shard_map/ppermute | solution.py:140
  13.3 0.1 collective-permute-done.2
  13.4 2.5 %collective-permute-start.8 = (bf16[8,4096]{1,0:T(8,128)(2,1)S(1)}, bf16[8,4096]{1,0:T(8,128)(2,1)S(1)}, u32[]{:S(2)}, u32[]{:S(2)}) collective-permute-start(bf16[8,4096]{1,0:T(8,128)(2,1)S(1)} %add_convert_fusion.refs_0_), channel_id=1, source_target_pairs={{0,24},{4,28},{8,16},{12,20},{16,8},{20,12},{24,0},{28,4},{1,25},{... | collective-permute-start | bytes 196616 | tf_op jit(solution)/shard_map/ppermute | solution.py:140
  15.9 0.5 %collective-permute-start.6 = (bf16[8,4096]{1,0:T(8,128)(2,1)S(1)}, bf16[8,4096]{1,0:T(8,128)(2,1)S(1)}, u32[]{:S(2)}, u32[]{:S(2)}) collective-permute-start(bf16[8,4096]{1,0:T(8,128)(2,1)S(1)} %add_convert_fusion.refs_0_), channel_id=1, source_target_pairs={{0,16},{4,20},{8,24},{12,28},{16,0},{20,4},{24,8},{28,12},{1,17},{... | collective-permute-start | bytes 196616 | tf_op jit(solution)/shard_map/ppermute | solution.py:140
  16.4 0.5 %collective-permute-start.4 = (bf16[8,4096]{1,0:T(8,128)(2,1)S(1)}, bf16[8,4096]{1,0:T(8,128)(2,1)S(1)}, u32[]{:S(2)}, u32[]{:S(2)}) collective-permute-start(bf16[8,4096]{1,0:T(8,128)(2,1)S(1)} %add_convert_fusion.refs_0_), channel_id=1, source_target_pairs={{0,8},{4,12},{8,0},{12,4},{16,24},{20,28},{24,16},{28,20},{1,9},{5... | collective-permute-start | bytes 196616 | tf_op jit(solution)/shard_map/ppermute | solution.py:140
  17.0 0.0 collective-permute-start.3
  17.0 2.3 %collective-permute-done.8.refs_6_ = bf16[8,4096]{1,0:T(8,128)(2,1)S(1)} collective-permute-done((bf16[8,4096]{1,0:T(8,128)(2,1)S(1)}, bf16[8,4096]{1,0:T(8,128)(2,1)S(1)}, u32[]{:S(2)}, u32[]{:S(2)}) %collective-permute-start.8) | collective-permute-done | bytes 65568 | tf_op jit(solution)/shard_map/ppermute | solution.py:140
  19.3 0.0 collective-permute-start.9
  19.3 0.9 %collective-permute-done.6.refs_4_ = bf16[8,4096]{1,0:T(8,128)(2,1)S(1)} collective-permute-done((bf16[8,4096]{1,0:T(8,128)(2,1)S(1)}, bf16[8,4096]{1,0:T(8,128)(2,1)S(1)}, u32[]{:S(2)}, u32[]{:S(2)}) %collective-permute-start.6) | collective-permute-done | bytes 65568 | tf_op jit(solution)/shard_map/ppermute | solution.py:140
  20.2 0.0 collective-permute-start.7
  20.2 0.5 %collective-permute-done.4.refs_2_ = bf16[8,4096]{1,0:T(8,128)(2,1)S(1)} collective-permute-done((bf16[8,4096]{1,0:T(8,128)(2,1)S(1)}, bf16[8,4096]{1,0:T(8,128)(2,1)S(1)}, u32[]{:S(2)}, u32[]{:S(2)}) %collective-permute-start.4) | collective-permute-done | bytes 65568 | tf_op jit(solution)/shard_map/ppermute | solution.py:140
  20.7 0.0 collective-permute-start.5
  20.7 0.0 collective-permute-done.3.refs_1_
  20.7 0.0 collective-permute-done.9.refs_7_
  20.7 0.7 %collective-permute-done.7.refs_5_ = bf16[8,4096]{1,0:T(8,128)(2,1)S(1)} collective-permute-done((bf16[8,4096]{1,0:T(8,128)(2,1)S(1)}, bf16[8,4096]{1,0:T(8,128)(2,1)S(1)}, u32[]{:S(2)}, u32[]{:S(2)}) %collective-permute-start.7) | collective-permute-done | bytes 65568 | tf_op jit(solution)/shard_map/ppermute | solution.py:140
  21.4 0.5 %collective-permute-done.5.refs_3_ = bf16[8,4096]{1,0:T(8,128)(2,1)S(1)} collective-permute-done((bf16[8,4096]{1,0:T(8,128)(2,1)S(1)}, bf16[8,4096]{1,0:T(8,128)(2,1)S(1)}, u32[]{:S(2)}, u32[]{:S(2)}) %collective-permute-start.5) | collective-permute-done | bytes 65568 | tf_op jit(solution)/shard_map/ppermute | solution.py:140
  22.0 0.0 copy-done
  22.0 1.0 %scores.1 = f32[64,64]{1,0:T(8,128)} custom-call(bf16[64,4096]{1,0:T(8,128)(2,1)S(1)} %copy-done, bf16[8,4096]{1,0:T(8,128)(2,1)S(1)} %add_convert_fusion.refs_0_, bf16[8,4096]{1,0:T(8,128)(2,1)S(1)} %collective-permute-done.3.refs_1_, bf16[8,4096]{1,0:T(8,128)(2,1)S(1)} %collective-permute-done.4.refs_2_, ...), custom_call_target="tpu_custom_call" | custom-call | tf_op jit(solution)/shard_map/scores/pallas_call | solution.py:129
  (1 shorter events, 0.0 us)
Async XLA Ops:
  0.0 22.0 %copy-start = (bf16[64,4096]{1,0:T(8,128)(2,1)S(1)}, bf16[64,4096]{1,0:T(8,128)(2,1)}, u32[]{:S(2)}) copy-start(bf16[64,4096]{1,0:T(8,128)(2,1)} %query.1) | copy-start | bytes 1572868
  2.9 7.9 %collective-permute-start = (bf16[8,4096]{1,0:T(8,128)(2,1)S(1)}, bf16[8,4096]{1,0:T(8,128)(2,1)S(1)}, u32[]{:S(2)}, u32[]{:S(2)}) collective-permute-start(bf16[8,4096]{1,0:T(8,128)(2,1)S(1)} %get-tuple-element.10), channel_id=1, source_target_pairs={{0,2},{1,3},{2,0},{3,1},{4,6},{5,7},{6,4},{7,5},{8,10},{9,11},{10,... | collective-permute-start | bytes 196616 | tf_op jit(solution)/shard_map/ppermute | solution.py:140
  7.1 6.2 %collective-permute-start.1 = (bf16[8,4096]{1,0:T(8,128)(2,1)S(1)}, bf16[8,4096]{1,0:T(8,128)(2,1)S(1)}, u32[]{:S(2)}, u32[]{:S(2)}) collective-permute-start(bf16[8,4096]{1,0:T(8,128)(2,1)S(1)} %get-tuple-element.11), channel_id=1, source_target_pairs={{0,3},{1,2},{2,1},{3,0},{4,7},{5,6},{6,5},{7,4},{8,11},{9,10},{10,... | collective-permute-start | bytes 196616 | tf_op jit(solution)/shard_map/ppermute | solution.py:140
  8.4 5.0 %collective-permute-start.2 = (bf16[8,4096]{1,0:T(8,128)(2,1)S(1)}, bf16[8,4096]{1,0:T(8,128)(2,1)S(1)}, u32[]{:S(2)}, u32[]{:S(2)}) collective-permute-start(bf16[8,4096]{1,0:T(8,128)(2,1)S(1)} %get-tuple-element.12), channel_id=1, source_target_pairs={{0,1},{1,0},{2,3},{3,2},{4,5},{5,4},{6,7},{7,6},{8,9},{9,8},{10,11... | collective-permute-start | bytes 196616 | tf_op jit(solution)/shard_map/ppermute | solution.py:140
  13.4 5.9 %collective-permute-start.8 = (bf16[8,4096]{1,0:T(8,128)(2,1)S(1)}, bf16[8,4096]{1,0:T(8,128)(2,1)S(1)}, u32[]{:S(2)}, u32[]{:S(2)}) collective-permute-start(bf16[8,4096]{1,0:T(8,128)(2,1)S(1)} %add_convert_fusion.refs_0_), channel_id=1, source_target_pairs={{0,24},{4,28},{8,16},{12,20},{16,8},{20,12},{24,0},{28,4},{1,25},{... | collective-permute-start | bytes 196616 | tf_op jit(solution)/shard_map/ppermute | solution.py:140
  15.9 4.3 %collective-permute-start.6 = (bf16[8,4096]{1,0:T(8,128)(2,1)S(1)}, bf16[8,4096]{1,0:T(8,128)(2,1)S(1)}, u32[]{:S(2)}, u32[]{:S(2)}) collective-permute-start(bf16[8,4096]{1,0:T(8,128)(2,1)S(1)} %add_convert_fusion.refs_0_), channel_id=1, source_target_pairs={{0,16},{4,20},{8,24},{12,28},{16,0},{20,4},{24,8},{28,12},{1,17},{... | collective-permute-start | bytes 196616 | tf_op jit(solution)/shard_map/ppermute | solution.py:140
  16.4 4.3 %collective-permute-start.4 = (bf16[8,4096]{1,0:T(8,128)(2,1)S(1)}, bf16[8,4096]{1,0:T(8,128)(2,1)S(1)}, u32[]{:S(2)}, u32[]{:S(2)}) collective-permute-start(bf16[8,4096]{1,0:T(8,128)(2,1)S(1)} %add_convert_fusion.refs_0_), channel_id=1, source_target_pairs={{0,8},{4,12},{8,0},{12,4},{16,24},{20,28},{24,16},{28,20},{1,9},{5... | collective-permute-start | bytes 196616 | tf_op jit(solution)/shard_map/ppermute | solution.py:140
  17.0 3.7 %collective-permute-start.3 = (bf16[8,4096]{1,0:T(8,128)(2,1)S(1)}, bf16[8,4096]{1,0:T(8,128)(2,1)S(1)}, u32[]{:S(2)}, u32[]{:S(2)}) collective-permute-start(bf16[8,4096]{1,0:T(8,128)(2,1)S(1)} %add_convert_fusion.refs_0_), channel_id=1, source_target_pairs={{0,4},{4,0},{8,12},{12,8},{16,20},{20,16},{24,28},{28,24},{1,5},{5... | collective-permute-start | bytes 196616 | tf_op jit(solution)/shard_map/ppermute | solution.py:140
  19.3 1.4 %collective-permute-start.9 = (bf16[8,4096]{1,0:T(8,128)(2,1)S(1)}, bf16[8,4096]{1,0:T(8,128)(2,1)S(1)}, u32[]{:S(2)}, u32[]{:S(2)}) collective-permute-start(bf16[8,4096]{1,0:T(8,128)(2,1)S(1)} %collective-permute-done.8.refs_6_), channel_id=1, source_target_pairs={{0,4},{4,0},{8,12},{12,8},{16,20},{20,16},{24,28},{28,24},{1,5},{5... | collective-permute-start | bytes 196616 | tf_op jit(solution)/shard_map/ppermute | solution.py:140
  20.2 1.3 %collective-permute-start.7 = (bf16[8,4096]{1,0:T(8,128)(2,1)S(1)}, bf16[8,4096]{1,0:T(8,128)(2,1)S(1)}, u32[]{:S(2)}, u32[]{:S(2)}) collective-permute-start(bf16[8,4096]{1,0:T(8,128)(2,1)S(1)} %collective-permute-done.6.refs_4_), channel_id=1, source_target_pairs={{0,4},{4,0},{8,12},{12,8},{16,20},{20,16},{24,28},{28,24},{1,5},{5... | collective-permute-start | bytes 196616 | tf_op jit(solution)/shard_map/ppermute | solution.py:140
  20.7 1.3 %collective-permute-start.5 = (bf16[8,4096]{1,0:T(8,128)(2,1)S(1)}, bf16[8,4096]{1,0:T(8,128)(2,1)S(1)}, u32[]{:S(2)}, u32[]{:S(2)}) collective-permute-start(bf16[8,4096]{1,0:T(8,128)(2,1)S(1)} %collective-permute-done.4.refs_2_), channel_id=1, source_target_pairs={{0,4},{4,0},{8,12},{12,8},{16,20},{20,16},{24,28},{28,24},{1,5},{5... | collective-permute-start | bytes 196616 | tf_op jit(solution)/shard_map/ppermute | solution.py:140

commit v7 on v6

--- a/solution.py
+++ b/solution.py
@@ -1,3 +1,5 @@
+import functools
+
 import jax
 import jax.numpy as jnp
 from jax import lax
@@ -87,7 +89,7 @@
     return pl.pallas_call(
         feature_kernel,
         out_shape=[
-            jax.ShapeDtypeStruct((doc_dev, feat), jnp.bfloat16 if s else jnp.float32)
+            jax.ShapeDtypeStruct((doc_dev, feat), jnp.bfloat16 if s % 2 else jnp.float32)
             for s in range(tok_count)
         ],
         in_specs=[far, far, far],
@@ -106,14 +108,15 @@
     )(*(pltpu.with_memory_space_constraint(x, pltpu.HBM) for x in (doc_lengths, owner_map, proj_rows)))
 
 
-def score_kernel(query, *refs):
+def score_kernel(flips, query, *refs):
     *blocks, scores = refs
     doc_dev = blocks[0].shape[0]
     features = jnp.concatenate([block[...] for block in blocks], axis=0)
     products = lax.dot_general(
         features, query[...], ROW_BY_ROW, preferred_element_type=jnp.float32
     )
-    parts = [products[i * doc_dev : (i + 1) * doc_dev] for i in range(len(blocks))]
+    places = [flips.index(i) for i in range(len(flips))]
+    parts = [products[i * doc_dev : (i + 1) * doc_dev] for i in places]
     ex = lax.axis_index("ex")
     flip = 1
     while flip < len(blocks):
@@ -127,13 +130,13 @@
     whole = pl.BlockSpec(memory_space=pltpu.VMEM)
     docs = len(blocks) * blocks[0].shape[0]
     return pl.pallas_call(
-        score_kernel,
+        functools.partial(score_kernel, tuple(blocks)),
         out_shape=jax.ShapeDtypeStruct((query_features.shape[0], docs), jnp.float32),
         in_specs=[whole] * (1 + len(blocks)),
         out_specs=whole,
         compiler_params=pltpu.CompilerParams(vmem_limit_bytes=16 * 1024 * 1024),
         name="scores",
-    )(*(pltpu.with_memory_space_constraint(x, pltpu.VMEM) for x in (query_features, *blocks)))
+    )(*(pltpu.with_memory_space_constraint(x, pltpu.VMEM) for x in (query_features, *blocks.values())))
 
 
 def exchange(block, axis, flip):
@@ -143,20 +146,26 @@
 def body(proj_rows, query_features, doc_lengths, owner_map):
     tok_count = lax.axis_size("tok")
     shares = feature_shares(proj_rows, doc_lengths, owner_map, tok_count)
-    total = shares[0]
-    for shift in sorted(range(1, tok_count), key=lambda flip: (flip < 2, flip)):
-        total = total + exchange(shares[shift], "tok", shift).astype(jnp.float32)
+    if tok_count == 4:
+        passed = exchange(shares[3], "tok", 1).astype(jnp.float32)
+        near = exchange(shares[1], "tok", 1).astype(jnp.float32)
+        far = exchange((shares[2] + passed).astype(jnp.bfloat16), "tok", 2).astype(jnp.float32)
+        total = shares[0] + near + far
+    else:
+        total = shares[0]
+        for flip in range(1, tok_count):
+            total = total + exchange(shares[flip].astype(jnp.bfloat16), "tok", flip).astype(jnp.float32)
     features = total.astype(jnp.bfloat16)
     ex_count = lax.axis_size("ex")
     if ex_count != 8:
         gathered = lax.all_gather(features, "ex", axis=0, tiled=True)
         return jnp.einsum("qf,df->qd", query_features, gathered, preferred_element_type=jnp.float32)
-    blocks = [features] + [None] * (ex_count - 1)
+    blocks = {0: features}
     for flip in (4, 2, 6):
         blocks[flip] = exchange(features, "ex", flip)
     for flip in (0, 4, 2, 6):
         blocks[flip + 1] = exchange(blocks[flip], "ex", 1)
-    return block_scores(query_features, blocks)
+    return block_scores(query_features, {flip: blocks[flip] for flip in (0, 1, 6, 7, 2, 3, 4, 5)})
 
 
 def solution(mesh):

time: 23.1 us -> 25.2 us (1.091)
  waiting for transfers between devices: 9.7 us -> 10.8 us
  starting transfers between devices: 9.25 us -> 10.2 us
    ppermute x10, waiting for transfers between devices: 9.7 us -> 10.8 us  [exchange(): lax.ppermute(block, axis, [(i, i ^ flip) for i in range(lax.axis_size(axi...]
    ppermute x10, starting transfers between devices: 9.25 us -> 10.2 us  [exchange(): lax.ppermute(block, axis, [(i, i ^ flip) for i in range(lax.axis_size(axi...]
  transfers between devices with their start and end apart: 10 -> 10, of which waited for: 8 -> 6; matrix products, arithmetic and copies ran while one was open for 0% -> 0% of each run, Pallas kernels for 0% -> 0%
where the time goes in v7:
time: 25.2 us; the launch traced here: 25 us
  waiting for transfers between devices  10.8 us (43%)
  starting transfers between devices  10.2 us (40%)
  Pallas kernels  3.92 us (16%)
    ppermute x10, waiting for transfers between devices, exchange(): lax.ppermute(block, axis, [(i, i ^ flip) for i in range(lax.axis_size(axi...  10.8 us
    ppermute x10, starting transfers between devices, exchange(): lax.ppermute(block, axis, [(i, i ^ flip) for i in range(lax.axis_size(axi...  10.2 us
    pallas_call x1, Pallas kernels, feature_shares(): pl.pallas_call(feature_kernel, out_shape=[jax.ShapeDtypeStruct((doc_dev,...  2.94 us
    pallas_call x1, Pallas kernels, block_scores(): pl.pallas_call(functools.partial(score_kernel, tuple(blocks)), out_shape=...  0.99 us
  transfers between devices with their start and end apart: 10, of which 6 were waited for; matrix products, arithmetic and copies ran while one was open for 0% of the time, Pallas kernels for 0%

profile of v7, /device:TPU:0, one launch (start us, length us, event | category | flops | bytes accessed | tf_op | source)
XLA Modules:
  0.0 25.0 jit_solution(5819781499838203056)
XLA Ops:
  0.0 0.0 copy-start
  0.0 2.9 %features.1 = (f32[8,4096]{1,0:T(8,128)S(1)}, bf16[8,4096]{1,0:T(8,128)(2,1)S(1)}, f32[8,4096]{1,0:T(8,128)S(1)}, bf16[8,4096]{1,0:T(8,128)(2,1)S(1)}) custom-call(s32[1,32]{1,0:T(1,128)} %lengths_hbm.1, s32[1,32]{1,0:T(1,128)} %owners_hbm.1, bf16[2048,128]{1,0:T(8,128)(2,1)} %rows_hbm.1), custom_call_target="tpu_custom_call" | custom-call | tf_op jit(solution)/shard_map/features/pallas_call | solution.py:89
  2.9 3.1 %collective-permute-start.1 = (bf16[8,4096]{1,0:T(8,128)(2,1)S(1)}, bf16[8,4096]{1,0:T(8,128)(2,1)S(1)}, u32[]{:S(2)}, u32[]{:S(2)}) collective-permute-start(bf16[8,4096]{1,0:T(8,128)(2,1)S(1)} %get-tuple-element.12), channel_id=1, source_target_pairs={{0,1},{1,0},{2,3},{3,2},{4,5},{5,4},{6,7},{7,6},{8,9},{9,8},{10,11... | collective-permute-start | bytes 196616 | tf_op jit(solution)/shard_map/ppermute | solution.py:143
  6.0 0.1 collective-permute-start
  6.1 2.3 %collective-permute-done.1 = bf16[8,4096]{1,0:T(8,128)(2,1)S(1)} collective-permute-done((bf16[8,4096]{1,0:T(8,128)(2,1)S(1)}, bf16[8,4096]{1,0:T(8,128)(2,1)S(1)}, u32[]{:S(2)}, u32[]{:S(2)}) %collective-permute-start.1) | collective-permute-done | bytes 65568 | tf_op jit(solution)/shard_map/ppermute | solution.py:143
  8.5 3.5 %collective-permute-start.2 = (bf16[8,4096]{1,0:T(8,128)(2,1)S(1)}, bf16[8,4096]{1,0:T(8,128)(2,1)S(1)}, u32[]{:S(2)}, u32[]{:S(2)}) collective-permute-start(bf16[8,4096]{1,0:T(8,128)(2,1)S(1)} %add_convert_fusion.1), channel_id=1, source_target_pairs={{0,2},{1,3},{2,0},{3,1},{4,6},{5,7},{6,4},{7,5},{8,10},{9,11},{10,... | collective-permute-start | bytes 196616 | tf_op jit(solution)/shard_map/ppermute | solution.py:143
  11.9 0.0 collective-permute-done
  11.9 2.2 %collective-permute-done.2 = bf16[8,4096]{1,0:T(8,128)(2,1)S(1)} collective-permute-done((bf16[8,4096]{1,0:T(8,128)(2,1)S(1)}, bf16[8,4096]{1,0:T(8,128)(2,1)S(1)}, u32[]{:S(2)}, u32[]{:S(2)}) %collective-permute-start.2) | collective-permute-done | bytes 65568 | tf_op jit(solution)/shard_map/ppermute | solution.py:143
  14.2 1.9 %collective-permute-start.8 = (bf16[8,4096]{1,0:T(8,128)(2,1)S(1)}, bf16[8,4096]{1,0:T(8,128)(2,1)S(1)}, u32[]{:S(2)}, u32[]{:S(2)}) collective-permute-start(bf16[8,4096]{1,0:T(8,128)(2,1)S(1)} %add_convert_fusion.refs_0_), channel_id=1, source_target_pairs={{0,16},{4,20},{8,24},{12,28},{16,0},{20,4},{24,8},{28,12},{1,17},{... | collective-permute-start | bytes 196616 | tf_op jit(solution)/shard_map/ppermute | solution.py:143
  16.1 1.5 %collective-permute-start.6 = (bf16[8,4096]{1,0:T(8,128)(2,1)S(1)}, bf16[8,4096]{1,0:T(8,128)(2,1)S(1)}, u32[]{:S(2)}, u32[]{:S(2)}) collective-permute-start(bf16[8,4096]{1,0:T(8,128)(2,1)S(1)} %add_convert_fusion.refs_0_), channel_id=1, source_target_pairs={{0,8},{4,12},{8,0},{12,4},{16,24},{20,28},{24,16},{28,20},{1,9},{5... | collective-permute-start | bytes 196616 | tf_op jit(solution)/shard_map/ppermute | solution.py:143
  17.6 0.1 collective-permute-start.4
  17.8 0.0 collective-permute-start.3
  17.8 1.2 %collective-permute-done.8.refs_6_ = bf16[8,4096]{1,0:T(8,128)(2,1)S(1)} collective-permute-done((bf16[8,4096]{1,0:T(8,128)(2,1)S(1)}, bf16[8,4096]{1,0:T(8,128)(2,1)S(1)}, u32[]{:S(2)}, u32[]{:S(2)}) %collective-permute-start.8) | collective-permute-done | bytes 65568 | tf_op jit(solution)/shard_map/ppermute | solution.py:143
  19.0 0.0 collective-permute-start.9
  19.0 1.4 %collective-permute-done.6.refs_4_ = bf16[8,4096]{1,0:T(8,128)(2,1)S(1)} collective-permute-done((bf16[8,4096]{1,0:T(8,128)(2,1)S(1)}, bf16[8,4096]{1,0:T(8,128)(2,1)S(1)}, u32[]{:S(2)}, u32[]{:S(2)}) %collective-permute-start.6) | collective-permute-done | bytes 65568 | tf_op jit(solution)/shard_map/ppermute | solution.py:143
  20.4 0.0 collective-permute-start.7
  20.4 2.4 %collective-permute-done.4.refs_2_ = bf16[8,4096]{1,0:T(8,128)(2,1)S(1)} collective-permute-done((bf16[8,4096]{1,0:T(8,128)(2,1)S(1)}, bf16[8,4096]{1,0:T(8,128)(2,1)S(1)}, u32[]{:S(2)}, u32[]{:S(2)}) %collective-permute-start.4) | collective-permute-done | bytes 65568 | tf_op jit(solution)/shard_map/ppermute | solution.py:143
  22.8 0.0 collective-permute-start.5
  22.8 0.0 collective-permute-done.3.refs_1_
  22.8 0.0 collective-permute-done.9.refs_7_
  22.8 0.0 collective-permute-done.7.refs_5_
  22.8 1.2 %collective-permute-done.5.refs_3_ = bf16[8,4096]{1,0:T(8,128)(2,1)S(1)} collective-permute-done((bf16[8,4096]{1,0:T(8,128)(2,1)S(1)}, bf16[8,4096]{1,0:T(8,128)(2,1)S(1)}, u32[]{:S(2)}, u32[]{:S(2)}) %collective-permute-start.5) | collective-permute-done | bytes 65568 | tf_op jit(solution)/shard_map/ppermute | solution.py:143
  24.0 0.0 copy-done
  24.0 1.0 %scores.1 = f32[64,64]{1,0:T(8,128)} custom-call(bf16[64,4096]{1,0:T(8,128)(2,1)S(1)} %copy-done, bf16[8,4096]{1,0:T(8,128)(2,1)S(1)} %add_convert_fusion.refs_0_, bf16[8,4096]{1,0:T(8,128)(2,1)S(1)} %collective-permute-done.3.refs_1_, bf16[8,4096]{1,0:T(8,128)(2,1)S(1)} %collective-permute-done.4.refs_2_, ...), custom_call_target="tpu_custom_call" | custom-call | tf_op jit(solution)/shard_map/scores/pallas_call | solution.py:132
  (2 shorter events, 0.0 us)
Async XLA Ops:
  0.0 24.0 %copy-start = (bf16[64,4096]{1,0:T(8,128)(2,1)S(1)}, bf16[64,4096]{1,0:T(8,128)(2,1)}, u32[]{:S(2)}) copy-start(bf16[64,4096]{1,0:T(8,128)(2,1)} %query.1) | copy-start | bytes 1572868
  2.9 5.5 %collective-permute-start.1 = (bf16[8,4096]{1,0:T(8,128)(2,1)S(1)}, bf16[8,4096]{1,0:T(8,128)(2,1)S(1)}, u32[]{:S(2)}, u32[]{:S(2)}) collective-permute-start(bf16[8,4096]{1,0:T(8,128)(2,1)S(1)} %get-tuple-element.12), channel_id=1, source_target_pairs={{0,1},{1,0},{2,3},{3,2},{4,5},{5,4},{6,7},{7,6},{8,9},{9,8},{10,11... | collective-permute-start | bytes 196616 | tf_op jit(solution)/shard_map/ppermute | solution.py:143
  6.0 5.9 %collective-permute-start = (bf16[8,4096]{1,0:T(8,128)(2,1)S(1)}, bf16[8,4096]{1,0:T(8,128)(2,1)S(1)}, u32[]{:S(2)}, u32[]{:S(2)}) collective-permute-start(bf16[8,4096]{1,0:T(8,128)(2,1)S(1)} %get-tuple-element.10), channel_id=1, source_target_pairs={{0,1},{1,0},{2,3},{3,2},{4,5},{5,4},{6,7},{7,6},{8,9},{9,8},{10,11... | collective-permute-start | bytes 196616 | tf_op jit(solution)/shard_map/ppermute | solution.py:143
  8.5 5.7 %collective-permute-start.2 = (bf16[8,4096]{1,0:T(8,128)(2,1)S(1)}, bf16[8,4096]{1,0:T(8,128)(2,1)S(1)}, u32[]{:S(2)}, u32[]{:S(2)}) collective-permute-start(bf16[8,4096]{1,0:T(8,128)(2,1)S(1)} %add_convert_fusion.1), channel_id=1, source_target_pairs={{0,2},{1,3},{2,0},{3,1},{4,6},{5,7},{6,4},{7,5},{8,10},{9,11},{10,... | collective-permute-start | bytes 196616 | tf_op jit(solution)/shard_map/ppermute | solution.py:143
  14.2 4.7 %collective-permute-start.8 = (bf16[8,4096]{1,0:T(8,128)(2,1)S(1)}, bf16[8,4096]{1,0:T(8,128)(2,1)S(1)}, u32[]{:S(2)}, u32[]{:S(2)}) collective-permute-start(bf16[8,4096]{1,0:T(8,128)(2,1)S(1)} %add_convert_fusion.refs_0_), channel_id=1, source_target_pairs={{0,16},{4,20},{8,24},{12,28},{16,0},{20,4},{24,8},{28,12},{1,17},{... | collective-permute-start | bytes 196616 | tf_op jit(solution)/shard_map/ppermute | solution.py:143
  16.1 4.3 %collective-permute-start.6 = (bf16[8,4096]{1,0:T(8,128)(2,1)S(1)}, bf16[8,4096]{1,0:T(8,128)(2,1)S(1)}, u32[]{:S(2)}, u32[]{:S(2)}) collective-permute-start(bf16[8,4096]{1,0:T(8,128)(2,1)S(1)} %add_convert_fusion.refs_0_), channel_id=1, source_target_pairs={{0,8},{4,12},{8,0},{12,4},{16,24},{20,28},{24,16},{28,20},{1,9},{5... | collective-permute-start | bytes 196616 | tf_op jit(solution)/shard_map/ppermute | solution.py:143
  17.6 5.2 %collective-permute-start.4 = (bf16[8,4096]{1,0:T(8,128)(2,1)S(1)}, bf16[8,4096]{1,0:T(8,128)(2,1)S(1)}, u32[]{:S(2)}, u32[]{:S(2)}) collective-permute-start(bf16[8,4096]{1,0:T(8,128)(2,1)S(1)} %add_convert_fusion.refs_0_), channel_id=1, source_target_pairs={{0,24},{4,28},{8,16},{12,20},{16,8},{20,12},{24,0},{28,4},{1,25},{... | collective-permute-start | bytes 196616 | tf_op jit(solution)/shard_map/ppermute | solution.py:143
  17.8 5.0 %collective-permute-start.3 = (bf16[8,4096]{1,0:T(8,128)(2,1)S(1)}, bf16[8,4096]{1,0:T(8,128)(2,1)S(1)}, u32[]{:S(2)}, u32[]{:S(2)}) collective-permute-start(bf16[8,4096]{1,0:T(8,128)(2,1)S(1)} %add_convert_fusion.refs_0_), channel_id=1, source_target_pairs={{0,4},{4,0},{8,12},{12,8},{16,20},{20,16},{24,28},{28,24},{1,5},{5... | collective-permute-start | bytes 196616 | tf_op jit(solution)/shard_map/ppermute | solution.py:143
  19.0 3.8 %collective-permute-start.9 = (bf16[8,4096]{1,0:T(8,128)(2,1)S(1)}, bf16[8,4096]{1,0:T(8,128)(2,1)S(1)}, u32[]{:S(2)}, u32[]{:S(2)}) collective-permute-start(bf16[8,4096]{1,0:T(8,128)(2,1)S(1)} %collective-permute-done.8.refs_6_), channel_id=1, source_target_pairs={{0,4},{4,0},{8,12},{12,8},{16,20},{20,16},{24,28},{28,24},{1,5},{5... | collective-permute-start | bytes 196616 | tf_op jit(solution)/shard_map/ppermute | solution.py:143
  20.4 2.4 %collective-permute-start.7 = (bf16[8,4096]{1,0:T(8,128)(2,1)S(1)}, bf16[8,4096]{1,0:T(8,128)(2,1)S(1)}, u32[]{:S(2)}, u32[]{:S(2)}) collective-permute-start(bf16[8,4096]{1,0:T(8,128)(2,1)S(1)} %collective-permute-done.6.refs_4_), channel_id=1, source_target_pairs={{0,4},{4,0},{8,12},{12,8},{16,20},{20,16},{24,28},{28,24},{1,5},{5... | collective-permute-start | bytes 196616 | tf_op jit(solution)/shard_map/ppermute | solution.py:143
  22.8 1.3 %collective-permute-start.5 = (bf16[8,4096]{1,0:T(8,128)(2,1)S(1)}, bf16[8,4096]{1,0:T(8,128)(2,1)S(1)}, u32[]{:S(2)}, u32[]{:S(2)}) collective-permute-start(bf16[8,4096]{1,0:T(8,128)(2,1)S(1)} %collective-permute-done.4.refs_2_), channel_id=1, source_target_pairs={{0,4},{4,0},{8,12},{12,8},{16,20},{20,16},{24,28},{28,24},{1,5},{5... | collective-permute-start | bytes 196616 | tf_op jit(solution)/shard_map/ppermute | solution.py:143

commit v8 on v6

--- a/solution.py
+++ b/solution.py
@@ -1,3 +1,5 @@
+import functools
+
 import jax
 import jax.numpy as jnp
 from jax import lax
@@ -106,34 +108,32 @@
     )(*(pltpu.with_memory_space_constraint(x, pltpu.HBM) for x in (doc_lengths, owner_map, proj_rows)))
 
 
-def score_kernel(query, *refs):
-    *blocks, scores = refs
-    doc_dev = blocks[0].shape[0]
-    features = jnp.concatenate([block[...] for block in blocks], axis=0)
+def score_kernel(doc_dev, query, mine, other, scores):
+    features = jnp.concatenate([mine[...], other[...]], axis=0)
     products = lax.dot_general(
         features, query[...], ROW_BY_ROW, preferred_element_type=jnp.float32
     )
-    parts = [products[i * doc_dev : (i + 1) * doc_dev] for i in range(len(blocks))]
-    ex = lax.axis_index("ex")
-    flip = 1
-    while flip < len(blocks):
-        swap = lax.rem(lax.div(ex, flip), 2) == 1
-        parts = [jnp.where(swap, parts[i ^ flip], parts[i]) for i in range(len(parts))]
-        flip *= 2
+    half = mine.shape[0]
+    odd = lax.rem(lax.axis_index("ex"), 2) == 1
+    parts = []
+    for i in range(0, half, doc_dev):
+        first, second = products[i : i + doc_dev], products[half + i : half + i + doc_dev]
+        parts += [jnp.where(odd, second, first), jnp.where(odd, first, second)]
     scores[...] = jnp.concatenate(parts, axis=0).T
 
 
-def block_scores(query_features, blocks):
+def block_scores(query_features, mine, other, doc_dev):
     whole = pl.BlockSpec(memory_space=pltpu.VMEM)
-    docs = len(blocks) * blocks[0].shape[0]
     return pl.pallas_call(
-        score_kernel,
-        out_shape=jax.ShapeDtypeStruct((query_features.shape[0], docs), jnp.float32),
-        in_specs=[whole] * (1 + len(blocks)),
+        functools.partial(score_kernel, doc_dev),
+        out_shape=jax.ShapeDtypeStruct(
+            (query_features.shape[0], mine.shape[0] + other.shape[0]), jnp.float32
+        ),
+        in_specs=[whole] * 3,
         out_specs=whole,
         compiler_params=pltpu.CompilerParams(vmem_limit_bytes=16 * 1024 * 1024),
         name="scores",
-    )(*(pltpu.with_memory_space_constraint(x, pltpu.VMEM) for x in (query_features, *blocks)))
+    )(*(pltpu.with_memory_space_constraint(x, pltpu.VMEM) for x in (query_features, mine, other)))
 
 
 def exchange(block, axis, flip):
@@ -151,12 +151,9 @@
     if ex_count != 8:
         gathered = lax.all_gather(features, "ex", axis=0, tiled=True)
         return jnp.einsum("qf,df->qd", query_features, gathered, preferred_element_type=jnp.float32)
-    blocks = [features] + [None] * (ex_count - 1)
-    for flip in (4, 2, 6):
-        blocks[flip] = exchange(features, "ex", flip)
-    for flip in (0, 4, 2, 6):
-        blocks[flip + 1] = exchange(blocks[flip], "ex", 1)
-    return block_scores(query_features, blocks)
+    cores = [list(range(core, ex_count, 2)) for core in range(2)]
+    mine = lax.all_gather(features, "ex", axis=0, tiled=True, axis_index_groups=cores)
+    return block_scores(query_features, mine, exchange(mine, "ex", 1), features.shape[0])
 
 
 def solution(mesh):

time: 23.1 us -> 25.3 us (1.095)
  blocking collectives: 0 us -> 9.23 us
  starting transfers between devices: 9.25 us -> 5.69 us
  waiting for transfers between devices: 9.7 us -> 6.27 us
    all_gather x0 -> x1, blocking collectives: none -> 9.23 us  [body(): lax.all_gather(features, 'ex', axis=0, tiled=True, axis_index_groups=cores)]
    ppermute x10 -> x4, starting transfers between devices: 9.25 us -> 5.69 us  [exchange(): lax.ppermute(block, axis, [(i, i ^ flip) for i in range(lax.axis_size(axi...]
    ppermute x10 -> x4, waiting for transfers between devices: 9.7 us -> 6.27 us  [exchange(): lax.ppermute(block, axis, [(i, i ^ flip) for i in range(lax.axis_size(axi...]
  transfers between devices with their start and end apart: 10 -> 4, of which waited for: 8 -> 4; matrix products, arithmetic and copies ran while one was open for 0% -> 0% of each run, Pallas kernels for 0% -> 0%
where the time goes in v8:
time: 25.3 us; the launch traced here: 25.2 us
  blocking collectives  9.23 us (36%)
  waiting for transfers between devices  6.27 us (25%)
  starting transfers between devices  5.69 us (22%)
  Pallas kernels  3.92 us (15%)
    all_gather x1, blocking collectives, body(): lax.all_gather(features, 'ex', axis=0, tiled=True, axis_index_groups=cores)  9.23 us
    ppermute x4, waiting for transfers between devices, exchange(): lax.ppermute(block, axis, [(i, i ^ flip) for i in range(lax.axis_size(axi...  6.27 us
    ppermute x4, starting transfers between devices, exchange(): lax.ppermute(block, axis, [(i, i ^ flip) for i in range(lax.axis_size(axi...  5.69 us
    pallas_call x1, Pallas kernels, feature_shares(): pl.pallas_call(feature_kernel, out_shape=[jax.ShapeDtypeStruct((doc_dev,...  2.94 us
    pallas_call x1, Pallas kernels, block_scores(): pl.pallas_call(functools.partial(score_kernel, doc_dev), out_shape=jax.Sh...  0.98 us
  transfers between devices with their start and end apart: 4, of which 4 were waited for; matrix products, arithmetic and copies ran while one was open for 0% of the time, Pallas kernels for 0%

profile of v8, /device:TPU:0, one launch (start us, length us, event | category | flops | bytes accessed | tf_op | source)
XLA Modules:
  0.0 25.2 jit_solution(1184307103877230092)
XLA Ops:
  0.0 0.0 copy-start
  0.0 2.9 %features.1 = (f32[8,4096]{1,0:T(8,128)S(1)}, bf16[8,4096]{1,0:T(8,128)(2,1)S(1)}, bf16[8,4096]{1,0:T(8,128)(2,1)S(1)}, bf16[8,4096]{1,0:T(8,128)(2,1)S(1)}) custom-call(s32[1,32]{1,0:T(1,128)} %lengths_hbm.1, s32[1,32]{1,0:T(1,128)} %owners_hbm.1, bf16[2048,128]{1,0:T(8,128)(2,1)} %rows_hbm.1), custom_call_target="tpu_custom_call" | custom-call | tf_op jit(solution)/shard_map/features/pallas_call | solution.py:89
  2.9 4.1 %collective-permute-start = (bf16[8,4096]{1,0:T(8,128)(2,1)S(1)}, bf16[8,4096]{1,0:T(8,128)(2,1)S(1)}, u32[]{:S(2)}, u32[]{:S(2)}) collective-permute-start(bf16[8,4096]{1,0:T(8,128)(2,1)S(1)} %get-tuple-element.10), channel_id=1, source_target_pairs={{0,2},{1,3},{2,0},{3,1},{4,6},{5,7},{6,4},{7,5},{8,10},{9,11},{10,... | collective-permute-start | bytes 196616 | tf_op jit(solution)/shard_map/ppermute | solution.py:140
  7.1 1.3 %collective-permute-start.1 = (bf16[8,4096]{1,0:T(8,128)(2,1)S(1)}, bf16[8,4096]{1,0:T(8,128)(2,1)S(1)}, u32[]{:S(2)}, u32[]{:S(2)}) collective-permute-start(bf16[8,4096]{1,0:T(8,128)(2,1)S(1)} %get-tuple-element.11), channel_id=1, source_target_pairs={{0,3},{1,2},{2,1},{3,0},{4,7},{5,6},{6,5},{7,4},{8,11},{9,10},{10,... | collective-permute-start | bytes 196616 | tf_op jit(solution)/shard_map/ppermute | solution.py:140
  8.4 0.2 collective-permute-start.2
  8.6 2.2 %collective-permute-done = bf16[8,4096]{1,0:T(8,128)(2,1)S(1)} collective-permute-done((bf16[8,4096]{1,0:T(8,128)(2,1)S(1)}, bf16[8,4096]{1,0:T(8,128)(2,1)S(1)}, u32[]{:S(2)}, u32[]{:S(2)}) %collective-permute-start) | collective-permute-done | bytes 65568 | tf_op jit(solution)/shard_map/ppermute | solution.py:140
  10.8 2.5 %collective-permute-done.1 = bf16[8,4096]{1,0:T(8,128)(2,1)S(1)} collective-permute-done((bf16[8,4096]{1,0:T(8,128)(2,1)S(1)}, bf16[8,4096]{1,0:T(8,128)(2,1)S(1)}, u32[]{:S(2)}, u32[]{:S(2)}) %collective-permute-start.1) | collective-permute-done | bytes 65568 | tf_op jit(solution)/shard_map/ppermute | solution.py:140
  13.3 0.1 collective-permute-done.2
  13.4 9.2 %all_gather.3.mine = bf16[32,4096]{1,0:T(8,128)(2,1)S(1)} all-gather(bf16[8,4096]{1,0:T(8,128)(2,1)S(1)} %add_convert_fusion), channel_id=1, replica_groups={{0,8,16,24},{4,12,20,28},{1,9,17,25},{5,13,21,29},{2,10,18,26},{6,14,22..., dimensions={0}, use_global_device_ids=true | all-gather | bytes 327680 | tf_op jit(solution)/shard_map/all_gather | solution.py:155
  22.6 0.0 collective-permute-start.3
  22.6 1.5 %collective-permute-done.3.other = bf16[32,4096]{1,0:T(8,128)(2,1)S(1)} collective-permute-done((bf16[32,4096]{1,0:T(8,128)(2,1)S(1)}, bf16[32,4096]{1,0:T(8,128)(2,1)S(1)}, u32[]{:S(2)}, u32[]{:S(2)}) %collective-permute-start.3) | collective-permute-done | bytes 262176 | tf_op jit(solution)/shard_map/ppermute | solution.py:140
  24.2 0.0 copy-done
  24.2 1.0 %scores.1 = f32[64,64]{1,0:T(8,128)} custom-call(bf16[64,4096]{1,0:T(8,128)(2,1)S(1)} %copy-done, bf16[32,4096]{1,0:T(8,128)(2,1)S(1)} %all_gather.3.mine, bf16[32,4096]{1,0:T(8,128)(2,1)S(1)} %collective-permute-done.3.other), custom_call_target="tpu_custom_call" | custom-call | tf_op jit(solution)/shard_map/scores/pallas_call | solution.py:127
  (1 shorter events, 0.0 us)
Async XLA Ops:
  0.0 24.2 %copy-start = (bf16[64,4096]{1,0:T(8,128)(2,1)S(1)}, bf16[64,4096]{1,0:T(8,128)(2,1)}, u32[]{:S(2)}) copy-start(bf16[64,4096]{1,0:T(8,128)(2,1)} %query.1) | copy-start | bytes 1572868
  2.9 7.9 %collective-permute-start = (bf16[8,4096]{1,0:T(8,128)(2,1)S(1)}, bf16[8,4096]{1,0:T(8,128)(2,1)S(1)}, u32[]{:S(2)}, u32[]{:S(2)}) collective-permute-start(bf16[8,4096]{1,0:T(8,128)(2,1)S(1)} %get-tuple-element.10), channel_id=1, source_target_pairs={{0,2},{1,3},{2,0},{3,1},{4,6},{5,7},{6,4},{7,5},{8,10},{9,11},{10,... | collective-permute-start | bytes 196616 | tf_op jit(solution)/shard_map/ppermute | solution.py:140
  7.1 6.2 %collective-permute-start.1 = (bf16[8,4096]{1,0:T(8,128)(2,1)S(1)}, bf16[8,4096]{1,0:T(8,128)(2,1)S(1)}, u32[]{:S(2)}, u32[]{:S(2)}) collective-permute-start(bf16[8,4096]{1,0:T(8,128)(2,1)S(1)} %get-tuple-element.11), channel_id=1, source_target_pairs={{0,3},{1,2},{2,1},{3,0},{4,7},{5,6},{6,5},{7,4},{8,11},{9,10},{10,... | collective-permute-start | bytes 196616 | tf_op jit(solution)/shard_map/ppermute | solution.py:140
  8.4 5.0 %collective-permute-start.2 = (bf16[8,4096]{1,0:T(8,128)(2,1)S(1)}, bf16[8,4096]{1,0:T(8,128)(2,1)S(1)}, u32[]{:S(2)}, u32[]{:S(2)}) collective-permute-start(bf16[8,4096]{1,0:T(8,128)(2,1)S(1)} %get-tuple-element.12), channel_id=1, source_target_pairs={{0,1},{1,0},{2,3},{3,2},{4,5},{5,4},{6,7},{7,6},{8,9},{9,8},{10,11... | collective-permute-start | bytes 196616 | tf_op jit(solution)/shard_map/ppermute | solution.py:140
  22.6 1.5 %collective-permute-start.3 = (bf16[32,4096]{1,0:T(8,128)(2,1)S(1)}, bf16[32,4096]{1,0:T(8,128)(2,1)S(1)}, u32[]{:S(2)}, u32[]{:S(2)}) collective-permute-start(bf16[32,4096]{1,0:T(8,128)(2,1)S(1)} %all_gather.3.mine), channel_id=1, source_target_pairs={{0,4},{4,0},{8,12},{12,8},{16,20},{20,16},{24,28},{28,24},{1,5},{5... | collective-permute-start | bytes 786440 | tf_op jit(solution)/shard_map/ppermute | solution.py:140

commit v9 on v6

--- a/solution.py
+++ b/solution.py
@@ -26,24 +26,20 @@
 
     copies[0].wait()
     copies[1].wait()
-    blocks = count // LANES
+    blocks, shift = count // LANES, doc_dev.bit_length() - 1
     token = lax.broadcasted_iota(jnp.int32, (blocks, LANES), 0) * LANES
     token = tok * count + token + lax.broadcasted_iota(jnp.int32, (blocks, LANES), 1)
-    share_of = jnp.zeros((blocks, LANES), jnp.int32)
-    row_of = jnp.zeros((blocks, LANES), jnp.int32)
+    slot_of = jnp.zeros((blocks, LANES), jnp.int32)
     size_row = lax.broadcasted_iota(jnp.int32, (doc_dev, LANES), 0)
+    size_slots = [((tok ^ s) << shift) + size_row for s in range(tok_count)]
     sizes = [jnp.ones((doc_dev, LANES), jnp.int32) for _ in shares]
     start = jnp.int32(0)
     for k in range(docs):
-        slot = owners[0, k]
-        share = lax.div(slot, doc_dev) ^ tok
-        row = lax.rem(slot, doc_dev)
-        here = token >= start
-        share_of = jnp.where(here, share, share_of)
-        row_of = jnp.where(here, row, row_of)
-        for s in range(tok_count):
-            sizes[s] = jnp.where(size_row == jnp.where(share == s, row, -1), lengths[0, k], sizes[s])
-        start = start + lengths[0, k]
+        slot, length = owners[0, k], lengths[0, k]
+        slot_of = jnp.where(token >= start, slot, slot_of)
+        sizes = [jnp.where(at == slot, length, size) for at, size in zip(size_slots, sizes)]
+        start = start + length
+    share_of, row_of = (slot_of >> shift) ^ tok, slot_of & (doc_dev - 1)
 
     eye = (
         lax.broadcasted_iota(jnp.int32, (2 * width, 2 * width), 0)
@@ -53,12 +49,15 @@
     for b in range(blocks):
         part = slice(b * LANES, (b + 1) * LANES)
         turned = lax.dot_general(eye, rows[part, :], ROW_BY_ROW, preferred_element_type=jnp.float32)
-        for s in range(tok_count):
-            kept = jnp.where(share_of[b : b + 1, :] == s, turned[:width], 0.0)
-            inputs[s * width : (s + 1) * width, part] = kept.astype(inputs.dtype)
-        for r in range(doc_dev):
-            kept = jnp.where(row_of[b : b + 1, :] == r, turned[width:], 0.0)
-            grads[r * width : (r + 1) * width, part] = kept.astype(grads.dtype)
+        for digits, values, target in (
+            (share_of, turned[:width], inputs),
+            (row_of, turned[width:], grads),
+        ):
+            digit = jnp.broadcast_to(digits[b : b + 1, :], (8, LANES))[None]
+            values = values.reshape(-1, 8, LANES)
+            for at in range(target.shape[0] // width):
+                kept = jnp.where(digit == at, values, 0.0).reshape(width, LANES)
+                target[at * width : (at + 1) * width, part] = kept.astype(target.dtype)
     product = lax.dot_general(
         grads[...], inputs[...], ROW_BY_ROW, preferred_element_type=jnp.float32
     )
@@ -110,8 +109,13 @@
     *blocks, scores = refs
     doc_dev = blocks[0].shape[0]
     features = jnp.concatenate([block[...] for block in blocks], axis=0)
-    products = lax.dot_general(
-        features, query[...], ROW_BY_ROW, preferred_element_type=jnp.float32
+    depth = features.shape[1] // 4
+    products = sum(
+        lax.dot_general(
+            features[:, at : at + depth], query[:, at : at + depth], ROW_BY_ROW,
+            preferred_element_type=jnp.float32,
+        )
+        for at in range(0, features.shape[1], depth)
     )
     parts = [products[i * doc_dev : (i + 1) * doc_dev] for i in range(len(blocks))]
     ex = lax.axis_index("ex")

time: 23.1 us -> 23.1 us (level)
  no operation moved by 1% of the time
where the time goes in v9:
time: 23.1 us; the launch traced here: 22.9 us
  waiting for transfers between devices  9.7 us (42%)
  starting transfers between devices  9.25 us (40%)
  Pallas kernels  3.89 us (17%)
    ppermute x10, waiting for transfers between devices, exchange(): lax.ppermute(block, axis, [(i, i ^ flip) for i in range(lax.axis_size(axi...  9.7 us
    ppermute x10, starting transfers between devices, exchange(): lax.ppermute(block, axis, [(i, i ^ flip) for i in range(lax.axis_size(axi...  9.25 us
    pallas_call x1, Pallas kernels, feature_shares(): pl.pallas_call(feature_kernel, out_shape=[jax.ShapeDtypeStruct((doc_dev,...  2.9 us
    pallas_call x1, Pallas kernels, block_scores(): pl.pallas_call(score_kernel, out_shape=jax.ShapeDtypeStruct((query_featur...  0.99 us
  transfers between devices with their start and end apart: 10, of which 8 were waited for; matrix products, arithmetic and copies ran while one was open for 0% of the time, Pallas kernels for 0%

profile of v9, /device:TPU:0, one launch (start us, length us, event | category | flops | bytes accessed | tf_op | source)
XLA Modules:
  0.0 22.9 jit_solution(12319537630305928992)
XLA Ops:
  0.0 0.0 copy-start
  0.0 2.9 %features.1 = (f32[8,4096]{1,0:T(8,128)S(1)}, bf16[8,4096]{1,0:T(8,128)(2,1)S(1)}, bf16[8,4096]{1,0:T(8,128)(2,1)S(1)}, bf16[8,4096]{1,0:T(8,128)(2,1)S(1)}) custom-call(s32[1,32]{1,0:T(1,128)} %lengths_hbm.1, s32[1,32]{1,0:T(1,128)} %owners_hbm.1, bf16[2048,128]{1,0:T(8,128)(2,1)} %rows_hbm.1), custom_call_target="tpu_custom_call" | custom-call | tf_op jit(solution)/shard_map/features/pallas_call | solution.py:86
  2.9 4.1 %collective-permute-start = (bf16[8,4096]{1,0:T(8,128)(2,1)S(1)}, bf16[8,4096]{1,0:T(8,128)(2,1)S(1)}, u32[]{:S(2)}, u32[]{:S(2)}) collective-permute-start(bf16[8,4096]{1,0:T(8,128)(2,1)S(1)} %get-tuple-element.10), channel_id=1, source_target_pairs={{0,2},{1,3},{2,0},{3,1},{4,6},{5,7},{6,4},{7,5},{8,10},{9,11},{10,... | collective-permute-start | bytes 196616 | tf_op jit(solution)/shard_map/ppermute | solution.py:144
  7.0 1.3 %collective-permute-start.1 = (bf16[8,4096]{1,0:T(8,128)(2,1)S(1)}, bf16[8,4096]{1,0:T(8,128)(2,1)S(1)}, u32[]{:S(2)}, u32[]{:S(2)}) collective-permute-start(bf16[8,4096]{1,0:T(8,128)(2,1)S(1)} %get-tuple-element.11), channel_id=1, source_target_pairs={{0,3},{1,2},{2,1},{3,0},{4,7},{5,6},{6,5},{7,4},{8,11},{9,10},{10,... | collective-permute-start | bytes 196616 | tf_op jit(solution)/shard_map/ppermute | solution.py:144
  8.4 0.2 collective-permute-start.2
  8.6 2.2 %collective-permute-done = bf16[8,4096]{1,0:T(8,128)(2,1)S(1)} collective-permute-done((bf16[8,4096]{1,0:T(8,128)(2,1)S(1)}, bf16[8,4096]{1,0:T(8,128)(2,1)S(1)}, u32[]{:S(2)}, u32[]{:S(2)}) %collective-permute-start) | collective-permute-done | bytes 65568 | tf_op jit(solution)/shard_map/ppermute | solution.py:144
  10.8 2.5 %collective-permute-done.1 = bf16[8,4096]{1,0:T(8,128)(2,1)S(1)} collective-permute-done((bf16[8,4096]{1,0:T(8,128)(2,1)S(1)}, bf16[8,4096]{1,0:T(8,128)(2,1)S(1)}, u32[]{:S(2)}, u32[]{:S(2)}) %collective-permute-start.1) | collective-permute-done | bytes 65568 | tf_op jit(solution)/shard_map/ppermute | solution.py:144
  13.2 0.1 collective-permute-done.2
  13.4 2.5 %collective-permute-start.8 = (bf16[8,4096]{1,0:T(8,128)(2,1)S(1)}, bf16[8,4096]{1,0:T(8,128)(2,1)S(1)}, u32[]{:S(2)}, u32[]{:S(2)}) collective-permute-start(bf16[8,4096]{1,0:T(8,128)(2,1)S(1)} %add_convert_fusion.refs_0_), channel_id=1, source_target_pairs={{0,24},{4,28},{8,16},{12,20},{16,8},{20,12},{24,0},{28,4},{1,25},{... | collective-permute-start | bytes 196616 | tf_op jit(solution)/shard_map/ppermute | solution.py:144
  15.9 0.5 %collective-permute-start.6 = (bf16[8,4096]{1,0:T(8,128)(2,1)S(1)}, bf16[8,4096]{1,0:T(8,128)(2,1)S(1)}, u32[]{:S(2)}, u32[]{:S(2)}) collective-permute-start(bf16[8,4096]{1,0:T(8,128)(2,1)S(1)} %add_convert_fusion.refs_0_), channel_id=1, source_target_pairs={{0,16},{4,20},{8,24},{12,28},{16,0},{20,4},{24,8},{28,12},{1,17},{... | collective-permute-start | bytes 196616 | tf_op jit(solution)/shard_map/ppermute | solution.py:144
  16.4 0.5 %collective-permute-start.4 = (bf16[8,4096]{1,0:T(8,128)(2,1)S(1)}, bf16[8,4096]{1,0:T(8,128)(2,1)S(1)}, u32[]{:S(2)}, u32[]{:S(2)}) collective-permute-start(bf16[8,4096]{1,0:T(8,128)(2,1)S(1)} %add_convert_fusion.refs_0_), channel_id=1, source_target_pairs={{0,8},{4,12},{8,0},{12,4},{16,24},{20,28},{24,16},{28,20},{1,9},{5... | collective-permute-start | bytes 196616 | tf_op jit(solution)/shard_map/ppermute | solution.py:144
  16.9 0.0 collective-permute-start.3
  16.9 2.3 %collective-permute-done.8.refs_6_ = bf16[8,4096]{1,0:T(8,128)(2,1)S(1)} collective-permute-done((bf16[8,4096]{1,0:T(8,128)(2,1)S(1)}, bf16[8,4096]{1,0:T(8,128)(2,1)S(1)}, u32[]{:S(2)}, u32[]{:S(2)}) %collective-permute-start.8) | collective-permute-done | bytes 65568 | tf_op jit(solution)/shard_map/ppermute | solution.py:144
  19.2 0.0 collective-permute-start.9
  19.2 0.9 %collective-permute-done.6.refs_4_ = bf16[8,4096]{1,0:T(8,128)(2,1)S(1)} collective-permute-done((bf16[8,4096]{1,0:T(8,128)(2,1)S(1)}, bf16[8,4096]{1,0:T(8,128)(2,1)S(1)}, u32[]{:S(2)}, u32[]{:S(2)}) %collective-permute-start.6) | collective-permute-done | bytes 65568 | tf_op jit(solution)/shard_map/ppermute | solution.py:144
  20.2 0.0 collective-permute-start.7
  20.2 0.5 %collective-permute-done.4.refs_2_ = bf16[8,4096]{1,0:T(8,128)(2,1)S(1)} collective-permute-done((bf16[8,4096]{1,0:T(8,128)(2,1)S(1)}, bf16[8,4096]{1,0:T(8,128)(2,1)S(1)}, u32[]{:S(2)}, u32[]{:S(2)}) %collective-permute-start.4) | collective-permute-done | bytes 65568 | tf_op jit(solution)/shard_map/ppermute | solution.py:144
  20.7 0.0 collective-permute-start.5
  20.7 0.0 collective-permute-done.3.refs_1_
  20.7 0.0 collective-permute-done.9.refs_7_
  20.7 0.7 %collective-permute-done.7.refs_5_ = bf16[8,4096]{1,0:T(8,128)(2,1)S(1)} collective-permute-done((bf16[8,4096]{1,0:T(8,128)(2,1)S(1)}, bf16[8,4096]{1,0:T(8,128)(2,1)S(1)}, u32[]{:S(2)}, u32[]{:S(2)}) %collective-permute-start.7) | collective-permute-done | bytes 65568 | tf_op jit(solution)/shard_map/ppermute | solution.py:144
  21.4 0.5 %collective-permute-done.5.refs_3_ = bf16[8,4096]{1,0:T(8,128)(2,1)S(1)} collective-permute-done((bf16[8,4096]{1,0:T(8,128)(2,1)S(1)}, bf16[8,4096]{1,0:T(8,128)(2,1)S(1)}, u32[]{:S(2)}, u32[]{:S(2)}) %collective-permute-start.5) | collective-permute-done | bytes 65568 | tf_op jit(solution)/shard_map/ppermute | solution.py:144
  21.9 0.0 copy-done
  21.9 1.0 %scores.1 = f32[64,64]{1,0:T(8,128)} custom-call(bf16[64,4096]{1,0:T(8,128)(2,1)S(1)} %copy-done, bf16[8,4096]{1,0:T(8,128)(2,1)S(1)} %add_convert_fusion.refs_0_, bf16[8,4096]{1,0:T(8,128)(2,1)S(1)} %collective-permute-done.3.refs_1_, bf16[8,4096]{1,0:T(8,128)(2,1)S(1)} %collective-permute-done.4.refs_2_, ...), custom_call_target="tpu_custom_call" | custom-call | tf_op jit(solution)/shard_map/scores/pallas_call | solution.py:133
  (1 shorter events, 0.0 us)
Async XLA Ops:
  0.0 21.9 %copy-start = (bf16[64,4096]{1,0:T(8,128)(2,1)S(1)}, bf16[64,4096]{1,0:T(8,128)(2,1)}, u32[]{:S(2)}) copy-start(bf16[64,4096]{1,0:T(8,128)(2,1)} %query.1) | copy-start | bytes 1572868
  2.9 7.9 %collective-permute-start = (bf16[8,4096]{1,0:T(8,128)(2,1)S(1)}, bf16[8,4096]{1,0:T(8,128)(2,1)S(1)}, u32[]{:S(2)}, u32[]{:S(2)}) collective-permute-start(bf16[8,4096]{1,0:T(8,128)(2,1)S(1)} %get-tuple-element.10), channel_id=1, source_target_pairs={{0,2},{1,3},{2,0},{3,1},{4,6},{5,7},{6,4},{7,5},{8,10},{9,11},{10,... | collective-permute-start | bytes 196616 | tf_op jit(solution)/shard_map/ppermute | solution.py:144
  7.0 6.2 %collective-permute-start.1 = (bf16[8,4096]{1,0:T(8,128)(2,1)S(1)}, bf16[8,4096]{1,0:T(8,128)(2,1)S(1)}, u32[]{:S(2)}, u32[]{:S(2)}) collective-permute-start(bf16[8,4096]{1,0:T(8,128)(2,1)S(1)} %get-tuple-element.11), channel_id=1, source_target_pairs={{0,3},{1,2},{2,1},{3,0},{4,7},{5,6},{6,5},{7,4},{8,11},{9,10},{10,... | collective-permute-start | bytes 196616 | tf_op jit(solution)/shard_map/ppermute | solution.py:144
  8.4 5.0 %collective-permute-start.2 = (bf16[8,4096]{1,0:T(8,128)(2,1)S(1)}, bf16[8,4096]{1,0:T(8,128)(2,1)S(1)}, u32[]{:S(2)}, u32[]{:S(2)}) collective-permute-start(bf16[8,4096]{1,0:T(8,128)(2,1)S(1)} %get-tuple-element.12), channel_id=1, source_target_pairs={{0,1},{1,0},{2,3},{3,2},{4,5},{5,4},{6,7},{7,6},{8,9},{9,8},{10,11... | collective-permute-start | bytes 196616 | tf_op jit(solution)/shard_map/ppermute | solution.py:144
  13.4 5.9 %collective-permute-start.8 = (bf16[8,4096]{1,0:T(8,128)(2,1)S(1)}, bf16[8,4096]{1,0:T(8,128)(2,1)S(1)}, u32[]{:S(2)}, u32[]{:S(2)}) collective-permute-start(bf16[8,4096]{1,0:T(8,128)(2,1)S(1)} %add_convert_fusion.refs_0_), channel_id=1, source_target_pairs={{0,24},{4,28},{8,16},{12,20},{16,8},{20,12},{24,0},{28,4},{1,25},{... | collective-permute-start | bytes 196616 | tf_op jit(solution)/shard_map/ppermute | solution.py:144
  15.9 4.3 %collective-permute-start.6 = (bf16[8,4096]{1,0:T(8,128)(2,1)S(1)}, bf16[8,4096]{1,0:T(8,128)(2,1)S(1)}, u32[]{:S(2)}, u32[]{:S(2)}) collective-permute-start(bf16[8,4096]{1,0:T(8,128)(2,1)S(1)} %add_convert_fusion.refs_0_), channel_id=1, source_target_pairs={{0,16},{4,20},{8,24},{12,28},{16,0},{20,4},{24,8},{28,12},{1,17},{... | collective-permute-start | bytes 196616 | tf_op jit(solution)/shard_map/ppermute | solution.py:144
  16.4 4.3 %collective-permute-start.4 = (bf16[8,4096]{1,0:T(8,128)(2,1)S(1)}, bf16[8,4096]{1,0:T(8,128)(2,1)S(1)}, u32[]{:S(2)}, u32[]{:S(2)}) collective-permute-start(bf16[8,4096]{1,0:T(8,128)(2,1)S(1)} %add_convert_fusion.refs_0_), channel_id=1, source_target_pairs={{0,8},{4,12},{8,0},{12,4},{16,24},{20,28},{24,16},{28,20},{1,9},{5... | collective-permute-start | bytes 196616 | tf_op jit(solution)/shard_map/ppermute | solution.py:144
  16.9 3.7 %collective-permute-start.3 = (bf16[8,4096]{1,0:T(8,128)(2,1)S(1)}, bf16[8,4096]{1,0:T(8,128)(2,1)S(1)}, u32[]{:S(2)}, u32[]{:S(2)}) collective-permute-start(bf16[8,4096]{1,0:T(8,128)(2,1)S(1)} %add_convert_fusion.refs_0_), channel_id=1, source_target_pairs={{0,4},{4,0},{8,12},{12,8},{16,20},{20,16},{24,28},{28,24},{1,5},{5... | collective-permute-start | bytes 196616 | tf_op jit(solution)/shard_map/ppermute | solution.py:144
  19.2 1.4 %collective-permute-start.9 = (bf16[8,4096]{1,0:T(8,128)(2,1)S(1)}, bf16[8,4096]{1,0:T(8,128)(2,1)S(1)}, u32[]{:S(2)}, u32[]{:S(2)}) collective-permute-start(bf16[8,4096]{1,0:T(8,128)(2,1)S(1)} %collective-permute-done.8.refs_6_), channel_id=1, source_target_pairs={{0,4},{4,0},{8,12},{12,8},{16,20},{20,16},{24,28},{28,24},{1,5},{5... | collective-permute-start | bytes 196616 | tf_op jit(solution)/shard_map/ppermute | solution.py:144
  20.2 1.3 %collective-permute-start.7 = (bf16[8,4096]{1,0:T(8,128)(2,1)S(1)}, bf16[8,4096]{1,0:T(8,128)(2,1)S(1)}, u32[]{:S(2)}, u32[]{:S(2)}) collective-permute-start(bf16[8,4096]{1,0:T(8,128)(2,1)S(1)} %collective-permute-done.6.refs_4_), channel_id=1, source_target_pairs={{0,4},{4,0},{8,12},{12,8},{16,20},{20,16},{24,28},{28,24},{1,5},{5... | collective-permute-start | bytes 196616 | tf_op jit(solution)/shard_map/ppermute | solution.py:144
  20.7 1.3 %collective-permute-start.5 = (bf16[8,4096]{1,0:T(8,128)(2,1)S(1)}, bf16[8,4096]{1,0:T(8,128)(2,1)S(1)}, u32[]{:S(2)}, u32[]{:S(2)}) collective-permute-start(bf16[8,4096]{1,0:T(8,128)(2,1)S(1)} %collective-permute-done.4.refs_2_), channel_id=1, source_target_pairs={{0,4},{4,0},{8,12},{12,8},{16,20},{20,16},{24,28},{28,24},{1,5},{5... | collective-permute-start | bytes 196616 | tf_op jit(solution)/shard_map/ppermute | solution.py:144

commit v10 on v9

--- a/solution.py
+++ b/solution.py
@@ -10,7 +10,7 @@
 
 
 def feature_kernel(lengths_hbm, owners_hbm, rows_hbm, *refs):
-    *shares, lengths, owners, rows, grads, inputs, sums, arrived = refs
+    *shares, lengths, owners, rows, digits, grads, inputs, sums, arrived = refs
     count, width = rows.shape[0], rows.shape[1] // 2
     copies = [
         pltpu.make_async_copy(source, target, arrived.at[i])
@@ -29,45 +29,62 @@
     blocks, shift = count // LANES, doc_dev.bit_length() - 1
     token = lax.broadcasted_iota(jnp.int32, (blocks, LANES), 0) * LANES
     token = tok * count + token + lax.broadcasted_iota(jnp.int32, (blocks, LANES), 1)
-    slot_of = jnp.zeros((blocks, LANES), jnp.int32)
     size_row = lax.broadcasted_iota(jnp.int32, (doc_dev, LANES), 0)
     size_slots = [((tok ^ s) << shift) + size_row for s in range(tok_count)]
-    sizes = [jnp.ones((doc_dev, LANES), jnp.int32) for _ in shares]
-    start = jnp.int32(0)
-    for k in range(docs):
+
+    def place(k, carry):
+        start, slot_of, *sizes = carry
         slot, length = owners[0, k], lengths[0, k]
         slot_of = jnp.where(token >= start, slot, slot_of)
         sizes = [jnp.where(at == slot, length, size) for at, size in zip(size_slots, sizes)]
-        start = start + length
-    share_of, row_of = (slot_of >> shift) ^ tok, slot_of & (doc_dev - 1)
+        return (start + length, slot_of, *sizes)
+
+    _, slot_of, *sizes = lax.fori_loop(
+        0,
+        docs,
+        place,
+        (jnp.int32(0), jnp.zeros((blocks, LANES), jnp.int32))
+        + (jnp.ones((doc_dev, LANES), jnp.int32),) * tok_count,
+        unroll=4,
+    )
+    digits[0] = (slot_of >> shift) ^ tok
+    digits[1] = slot_of & (doc_dev - 1)
 
     eye = (
         lax.broadcasted_iota(jnp.int32, (2 * width, 2 * width), 0)
         == lax.broadcasted_iota(jnp.int32, (2 * width, 2 * width), 1)
     ).astype(rows.dtype)
     copies[2].wait()
-    for b in range(blocks):
-        part = slice(b * LANES, (b + 1) * LANES)
+
+    @pl.loop(0, blocks)
+    def _(b):
+        part = pl.ds(pl.multiple_of(b * LANES, LANES), LANES)
         turned = lax.dot_general(eye, rows[part, :], ROW_BY_ROW, preferred_element_type=jnp.float32)
-        for digits, values, target in (
-            (share_of, turned[:width], inputs),
-            (row_of, turned[width:], grads),
-        ):
-            digit = jnp.broadcast_to(digits[b : b + 1, :], (8, LANES))[None]
-            values = values.reshape(-1, 8, LANES)
+        for i, target in enumerate((inputs, grads)):
+            digit = jnp.broadcast_to(digits[i, pl.ds(b, 1), :], (8, LANES))[None]
+            values = turned[i * width : (i + 1) * width].reshape(-1, 8, LANES)
             for at in range(target.shape[0] // width):
                 kept = jnp.where(digit == at, values, 0.0).reshape(width, LANES)
                 target[at * width : (at + 1) * width, part] = kept.astype(target.dtype)
-    product = lax.dot_general(
-        grads[...], inputs[...], ROW_BY_ROW, preferred_element_type=jnp.float32
-    )
-    for p in range(sums.shape[0]):
-        sums[p] = product[:, p * LANES : (p + 1) * LANES]
+
+    sums[...] = jnp.zeros_like(sums)
+    depth = count // 4
+
+    @pl.loop(0, 4)
+    def _(c):
+        part = pl.ds(pl.multiple_of(c * depth, depth), depth)
+        product = lax.dot_general(
+            grads[:, part], inputs[:, part], ROW_BY_ROW, preferred_element_type=jnp.float32
+        )
+        for p in range(sums.shape[0]):
+            sums[p] += product[:, p * LANES : (p + 1) * LANES]
 
     scales = [1.0 / jnp.sqrt(size.astype(jnp.float32)) for size in sizes]
     low_half = lax.broadcasted_iota(jnp.int32, (doc_dev, LANES), 1) < width
-    for m in range(width // 2):
-        out = slice(m * LANES, (m + 1) * LANES)
+
+    @pl.loop(0, width // 2, unroll=4)
+    def _(m):
+        out = pl.ds(pl.multiple_of(m * LANES, LANES), LANES)
         for s in range(0, tok_count, 2):
             first = sums[s // 2, pl.ds(2 * m, doc_dev, stride=width), :]
             second = sums[s // 2, pl.ds(2 * m + 1, doc_dev, stride=width), :]
@@ -95,6 +112,7 @@
             pltpu.SMEM(doc_lengths.shape, jnp.int32),
             pltpu.SMEM(owner_map.shape, jnp.int32),
             pltpu.VMEM(proj_rows.shape, proj_rows.dtype),
+            pltpu.VMEM((2, count // LANES, LANES), jnp.int32),
             pltpu.VMEM((doc_dev * width, count), jnp.bfloat16),
             pltpu.VMEM((tok_count * width, count), jnp.bfloat16),
             pltpu.VMEM((tok_count // 2, doc_dev * width, LANES), jnp.float32),
@@ -108,15 +126,16 @@
 def score_kernel(query, *refs):
     *blocks, scores = refs
     doc_dev = blocks[0].shape[0]
-    features = jnp.concatenate([block[...] for block in blocks], axis=0)
-    depth = features.shape[1] // 4
-    products = sum(
-        lax.dot_general(
-            features[:, at : at + depth], query[:, at : at + depth], ROW_BY_ROW,
-            preferred_element_type=jnp.float32,
+    docs, depth = len(blocks) * doc_dev, query.shape[1] // 4
+
+    def add(c, total):
+        part = pl.ds(pl.multiple_of(c * depth, depth), depth)
+        features = jnp.concatenate([block[:, part] for block in blocks], axis=0)
+        return total + lax.dot_general(
+            features, query[:, part], ROW_BY_ROW, preferred_element_type=jnp.float32
         )
-        for at in range(0, features.shape[1], depth)
-    )
+
+    products = lax.fori_loop(0, 4, add, jnp.zeros((docs, query.shape[0]), jnp.float32))
     parts = [products[i * doc_dev : (i + 1) * doc_dev] for i in range(len(blocks))]
     ex = lax.axis_index("ex")
     flip = 1

time: 23.1 us -> 27.3 us (1.18)
  Pallas kernels: 3.89 us -> 8.1 us
    pallas_call x1, Pallas kernels: 2.9 us -> 6.68 us  [feature_shares(): pl.pallas_call(feature_kernel, out_shape=[jax.ShapeDtypeStruct((doc_dev,...]
    pallas_call x1, Pallas kernels: 0.99 us -> 1.42 us  [block_scores(): pl.pallas_call(score_kernel, out_shape=jax.ShapeDtypeStruct((query_featur...]
where the time goes in v10:
time: 27.3 us; the launch traced here: 27.1 us
  waiting for transfers between devices  9.7 us (36%)
  starting transfers between devices  9.25 us (34%)
  Pallas kernels  8.1 us (30%)
    ppermute x10, waiting for transfers between devices, exchange(): lax.ppermute(block, axis, [(i, i ^ flip) for i in range(lax.axis_size(axi...  9.7 us
    ppermute x10, starting transfers between devices, exchange(): lax.ppermute(block, axis, [(i, i ^ flip) for i in range(lax.axis_size(axi...  9.25 us
    pallas_call x1, Pallas kernels, feature_shares(): pl.pallas_call(feature_kernel, out_shape=[jax.ShapeDtypeStruct((doc_dev,...  6.68 us
    pallas_call x1, Pallas kernels, block_scores(): pl.pallas_call(score_kernel, out_shape=jax.ShapeDtypeStruct((query_featur...  1.42 us
  transfers between devices with their start and end apart: 10, of which 8 were waited for; matrix products, arithmetic and copies ran while one was open for 0% of the time, Pallas kernels for 0%

profile of v10, /device:TPU:0, one launch (start us, length us, event | category | flops | bytes accessed | tf_op | source)
XLA Modules:
  0.0 27.1 jit_solution(6886723681238542142)
XLA Ops:
  0.0 0.0 copy-start
  0.0 6.7 %features.1 = (f32[8,4096]{1,0:T(8,128)S(1)}, bf16[8,4096]{1,0:T(8,128)(2,1)S(1)}, bf16[8,4096]{1,0:T(8,128)(2,1)S(1)}, bf16[8,4096]{1,0:T(8,128)(2,1)S(1)}) custom-call(s32[1,32]{1,0:T(1,128)} %lengths_hbm.1, s32[1,32]{1,0:T(1,128)} %owners_hbm.1, bf16[2048,128]{1,0:T(8,128)(2,1)} %rows_hbm.1), custom_call_target="tpu_custom_call" | custom-call | tf_op jit(solution)/shard_map/features/pallas_call | solution.py:103
  6.7 4.1 %collective-permute-start = (bf16[8,4096]{1,0:T(8,128)(2,1)S(1)}, bf16[8,4096]{1,0:T(8,128)(2,1)S(1)}, u32[]{:S(2)}, u32[]{:S(2)}) collective-permute-start(bf16[8,4096]{1,0:T(8,128)(2,1)S(1)} %get-tuple-element.10), channel_id=1, source_target_pairs={{0,2},{1,3},{2,0},{3,1},{4,6},{5,7},{6,4},{7,5},{8,10},{9,11},{10,... | collective-permute-start | bytes 196616 | tf_op jit(solution)/shard_map/ppermute | solution.py:163
  10.8 1.3 %collective-permute-start.1 = (bf16[8,4096]{1,0:T(8,128)(2,1)S(1)}, bf16[8,4096]{1,0:T(8,128)(2,1)S(1)}, u32[]{:S(2)}, u32[]{:S(2)}) collective-permute-start(bf16[8,4096]{1,0:T(8,128)(2,1)S(1)} %get-tuple-element.11), channel_id=1, source_target_pairs={{0,3},{1,2},{2,1},{3,0},{4,7},{5,6},{6,5},{7,4},{8,11},{9,10},{10,... | collective-permute-start | bytes 196616 | tf_op jit(solution)/shard_map/ppermute | solution.py:163
  12.1 0.3 collective-permute-start.2
  12.4 2.2 %collective-permute-done = bf16[8,4096]{1,0:T(8,128)(2,1)S(1)} collective-permute-done((bf16[8,4096]{1,0:T(8,128)(2,1)S(1)}, bf16[8,4096]{1,0:T(8,128)(2,1)S(1)}, u32[]{:S(2)}, u32[]{:S(2)}) %collective-permute-start) | collective-permute-done | bytes 65568 | tf_op jit(solution)/shard_map/ppermute | solution.py:163
  14.6 2.5 %collective-permute-done.1 = bf16[8,4096]{1,0:T(8,128)(2,1)S(1)} collective-permute-done((bf16[8,4096]{1,0:T(8,128)(2,1)S(1)}, bf16[8,4096]{1,0:T(8,128)(2,1)S(1)}, u32[]{:S(2)}, u32[]{:S(2)}) %collective-permute-start.1) | collective-permute-done | bytes 65568 | tf_op jit(solution)/shard_map/ppermute | solution.py:163
  17.0 0.1 collective-permute-done.2
  17.1 2.5 %collective-permute-start.8 = (bf16[8,4096]{1,0:T(8,128)(2,1)S(1)}, bf16[8,4096]{1,0:T(8,128)(2,1)S(1)}, u32[]{:S(2)}, u32[]{:S(2)}) collective-permute-start(bf16[8,4096]{1,0:T(8,128)(2,1)S(1)} %add_convert_fusion.refs_0_), channel_id=1, source_target_pairs={{0,24},{4,28},{8,16},{12,20},{16,8},{20,12},{24,0},{28,4},{1,25},{... | collective-permute-start | bytes 196616 | tf_op jit(solution)/shard_map/ppermute | solution.py:163
  19.6 0.5 %collective-permute-start.6 = (bf16[8,4096]{1,0:T(8,128)(2,1)S(1)}, bf16[8,4096]{1,0:T(8,128)(2,1)S(1)}, u32[]{:S(2)}, u32[]{:S(2)}) collective-permute-start(bf16[8,4096]{1,0:T(8,128)(2,1)S(1)} %add_convert_fusion.refs_0_), channel_id=1, source_target_pairs={{0,16},{4,20},{8,24},{12,28},{16,0},{20,4},{24,8},{28,12},{1,17},{... | collective-permute-start | bytes 196616 | tf_op jit(solution)/shard_map/ppermute | solution.py:163
  20.2 0.5 %collective-permute-start.4 = (bf16[8,4096]{1,0:T(8,128)(2,1)S(1)}, bf16[8,4096]{1,0:T(8,128)(2,1)S(1)}, u32[]{:S(2)}, u32[]{:S(2)}) collective-permute-start(bf16[8,4096]{1,0:T(8,128)(2,1)S(1)} %add_convert_fusion.refs_0_), channel_id=1, source_target_pairs={{0,8},{4,12},{8,0},{12,4},{16,24},{20,28},{24,16},{28,20},{1,9},{5... | collective-permute-start | bytes 196616 | tf_op jit(solution)/shard_map/ppermute | solution.py:163
  20.7 0.0 collective-permute-start.3
  20.7 2.3 %collective-permute-done.8.refs_6_ = bf16[8,4096]{1,0:T(8,128)(2,1)S(1)} collective-permute-done((bf16[8,4096]{1,0:T(8,128)(2,1)S(1)}, bf16[8,4096]{1,0:T(8,128)(2,1)S(1)}, u32[]{:S(2)}, u32[]{:S(2)}) %collective-permute-start.8) | collective-permute-done | bytes 65568 | tf_op jit(solution)/shard_map/ppermute | solution.py:163
  23.0 0.0 collective-permute-start.9
  23.0 0.9 %collective-permute-done.6.refs_4_ = bf16[8,4096]{1,0:T(8,128)(2,1)S(1)} collective-permute-done((bf16[8,4096]{1,0:T(8,128)(2,1)S(1)}, bf16[8,4096]{1,0:T(8,128)(2,1)S(1)}, u32[]{:S(2)}, u32[]{:S(2)}) %collective-permute-start.6) | collective-permute-done | bytes 65568 | tf_op jit(solution)/shard_map/ppermute | solution.py:163
  23.9 0.0 collective-permute-start.7
  23.9 0.5 %collective-permute-done.4.refs_2_ = bf16[8,4096]{1,0:T(8,128)(2,1)S(1)} collective-permute-done((bf16[8,4096]{1,0:T(8,128)(2,1)S(1)}, bf16[8,4096]{1,0:T(8,128)(2,1)S(1)}, u32[]{:S(2)}, u32[]{:S(2)}) %collective-permute-start.4) | collective-permute-done | bytes 65568 | tf_op jit(solution)/shard_map/ppermute | solution.py:163
  24.4 0.0 collective-permute-start.5
  24.4 0.0 collective-permute-done.3.refs_1_
  24.4 0.0 collective-permute-done.9.refs_7_
  24.4 0.7 %collective-permute-done.7.refs_5_ = bf16[8,4096]{1,0:T(8,128)(2,1)S(1)} collective-permute-done((bf16[8,4096]{1,0:T(8,128)(2,1)S(1)}, bf16[8,4096]{1,0:T(8,128)(2,1)S(1)}, u32[]{:S(2)}, u32[]{:S(2)}) %collective-permute-start.7) | collective-permute-done | bytes 65568 | tf_op jit(solution)/shard_map/ppermute | solution.py:163
  25.2 0.5 %collective-permute-done.5.refs_3_ = bf16[8,4096]{1,0:T(8,128)(2,1)S(1)} collective-permute-done((bf16[8,4096]{1,0:T(8,128)(2,1)S(1)}, bf16[8,4096]{1,0:T(8,128)(2,1)S(1)}, u32[]{:S(2)}, u32[]{:S(2)}) %collective-permute-start.5) | collective-permute-done | bytes 65568 | tf_op jit(solution)/shard_map/ppermute | solution.py:163
  25.7 0.0 copy-done
  25.7 1.4 %scores.1 = f32[64,64]{1,0:T(8,128)} custom-call(bf16[64,4096]{1,0:T(8,128)(2,1)S(1)} %copy-done, bf16[8,4096]{1,0:T(8,128)(2,1)S(1)} %add_convert_fusion.refs_0_, bf16[8,4096]{1,0:T(8,128)(2,1)S(1)} %collective-permute-done.3.refs_1_, bf16[8,4096]{1,0:T(8,128)(2,1)S(1)} %collective-permute-done.4.refs_2_, ...), custom_call_target="tpu_custom_call" | custom-call | tf_op jit(solution)/shard_map/scores/pallas_call | solution.py:152
  (1 shorter events, 0.0 us)
Async XLA Ops:
  0.0 25.7 %copy-start = (bf16[64,4096]{1,0:T(8,128)(2,1)S(1)}, bf16[64,4096]{1,0:T(8,128)(2,1)}, u32[]{:S(2)}) copy-start(bf16[64,4096]{1,0:T(8,128)(2,1)} %query.1) | copy-start | bytes 1572868
  6.7 7.9 %collective-permute-start = (bf16[8,4096]{1,0:T(8,128)(2,1)S(1)}, bf16[8,4096]{1,0:T(8,128)(2,1)S(1)}, u32[]{:S(2)}, u32[]{:S(2)}) collective-permute-start(bf16[8,4096]{1,0:T(8,128)(2,1)S(1)} %get-tuple-element.10), channel_id=1, source_target_pairs={{0,2},{1,3},{2,0},{3,1},{4,6},{5,7},{6,4},{7,5},{8,10},{9,11},{10,... | collective-permute-start | bytes 196616 | tf_op jit(solution)/shard_map/ppermute | solution.py:163
  10.8 6.2 %collective-permute-start.1 = (bf16[8,4096]{1,0:T(8,128)(2,1)S(1)}, bf16[8,4096]{1,0:T(8,128)(2,1)S(1)}, u32[]{:S(2)}, u32[]{:S(2)}) collective-permute-start(bf16[8,4096]{1,0:T(8,128)(2,1)S(1)} %get-tuple-element.11), channel_id=1, source_target_pairs={{0,3},{1,2},{2,1},{3,0},{4,7},{5,6},{6,5},{7,4},{8,11},{9,10},{10,... | collective-permute-start | bytes 196616 | tf_op jit(solution)/shard_map/ppermute | solution.py:163
  12.1 5.0 %collective-permute-start.2 = (bf16[8,4096]{1,0:T(8,128)(2,1)S(1)}, bf16[8,4096]{1,0:T(8,128)(2,1)S(1)}, u32[]{:S(2)}, u32[]{:S(2)}) collective-permute-start(bf16[8,4096]{1,0:T(8,128)(2,1)S(1)} %get-tuple-element.12), channel_id=1, source_target_pairs={{0,1},{1,0},{2,3},{3,2},{4,5},{5,4},{6,7},{7,6},{8,9},{9,8},{10,11... | collective-permute-start | bytes 196616 | tf_op jit(solution)/shard_map/ppermute | solution.py:163
  17.1 5.9 %collective-permute-start.8 = (bf16[8,4096]{1,0:T(8,128)(2,1)S(1)}, bf16[8,4096]{1,0:T(8,128)(2,1)S(1)}, u32[]{:S(2)}, u32[]{:S(2)}) collective-permute-start(bf16[8,4096]{1,0:T(8,128)(2,1)S(1)} %add_convert_fusion.refs_0_), channel_id=1, source_target_pairs={{0,24},{4,28},{8,16},{12,20},{16,8},{20,12},{24,0},{28,4},{1,25},{... | collective-permute-start | bytes 196616 | tf_op jit(solution)/shard_map/ppermute | solution.py:163
  19.6 4.3 %collective-permute-start.6 = (bf16[8,4096]{1,0:T(8,128)(2,1)S(1)}, bf16[8,4096]{1,0:T(8,128)(2,1)S(1)}, u32[]{:S(2)}, u32[]{:S(2)}) collective-permute-start(bf16[8,4096]{1,0:T(8,128)(2,1)S(1)} %add_convert_fusion.refs_0_), channel_id=1, source_target_pairs={{0,16},{4,20},{8,24},{12,28},{16,0},{20,4},{24,8},{28,12},{1,17},{... | collective-permute-start | bytes 196616 | tf_op jit(solution)/shard_map/ppermute | solution.py:163
  20.2 4.3 %collective-permute-start.4 = (bf16[8,4096]{1,0:T(8,128)(2,1)S(1)}, bf16[8,4096]{1,0:T(8,128)(2,1)S(1)}, u32[]{:S(2)}, u32[]{:S(2)}) collective-permute-start(bf16[8,4096]{1,0:T(8,128)(2,1)S(1)} %add_convert_fusion.refs_0_), channel_id=1, source_target_pairs={{0,8},{4,12},{8,0},{12,4},{16,24},{20,28},{24,16},{28,20},{1,9},{5... | collective-permute-start | bytes 196616 | tf_op jit(solution)/shard_map/ppermute | solution.py:163
  20.7 3.8 %collective-permute-start.3 = (bf16[8,4096]{1,0:T(8,128)(2,1)S(1)}, bf16[8,4096]{1,0:T(8,128)(2,1)S(1)}, u32[]{:S(2)}, u32[]{:S(2)}) collective-permute-start(bf16[8,4096]{1,0:T(8,128)(2,1)S(1)} %add_convert_fusion.refs_0_), channel_id=1, source_target_pairs={{0,4},{4,0},{8,12},{12,8},{16,20},{20,16},{24,28},{28,24},{1,5},{5... | collective-permute-start | bytes 196616 | tf_op jit(solution)/shard_map/ppermute | solution.py:163
  23.0 1.5 %collective-permute-start.9 = (bf16[8,4096]{1,0:T(8,128)(2,1)S(1)}, bf16[8,4096]{1,0:T(8,128)(2,1)S(1)}, u32[]{:S(2)}, u32[]{:S(2)}) collective-permute-start(bf16[8,4096]{1,0:T(8,128)(2,1)S(1)} %collective-permute-done.8.refs_6_), channel_id=1, source_target_pairs={{0,4},{4,0},{8,12},{12,8},{16,20},{20,16},{24,28},{28,24},{1,5},{5... | collective-permute-start | bytes 196616 | tf_op jit(solution)/shard_map/ppermute | solution.py:163
  23.9 1.3 %collective-permute-start.7 = (bf16[8,4096]{1,0:T(8,128)(2,1)S(1)}, bf16[8,4096]{1,0:T(8,128)(2,1)S(1)}, u32[]{:S(2)}, u32[]{:S(2)}) collective-permute-start(bf16[8,4096]{1,0:T(8,128)(2,1)S(1)} %collective-permute-done.6.refs_4_), channel_id=1, source_target_pairs={{0,4},{4,0},{8,12},{12,8},{16,20},{20,16},{24,28},{28,24},{1,5},{5... | collective-permute-start | bytes 196616 | tf_op jit(solution)/shard_map/ppermute | solution.py:163
  24.4 1.3 %collective-permute-start.5 = (bf16[8,4096]{1,0:T(8,128)(2,1)S(1)}, bf16[8,4096]{1,0:T(8,128)(2,1)S(1)}, u32[]{:S(2)}, u32[]{:S(2)}) collective-permute-start(bf16[8,4096]{1,0:T(8,128)(2,1)S(1)} %collective-permute-done.4.refs_2_), channel_id=1, source_target_pairs={{0,4},{4,0},{8,12},{12,8},{16,20},{20,16},{24,28},{28,24},{1,5},{5... | collective-permute-start | bytes 196616 | tf_op jit(solution)/shard_map/ppermute | solution.py:163

commit v11 on v9

--- a/solution.py
+++ b/solution.py
@@ -41,26 +41,30 @@
         start = start + length
     share_of, row_of = (slot_of >> shift) ^ tok, slot_of & (doc_dev - 1)
 
-    eye = (
-        lax.broadcasted_iota(jnp.int32, (2 * width, 2 * width), 0)
-        == lax.broadcasted_iota(jnp.int32, (2 * width, 2 * width), 1)
+    pick = (
+        lax.broadcasted_iota(jnp.int32, (width, 2 * width), 0) + width
+        == lax.broadcasted_iota(jnp.int32, (width, 2 * width), 1)
     ).astype(rows.dtype)
+    share_columns = share_of.T
+    half = lax.broadcasted_iota(jnp.int32, (LANES, LANES), 1) // width
     copies[2].wait()
-    for b in range(blocks):
-        part = slice(b * LANES, (b + 1) * LANES)
-        turned = lax.dot_general(eye, rows[part, :], ROW_BY_ROW, preferred_element_type=jnp.float32)
-        for digits, values, target in (
-            (share_of, turned[:width], inputs),
-            (row_of, turned[width:], grads),
-        ):
-            digit = jnp.broadcast_to(digits[b : b + 1, :], (8, LANES))[None]
-            values = values.reshape(-1, 8, LANES)
-            for at in range(target.shape[0] // width):
+    for b in range(0, blocks, 2):
+        both = slice(b * LANES, (b + 2) * LANES)
+        turned = lax.dot_general(pick, rows[both, :], ROW_BY_ROW, preferred_element_type=jnp.float32)
+        for c in (b, b + 1):
+            part = slice(c * LANES, (c + 1) * LANES)
+            digit = jnp.broadcast_to(row_of[c : c + 1, :], (8, LANES))[None]
+            values = turned[:, (c - b) * LANES : (c - b + 1) * LANES].reshape(-1, 8, LANES)
+            for at in range(doc_dev):
                 kept = jnp.where(digit == at, values, 0.0).reshape(width, LANES)
-                target[at * width : (at + 1) * width, part] = kept.astype(target.dtype)
-    product = lax.dot_general(
-        grads[...], inputs[...], ROW_BY_ROW, preferred_element_type=jnp.float32
-    )
+                grads[at * width : (at + 1) * width, part] = kept.astype(grads.dtype)
+            values = rows[part, :].astype(jnp.float32)
+            values = jnp.where(half == 0, values, pltpu.roll(values, width, 1))
+            digit = jnp.broadcast_to(share_columns[:, c : c + 1], (LANES, LANES)) - half
+            for at in range(0, tok_count, 2):
+                kept = jnp.where(digit == at, values, 0.0)
+                inputs[part, at * width : at * width + LANES] = kept.astype(inputs.dtype)
+    product = jnp.dot(grads[...], inputs[...], preferred_element_type=jnp.float32)
     for p in range(sums.shape[0]):
         sums[p] = product[:, p * LANES : (p + 1) * LANES]
 
@@ -96,7 +100,7 @@
             pltpu.SMEM(owner_map.shape, jnp.int32),
             pltpu.VMEM(proj_rows.shape, proj_rows.dtype),
             pltpu.VMEM((doc_dev * width, count), jnp.bfloat16),
-            pltpu.VMEM((tok_count * width, count), jnp.bfloat16),
+            pltpu.VMEM((count, tok_count * width), jnp.bfloat16),
             pltpu.VMEM((tok_count // 2, doc_dev * width, LANES), jnp.float32),
             pltpu.SemaphoreType.DMA((3,)),
         ],
@@ -105,18 +109,29 @@
     )(*(pltpu.with_memory_space_constraint(x, pltpu.HBM) for x in (doc_lengths, owner_map, proj_rows)))
 
 
+def turn_kernel(query, turned):
+    turned[...] = query[...].T
+
+
+def turned_query(query_features):
+    whole = pl.BlockSpec(memory_space=pltpu.VMEM)
+    shape = query_features.shape[::-1]
+    return pl.pallas_call(
+        turn_kernel,
+        out_shape=jax.ShapeDtypeStruct(shape, query_features.dtype),
+        in_specs=[whole],
+        out_specs=whole,
+        cost_estimate=pl.CostEstimate(flops=0, bytes_accessed=2 * query_features.nbytes, transcendentals=0),
+        compiler_params=pltpu.CompilerParams(vmem_limit_bytes=16 * 1024 * 1024),
+        name="turned_query",
+    )(pltpu.with_memory_space_constraint(query_features, pltpu.VMEM))
+
+
 def score_kernel(query, *refs):
     *blocks, scores = refs
     doc_dev = blocks[0].shape[0]
     features = jnp.concatenate([block[...] for block in blocks], axis=0)
-    depth = features.shape[1] // 4
-    products = sum(
-        lax.dot_general(
-            features[:, at : at + depth], query[:, at : at + depth], ROW_BY_ROW,
-            preferred_element_type=jnp.float32,
-        )
-        for at in range(0, features.shape[1], depth)
-    )
+    products = jnp.dot(features, query[...], preferred_element_type=jnp.float32)
     parts = [products[i * doc_dev : (i + 1) * doc_dev] for i in range(len(blocks))]
     ex = lax.axis_index("ex")
     flip = 1
@@ -127,17 +142,17 @@
     scores[...] = jnp.concatenate(parts, axis=0).T
 
 
-def block_scores(query_features, blocks):
+def block_scores(query, blocks):
     whole = pl.BlockSpec(memory_space=pltpu.VMEM)
     docs = len(blocks) * blocks[0].shape[0]
     return pl.pallas_call(
         score_kernel,
-        out_shape=jax.ShapeDtypeStruct((query_features.shape[0], docs), jnp.float32),
+        out_shape=jax.ShapeDtypeStruct((query.shape[1], docs), jnp.float32),
         in_specs=[whole] * (1 + len(blocks)),
         out_specs=whole,
         compiler_params=pltpu.CompilerParams(vmem_limit_bytes=16 * 1024 * 1024),
         name="scores",
-    )(*(pltpu.with_memory_space_constraint(x, pltpu.VMEM) for x in (query_features, *blocks)))
+    )(*(pltpu.with_memory_space_constraint(x, pltpu.VMEM) for x in (query, *blocks)))
 
 
 def exchange(block, axis, flip):
@@ -160,7 +175,7 @@
         blocks[flip] = exchange(features, "ex", flip)
     for flip in (0, 4, 2, 6):
         blocks[flip + 1] = exchange(blocks[flip], "ex", 1)
-    return block_scores(query_features, blocks)
+    return block_scores(turned_query(query_features), blocks)
 
 
 def solution(mesh):

time: 23.1 us -> 23.1 us (level)
  Pallas kernels: 3.89 us -> 4.27 us
  waiting for transfers between devices: 9.7 us -> 9.33 us
    ppermute x10, waiting for transfers between devices: 9.7 us -> 9.33 us  [exchange(): lax.ppermute(block, axis, [(i, i ^ flip) for i in range(lax.axis_size(axi...]
    pallas_call x1 -> x2, Pallas kernels: 0.99 us -> 1.35 us  [the longest x1 1.01 us: block_scores(): pl.pallas_call(score_kernel, out_shape=jax.ShapeDtypeStruct((query.shape[...]
  transfers between devices with their start and end apart: 10 -> 10, of which waited for: 8 -> 8; matrix products, arithmetic and copies ran while one was open for 0% -> 0% of each run, Pallas kernels for 0% -> 2%
where the time goes in v11:
time: 23.1 us; the launch traced here: 22.9 us
  waiting for transfers between devices  9.33 us (40%)
  starting transfers between devices  9.26 us (40%)
  Pallas kernels  4.27 us (18%)
    ppermute x10, waiting for transfers between devices, exchange(): lax.ppermute(block, axis, [(i, i ^ flip) for i in range(lax.axis_size(axi...  9.33 us
    ppermute x10, starting transfers between devices, exchange(): lax.ppermute(block, axis, [(i, i ^ flip) for i in range(lax.axis_size(axi...  9.26 us
    pallas_call x1, Pallas kernels, feature_shares(): pl.pallas_call(feature_kernel, out_shape=[jax.ShapeDtypeStruct((doc_dev,...  2.92 us
    pallas_call x1, Pallas kernels, block_scores(): pl.pallas_call(score_kernel, out_shape=jax.ShapeDtypeStruct((query.shape[...  1.01 us
  transfers between devices with their start and end apart: 10, of which 8 were waited for; matrix products, arithmetic and copies ran while one was open for 0% of the time, Pallas kernels for 2%

profile of v11, /device:TPU:0, one launch (start us, length us, event | category | flops | bytes accessed | tf_op | source)
XLA Modules:
  0.0 22.9 jit_solution(10187219888306914378)
XLA Ops:
  0.0 2.9 %features.1 = (f32[8,4096]{1,0:T(8,128)S(1)}, bf16[8,4096]{1,0:T(8,128)(2,1)S(1)}, bf16[8,4096]{1,0:T(8,128)(2,1)S(1)}, bf16[8,4096]{1,0:T(8,128)(2,1)S(1)}) custom-call(s32[1,32]{1,0:T(1,128)} %lengths_hbm.1, s32[1,32]{1,0:T(1,128)} %owners_hbm.1, bf16[2048,128]{1,0:T(8,128)(2,1)} %rows_hbm.1), custom_call_target="tpu_custom_call" | custom-call | tf_op jit(solution)/shard_map/features/pallas_call | solution.py:90
  2.9 4.1 %collective-permute-start = (bf16[8,4096]{1,0:T(8,128)(2,1)S(1)}, bf16[8,4096]{1,0:T(8,128)(2,1)S(1)}, u32[]{:S(2)}, u32[]{:S(2)}) collective-permute-start(bf16[8,4096]{1,0:T(8,128)(2,1)S(1)} %get-tuple-element.10), channel_id=1, source_target_pairs={{0,2},{1,3},{2,0},{3,1},{4,6},{5,7},{6,4},{7,5},{8,10},{9,11},{10,... | collective-permute-start | bytes 196616 | tf_op jit(solution)/shard_map/ppermute | solution.py:159
  7.0 1.3 %collective-permute-start.1 = (bf16[8,4096]{1,0:T(8,128)(2,1)S(1)}, bf16[8,4096]{1,0:T(8,128)(2,1)S(1)}, u32[]{:S(2)}, u32[]{:S(2)}) collective-permute-start(bf16[8,4096]{1,0:T(8,128)(2,1)S(1)} %get-tuple-element.11), channel_id=1, source_target_pairs={{0,3},{1,2},{2,1},{3,0},{4,7},{5,6},{6,5},{7,4},{8,11},{9,10},{10,... | collective-permute-start | bytes 196616 | tf_op jit(solution)/shard_map/ppermute | solution.py:159
  8.4 0.2 %collective-permute-start.2 = (bf16[8,4096]{1,0:T(8,128)(2,1)S(1)}, bf16[8,4096]{1,0:T(8,128)(2,1)S(1)}, u32[]{:S(2)}, u32[]{:S(2)}) collective-permute-start(bf16[8,4096]{1,0:T(8,128)(2,1)S(1)} %get-tuple-element.12), channel_id=1, source_target_pairs={{0,1},{1,0},{2,3},{3,2},{4,5},{5,4},{6,7},{7,6},{8,9},{9,8},{10,11... | collective-permute-start | bytes 196616 | tf_op jit(solution)/shard_map/ppermute | solution.py:159
  8.6 2.2 %collective-permute-done = bf16[8,4096]{1,0:T(8,128)(2,1)S(1)} collective-permute-done((bf16[8,4096]{1,0:T(8,128)(2,1)S(1)}, bf16[8,4096]{1,0:T(8,128)(2,1)S(1)}, u32[]{:S(2)}, u32[]{:S(2)}) %collective-permute-start) | collective-permute-done | bytes 65568 | tf_op jit(solution)/shard_map/ppermute | solution.py:159
  10.8 2.5 %collective-permute-done.1 = bf16[8,4096]{1,0:T(8,128)(2,1)S(1)} collective-permute-done((bf16[8,4096]{1,0:T(8,128)(2,1)S(1)}, bf16[8,4096]{1,0:T(8,128)(2,1)S(1)}, u32[]{:S(2)}, u32[]{:S(2)}) %collective-permute-start.1) | collective-permute-done | bytes 65568 | tf_op jit(solution)/shard_map/ppermute | solution.py:159
  13.3 0.1 collective-permute-done.2
  13.4 2.5 %collective-permute-start.8 = (bf16[8,4096]{1,0:T(8,128)(2,1)S(1)}, bf16[8,4096]{1,0:T(8,128)(2,1)S(1)}, u32[]{:S(2)}, u32[]{:S(2)}) collective-permute-start(bf16[8,4096]{1,0:T(8,128)(2,1)S(1)} %add_convert_fusion.refs_0_), channel_id=1, source_target_pairs={{0,24},{4,28},{8,16},{12,20},{16,8},{20,12},{24,0},{28,4},{1,25},{... | collective-permute-start | bytes 196616 | tf_op jit(solution)/shard_map/ppermute | solution.py:159
  15.9 0.5 %collective-permute-start.6 = (bf16[8,4096]{1,0:T(8,128)(2,1)S(1)}, bf16[8,4096]{1,0:T(8,128)(2,1)S(1)}, u32[]{:S(2)}, u32[]{:S(2)}) collective-permute-start(bf16[8,4096]{1,0:T(8,128)(2,1)S(1)} %add_convert_fusion.refs_0_), channel_id=1, source_target_pairs={{0,16},{4,20},{8,24},{12,28},{16,0},{20,4},{24,8},{28,12},{1,17},{... | collective-permute-start | bytes 196616 | tf_op jit(solution)/shard_map/ppermute | solution.py:159
  16.4 0.5 %collective-permute-start.4 = (bf16[8,4096]{1,0:T(8,128)(2,1)S(1)}, bf16[8,4096]{1,0:T(8,128)(2,1)S(1)}, u32[]{:S(2)}, u32[]{:S(2)}) collective-permute-start(bf16[8,4096]{1,0:T(8,128)(2,1)S(1)} %add_convert_fusion.refs_0_), channel_id=1, source_target_pairs={{0,8},{4,12},{8,0},{12,4},{16,24},{20,28},{24,16},{28,20},{1,9},{5... | collective-permute-start | bytes 196616 | tf_op jit(solution)/shard_map/ppermute | solution.py:159
  16.9 0.0 collective-permute-start.3
  17.0 2.3 %collective-permute-done.8.refs_6_ = bf16[8,4096]{1,0:T(8,128)(2,1)S(1)} collective-permute-done((bf16[8,4096]{1,0:T(8,128)(2,1)S(1)}, bf16[8,4096]{1,0:T(8,128)(2,1)S(1)}, u32[]{:S(2)}, u32[]{:S(2)}) %collective-permute-start.8) | collective-permute-done | bytes 65568 | tf_op jit(solution)/shard_map/ppermute | solution.py:159
  19.3 0.0 collective-permute-start.9
  19.3 0.9 %collective-permute-done.6.refs_4_ = bf16[8,4096]{1,0:T(8,128)(2,1)S(1)} collective-permute-done((bf16[8,4096]{1,0:T(8,128)(2,1)S(1)}, bf16[8,4096]{1,0:T(8,128)(2,1)S(1)}, u32[]{:S(2)}, u32[]{:S(2)}) %collective-permute-start.6) | collective-permute-done | bytes 65568 | tf_op jit(solution)/shard_map/ppermute | solution.py:159
  20.2 0.0 collective-permute-start.7
  20.2 0.5 %collective-permute-done.4.refs_2_ = bf16[8,4096]{1,0:T(8,128)(2,1)S(1)} collective-permute-done((bf16[8,4096]{1,0:T(8,128)(2,1)S(1)}, bf16[8,4096]{1,0:T(8,128)(2,1)S(1)}, u32[]{:S(2)}, u32[]{:S(2)}) %collective-permute-start.4) | collective-permute-done | bytes 65568 | tf_op jit(solution)/shard_map/ppermute | solution.py:159
  20.7 0.0 collective-permute-start.5
  20.7 0.0 copy-done
  20.7 0.3 %turned_query.1.query = bf16[4096,64]{1,0:T(8,128)(2,1)S(1)} custom-call(bf16[64,4096]{1,0:T(8,128)(2,1)S(1)} %copy-done), custom_call_target="tpu_custom_call" | custom-call | bytes 1048576 | tf_op jit(solution)/shard_map/turned_query/pallas_call | solution.py:119
  21.0 0.0 collective-permute-done.3.refs_1_
  21.1 0.0 collective-permute-done.9.refs_7_
  21.1 0.4 %collective-permute-done.7.refs_5_ = bf16[8,4096]{1,0:T(8,128)(2,1)S(1)} collective-permute-done((bf16[8,4096]{1,0:T(8,128)(2,1)S(1)}, bf16[8,4096]{1,0:T(8,128)(2,1)S(1)}, u32[]{:S(2)}, u32[]{:S(2)}) %collective-permute-start.7) | collective-permute-done | bytes 65568 | tf_op jit(solution)/shard_map/ppermute | solution.py:159
  21.4 0.5 %collective-permute-done.5.refs_3_ = bf16[8,4096]{1,0:T(8,128)(2,1)S(1)} collective-permute-done((bf16[8,4096]{1,0:T(8,128)(2,1)S(1)}, bf16[8,4096]{1,0:T(8,128)(2,1)S(1)}, u32[]{:S(2)}, u32[]{:S(2)}) %collective-permute-start.5) | collective-permute-done | bytes 65568 | tf_op jit(solution)/shard_map/ppermute | solution.py:159
  21.9 1.0 %scores.1 = f32[64,64]{1,0:T(8,128)} custom-call(bf16[4096,64]{1,0:T(8,128)(2,1)S(1)} %turned_query.1.query, bf16[8,4096]{1,0:T(8,128)(2,1)S(1)} %add_convert_fusion.refs_0_, bf16[8,4096]{1,0:T(8,128)(2,1)S(1)} %collective-permute-done.3.refs_1_, bf16[8,4096]{1,0:T(8,128)(2,1)S(1)} %collective-permute-done.4.refs_2_, ...), custom_call_target="tpu_custom_call" | custom-call | tf_op jit(solution)/shard_map/scores/pallas_call | solution.py:148
  (2 shorter events, 0.0 us)
Async XLA Ops:
  0.0 20.7 %copy-start = (bf16[64,4096]{1,0:T(8,128)(2,1)S(1)}, bf16[64,4096]{1,0:T(8,128)(2,1)}, u32[]{:S(2)}) copy-start(bf16[64,4096]{1,0:T(8,128)(2,1)} %query.1) | copy-start | bytes 1572868
  2.9 7.9 %collective-permute-start = (bf16[8,4096]{1,0:T(8,128)(2,1)S(1)}, bf16[8,4096]{1,0:T(8,128)(2,1)S(1)}, u32[]{:S(2)}, u32[]{:S(2)}) collective-permute-start(bf16[8,4096]{1,0:T(8,128)(2,1)S(1)} %get-tuple-element.10), channel_id=1, source_target_pairs={{0,2},{1,3},{2,0},{3,1},{4,6},{5,7},{6,4},{7,5},{8,10},{9,11},{10,... | collective-permute-start | bytes 196616 | tf_op jit(solution)/shard_map/ppermute | solution.py:159
  7.0 6.2 %collective-permute-start.1 = (bf16[8,4096]{1,0:T(8,128)(2,1)S(1)}, bf16[8,4096]{1,0:T(8,128)(2,1)S(1)}, u32[]{:S(2)}, u32[]{:S(2)}) collective-permute-start(bf16[8,4096]{1,0:T(8,128)(2,1)S(1)} %get-tuple-element.11), channel_id=1, source_target_pairs={{0,3},{1,2},{2,1},{3,0},{4,7},{5,6},{6,5},{7,4},{8,11},{9,10},{10,... | collective-permute-start | bytes 196616 | tf_op jit(solution)/shard_map/ppermute | solution.py:159
  8.4 5.0 %collective-permute-start.2 = (bf16[8,4096]{1,0:T(8,128)(2,1)S(1)}, bf16[8,4096]{1,0:T(8,128)(2,1)S(1)}, u32[]{:S(2)}, u32[]{:S(2)}) collective-permute-start(bf16[8,4096]{1,0:T(8,128)(2,1)S(1)} %get-tuple-element.12), channel_id=1, source_target_pairs={{0,1},{1,0},{2,3},{3,2},{4,5},{5,4},{6,7},{7,6},{8,9},{9,8},{10,11... | collective-permute-start | bytes 196616 | tf_op jit(solution)/shard_map/ppermute | solution.py:159
  13.4 5.9 %collective-permute-start.8 = (bf16[8,4096]{1,0:T(8,128)(2,1)S(1)}, bf16[8,4096]{1,0:T(8,128)(2,1)S(1)}, u32[]{:S(2)}, u32[]{:S(2)}) collective-permute-start(bf16[8,4096]{1,0:T(8,128)(2,1)S(1)} %add_convert_fusion.refs_0_), channel_id=1, source_target_pairs={{0,24},{4,28},{8,16},{12,20},{16,8},{20,12},{24,0},{28,4},{1,25},{... | collective-permute-start | bytes 196616 | tf_op jit(solution)/shard_map/ppermute | solution.py:159
  15.9 4.3 %collective-permute-start.6 = (bf16[8,4096]{1,0:T(8,128)(2,1)S(1)}, bf16[8,4096]{1,0:T(8,128)(2,1)S(1)}, u32[]{:S(2)}, u32[]{:S(2)}) collective-permute-start(bf16[8,4096]{1,0:T(8,128)(2,1)S(1)} %add_convert_fusion.refs_0_), channel_id=1, source_target_pairs={{0,16},{4,20},{8,24},{12,28},{16,0},{20,4},{24,8},{28,12},{1,17},{... | collective-permute-start | bytes 196616 | tf_op jit(solution)/shard_map/ppermute | solution.py:159
  16.4 4.3 %collective-permute-start.4 = (bf16[8,4096]{1,0:T(8,128)(2,1)S(1)}, bf16[8,4096]{1,0:T(8,128)(2,1)S(1)}, u32[]{:S(2)}, u32[]{:S(2)}) collective-permute-start(bf16[8,4096]{1,0:T(8,128)(2,1)S(1)} %add_convert_fusion.refs_0_), channel_id=1, source_target_pairs={{0,8},{4,12},{8,0},{12,4},{16,24},{20,28},{24,16},{28,20},{1,9},{5... | collective-permute-start | bytes 196616 | tf_op jit(solution)/shard_map/ppermute | solution.py:159
  16.9 4.1 %collective-permute-start.3 = (bf16[8,4096]{1,0:T(8,128)(2,1)S(1)}, bf16[8,4096]{1,0:T(8,128)(2,1)S(1)}, u32[]{:S(2)}, u32[]{:S(2)}) collective-permute-start(bf16[8,4096]{1,0:T(8,128)(2,1)S(1)} %add_convert_fusion.refs_0_), channel_id=1, source_target_pairs={{0,4},{4,0},{8,12},{12,8},{16,20},{20,16},{24,28},{28,24},{1,5},{5... | collective-permute-start | bytes 196616 | tf_op jit(solution)/shard_map/ppermute | solution.py:159
  19.3 1.8 %collective-permute-start.9 = (bf16[8,4096]{1,0:T(8,128)(2,1)S(1)}, bf16[8,4096]{1,0:T(8,128)(2,1)S(1)}, u32[]{:S(2)}, u32[]{:S(2)}) collective-permute-start(bf16[8,4096]{1,0:T(8,128)(2,1)S(1)} %collective-permute-done.8.refs_6_), channel_id=1, source_target_pairs={{0,4},{4,0},{8,12},{12,8},{16,20},{20,16},{24,28},{28,24},{1,5},{5... | collective-permute-start | bytes 196616 | tf_op jit(solution)/shard_map/ppermute | solution.py:159
  20.2 1.3 %collective-permute-start.7 = (bf16[8,4096]{1,0:T(8,128)(2,1)S(1)}, bf16[8,4096]{1,0:T(8,128)(2,1)S(1)}, u32[]{:S(2)}, u32[]{:S(2)}) collective-permute-start(bf16[8,4096]{1,0:T(8,128)(2,1)S(1)} %collective-permute-done.6.refs_4_), channel_id=1, source_target_pairs={{0,4},{4,0},{8,12},{12,8},{16,20},{20,16},{24,28},{28,24},{1,5},{5... | collective-permute-start | bytes 196616 | tf_op jit(solution)/shard_map/ppermute | solution.py:159
  20.7 1.3 %collective-permute-start.5 = (bf16[8,4096]{1,0:T(8,128)(2,1)S(1)}, bf16[8,4096]{1,0:T(8,128)(2,1)S(1)}, u32[]{:S(2)}, u32[]{:S(2)}) collective-permute-start(bf16[8,4096]{1,0:T(8,128)(2,1)S(1)} %collective-permute-done.4.refs_2_), channel_id=1, source_target_pairs={{0,4},{4,0},{8,12},{12,8},{16,20},{20,16},{24,28},{28,24},{1,5},{5... | collective-permute-start | bytes 196616 | tf_op jit(solution)/shard_map/ppermute | solution.py:159

commit v12 on v9

--- a/solution.py
+++ b/solution.py
@@ -10,7 +10,7 @@
 
 
 def feature_kernel(lengths_hbm, owners_hbm, rows_hbm, *refs):
-    *shares, lengths, owners, rows, grads, inputs, sums, arrived = refs
+    *shares, lengths, owners, rows, grads, inputs, arrived = refs
     count, width = rows.shape[0], rows.shape[1] // 2
     copies = [
         pltpu.make_async_copy(source, target, arrived.at[i])
@@ -41,36 +41,38 @@
         start = start + length
     share_of, row_of = (slot_of >> shift) ^ tok, slot_of & (doc_dev - 1)
 
-    eye = (
-        lax.broadcasted_iota(jnp.int32, (2 * width, 2 * width), 0)
-        == lax.broadcasted_iota(jnp.int32, (2 * width, 2 * width), 1)
+    spread = doc_dev * width
+    pick = (
+        lax.broadcasted_iota(jnp.int32, (spread, 2 * width), 0) // doc_dev + width
+        == lax.broadcasted_iota(jnp.int32, (spread, 2 * width), 1)
     ).astype(rows.dtype)
+    share_columns = share_of.T
+    half = lax.broadcasted_iota(jnp.int32, (LANES, LANES), 1) // width
     copies[2].wait()
-    for b in range(blocks):
-        part = slice(b * LANES, (b + 1) * LANES)
-        turned = lax.dot_general(eye, rows[part, :], ROW_BY_ROW, preferred_element_type=jnp.float32)
-        for digits, values, target in (
-            (share_of, turned[:width], inputs),
-            (row_of, turned[width:], grads),
-        ):
-            digit = jnp.broadcast_to(digits[b : b + 1, :], (8, LANES))[None]
-            values = values.reshape(-1, 8, LANES)
-            for at in range(target.shape[0] // width):
-                kept = jnp.where(digit == at, values, 0.0).reshape(width, LANES)
-                target[at * width : (at + 1) * width, part] = kept.astype(target.dtype)
-    product = lax.dot_general(
-        grads[...], inputs[...], ROW_BY_ROW, preferred_element_type=jnp.float32
-    )
-    for p in range(sums.shape[0]):
-        sums[p] = product[:, p * LANES : (p + 1) * LANES]
+    for b in range(0, blocks, 2):
+        both = slice(b * LANES, (b + 2) * LANES)
+        turned = lax.dot_general(pick, rows[both, :], ROW_BY_ROW, preferred_element_type=jnp.float32)
+        for c in (b, b + 1):
+            part = slice(c * LANES, (c + 1) * LANES)
+            values = turned[:, (c - b) * LANES : (c - b + 1) * LANES].reshape(width, doc_dev, LANES)
+            kept = jnp.where((row_of[c : c + 1, :] == size_row)[None], values, 0.0)
+            grads[:, part] = kept.reshape(spread, LANES).astype(grads.dtype)
+            values = rows[part, :].astype(jnp.float32)
+            values = jnp.where(half == 0, values, pltpu.roll(values, width, 1))
+            digit = jnp.broadcast_to(share_columns[:, c : c + 1], (LANES, LANES)) - half
+            for at in range(0, tok_count, 2):
+                kept = jnp.where(digit == at, values, 0.0)
+                inputs[part, at * width : at * width + LANES] = kept.astype(inputs.dtype)
+    product = jnp.dot(grads[...], inputs[...], preferred_element_type=jnp.float32)
 
     scales = [1.0 / jnp.sqrt(size.astype(jnp.float32)) for size in sizes]
     low_half = lax.broadcasted_iota(jnp.int32, (doc_dev, LANES), 1) < width
     for m in range(width // 2):
         out = slice(m * LANES, (m + 1) * LANES)
         for s in range(0, tok_count, 2):
-            first = sums[s // 2, pl.ds(2 * m, doc_dev, stride=width), :]
-            second = sums[s // 2, pl.ds(2 * m + 1, doc_dev, stride=width), :]
+            pair = slice(s * width, s * width + LANES)
+            first = product[2 * m * doc_dev : (2 * m + 1) * doc_dev, pair]
+            second = product[(2 * m + 1) * doc_dev : (2 * m + 2) * doc_dev, pair]
             left = jnp.where(low_half, first, pltpu.roll(second, width, 1))
             right = jnp.where(low_half, pltpu.roll(first, width, 1), second)
             shares[s][:, out] = (left * scales[s]).astype(shares[s].dtype)
@@ -96,8 +98,7 @@
             pltpu.SMEM(owner_map.shape, jnp.int32),
             pltpu.VMEM(proj_rows.shape, proj_rows.dtype),
             pltpu.VMEM((doc_dev * width, count), jnp.bfloat16),
-            pltpu.VMEM((tok_count * width, count), jnp.bfloat16),
-            pltpu.VMEM((tok_count // 2, doc_dev * width, LANES), jnp.float32),
+            pltpu.VMEM((count, tok_count * width), jnp.bfloat16),
             pltpu.SemaphoreType.DMA((3,)),
         ],
         compiler_params=pltpu.CompilerParams(vmem_limit_bytes=32 * 1024 * 1024),

time: 23.1 us -> 23.1 us (level)
  no operation moved by 1% of the time
where the time goes in v12:
time: 23.1 us; the launch traced here: 23 us
  waiting for transfers between devices  9.7 us (42%)
  starting transfers between devices  9.25 us (40%)
  Pallas kernels  3.96 us (17%)
    ppermute x10, waiting for transfers between devices, exchange(): lax.ppermute(block, axis, [(i, i ^ flip) for i in range(lax.axis_size(axi...  9.7 us
    ppermute x10, starting transfers between devices, exchange(): lax.ppermute(block, axis, [(i, i ^ flip) for i in range(lax.axis_size(axi...  9.25 us
    pallas_call x1, Pallas kernels, feature_shares(): pl.pallas_call(feature_kernel, out_shape=[jax.ShapeDtypeStruct((doc_dev,...  2.98 us
    pallas_call x1, Pallas kernels, block_scores(): pl.pallas_call(score_kernel, out_shape=jax.ShapeDtypeStruct((query_featur...  0.99 us
  transfers between devices with their start and end apart: 10, of which 8 were waited for; matrix products, arithmetic and copies ran while one was open for 0% of the time, Pallas kernels for 0%

profile of v12, /device:TPU:0, one launch (start us, length us, event | category | flops | bytes accessed | tf_op | source)
XLA Modules:
  0.0 23.0 jit_solution(7690788407924587969)
XLA Ops:
  0.0 0.0 copy-start
  0.0 3.0 %features.1 = (f32[8,4096]{1,0:T(8,128)S(1)}, bf16[8,4096]{1,0:T(8,128)(2,1)S(1)}, bf16[8,4096]{1,0:T(8,128)(2,1)S(1)}, bf16[8,4096]{1,0:T(8,128)(2,1)S(1)}) custom-call(s32[1,32]{1,0:T(1,128)} %lengths_hbm.1, s32[1,32]{1,0:T(1,128)} %owners_hbm.1, bf16[2048,128]{1,0:T(8,128)(2,1)} %rows_hbm.1), custom_call_target="tpu_custom_call" | custom-call | tf_op jit(solution)/shard_map/features/pallas_call | solution.py:88
  3.0 4.1 %collective-permute-start = (bf16[8,4096]{1,0:T(8,128)(2,1)S(1)}, bf16[8,4096]{1,0:T(8,128)(2,1)S(1)}, u32[]{:S(2)}, u32[]{:S(2)}) collective-permute-start(bf16[8,4096]{1,0:T(8,128)(2,1)S(1)} %get-tuple-element.10), channel_id=1, source_target_pairs={{0,2},{1,3},{2,0},{3,1},{4,6},{5,7},{6,4},{7,5},{8,10},{9,11},{10,... | collective-permute-start | bytes 196616 | tf_op jit(solution)/shard_map/ppermute | solution.py:145
  7.1 1.3 %collective-permute-start.1 = (bf16[8,4096]{1,0:T(8,128)(2,1)S(1)}, bf16[8,4096]{1,0:T(8,128)(2,1)S(1)}, u32[]{:S(2)}, u32[]{:S(2)}) collective-permute-start(bf16[8,4096]{1,0:T(8,128)(2,1)S(1)} %get-tuple-element.11), channel_id=1, source_target_pairs={{0,3},{1,2},{2,1},{3,0},{4,7},{5,6},{6,5},{7,4},{8,11},{9,10},{10,... | collective-permute-start | bytes 196616 | tf_op jit(solution)/shard_map/ppermute | solution.py:145
  8.4 0.2 %collective-permute-start.2 = (bf16[8,4096]{1,0:T(8,128)(2,1)S(1)}, bf16[8,4096]{1,0:T(8,128)(2,1)S(1)}, u32[]{:S(2)}, u32[]{:S(2)}) collective-permute-start(bf16[8,4096]{1,0:T(8,128)(2,1)S(1)} %get-tuple-element.12), channel_id=1, source_target_pairs={{0,1},{1,0},{2,3},{3,2},{4,5},{5,4},{6,7},{7,6},{8,9},{9,8},{10,11... | collective-permute-start | bytes 196616 | tf_op jit(solution)/shard_map/ppermute | solution.py:145
  8.7 2.2 %collective-permute-done = bf16[8,4096]{1,0:T(8,128)(2,1)S(1)} collective-permute-done((bf16[8,4096]{1,0:T(8,128)(2,1)S(1)}, bf16[8,4096]{1,0:T(8,128)(2,1)S(1)}, u32[]{:S(2)}, u32[]{:S(2)}) %collective-permute-start) | collective-permute-done | bytes 65568 | tf_op jit(solution)/shard_map/ppermute | solution.py:145
  10.8 2.5 %collective-permute-done.1 = bf16[8,4096]{1,0:T(8,128)(2,1)S(1)} collective-permute-done((bf16[8,4096]{1,0:T(8,128)(2,1)S(1)}, bf16[8,4096]{1,0:T(8,128)(2,1)S(1)}, u32[]{:S(2)}, u32[]{:S(2)}) %collective-permute-start.1) | collective-permute-done | bytes 65568 | tf_op jit(solution)/shard_map/ppermute | solution.py:145
  13.3 0.1 collective-permute-done.2
  13.4 2.5 %collective-permute-start.8 = (bf16[8,4096]{1,0:T(8,128)(2,1)S(1)}, bf16[8,4096]{1,0:T(8,128)(2,1)S(1)}, u32[]{:S(2)}, u32[]{:S(2)}) collective-permute-start(bf16[8,4096]{1,0:T(8,128)(2,1)S(1)} %add_convert_fusion.refs_0_), channel_id=1, source_target_pairs={{0,24},{4,28},{8,16},{12,20},{16,8},{20,12},{24,0},{28,4},{1,25},{... | collective-permute-start | bytes 196616 | tf_op jit(solution)/shard_map/ppermute | solution.py:145
  16.0 0.5 %collective-permute-start.6 = (bf16[8,4096]{1,0:T(8,128)(2,1)S(1)}, bf16[8,4096]{1,0:T(8,128)(2,1)S(1)}, u32[]{:S(2)}, u32[]{:S(2)}) collective-permute-start(bf16[8,4096]{1,0:T(8,128)(2,1)S(1)} %add_convert_fusion.refs_0_), channel_id=1, source_target_pairs={{0,16},{4,20},{8,24},{12,28},{16,0},{20,4},{24,8},{28,12},{1,17},{... | collective-permute-start | bytes 196616 | tf_op jit(solution)/shard_map/ppermute | solution.py:145
  16.5 0.5 %collective-permute-start.4 = (bf16[8,4096]{1,0:T(8,128)(2,1)S(1)}, bf16[8,4096]{1,0:T(8,128)(2,1)S(1)}, u32[]{:S(2)}, u32[]{:S(2)}) collective-permute-start(bf16[8,4096]{1,0:T(8,128)(2,1)S(1)} %add_convert_fusion.refs_0_), channel_id=1, source_target_pairs={{0,8},{4,12},{8,0},{12,4},{16,24},{20,28},{24,16},{28,20},{1,9},{5... | collective-permute-start | bytes 196616 | tf_op jit(solution)/shard_map/ppermute | solution.py:145
  17.0 0.0 collective-permute-start.3
  17.0 2.3 %collective-permute-done.8.refs_6_ = bf16[8,4096]{1,0:T(8,128)(2,1)S(1)} collective-permute-done((bf16[8,4096]{1,0:T(8,128)(2,1)S(1)}, bf16[8,4096]{1,0:T(8,128)(2,1)S(1)}, u32[]{:S(2)}, u32[]{:S(2)}) %collective-permute-start.8) | collective-permute-done | bytes 65568 | tf_op jit(solution)/shard_map/ppermute | solution.py:145
  19.3 0.0 collective-permute-start.9
  19.3 0.9 %collective-permute-done.6.refs_4_ = bf16[8,4096]{1,0:T(8,128)(2,1)S(1)} collective-permute-done((bf16[8,4096]{1,0:T(8,128)(2,1)S(1)}, bf16[8,4096]{1,0:T(8,128)(2,1)S(1)}, u32[]{:S(2)}, u32[]{:S(2)}) %collective-permute-start.6) | collective-permute-done | bytes 65568 | tf_op jit(solution)/shard_map/ppermute | solution.py:145
  20.2 0.0 collective-permute-start.7
  20.2 0.5 %collective-permute-done.4.refs_2_ = bf16[8,4096]{1,0:T(8,128)(2,1)S(1)} collective-permute-done((bf16[8,4096]{1,0:T(8,128)(2,1)S(1)}, bf16[8,4096]{1,0:T(8,128)(2,1)S(1)}, u32[]{:S(2)}, u32[]{:S(2)}) %collective-permute-start.4) | collective-permute-done | bytes 65568 | tf_op jit(solution)/shard_map/ppermute | solution.py:145
  20.7 0.0 collective-permute-start.5
  20.7 0.0 collective-permute-done.3.refs_1_
  20.7 0.0 collective-permute-done.9.refs_7_
  20.7 0.7 %collective-permute-done.7.refs_5_ = bf16[8,4096]{1,0:T(8,128)(2,1)S(1)} collective-permute-done((bf16[8,4096]{1,0:T(8,128)(2,1)S(1)}, bf16[8,4096]{1,0:T(8,128)(2,1)S(1)}, u32[]{:S(2)}, u32[]{:S(2)}) %collective-permute-start.7) | collective-permute-done | bytes 65568 | tf_op jit(solution)/shard_map/ppermute | solution.py:145
  21.5 0.5 %collective-permute-done.5.refs_3_ = bf16[8,4096]{1,0:T(8,128)(2,1)S(1)} collective-permute-done((bf16[8,4096]{1,0:T(8,128)(2,1)S(1)}, bf16[8,4096]{1,0:T(8,128)(2,1)S(1)}, u32[]{:S(2)}, u32[]{:S(2)}) %collective-permute-start.5) | collective-permute-done | bytes 65568 | tf_op jit(solution)/shard_map/ppermute | solution.py:145
  22.0 0.0 copy-done
  22.0 1.0 %scores.1 = f32[64,64]{1,0:T(8,128)} custom-call(bf16[64,4096]{1,0:T(8,128)(2,1)S(1)} %copy-done, bf16[8,4096]{1,0:T(8,128)(2,1)S(1)} %add_convert_fusion.refs_0_, bf16[8,4096]{1,0:T(8,128)(2,1)S(1)} %collective-permute-done.3.refs_1_, bf16[8,4096]{1,0:T(8,128)(2,1)S(1)} %collective-permute-done.4.refs_2_, ...), custom_call_target="tpu_custom_call" | custom-call | tf_op jit(solution)/shard_map/scores/pallas_call | solution.py:134
  (1 shorter events, 0.0 us)
Async XLA Ops:
  0.0 22.0 %copy-start = (bf16[64,4096]{1,0:T(8,128)(2,1)S(1)}, bf16[64,4096]{1,0:T(8,128)(2,1)}, u32[]{:S(2)}) copy-start(bf16[64,4096]{1,0:T(8,128)(2,1)} %query.1) | copy-start | bytes 1572868
  3.0 7.9 %collective-permute-start = (bf16[8,4096]{1,0:T(8,128)(2,1)S(1)}, bf16[8,4096]{1,0:T(8,128)(2,1)S(1)}, u32[]{:S(2)}, u32[]{:S(2)}) collective-permute-start(bf16[8,4096]{1,0:T(8,128)(2,1)S(1)} %get-tuple-element.10), channel_id=1, source_target_pairs={{0,2},{1,3},{2,0},{3,1},{4,6},{5,7},{6,4},{7,5},{8,10},{9,11},{10,... | collective-permute-start | bytes 196616 | tf_op jit(solution)/shard_map/ppermute | solution.py:145
  7.1 6.2 %collective-permute-start.1 = (bf16[8,4096]{1,0:T(8,128)(2,1)S(1)}, bf16[8,4096]{1,0:T(8,128)(2,1)S(1)}, u32[]{:S(2)}, u32[]{:S(2)}) collective-permute-start(bf16[8,4096]{1,0:T(8,128)(2,1)S(1)} %get-tuple-element.11), channel_id=1, source_target_pairs={{0,3},{1,2},{2,1},{3,0},{4,7},{5,6},{6,5},{7,4},{8,11},{9,10},{10,... | collective-permute-start | bytes 196616 | tf_op jit(solution)/shard_map/ppermute | solution.py:145
  8.4 5.0 %collective-permute-start.2 = (bf16[8,4096]{1,0:T(8,128)(2,1)S(1)}, bf16[8,4096]{1,0:T(8,128)(2,1)S(1)}, u32[]{:S(2)}, u32[]{:S(2)}) collective-permute-start(bf16[8,4096]{1,0:T(8,128)(2,1)S(1)} %get-tuple-element.12), channel_id=1, source_target_pairs={{0,1},{1,0},{2,3},{3,2},{4,5},{5,4},{6,7},{7,6},{8,9},{9,8},{10,11... | collective-permute-start | bytes 196616 | tf_op jit(solution)/shard_map/ppermute | solution.py:145
  13.4 5.9 %collective-permute-start.8 = (bf16[8,4096]{1,0:T(8,128)(2,1)S(1)}, bf16[8,4096]{1,0:T(8,128)(2,1)S(1)}, u32[]{:S(2)}, u32[]{:S(2)}) collective-permute-start(bf16[8,4096]{1,0:T(8,128)(2,1)S(1)} %add_convert_fusion.refs_0_), channel_id=1, source_target_pairs={{0,24},{4,28},{8,16},{12,20},{16,8},{20,12},{24,0},{28,4},{1,25},{... | collective-permute-start | bytes 196616 | tf_op jit(solution)/shard_map/ppermute | solution.py:145
  16.0 4.3 %collective-permute-start.6 = (bf16[8,4096]{1,0:T(8,128)(2,1)S(1)}, bf16[8,4096]{1,0:T(8,128)(2,1)S(1)}, u32[]{:S(2)}, u32[]{:S(2)}) collective-permute-start(bf16[8,4096]{1,0:T(8,128)(2,1)S(1)} %add_convert_fusion.refs_0_), channel_id=1, source_target_pairs={{0,16},{4,20},{8,24},{12,28},{16,0},{20,4},{24,8},{28,12},{1,17},{... | collective-permute-start | bytes 196616 | tf_op jit(solution)/shard_map/ppermute | solution.py:145
  16.5 4.3 %collective-permute-start.4 = (bf16[8,4096]{1,0:T(8,128)(2,1)S(1)}, bf16[8,4096]{1,0:T(8,128)(2,1)S(1)}, u32[]{:S(2)}, u32[]{:S(2)}) collective-permute-start(bf16[8,4096]{1,0:T(8,128)(2,1)S(1)} %add_convert_fusion.refs_0_), channel_id=1, source_target_pairs={{0,8},{4,12},{8,0},{12,4},{16,24},{20,28},{24,16},{28,20},{1,9},{5... | collective-permute-start | bytes 196616 | tf_op jit(solution)/shard_map/ppermute | solution.py:145
  17.0 3.7 %collective-permute-start.3 = (bf16[8,4096]{1,0:T(8,128)(2,1)S(1)}, bf16[8,4096]{1,0:T(8,128)(2,1)S(1)}, u32[]{:S(2)}, u32[]{:S(2)}) collective-permute-start(bf16[8,4096]{1,0:T(8,128)(2,1)S(1)} %add_convert_fusion.refs_0_), channel_id=1, source_target_pairs={{0,4},{4,0},{8,12},{12,8},{16,20},{20,16},{24,28},{28,24},{1,5},{5... | collective-permute-start | bytes 196616 | tf_op jit(solution)/shard_map/ppermute | solution.py:145
  19.3 1.4 %collective-permute-start.9 = (bf16[8,4096]{1,0:T(8,128)(2,1)S(1)}, bf16[8,4096]{1,0:T(8,128)(2,1)S(1)}, u32[]{:S(2)}, u32[]{:S(2)}) collective-permute-start(bf16[8,4096]{1,0:T(8,128)(2,1)S(1)} %collective-permute-done.8.refs_6_), channel_id=1, source_target_pairs={{0,4},{4,0},{8,12},{12,8},{16,20},{20,16},{24,28},{28,24},{1,5},{5... | collective-permute-start | bytes 196616 | tf_op jit(solution)/shard_map/ppermute | solution.py:145
  20.2 1.3 %collective-permute-start.7 = (bf16[8,4096]{1,0:T(8,128)(2,1)S(1)}, bf16[8,4096]{1,0:T(8,128)(2,1)S(1)}, u32[]{:S(2)}, u32[]{:S(2)}) collective-permute-start(bf16[8,4096]{1,0:T(8,128)(2,1)S(1)} %collective-permute-done.6.refs_4_), channel_id=1, source_target_pairs={{0,4},{4,0},{8,12},{12,8},{16,20},{20,16},{24,28},{28,24},{1,5},{5... | collective-permute-start | bytes 196616 | tf_op jit(solution)/shard_map/ppermute | solution.py:145
  20.7 1.3 %collective-permute-start.5 = (bf16[8,4096]{1,0:T(8,128)(2,1)S(1)}, bf16[8,4096]{1,0:T(8,128)(2,1)S(1)}, u32[]{:S(2)}, u32[]{:S(2)}) collective-permute-start(bf16[8,4096]{1,0:T(8,128)(2,1)S(1)} %collective-permute-done.4.refs_2_), channel_id=1, source_target_pairs={{0,4},{4,0},{8,12},{12,8},{16,20},{20,16},{24,28},{28,24},{1,5},{5... | collective-permute-start | bytes 196616 | tf_op jit(solution)/shard_map/ppermute | solution.py:145

commit v13 on v12

--- a/solution.py
+++ b/solution.py
@@ -12,11 +12,13 @@
 def feature_kernel(lengths_hbm, owners_hbm, rows_hbm, *refs):
     *shares, lengths, owners, rows, grads, inputs, arrived = refs
     count, width = rows.shape[0], rows.shape[1] // 2
+    piece = 2 * LANES
+    pieces = [pl.ds(at, piece) for at in range(0, count, piece)]
+    pairs = [(lengths_hbm, lengths), (owners_hbm, owners)]
+    pairs += [(rows_hbm.at[part], rows.at[part]) for part in pieces]
     copies = [
         pltpu.make_async_copy(source, target, arrived.at[i])
-        for i, (source, target) in enumerate(
-            ((lengths_hbm, lengths), (owners_hbm, owners), (rows_hbm, rows))
-        )
+        for i, (source, target) in enumerate(pairs)
     ]
     for copy in copies:
         copy.start()
@@ -48,8 +50,8 @@
     ).astype(rows.dtype)
     share_columns = share_of.T
     half = lax.broadcasted_iota(jnp.int32, (LANES, LANES), 1) // width
-    copies[2].wait()
     for b in range(0, blocks, 2):
+        copies[2 + b // 2].wait()
         both = slice(b * LANES, (b + 2) * LANES)
         turned = lax.dot_general(pick, rows[both, :], ROW_BY_ROW, preferred_element_type=jnp.float32)
         for c in (b, b + 1):
@@ -99,7 +101,7 @@
             pltpu.VMEM(proj_rows.shape, proj_rows.dtype),
             pltpu.VMEM((doc_dev * width, count), jnp.bfloat16),
             pltpu.VMEM((count, tok_count * width), jnp.bfloat16),
-            pltpu.SemaphoreType.DMA((3,)),
+            pltpu.SemaphoreType.DMA((2 + count // (2 * LANES),)),
         ],
         compiler_params=pltpu.CompilerParams(vmem_limit_bytes=32 * 1024 * 1024),
         name="features",

time: 23.1 us -> 24.6 us (1.065)
  Pallas kernels: 3.96 us -> 5.43 us
    pallas_call x1, Pallas kernels: 2.98 us -> 4.44 us  [feature_shares(): pl.pallas_call(feature_kernel, out_shape=[jax.ShapeDtypeStruct((doc_dev,...]
where the time goes in v13:
time: 24.6 us; the launch traced here: 24.4 us
  waiting for transfers between devices  9.7 us (39%)
  starting transfers between devices  9.25 us (38%)
  Pallas kernels  5.43 us (22%)
    ppermute x10, waiting for transfers between devices, exchange(): lax.ppermute(block, axis, [(i, i ^ flip) for i in range(lax.axis_size(axi...  9.7 us
    ppermute x10, starting transfers between devices, exchange(): lax.ppermute(block, axis, [(i, i ^ flip) for i in range(lax.axis_size(axi...  9.25 us
    pallas_call x1, Pallas kernels, feature_shares(): pl.pallas_call(feature_kernel, out_shape=[jax.ShapeDtypeStruct((doc_dev,...  4.44 us
    pallas_call x1, Pallas kernels, block_scores(): pl.pallas_call(score_kernel, out_shape=jax.ShapeDtypeStruct((query_featur...  0.99 us
  transfers between devices with their start and end apart: 10, of which 8 were waited for; matrix products, arithmetic and copies ran while one was open for 0% of the time, Pallas kernels for 0%

profile of v13, /device:TPU:0, one launch (start us, length us, event | category | flops | bytes accessed | tf_op | source)
XLA Modules:
  0.0 24.4 jit_solution(6080031778325647045)
XLA Ops:
  0.0 0.0 copy-start
  0.0 4.4 %features.1 = (f32[8,4096]{1,0:T(8,128)S(1)}, bf16[8,4096]{1,0:T(8,128)(2,1)S(1)}, bf16[8,4096]{1,0:T(8,128)(2,1)S(1)}, bf16[8,4096]{1,0:T(8,128)(2,1)S(1)}) custom-call(s32[1,32]{1,0:T(1,128)} %lengths_hbm.1, s32[1,32]{1,0:T(1,128)} %owners_hbm.1, bf16[2048,128]{1,0:T(8,128)(2,1)} %rows_hbm.1), custom_call_target="tpu_custom_call" | custom-call | tf_op jit(solution)/shard_map/features/pallas_call | solution.py:90
  4.5 4.1 %collective-permute-start = (bf16[8,4096]{1,0:T(8,128)(2,1)S(1)}, bf16[8,4096]{1,0:T(8,128)(2,1)S(1)}, u32[]{:S(2)}, u32[]{:S(2)}) collective-permute-start(bf16[8,4096]{1,0:T(8,128)(2,1)S(1)} %get-tuple-element.10), channel_id=1, source_target_pairs={{0,2},{1,3},{2,0},{3,1},{4,6},{5,7},{6,4},{7,5},{8,10},{9,11},{10,... | collective-permute-start | bytes 196616 | tf_op jit(solution)/shard_map/ppermute | solution.py:147
  8.6 1.3 %collective-permute-start.1 = (bf16[8,4096]{1,0:T(8,128)(2,1)S(1)}, bf16[8,4096]{1,0:T(8,128)(2,1)S(1)}, u32[]{:S(2)}, u32[]{:S(2)}) collective-permute-start(bf16[8,4096]{1,0:T(8,128)(2,1)S(1)} %get-tuple-element.11), channel_id=1, source_target_pairs={{0,3},{1,2},{2,1},{3,0},{4,7},{5,6},{6,5},{7,4},{8,11},{9,10},{10,... | collective-permute-start | bytes 196616 | tf_op jit(solution)/shard_map/ppermute | solution.py:147
  9.9 0.2 collective-permute-start.2
  10.1 2.2 %collective-permute-done = bf16[8,4096]{1,0:T(8,128)(2,1)S(1)} collective-permute-done((bf16[8,4096]{1,0:T(8,128)(2,1)S(1)}, bf16[8,4096]{1,0:T(8,128)(2,1)S(1)}, u32[]{:S(2)}, u32[]{:S(2)}) %collective-permute-start) | collective-permute-done | bytes 65568 | tf_op jit(solution)/shard_map/ppermute | solution.py:147
  12.3 2.5 %collective-permute-done.1 = bf16[8,4096]{1,0:T(8,128)(2,1)S(1)} collective-permute-done((bf16[8,4096]{1,0:T(8,128)(2,1)S(1)}, bf16[8,4096]{1,0:T(8,128)(2,1)S(1)}, u32[]{:S(2)}, u32[]{:S(2)}) %collective-permute-start.1) | collective-permute-done | bytes 65568 | tf_op jit(solution)/shard_map/ppermute | solution.py:147
  14.8 0.1 collective-permute-done.2
  14.9 2.5 %collective-permute-start.8 = (bf16[8,4096]{1,0:T(8,128)(2,1)S(1)}, bf16[8,4096]{1,0:T(8,128)(2,1)S(1)}, u32[]{:S(2)}, u32[]{:S(2)}) collective-permute-start(bf16[8,4096]{1,0:T(8,128)(2,1)S(1)} %add_convert_fusion.refs_0_), channel_id=1, source_target_pairs={{0,24},{4,28},{8,16},{12,20},{16,8},{20,12},{24,0},{28,4},{1,25},{... | collective-permute-start | bytes 196616 | tf_op jit(solution)/shard_map/ppermute | solution.py:147
  17.4 0.5 %collective-permute-start.6 = (bf16[8,4096]{1,0:T(8,128)(2,1)S(1)}, bf16[8,4096]{1,0:T(8,128)(2,1)S(1)}, u32[]{:S(2)}, u32[]{:S(2)}) collective-permute-start(bf16[8,4096]{1,0:T(8,128)(2,1)S(1)} %add_convert_fusion.refs_0_), channel_id=1, source_target_pairs={{0,16},{4,20},{8,24},{12,28},{16,0},{20,4},{24,8},{28,12},{1,17},{... | collective-permute-start | bytes 196616 | tf_op jit(solution)/shard_map/ppermute | solution.py:147
  17.9 0.5 %collective-permute-start.4 = (bf16[8,4096]{1,0:T(8,128)(2,1)S(1)}, bf16[8,4096]{1,0:T(8,128)(2,1)S(1)}, u32[]{:S(2)}, u32[]{:S(2)}) collective-permute-start(bf16[8,4096]{1,0:T(8,128)(2,1)S(1)} %add_convert_fusion.refs_0_), channel_id=1, source_target_pairs={{0,8},{4,12},{8,0},{12,4},{16,24},{20,28},{24,16},{28,20},{1,9},{5... | collective-permute-start | bytes 196616 | tf_op jit(solution)/shard_map/ppermute | solution.py:147
  18.5 0.0 collective-permute-start.3
  18.5 2.3 %collective-permute-done.8.refs_6_ = bf16[8,4096]{1,0:T(8,128)(2,1)S(1)} collective-permute-done((bf16[8,4096]{1,0:T(8,128)(2,1)S(1)}, bf16[8,4096]{1,0:T(8,128)(2,1)S(1)}, u32[]{:S(2)}, u32[]{:S(2)}) %collective-permute-start.8) | collective-permute-done | bytes 65568 | tf_op jit(solution)/shard_map/ppermute | solution.py:147
  20.8 0.0 collective-permute-start.9
  20.8 0.9 %collective-permute-done.6.refs_4_ = bf16[8,4096]{1,0:T(8,128)(2,1)S(1)} collective-permute-done((bf16[8,4096]{1,0:T(8,128)(2,1)S(1)}, bf16[8,4096]{1,0:T(8,128)(2,1)S(1)}, u32[]{:S(2)}, u32[]{:S(2)}) %collective-permute-start.6) | collective-permute-done | bytes 65568 | tf_op jit(solution)/shard_map/ppermute | solution.py:147
  21.7 0.0 collective-permute-start.7
  21.7 0.5 %collective-permute-done.4.refs_2_ = bf16[8,4096]{1,0:T(8,128)(2,1)S(1)} collective-permute-done((bf16[8,4096]{1,0:T(8,128)(2,1)S(1)}, bf16[8,4096]{1,0:T(8,128)(2,1)S(1)}, u32[]{:S(2)}, u32[]{:S(2)}) %collective-permute-start.4) | collective-permute-done | bytes 65568 | tf_op jit(solution)/shard_map/ppermute | solution.py:147
  22.2 0.0 collective-permute-start.5
  22.2 0.0 collective-permute-done.3.refs_1_
  22.2 0.0 collective-permute-done.9.refs_7_
  22.2 0.7 %collective-permute-done.7.refs_5_ = bf16[8,4096]{1,0:T(8,128)(2,1)S(1)} collective-permute-done((bf16[8,4096]{1,0:T(8,128)(2,1)S(1)}, bf16[8,4096]{1,0:T(8,128)(2,1)S(1)}, u32[]{:S(2)}, u32[]{:S(2)}) %collective-permute-start.7) | collective-permute-done | bytes 65568 | tf_op jit(solution)/shard_map/ppermute | solution.py:147
  22.9 0.5 %collective-permute-done.5.refs_3_ = bf16[8,4096]{1,0:T(8,128)(2,1)S(1)} collective-permute-done((bf16[8,4096]{1,0:T(8,128)(2,1)S(1)}, bf16[8,4096]{1,0:T(8,128)(2,1)S(1)}, u32[]{:S(2)}, u32[]{:S(2)}) %collective-permute-start.5) | collective-permute-done | bytes 65568 | tf_op jit(solution)/shard_map/ppermute | solution.py:147
  23.5 0.0 copy-done
  23.5 1.0 %scores.1 = f32[64,64]{1,0:T(8,128)} custom-call(bf16[64,4096]{1,0:T(8,128)(2,1)S(1)} %copy-done, bf16[8,4096]{1,0:T(8,128)(2,1)S(1)} %add_convert_fusion.refs_0_, bf16[8,4096]{1,0:T(8,128)(2,1)S(1)} %collective-permute-done.3.refs_1_, bf16[8,4096]{1,0:T(8,128)(2,1)S(1)} %collective-permute-done.4.refs_2_, ...), custom_call_target="tpu_custom_call" | custom-call | tf_op jit(solution)/shard_map/scores/pallas_call | solution.py:136
  (1 shorter events, 0.0 us)
Async XLA Ops:
  0.0 23.5 %copy-start = (bf16[64,4096]{1,0:T(8,128)(2,1)S(1)}, bf16[64,4096]{1,0:T(8,128)(2,1)}, u32[]{:S(2)}) copy-start(bf16[64,4096]{1,0:T(8,128)(2,1)} %query.1) | copy-start | bytes 1572868
  4.5 7.9 %collective-permute-start = (bf16[8,4096]{1,0:T(8,128)(2,1)S(1)}, bf16[8,4096]{1,0:T(8,128)(2,1)S(1)}, u32[]{:S(2)}, u32[]{:S(2)}) collective-permute-start(bf16[8,4096]{1,0:T(8,128)(2,1)S(1)} %get-tuple-element.10), channel_id=1, source_target_pairs={{0,2},{1,3},{2,0},{3,1},{4,6},{5,7},{6,4},{7,5},{8,10},{9,11},{10,... | collective-permute-start | bytes 196616 | tf_op jit(solution)/shard_map/ppermute | solution.py:147
  8.6 6.2 %collective-permute-start.1 = (bf16[8,4096]{1,0:T(8,128)(2,1)S(1)}, bf16[8,4096]{1,0:T(8,128)(2,1)S(1)}, u32[]{:S(2)}, u32[]{:S(2)}) collective-permute-start(bf16[8,4096]{1,0:T(8,128)(2,1)S(1)} %get-tuple-element.11), channel_id=1, source_target_pairs={{0,3},{1,2},{2,1},{3,0},{4,7},{5,6},{6,5},{7,4},{8,11},{9,10},{10,... | collective-permute-start | bytes 196616 | tf_op jit(solution)/shard_map/ppermute | solution.py:147
  9.9 5.0 %collective-permute-start.2 = (bf16[8,4096]{1,0:T(8,128)(2,1)S(1)}, bf16[8,4096]{1,0:T(8,128)(2,1)S(1)}, u32[]{:S(2)}, u32[]{:S(2)}) collective-permute-start(bf16[8,4096]{1,0:T(8,128)(2,1)S(1)} %get-tuple-element.12), channel_id=1, source_target_pairs={{0,1},{1,0},{2,3},{3,2},{4,5},{5,4},{6,7},{7,6},{8,9},{9,8},{10,11... | collective-permute-start | bytes 196616 | tf_op jit(solution)/shard_map/ppermute | solution.py:147
  14.9 5.9 %collective-permute-start.8 = (bf16[8,4096]{1,0:T(8,128)(2,1)S(1)}, bf16[8,4096]{1,0:T(8,128)(2,1)S(1)}, u32[]{:S(2)}, u32[]{:S(2)}) collective-permute-start(bf16[8,4096]{1,0:T(8,128)(2,1)S(1)} %add_convert_fusion.refs_0_), channel_id=1, source_target_pairs={{0,24},{4,28},{8,16},{12,20},{16,8},{20,12},{24,0},{28,4},{1,25},{... | collective-permute-start | bytes 196616 | tf_op jit(solution)/shard_map/ppermute | solution.py:147
  17.4 4.3 %collective-permute-start.6 = (bf16[8,4096]{1,0:T(8,128)(2,1)S(1)}, bf16[8,4096]{1,0:T(8,128)(2,1)S(1)}, u32[]{:S(2)}, u32[]{:S(2)}) collective-permute-start(bf16[8,4096]{1,0:T(8,128)(2,1)S(1)} %add_convert_fusion.refs_0_), channel_id=1, source_target_pairs={{0,16},{4,20},{8,24},{12,28},{16,0},{20,4},{24,8},{28,12},{1,17},{... | collective-permute-start | bytes 196616 | tf_op jit(solution)/shard_map/ppermute | solution.py:147
  17.9 4.3 %collective-permute-start.4 = (bf16[8,4096]{1,0:T(8,128)(2,1)S(1)}, bf16[8,4096]{1,0:T(8,128)(2,1)S(1)}, u32[]{:S(2)}, u32[]{:S(2)}) collective-permute-start(bf16[8,4096]{1,0:T(8,128)(2,1)S(1)} %add_convert_fusion.refs_0_), channel_id=1, source_target_pairs={{0,8},{4,12},{8,0},{12,4},{16,24},{20,28},{24,16},{28,20},{1,9},{5... | collective-permute-start | bytes 196616 | tf_op jit(solution)/shard_map/ppermute | solution.py:147
  18.5 3.7 %collective-permute-start.3 = (bf16[8,4096]{1,0:T(8,128)(2,1)S(1)}, bf16[8,4096]{1,0:T(8,128)(2,1)S(1)}, u32[]{:S(2)}, u32[]{:S(2)}) collective-permute-start(bf16[8,4096]{1,0:T(8,128)(2,1)S(1)} %add_convert_fusion.refs_0_), channel_id=1, source_target_pairs={{0,4},{4,0},{8,12},{12,8},{16,20},{20,16},{24,28},{28,24},{1,5},{5... | collective-permute-start | bytes 196616 | tf_op jit(solution)/shard_map/ppermute | solution.py:147
  20.8 1.4 %collective-permute-start.9 = (bf16[8,4096]{1,0:T(8,128)(2,1)S(1)}, bf16[8,4096]{1,0:T(8,128)(2,1)S(1)}, u32[]{:S(2)}, u32[]{:S(2)}) collective-permute-start(bf16[8,4096]{1,0:T(8,128)(2,1)S(1)} %collective-permute-done.8.refs_6_), channel_id=1, source_target_pairs={{0,4},{4,0},{8,12},{12,8},{16,20},{20,16},{24,28},{28,24},{1,5},{5... | collective-permute-start | bytes 196616 | tf_op jit(solution)/shard_map/ppermute | solution.py:147
  21.7 1.3 %collective-permute-start.7 = (bf16[8,4096]{1,0:T(8,128)(2,1)S(1)}, bf16[8,4096]{1,0:T(8,128)(2,1)S(1)}, u32[]{:S(2)}, u32[]{:S(2)}) collective-permute-start(bf16[8,4096]{1,0:T(8,128)(2,1)S(1)} %collective-permute-done.6.refs_4_), channel_id=1, source_target_pairs={{0,4},{4,0},{8,12},{12,8},{16,20},{20,16},{24,28},{28,24},{1,5},{5... | collective-permute-start | bytes 196616 | tf_op jit(solution)/shard_map/ppermute | solution.py:147
  22.2 1.3 %collective-permute-start.5 = (bf16[8,4096]{1,0:T(8,128)(2,1)S(1)}, bf16[8,4096]{1,0:T(8,128)(2,1)S(1)}, u32[]{:S(2)}, u32[]{:S(2)}) collective-permute-start(bf16[8,4096]{1,0:T(8,128)(2,1)S(1)} %collective-permute-done.4.refs_2_), channel_id=1, source_target_pairs={{0,4},{4,0},{8,12},{12,8},{16,20},{20,16},{24,28},{28,24},{1,5},{5... | collective-permute-start | bytes 196616 | tf_op jit(solution)/shard_map/ppermute | solution.py:147

commit v14 on v12

--- a/solution.py
+++ b/solution.py
@@ -10,7 +10,7 @@
 
 
 def feature_kernel(lengths_hbm, owners_hbm, rows_hbm, *refs):
-    *shares, lengths, owners, rows, grads, inputs, arrived = refs
+    *shares, lengths, owners, rows, grads, inputs, sums, arrived = refs
     count, width = rows.shape[0], rows.shape[1] // 2
     copies = [
         pltpu.make_async_copy(source, target, arrived.at[i])
@@ -41,38 +41,45 @@
         start = start + length
     share_of, row_of = (slot_of >> shift) ^ tok, slot_of & (doc_dev - 1)
 
-    spread = doc_dev * width
     pick = (
-        lax.broadcasted_iota(jnp.int32, (spread, 2 * width), 0) // doc_dev + width
-        == lax.broadcasted_iota(jnp.int32, (spread, 2 * width), 1)
+        lax.broadcasted_iota(jnp.int32, (width, 2 * width), 0) + width
+        == lax.broadcasted_iota(jnp.int32, (width, 2 * width), 1)
     ).astype(rows.dtype)
     share_columns = share_of.T
     half = lax.broadcasted_iota(jnp.int32, (LANES, LANES), 1) // width
     copies[2].wait()
+    product, run = 0.0, 4 * LANES
     for b in range(0, blocks, 2):
         both = slice(b * LANES, (b + 2) * LANES)
         turned = lax.dot_general(pick, rows[both, :], ROW_BY_ROW, preferred_element_type=jnp.float32)
         for c in (b, b + 1):
             part = slice(c * LANES, (c + 1) * LANES)
-            values = turned[:, (c - b) * LANES : (c - b + 1) * LANES].reshape(width, doc_dev, LANES)
-            kept = jnp.where((row_of[c : c + 1, :] == size_row)[None], values, 0.0)
-            grads[:, part] = kept.reshape(spread, LANES).astype(grads.dtype)
+            digit = jnp.broadcast_to(row_of[c : c + 1, :], (8, LANES))[None]
+            values = turned[:, (c - b) * LANES : (c - b + 1) * LANES].reshape(-1, 8, LANES)
+            for at in range(doc_dev):
+                kept = jnp.where(digit == at, values, 0.0).reshape(width, LANES)
+                grads[at * width : (at + 1) * width, part] = kept.astype(grads.dtype)
             values = rows[part, :].astype(jnp.float32)
             values = jnp.where(half == 0, values, pltpu.roll(values, width, 1))
             digit = jnp.broadcast_to(share_columns[:, c : c + 1], (LANES, LANES)) - half
             for at in range(0, tok_count, 2):
                 kept = jnp.where(digit == at, values, 0.0)
                 inputs[part, at * width : at * width + LANES] = kept.astype(inputs.dtype)
-    product = jnp.dot(grads[...], inputs[...], preferred_element_type=jnp.float32)
+        if (b + 2) * LANES % run == 0:
+            done = slice((b + 2) * LANES - run, (b + 2) * LANES)
+            product += jnp.dot(
+                grads[:, done], inputs[done, :], preferred_element_type=jnp.float32
+            )
+    for p in range(sums.shape[0]):
+        sums[p] = product[:, p * LANES : (p + 1) * LANES]
 
     scales = [1.0 / jnp.sqrt(size.astype(jnp.float32)) for size in sizes]
     low_half = lax.broadcasted_iota(jnp.int32, (doc_dev, LANES), 1) < width
     for m in range(width // 2):
         out = slice(m * LANES, (m + 1) * LANES)
         for s in range(0, tok_count, 2):
-            pair = slice(s * width, s * width + LANES)
-            first = product[2 * m * doc_dev : (2 * m + 1) * doc_dev, pair]
-            second = product[(2 * m + 1) * doc_dev : (2 * m + 2) * doc_dev, pair]
+            first = sums[s // 2, pl.ds(2 * m, doc_dev, stride=width), :]
+            second = sums[s // 2, pl.ds(2 * m + 1, doc_dev, stride=width), :]
             left = jnp.where(low_half, first, pltpu.roll(second, width, 1))
             right = jnp.where(low_half, pltpu.roll(first, width, 1), second)
             shares[s][:, out] = (left * scales[s]).astype(shares[s].dtype)
@@ -99,6 +106,7 @@
             pltpu.VMEM(proj_rows.shape, proj_rows.dtype),
             pltpu.VMEM((doc_dev * width, count), jnp.bfloat16),
             pltpu.VMEM((count, tok_count * width), jnp.bfloat16),
+            pltpu.VMEM((tok_count // 2, doc_dev * width, LANES), jnp.float32),
             pltpu.SemaphoreType.DMA((3,)),
         ],
         compiler_params=pltpu.CompilerParams(vmem_limit_bytes=32 * 1024 * 1024),

time: 23.1 us -> 23.4 us (1.013)
  Pallas kernels: 3.96 us -> 4.23 us
    pallas_call x1, Pallas kernels: 2.98 us -> 3.24 us  [feature_shares(): pl.pallas_call(feature_kernel, out_shape=[jax.ShapeDtypeStruct((doc_dev,...]
where the time goes in v14:
time: 23.4 us; the launch traced here: 23.2 us
  waiting for transfers between devices  9.7 us (41%)
  starting transfers between devices  9.25 us (40%)
  Pallas kernels  4.23 us (18%)
    ppermute x10, waiting for transfers between devices, exchange(): lax.ppermute(block, axis, [(i, i ^ flip) for i in range(lax.axis_size(axi...  9.7 us
    ppermute x10, starting transfers between devices, exchange(): lax.ppermute(block, axis, [(i, i ^ flip) for i in range(lax.axis_size(axi...  9.25 us
    pallas_call x1, Pallas kernels, feature_shares(): pl.pallas_call(feature_kernel, out_shape=[jax.ShapeDtypeStruct((doc_dev,...  3.24 us
    pallas_call x1, Pallas kernels, block_scores(): pl.pallas_call(score_kernel, out_shape=jax.ShapeDtypeStruct((query_featur...  0.99 us
  transfers between devices with their start and end apart: 10, of which 8 were waited for; matrix products, arithmetic and copies ran while one was open for 0% of the time, Pallas kernels for 0%

profile of v14, /device:TPU:0, one launch (start us, length us, event | category | flops | bytes accessed | tf_op | source)
XLA Modules:
  0.0 23.2 jit_solution(3078471904128425221)
XLA Ops:
  0.0 0.0 copy-start
  0.0 3.2 %features.1 = (f32[8,4096]{1,0:T(8,128)S(1)}, bf16[8,4096]{1,0:T(8,128)(2,1)S(1)}, bf16[8,4096]{1,0:T(8,128)(2,1)S(1)}, bf16[8,4096]{1,0:T(8,128)(2,1)S(1)}) custom-call(s32[1,32]{1,0:T(1,128)} %lengths_hbm.1, s32[1,32]{1,0:T(1,128)} %owners_hbm.1, bf16[2048,128]{1,0:T(8,128)(2,1)} %rows_hbm.1), custom_call_target="tpu_custom_call" | custom-call | tf_op jit(solution)/shard_map/features/pallas_call | solution.py:95
  3.2 4.1 %collective-permute-start = (bf16[8,4096]{1,0:T(8,128)(2,1)S(1)}, bf16[8,4096]{1,0:T(8,128)(2,1)S(1)}, u32[]{:S(2)}, u32[]{:S(2)}) collective-permute-start(bf16[8,4096]{1,0:T(8,128)(2,1)S(1)} %get-tuple-element.10), channel_id=1, source_target_pairs={{0,2},{1,3},{2,0},{3,1},{4,6},{5,7},{6,4},{7,5},{8,10},{9,11},{10,... | collective-permute-start | bytes 196616 | tf_op jit(solution)/shard_map/ppermute | solution.py:153
  7.4 1.3 %collective-permute-start.1 = (bf16[8,4096]{1,0:T(8,128)(2,1)S(1)}, bf16[8,4096]{1,0:T(8,128)(2,1)S(1)}, u32[]{:S(2)}, u32[]{:S(2)}) collective-permute-start(bf16[8,4096]{1,0:T(8,128)(2,1)S(1)} %get-tuple-element.11), channel_id=1, source_target_pairs={{0,3},{1,2},{2,1},{3,0},{4,7},{5,6},{6,5},{7,4},{8,11},{9,10},{10,... | collective-permute-start | bytes 196616 | tf_op jit(solution)/shard_map/ppermute | solution.py:153
  8.7 0.2 collective-permute-start.2
  8.9 2.2 %collective-permute-done = bf16[8,4096]{1,0:T(8,128)(2,1)S(1)} collective-permute-done((bf16[8,4096]{1,0:T(8,128)(2,1)S(1)}, bf16[8,4096]{1,0:T(8,128)(2,1)S(1)}, u32[]{:S(2)}, u32[]{:S(2)}) %collective-permute-start) | collective-permute-done | bytes 65568 | tf_op jit(solution)/shard_map/ppermute | solution.py:153
  11.1 2.5 %collective-permute-done.1 = bf16[8,4096]{1,0:T(8,128)(2,1)S(1)} collective-permute-done((bf16[8,4096]{1,0:T(8,128)(2,1)S(1)}, bf16[8,4096]{1,0:T(8,128)(2,1)S(1)}, u32[]{:S(2)}, u32[]{:S(2)}) %collective-permute-start.1) | collective-permute-done | bytes 65568 | tf_op jit(solution)/shard_map/ppermute | solution.py:153
  13.6 0.1 collective-permute-done.2
  13.7 2.5 %collective-permute-start.8 = (bf16[8,4096]{1,0:T(8,128)(2,1)S(1)}, bf16[8,4096]{1,0:T(8,128)(2,1)S(1)}, u32[]{:S(2)}, u32[]{:S(2)}) collective-permute-start(bf16[8,4096]{1,0:T(8,128)(2,1)S(1)} %add_convert_fusion.refs_0_), channel_id=1, source_target_pairs={{0,24},{4,28},{8,16},{12,20},{16,8},{20,12},{24,0},{28,4},{1,25},{... | collective-permute-start | bytes 196616 | tf_op jit(solution)/shard_map/ppermute | solution.py:153
  16.2 0.5 %collective-permute-start.6 = (bf16[8,4096]{1,0:T(8,128)(2,1)S(1)}, bf16[8,4096]{1,0:T(8,128)(2,1)S(1)}, u32[]{:S(2)}, u32[]{:S(2)}) collective-permute-start(bf16[8,4096]{1,0:T(8,128)(2,1)S(1)} %add_convert_fusion.refs_0_), channel_id=1, source_target_pairs={{0,16},{4,20},{8,24},{12,28},{16,0},{20,4},{24,8},{28,12},{1,17},{... | collective-permute-start | bytes 196616 | tf_op jit(solution)/shard_map/ppermute | solution.py:153
  16.7 0.5 %collective-permute-start.4 = (bf16[8,4096]{1,0:T(8,128)(2,1)S(1)}, bf16[8,4096]{1,0:T(8,128)(2,1)S(1)}, u32[]{:S(2)}, u32[]{:S(2)}) collective-permute-start(bf16[8,4096]{1,0:T(8,128)(2,1)S(1)} %add_convert_fusion.refs_0_), channel_id=1, source_target_pairs={{0,8},{4,12},{8,0},{12,4},{16,24},{20,28},{24,16},{28,20},{1,9},{5... | collective-permute-start | bytes 196616 | tf_op jit(solution)/shard_map/ppermute | solution.py:153
  17.3 0.0 collective-permute-start.3
  17.3 2.3 %collective-permute-done.8.refs_6_ = bf16[8,4096]{1,0:T(8,128)(2,1)S(1)} collective-permute-done((bf16[8,4096]{1,0:T(8,128)(2,1)S(1)}, bf16[8,4096]{1,0:T(8,128)(2,1)S(1)}, u32[]{:S(2)}, u32[]{:S(2)}) %collective-permute-start.8) | collective-permute-done | bytes 65568 | tf_op jit(solution)/shard_map/ppermute | solution.py:153
  19.6 0.0 collective-permute-start.9
  19.6 0.9 %collective-permute-done.6.refs_4_ = bf16[8,4096]{1,0:T(8,128)(2,1)S(1)} collective-permute-done((bf16[8,4096]{1,0:T(8,128)(2,1)S(1)}, bf16[8,4096]{1,0:T(8,128)(2,1)S(1)}, u32[]{:S(2)}, u32[]{:S(2)}) %collective-permute-start.6) | collective-permute-done | bytes 65568 | tf_op jit(solution)/shard_map/ppermute | solution.py:153
  20.5 0.0 collective-permute-start.7
  20.5 0.5 %collective-permute-done.4.refs_2_ = bf16[8,4096]{1,0:T(8,128)(2,1)S(1)} collective-permute-done((bf16[8,4096]{1,0:T(8,128)(2,1)S(1)}, bf16[8,4096]{1,0:T(8,128)(2,1)S(1)}, u32[]{:S(2)}, u32[]{:S(2)}) %collective-permute-start.4) | collective-permute-done | bytes 65568 | tf_op jit(solution)/shard_map/ppermute | solution.py:153
  21.0 0.0 collective-permute-start.5
  21.0 0.0 collective-permute-done.3.refs_1_
  21.0 0.0 collective-permute-done.9.refs_7_
  21.0 0.7 %collective-permute-done.7.refs_5_ = bf16[8,4096]{1,0:T(8,128)(2,1)S(1)} collective-permute-done((bf16[8,4096]{1,0:T(8,128)(2,1)S(1)}, bf16[8,4096]{1,0:T(8,128)(2,1)S(1)}, u32[]{:S(2)}, u32[]{:S(2)}) %collective-permute-start.7) | collective-permute-done | bytes 65568 | tf_op jit(solution)/shard_map/ppermute | solution.py:153
  21.7 0.5 %collective-permute-done.5.refs_3_ = bf16[8,4096]{1,0:T(8,128)(2,1)S(1)} collective-permute-done((bf16[8,4096]{1,0:T(8,128)(2,1)S(1)}, bf16[8,4096]{1,0:T(8,128)(2,1)S(1)}, u32[]{:S(2)}, u32[]{:S(2)}) %collective-permute-start.5) | collective-permute-done | bytes 65568 | tf_op jit(solution)/shard_map/ppermute | solution.py:153
  22.2 0.0 copy-done
  22.3 1.0 %scores.1 = f32[64,64]{1,0:T(8,128)} custom-call(bf16[64,4096]{1,0:T(8,128)(2,1)S(1)} %copy-done, bf16[8,4096]{1,0:T(8,128)(2,1)S(1)} %add_convert_fusion.refs_0_, bf16[8,4096]{1,0:T(8,128)(2,1)S(1)} %collective-permute-done.3.refs_1_, bf16[8,4096]{1,0:T(8,128)(2,1)S(1)} %collective-permute-done.4.refs_2_, ...), custom_call_target="tpu_custom_call" | custom-call | tf_op jit(solution)/shard_map/scores/pallas_call | solution.py:142
  (1 shorter events, 0.0 us)
Async XLA Ops:
  0.0 22.3 %copy-start = (bf16[64,4096]{1,0:T(8,128)(2,1)S(1)}, bf16[64,4096]{1,0:T(8,128)(2,1)}, u32[]{:S(2)}) copy-start(bf16[64,4096]{1,0:T(8,128)(2,1)} %query.1) | copy-start | bytes 1572868
  3.2 7.9 %collective-permute-start = (bf16[8,4096]{1,0:T(8,128)(2,1)S(1)}, bf16[8,4096]{1,0:T(8,128)(2,1)S(1)}, u32[]{:S(2)}, u32[]{:S(2)}) collective-permute-start(bf16[8,4096]{1,0:T(8,128)(2,1)S(1)} %get-tuple-element.10), channel_id=1, source_target_pairs={{0,2},{1,3},{2,0},{3,1},{4,6},{5,7},{6,4},{7,5},{8,10},{9,11},{10,... | collective-permute-start | bytes 196616 | tf_op jit(solution)/shard_map/ppermute | solution.py:153
  7.4 6.2 %collective-permute-start.1 = (bf16[8,4096]{1,0:T(8,128)(2,1)S(1)}, bf16[8,4096]{1,0:T(8,128)(2,1)S(1)}, u32[]{:S(2)}, u32[]{:S(2)}) collective-permute-start(bf16[8,4096]{1,0:T(8,128)(2,1)S(1)} %get-tuple-element.11), channel_id=1, source_target_pairs={{0,3},{1,2},{2,1},{3,0},{4,7},{5,6},{6,5},{7,4},{8,11},{9,10},{10,... | collective-permute-start | bytes 196616 | tf_op jit(solution)/shard_map/ppermute | solution.py:153
  8.7 5.0 %collective-permute-start.2 = (bf16[8,4096]{1,0:T(8,128)(2,1)S(1)}, bf16[8,4096]{1,0:T(8,128)(2,1)S(1)}, u32[]{:S(2)}, u32[]{:S(2)}) collective-permute-start(bf16[8,4096]{1,0:T(8,128)(2,1)S(1)} %get-tuple-element.12), channel_id=1, source_target_pairs={{0,1},{1,0},{2,3},{3,2},{4,5},{5,4},{6,7},{7,6},{8,9},{9,8},{10,11... | collective-permute-start | bytes 196616 | tf_op jit(solution)/shard_map/ppermute | solution.py:153
  13.7 5.9 %collective-permute-start.8 = (bf16[8,4096]{1,0:T(8,128)(2,1)S(1)}, bf16[8,4096]{1,0:T(8,128)(2,1)S(1)}, u32[]{:S(2)}, u32[]{:S(2)}) collective-permute-start(bf16[8,4096]{1,0:T(8,128)(2,1)S(1)} %add_convert_fusion.refs_0_), channel_id=1, source_target_pairs={{0,24},{4,28},{8,16},{12,20},{16,8},{20,12},{24,0},{28,4},{1,25},{... | collective-permute-start | bytes 196616 | tf_op jit(solution)/shard_map/ppermute | solution.py:153
  16.2 4.3 %collective-permute-start.6 = (bf16[8,4096]{1,0:T(8,128)(2,1)S(1)}, bf16[8,4096]{1,0:T(8,128)(2,1)S(1)}, u32[]{:S(2)}, u32[]{:S(2)}) collective-permute-start(bf16[8,4096]{1,0:T(8,128)(2,1)S(1)} %add_convert_fusion.refs_0_), channel_id=1, source_target_pairs={{0,16},{4,20},{8,24},{12,28},{16,0},{20,4},{24,8},{28,12},{1,17},{... | collective-permute-start | bytes 196616 | tf_op jit(solution)/shard_map/ppermute | solution.py:153
  16.7 4.3 %collective-permute-start.4 = (bf16[8,4096]{1,0:T(8,128)(2,1)S(1)}, bf16[8,4096]{1,0:T(8,128)(2,1)S(1)}, u32[]{:S(2)}, u32[]{:S(2)}) collective-permute-start(bf16[8,4096]{1,0:T(8,128)(2,1)S(1)} %add_convert_fusion.refs_0_), channel_id=1, source_target_pairs={{0,8},{4,12},{8,0},{12,4},{16,24},{20,28},{24,16},{28,20},{1,9},{5... | collective-permute-start | bytes 196616 | tf_op jit(solution)/shard_map/ppermute | solution.py:153
  17.3 3.7 %collective-permute-start.3 = (bf16[8,4096]{1,0:T(8,128)(2,1)S(1)}, bf16[8,4096]{1,0:T(8,128)(2,1)S(1)}, u32[]{:S(2)}, u32[]{:S(2)}) collective-permute-start(bf16[8,4096]{1,0:T(8,128)(2,1)S(1)} %add_convert_fusion.refs_0_), channel_id=1, source_target_pairs={{0,4},{4,0},{8,12},{12,8},{16,20},{20,16},{24,28},{28,24},{1,5},{5... | collective-permute-start | bytes 196616 | tf_op jit(solution)/shard_map/ppermute | solution.py:153
  19.6 1.4 %collective-permute-start.9 = (bf16[8,4096]{1,0:T(8,128)(2,1)S(1)}, bf16[8,4096]{1,0:T(8,128)(2,1)S(1)}, u32[]{:S(2)}, u32[]{:S(2)}) collective-permute-start(bf16[8,4096]{1,0:T(8,128)(2,1)S(1)} %collective-permute-done.8.refs_6_), channel_id=1, source_target_pairs={{0,4},{4,0},{8,12},{12,8},{16,20},{20,16},{24,28},{28,24},{1,5},{5... | collective-permute-start | bytes 196616 | tf_op jit(solution)/shard_map/ppermute | solution.py:153
  20.5 1.3 %collective-permute-start.7 = (bf16[8,4096]{1,0:T(8,128)(2,1)S(1)}, bf16[8,4096]{1,0:T(8,128)(2,1)S(1)}, u32[]{:S(2)}, u32[]{:S(2)}) collective-permute-start(bf16[8,4096]{1,0:T(8,128)(2,1)S(1)} %collective-permute-done.6.refs_4_), channel_id=1, source_target_pairs={{0,4},{4,0},{8,12},{12,8},{16,20},{20,16},{24,28},{28,24},{1,5},{5... | collective-permute-start | bytes 196616 | tf_op jit(solution)/shard_map/ppermute | solution.py:153
  21.0 1.3 %collective-permute-start.5 = (bf16[8,4096]{1,0:T(8,128)(2,1)S(1)}, bf16[8,4096]{1,0:T(8,128)(2,1)S(1)}, u32[]{:S(2)}, u32[]{:S(2)}) collective-permute-start(bf16[8,4096]{1,0:T(8,128)(2,1)S(1)} %collective-permute-done.4.refs_2_), channel_id=1, source_target_pairs={{0,4},{4,0},{8,12},{12,8},{16,20},{20,16},{24,28},{28,24},{1,5},{5... | collective-permute-start | bytes 196616 | tf_op jit(solution)/shard_map/ppermute | solution.py:153

commit v15 on v9

--- a/solution.py
+++ b/solution.py
@@ -109,35 +109,44 @@
     *blocks, scores = refs
     doc_dev = blocks[0].shape[0]
     features = jnp.concatenate([block[...] for block in blocks], axis=0)
-    depth = features.shape[1] // 4
-    products = sum(
-        lax.dot_general(
-            features[:, at : at + depth], query[:, at : at + depth], ROW_BY_ROW,
-            preferred_element_type=jnp.float32,
-        )
-        for at in range(0, features.shape[1], depth)
+    products = lax.dot_general(
+        features, query[...], ROW_BY_ROW, preferred_element_type=jnp.float32
     )
-    parts = [products[i * doc_dev : (i + 1) * doc_dev] for i in range(len(blocks))]
+    own, second, first, third, own_next, second_next, first_next, third_next = (
+        products[i * doc_dev : (i + 1) * doc_dev] for i in range(len(blocks))
+    )
     ex = lax.axis_index("ex")
+    odd = lax.rem(ex, 2) == 1
+    parts = [
+        own,
+        own_next,
+        jnp.where(odd, first, second),
+        jnp.where(odd, second_next, first_next),
+        jnp.where(odd, second, first),
+        jnp.where(odd, first_next, second_next),
+        third,
+        third_next,
+    ]
     flip = 1
-    while flip < len(blocks):
+    while flip < len(parts):
         swap = lax.rem(lax.div(ex, flip), 2) == 1
         parts = [jnp.where(swap, parts[i ^ flip], parts[i]) for i in range(len(parts))]
         flip *= 2
     scores[...] = jnp.concatenate(parts, axis=0).T
 
 
-def block_scores(query_features, blocks):
+def block_scores(query_features, held, held_next):
     whole = pl.BlockSpec(memory_space=pltpu.VMEM)
-    docs = len(blocks) * blocks[0].shape[0]
+    operands = (query_features, *held, *held_next)
+    docs = (len(operands) - 1) * held[0].shape[0]
     return pl.pallas_call(
         score_kernel,
         out_shape=jax.ShapeDtypeStruct((query_features.shape[0], docs), jnp.float32),
-        in_specs=[whole] * (1 + len(blocks)),
+        in_specs=[whole] * len(operands),
         out_specs=whole,
         compiler_params=pltpu.CompilerParams(vmem_limit_bytes=16 * 1024 * 1024),
         name="scores",
-    )(*(pltpu.with_memory_space_constraint(x, pltpu.VMEM) for x in (query_features, *blocks)))
+    )(*(pltpu.with_memory_space_constraint(x, pltpu.VMEM) for x in operands))
 
 
 def exchange(block, axis, flip):
@@ -155,12 +164,11 @@
     if ex_count != 8:
         gathered = lax.all_gather(features, "ex", axis=0, tiled=True)
         return jnp.einsum("qf,df->qd", query_features, gathered, preferred_element_type=jnp.float32)
-    blocks = [features] + [None] * (ex_count - 1)
-    for flip in (4, 2, 6):
-        blocks[flip] = exchange(features, "ex", flip)
-    for flip in (0, 4, 2, 6):
-        blocks[flip + 1] = exchange(blocks[flip], "ex", 1)
-    return block_scores(query_features, blocks)
+    turns = [[(i, i ^ (first if i % 2 else 6 - first)) for i in range(ex_count)] for first in (2, 4)]
+    third = exchange(features, "ex", 6)
+    first, second = (lax.ppermute(features, "ex", turn) for turn in turns)
+    held = (features, second, first, third)
+    return block_scores(query_features, held, [exchange(block, "ex", 1) for block in held])
 
 
 def solution(mesh):

time: 23.1 us -> 23.1 us (level)
    ppermute x0 -> x2, waiting for transfers between devices: none -> 2.05 us  [body(): first, second = (lax.ppermute(features, 'ex', turn) for turn in turns)]
    ppermute x10 -> x8, waiting for transfers between devices: 9.7 us -> 7.66 us  [exchange(): lax.ppermute(block, axis, [(i, i ^ flip) for i in range(lax.axis_size(axi...]
    ppermute x10 -> x8, starting transfers between devices: 9.25 us -> 8.21 us  [exchange(): lax.ppermute(block, axis, [(i, i ^ flip) for i in range(lax.axis_size(axi...]
    ppermute x0 -> x2, starting transfers between devices: none -> 1.04 us  [body(): first, second = (lax.ppermute(features, 'ex', turn) for turn in turns)]
where the time goes in v15:
time: 23.1 us; the launch traced here: 22.9 us
  waiting for transfers between devices  9.7 us (42%)
  starting transfers between devices  9.25 us (40%)
  Pallas kernels  3.89 us (17%)
    ppermute x8, starting transfers between devices, exchange(): lax.ppermute(block, axis, [(i, i ^ flip) for i in range(lax.axis_size(axi...  8.21 us
    ppermute x8, waiting for transfers between devices, exchange(): lax.ppermute(block, axis, [(i, i ^ flip) for i in range(lax.axis_size(axi...  7.66 us
    pallas_call x1, Pallas kernels, feature_shares(): pl.pallas_call(feature_kernel, out_shape=[jax.ShapeDtypeStruct((doc_dev,...  2.9 us
    ppermute x2, waiting for transfers between devices, body(): first, second = (lax.ppermute(features, 'ex', turn) for turn in turns)  2.05 us
    ppermute x2, starting transfers between devices, body(): first, second = (lax.ppermute(features, 'ex', turn) for turn in turns)  1.04 us
    pallas_call x1, Pallas kernels, block_scores(): pl.pallas_call(score_kernel, out_shape=jax.ShapeDtypeStruct((query_featur...  0.99 us
  transfers between devices with their start and end apart: 10, of which 8 were waited for; matrix products, arithmetic and copies ran while one was open for 0% of the time, Pallas kernels for 0%

profile of v15, /device:TPU:0, one launch (start us, length us, event | category | flops | bytes accessed | tf_op | source)
XLA Modules:
  0.0 22.9 jit_solution(12072825058635149290)
XLA Ops:
  0.0 0.0 copy-start
  0.0 2.9 %features.1 = (f32[8,4096]{1,0:T(8,128)S(1)}, bf16[8,4096]{1,0:T(8,128)(2,1)S(1)}, bf16[8,4096]{1,0:T(8,128)(2,1)S(1)}, bf16[8,4096]{1,0:T(8,128)(2,1)S(1)}) custom-call(s32[1,32]{1,0:T(1,128)} %lengths_hbm.1, s32[1,32]{1,0:T(1,128)} %owners_hbm.1, bf16[2048,128]{1,0:T(8,128)(2,1)} %rows_hbm.1), custom_call_target="tpu_custom_call" | custom-call | tf_op jit(solution)/shard_map/features/pallas_call | solution.py:86
  2.9 4.1 %collective-permute-start = (bf16[8,4096]{1,0:T(8,128)(2,1)S(1)}, bf16[8,4096]{1,0:T(8,128)(2,1)S(1)}, u32[]{:S(2)}, u32[]{:S(2)}) collective-permute-start(bf16[8,4096]{1,0:T(8,128)(2,1)S(1)} %get-tuple-element.10), channel_id=1, source_target_pairs={{0,2},{1,3},{2,0},{3,1},{4,6},{5,7},{6,4},{7,5},{8,10},{9,11},{10,... | collective-permute-start | bytes 196616 | tf_op jit(solution)/shard_map/ppermute | solution.py:153
  7.0 1.3 %collective-permute-start.1 = (bf16[8,4096]{1,0:T(8,128)(2,1)S(1)}, bf16[8,4096]{1,0:T(8,128)(2,1)S(1)}, u32[]{:S(2)}, u32[]{:S(2)}) collective-permute-start(bf16[8,4096]{1,0:T(8,128)(2,1)S(1)} %get-tuple-element.11), channel_id=1, source_target_pairs={{0,3},{1,2},{2,1},{3,0},{4,7},{5,6},{6,5},{7,4},{8,11},{9,10},{10,... | collective-permute-start | bytes 196616 | tf_op jit(solution)/shard_map/ppermute | solution.py:153
  8.4 0.2 collective-permute-start.2
  8.6 2.2 %collective-permute-done = bf16[8,4096]{1,0:T(8,128)(2,1)S(1)} collective-permute-done((bf16[8,4096]{1,0:T(8,128)(2,1)S(1)}, bf16[8,4096]{1,0:T(8,128)(2,1)S(1)}, u32[]{:S(2)}, u32[]{:S(2)}) %collective-permute-start) | collective-permute-done | bytes 65568 | tf_op jit(solution)/shard_map/ppermute | solution.py:153
  10.8 2.5 %collective-permute-done.1 = bf16[8,4096]{1,0:T(8,128)(2,1)S(1)} collective-permute-done((bf16[8,4096]{1,0:T(8,128)(2,1)S(1)}, bf16[8,4096]{1,0:T(8,128)(2,1)S(1)}, u32[]{:S(2)}, u32[]{:S(2)}) %collective-permute-start.1) | collective-permute-done | bytes 65568 | tf_op jit(solution)/shard_map/ppermute | solution.py:153
  13.2 0.1 collective-permute-done.2
  13.4 2.5 %collective-permute-start.5 = (bf16[8,4096]{1,0:T(8,128)(2,1)S(1)}, bf16[8,4096]{1,0:T(8,128)(2,1)S(1)}, u32[]{:S(2)}, u32[]{:S(2)}) collective-permute-start(bf16[8,4096]{1,0:T(8,128)(2,1)S(1)} %add_convert_fusion.refs_0_), channel_id=1, source_target_pairs={{0,24},{4,28},{8,16},{12,20},{16,8},{20,12},{24,0},{28,4},{1,25},{... | collective-permute-start | bytes 196616 | tf_op jit(solution)/shard_map/ppermute | solution.py:153
  15.9 0.5 %collective-permute-start.4 = (bf16[8,4096]{1,0:T(8,128)(2,1)S(1)}, bf16[8,4096]{1,0:T(8,128)(2,1)S(1)}, u32[]{:S(2)}, u32[]{:S(2)}) collective-permute-start(bf16[8,4096]{1,0:T(8,128)(2,1)S(1)} %add_convert_fusion.refs_0_), channel_id=1, source_target_pairs={{0,16},{4,12},{8,24},{12,4},{16,0},{20,28},{24,8},{28,20},{1,17},{... | collective-permute-start | bytes 196616 | tf_op jit(solution)/shard_map/ppermute | solution.py:169
  16.4 0.5 %collective-permute-start.3 = (bf16[8,4096]{1,0:T(8,128)(2,1)S(1)}, bf16[8,4096]{1,0:T(8,128)(2,1)S(1)}, u32[]{:S(2)}, u32[]{:S(2)}) collective-permute-start(bf16[8,4096]{1,0:T(8,128)(2,1)S(1)} %add_convert_fusion.refs_0_), channel_id=1, source_target_pairs={{0,8},{4,20},{8,0},{12,28},{16,24},{20,4},{24,16},{28,12},{1,9},{5... | collective-permute-start | bytes 196616 | tf_op jit(solution)/shard_map/ppermute | solution.py:169
  16.9 0.0 collective-permute-start.6
  16.9 1.7 %collective-permute-done.5.refs_3_ = bf16[8,4096]{1,0:T(8,128)(2,1)S(1)} collective-permute-done((bf16[8,4096]{1,0:T(8,128)(2,1)S(1)}, bf16[8,4096]{1,0:T(8,128)(2,1)S(1)}, u32[]{:S(2)}, u32[]{:S(2)}) %collective-permute-start.5) | collective-permute-done | bytes 65568 | tf_op jit(solution)/shard_map/ppermute | solution.py:153
  18.6 0.0 collective-permute-start.9
  18.6 1.5 %collective-permute-done.4.refs_2_ = bf16[8,4096]{1,0:T(8,128)(2,1)S(1)} collective-permute-done((bf16[8,4096]{1,0:T(8,128)(2,1)S(1)}, bf16[8,4096]{1,0:T(8,128)(2,1)S(1)}, u32[]{:S(2)}, u32[]{:S(2)}) %collective-permute-start.4) | collective-permute-done | bytes 65568 | tf_op jit(solution)/shard_map/ppermute | solution.py:169
  20.2 0.0 collective-permute-start.8
  20.2 0.5 %collective-permute-done.3.refs_1_ = bf16[8,4096]{1,0:T(8,128)(2,1)S(1)} collective-permute-done((bf16[8,4096]{1,0:T(8,128)(2,1)S(1)}, bf16[8,4096]{1,0:T(8,128)(2,1)S(1)}, u32[]{:S(2)}, u32[]{:S(2)}) %collective-permute-start.3) | collective-permute-done | bytes 65568 | tf_op jit(solution)/shard_map/ppermute | solution.py:169
  20.7 0.0 collective-permute-start.7
  20.7 0.0 collective-permute-done.6.refs_4_
  20.7 0.0 collective-permute-done.9.refs_7_
  20.7 0.7 %collective-permute-done.8.refs_6_ = bf16[8,4096]{1,0:T(8,128)(2,1)S(1)} collective-permute-done((bf16[8,4096]{1,0:T(8,128)(2,1)S(1)}, bf16[8,4096]{1,0:T(8,128)(2,1)S(1)}, u32[]{:S(2)}, u32[]{:S(2)}) %collective-permute-start.8) | collective-permute-done | bytes 65568 | tf_op jit(solution)/shard_map/ppermute | solution.py:153
  21.4 0.5 %collective-permute-done.7.refs_5_ = bf16[8,4096]{1,0:T(8,128)(2,1)S(1)} collective-permute-done((bf16[8,4096]{1,0:T(8,128)(2,1)S(1)}, bf16[8,4096]{1,0:T(8,128)(2,1)S(1)}, u32[]{:S(2)}, u32[]{:S(2)}) %collective-permute-start.7) | collective-permute-done | bytes 65568 | tf_op jit(solution)/shard_map/ppermute | solution.py:153
  21.9 0.0 copy-done
  21.9 1.0 %scores.1 = f32[64,64]{1,0:T(8,128)} custom-call(bf16[64,4096]{1,0:T(8,128)(2,1)S(1)} %copy-done, bf16[8,4096]{1,0:T(8,128)(2,1)S(1)} %add_convert_fusion.refs_0_, bf16[8,4096]{1,0:T(8,128)(2,1)S(1)} %collective-permute-done.3.refs_1_, bf16[8,4096]{1,0:T(8,128)(2,1)S(1)} %collective-permute-done.4.refs_2_, ...), custom_call_target="tpu_custom_call" | custom-call | tf_op jit(solution)/shard_map/scores/pallas_call | solution.py:142
  (1 shorter events, 0.0 us)
Async XLA Ops:
  0.0 21.9 %copy-start = (bf16[64,4096]{1,0:T(8,128)(2,1)S(1)}, bf16[64,4096]{1,0:T(8,128)(2,1)}, u32[]{:S(2)}) copy-start(bf16[64,4096]{1,0:T(8,128)(2,1)} %query.1) | copy-start | bytes 1572868
  2.9 7.9 %collective-permute-start = (bf16[8,4096]{1,0:T(8,128)(2,1)S(1)}, bf16[8,4096]{1,0:T(8,128)(2,1)S(1)}, u32[]{:S(2)}, u32[]{:S(2)}) collective-permute-start(bf16[8,4096]{1,0:T(8,128)(2,1)S(1)} %get-tuple-element.10), channel_id=1, source_target_pairs={{0,2},{1,3},{2,0},{3,1},{4,6},{5,7},{6,4},{7,5},{8,10},{9,11},{10,... | collective-permute-start | bytes 196616 | tf_op jit(solution)/shard_map/ppermute | solution.py:153
  7.0 6.2 %collective-permute-start.1 = (bf16[8,4096]{1,0:T(8,128)(2,1)S(1)}, bf16[8,4096]{1,0:T(8,128)(2,1)S(1)}, u32[]{:S(2)}, u32[]{:S(2)}) collective-permute-start(bf16[8,4096]{1,0:T(8,128)(2,1)S(1)} %get-tuple-element.11), channel_id=1, source_target_pairs={{0,3},{1,2},{2,1},{3,0},{4,7},{5,6},{6,5},{7,4},{8,11},{9,10},{10,... | collective-permute-start | bytes 196616 | tf_op jit(solution)/shard_map/ppermute | solution.py:153
  8.4 5.0 %collective-permute-start.2 = (bf16[8,4096]{1,0:T(8,128)(2,1)S(1)}, bf16[8,4096]{1,0:T(8,128)(2,1)S(1)}, u32[]{:S(2)}, u32[]{:S(2)}) collective-permute-start(bf16[8,4096]{1,0:T(8,128)(2,1)S(1)} %get-tuple-element.12), channel_id=1, source_target_pairs={{0,1},{1,0},{2,3},{3,2},{4,5},{5,4},{6,7},{7,6},{8,9},{9,8},{10,11... | collective-permute-start | bytes 196616 | tf_op jit(solution)/shard_map/ppermute | solution.py:153
  13.4 5.2 %collective-permute-start.5 = (bf16[8,4096]{1,0:T(8,128)(2,1)S(1)}, bf16[8,4096]{1,0:T(8,128)(2,1)S(1)}, u32[]{:S(2)}, u32[]{:S(2)}) collective-permute-start(bf16[8,4096]{1,0:T(8,128)(2,1)S(1)} %add_convert_fusion.refs_0_), channel_id=1, source_target_pairs={{0,24},{4,28},{8,16},{12,20},{16,8},{20,12},{24,0},{28,4},{1,25},{... | collective-permute-start | bytes 196616 | tf_op jit(solution)/shard_map/ppermute | solution.py:153
  15.9 4.3 %collective-permute-start.4 = (bf16[8,4096]{1,0:T(8,128)(2,1)S(1)}, bf16[8,4096]{1,0:T(8,128)(2,1)S(1)}, u32[]{:S(2)}, u32[]{:S(2)}) collective-permute-start(bf16[8,4096]{1,0:T(8,128)(2,1)S(1)} %add_convert_fusion.refs_0_), channel_id=1, source_target_pairs={{0,16},{4,12},{8,24},{12,4},{16,0},{20,28},{24,8},{28,20},{1,17},{... | collective-permute-start | bytes 196616 | tf_op jit(solution)/shard_map/ppermute | solution.py:169
  16.4 4.3 %collective-permute-start.3 = (bf16[8,4096]{1,0:T(8,128)(2,1)S(1)}, bf16[8,4096]{1,0:T(8,128)(2,1)S(1)}, u32[]{:S(2)}, u32[]{:S(2)}) collective-permute-start(bf16[8,4096]{1,0:T(8,128)(2,1)S(1)} %add_convert_fusion.refs_0_), channel_id=1, source_target_pairs={{0,8},{4,20},{8,0},{12,28},{16,24},{20,4},{24,16},{28,12},{1,9},{5... | collective-permute-start | bytes 196616 | tf_op jit(solution)/shard_map/ppermute | solution.py:169
  16.9 3.7 %collective-permute-start.6 = (bf16[8,4096]{1,0:T(8,128)(2,1)S(1)}, bf16[8,4096]{1,0:T(8,128)(2,1)S(1)}, u32[]{:S(2)}, u32[]{:S(2)}) collective-permute-start(bf16[8,4096]{1,0:T(8,128)(2,1)S(1)} %add_convert_fusion.refs_0_), channel_id=1, source_target_pairs={{0,4},{4,0},{8,12},{12,8},{16,20},{20,16},{24,28},{28,24},{1,5},{5... | collective-permute-start | bytes 196616 | tf_op jit(solution)/shard_map/ppermute | solution.py:153
  18.6 2.1 %collective-permute-start.9 = (bf16[8,4096]{1,0:T(8,128)(2,1)S(1)}, bf16[8,4096]{1,0:T(8,128)(2,1)S(1)}, u32[]{:S(2)}, u32[]{:S(2)}) collective-permute-start(bf16[8,4096]{1,0:T(8,128)(2,1)S(1)} %collective-permute-done.5.refs_3_), channel_id=1, source_target_pairs={{0,4},{4,0},{8,12},{12,8},{16,20},{20,16},{24,28},{28,24},{1,5},{5... | collective-permute-start | bytes 196616 | tf_op jit(solution)/shard_map/ppermute | solution.py:153
  20.2 1.3 %collective-permute-start.8 = (bf16[8,4096]{1,0:T(8,128)(2,1)S(1)}, bf16[8,4096]{1,0:T(8,128)(2,1)S(1)}, u32[]{:S(2)}, u32[]{:S(2)}) collective-permute-start(bf16[8,4096]{1,0:T(8,128)(2,1)S(1)} %collective-permute-done.4.refs_2_), channel_id=1, source_target_pairs={{0,4},{4,0},{8,12},{12,8},{16,20},{20,16},{24,28},{28,24},{1,5},{5... | collective-permute-start | bytes 196616 | tf_op jit(solution)/shard_map/ppermute | solution.py:153
  20.7 1.3 %collective-permute-start.7 = (bf16[8,4096]{1,0:T(8,128)(2,1)S(1)}, bf16[8,4096]{1,0:T(8,128)(2,1)S(1)}, u32[]{:S(2)}, u32[]{:S(2)}) collective-permute-start(bf16[8,4096]{1,0:T(8,128)(2,1)S(1)} %collective-permute-done.3.refs_1_), channel_id=1, source_target_pairs={{0,4},{4,0},{8,12},{12,8},{16,20},{20,16},{24,28},{28,24},{1,5},{5... | collective-permute-start | bytes 196616 | tf_op jit(solution)/shard_map/ppermute | solution.py:153

commit v16 on v15

--- a/solution.py
+++ b/solution.py
@@ -49,15 +49,16 @@
     for b in range(blocks):
         part = slice(b * LANES, (b + 1) * LANES)
         turned = lax.dot_general(eye, rows[part, :], ROW_BY_ROW, preferred_element_type=jnp.float32)
+        turned = turned.astype(rows.dtype)
         for digits, values, target in (
             (share_of, turned[:width], inputs),
             (row_of, turned[width:], grads),
         ):
-            digit = jnp.broadcast_to(digits[b : b + 1, :], (8, LANES))[None]
-            values = values.reshape(-1, 8, LANES)
+            digit = jnp.broadcast_to(digits[b : b + 1, :], (16, LANES))
+            values = values.reshape(-1, 16, LANES)
             for at in range(target.shape[0] // width):
-                kept = jnp.where(digit == at, values, 0.0).reshape(width, LANES)
-                target[at * width : (at + 1) * width, part] = kept.astype(target.dtype)
+                mask = jnp.where(digit == at, 1.0, 0.0).astype(values.dtype)
+                target[at * width : (at + 1) * width, part] = (values * mask[None]).reshape(width, LANES)
     product = lax.dot_general(
         grads[...], inputs[...], ROW_BY_ROW, preferred_element_type=jnp.float32
     )

time: 23.1 us -> 23.1 us (level)
  no operation moved by 1% of the time
where the time goes in v16:
time: 23.1 us; the launch traced here: 23 us
  waiting for transfers between devices  9.7 us (42%)
  starting transfers between devices  9.25 us (40%)
  Pallas kernels  3.96 us (17%)
    ppermute x8, starting transfers between devices, exchange(): lax.ppermute(block, axis, [(i, i ^ flip) for i in range(lax.axis_size(axi...  8.21 us
    ppermute x8, waiting for transfers between devices, exchange(): lax.ppermute(block, axis, [(i, i ^ flip) for i in range(lax.axis_size(axi...  7.65 us
    pallas_call x1, Pallas kernels, feature_shares(): pl.pallas_call(feature_kernel, out_shape=[jax.ShapeDtypeStruct((doc_dev,...  2.97 us
    ppermute x2, waiting for transfers between devices, body(): first, second = (lax.ppermute(features, 'ex', turn) for turn in turns)  2.05 us
    ppermute x2, starting transfers between devices, body(): first, second = (lax.ppermute(features, 'ex', turn) for turn in turns)  1.04 us
    pallas_call x1, Pallas kernels, block_scores(): pl.pallas_call(score_kernel, out_shape=jax.ShapeDtypeStruct((query_featur...  0.99 us
  transfers between devices with their start and end apart: 10, of which 8 were waited for; matrix products, arithmetic and copies ran while one was open for 0% of the time, Pallas kernels for 0%

profile of v16, /device:TPU:0, one launch (start us, length us, event | category | flops | bytes accessed | tf_op | source)
XLA Modules:
  0.0 23.0 jit_solution(13533768830169877792)
XLA Ops:
  0.0 0.0 copy-start
  0.0 3.0 %features.1 = (f32[8,4096]{1,0:T(8,128)S(1)}, bf16[8,4096]{1,0:T(8,128)(2,1)S(1)}, bf16[8,4096]{1,0:T(8,128)(2,1)S(1)}, bf16[8,4096]{1,0:T(8,128)(2,1)S(1)}) custom-call(s32[1,32]{1,0:T(1,128)} %lengths_hbm.1, s32[1,32]{1,0:T(1,128)} %owners_hbm.1, bf16[2048,128]{1,0:T(8,128)(2,1)} %rows_hbm.1), custom_call_target="tpu_custom_call" | custom-call | tf_op jit(solution)/shard_map/features/pallas_call | solution.py:87
  3.0 4.1 %collective-permute-start = (bf16[8,4096]{1,0:T(8,128)(2,1)S(1)}, bf16[8,4096]{1,0:T(8,128)(2,1)S(1)}, u32[]{:S(2)}, u32[]{:S(2)}) collective-permute-start(bf16[8,4096]{1,0:T(8,128)(2,1)S(1)} %get-tuple-element.10), channel_id=1, source_target_pairs={{0,2},{1,3},{2,0},{3,1},{4,6},{5,7},{6,4},{7,5},{8,10},{9,11},{10,... | collective-permute-start | bytes 196616 | tf_op jit(solution)/shard_map/ppermute | solution.py:154
  7.1 1.3 %collective-permute-start.1 = (bf16[8,4096]{1,0:T(8,128)(2,1)S(1)}, bf16[8,4096]{1,0:T(8,128)(2,1)S(1)}, u32[]{:S(2)}, u32[]{:S(2)}) collective-permute-start(bf16[8,4096]{1,0:T(8,128)(2,1)S(1)} %get-tuple-element.11), channel_id=1, source_target_pairs={{0,3},{1,2},{2,1},{3,0},{4,7},{5,6},{6,5},{7,4},{8,11},{9,10},{10,... | collective-permute-start | bytes 196616 | tf_op jit(solution)/shard_map/ppermute | solution.py:154
  8.4 0.2 %collective-permute-start.2 = (bf16[8,4096]{1,0:T(8,128)(2,1)S(1)}, bf16[8,4096]{1,0:T(8,128)(2,1)S(1)}, u32[]{:S(2)}, u32[]{:S(2)}) collective-permute-start(bf16[8,4096]{1,0:T(8,128)(2,1)S(1)} %get-tuple-element.12), channel_id=1, source_target_pairs={{0,1},{1,0},{2,3},{3,2},{4,5},{5,4},{6,7},{7,6},{8,9},{9,8},{10,11... | collective-permute-start | bytes 196616 | tf_op jit(solution)/shard_map/ppermute | solution.py:154
  8.7 2.2 %collective-permute-done = bf16[8,4096]{1,0:T(8,128)(2,1)S(1)} collective-permute-done((bf16[8,4096]{1,0:T(8,128)(2,1)S(1)}, bf16[8,4096]{1,0:T(8,128)(2,1)S(1)}, u32[]{:S(2)}, u32[]{:S(2)}) %collective-permute-start) | collective-permute-done | bytes 65568 | tf_op jit(solution)/shard_map/ppermute | solution.py:154
  10.8 2.5 %collective-permute-done.1 = bf16[8,4096]{1,0:T(8,128)(2,1)S(1)} collective-permute-done((bf16[8,4096]{1,0:T(8,128)(2,1)S(1)}, bf16[8,4096]{1,0:T(8,128)(2,1)S(1)}, u32[]{:S(2)}, u32[]{:S(2)}) %collective-permute-start.1) | collective-permute-done | bytes 65568 | tf_op jit(solution)/shard_map/ppermute | solution.py:154
  13.3 0.1 collective-permute-done.2
  13.4 2.5 %collective-permute-start.5 = (bf16[8,4096]{1,0:T(8,128)(2,1)S(1)}, bf16[8,4096]{1,0:T(8,128)(2,1)S(1)}, u32[]{:S(2)}, u32[]{:S(2)}) collective-permute-start(bf16[8,4096]{1,0:T(8,128)(2,1)S(1)} %add_convert_fusion.refs_0_), channel_id=1, source_target_pairs={{0,24},{4,28},{8,16},{12,20},{16,8},{20,12},{24,0},{28,4},{1,25},{... | collective-permute-start | bytes 196616 | tf_op jit(solution)/shard_map/ppermute | solution.py:154
  16.0 0.5 %collective-permute-start.4 = (bf16[8,4096]{1,0:T(8,128)(2,1)S(1)}, bf16[8,4096]{1,0:T(8,128)(2,1)S(1)}, u32[]{:S(2)}, u32[]{:S(2)}) collective-permute-start(bf16[8,4096]{1,0:T(8,128)(2,1)S(1)} %add_convert_fusion.refs_0_), channel_id=1, source_target_pairs={{0,16},{4,12},{8,24},{12,4},{16,0},{20,28},{24,8},{28,20},{1,17},{... | collective-permute-start | bytes 196616 | tf_op jit(solution)/shard_map/ppermute | solution.py:170
  16.5 0.5 %collective-permute-start.3 = (bf16[8,4096]{1,0:T(8,128)(2,1)S(1)}, bf16[8,4096]{1,0:T(8,128)(2,1)S(1)}, u32[]{:S(2)}, u32[]{:S(2)}) collective-permute-start(bf16[8,4096]{1,0:T(8,128)(2,1)S(1)} %add_convert_fusion.refs_0_), channel_id=1, source_target_pairs={{0,8},{4,20},{8,0},{12,28},{16,24},{20,4},{24,16},{28,12},{1,9},{5... | collective-permute-start | bytes 196616 | tf_op jit(solution)/shard_map/ppermute | solution.py:170
  17.0 0.0 collective-permute-start.6
  17.0 1.7 %collective-permute-done.5.refs_3_ = bf16[8,4096]{1,0:T(8,128)(2,1)S(1)} collective-permute-done((bf16[8,4096]{1,0:T(8,128)(2,1)S(1)}, bf16[8,4096]{1,0:T(8,128)(2,1)S(1)}, u32[]{:S(2)}, u32[]{:S(2)}) %collective-permute-start.5) | collective-permute-done | bytes 65568 | tf_op jit(solution)/shard_map/ppermute | solution.py:154
  18.7 0.0 collective-permute-start.9
  18.7 1.5 %collective-permute-done.4.refs_2_ = bf16[8,4096]{1,0:T(8,128)(2,1)S(1)} collective-permute-done((bf16[8,4096]{1,0:T(8,128)(2,1)S(1)}, bf16[8,4096]{1,0:T(8,128)(2,1)S(1)}, u32[]{:S(2)}, u32[]{:S(2)}) %collective-permute-start.4) | collective-permute-done | bytes 65568 | tf_op jit(solution)/shard_map/ppermute | solution.py:170
  20.2 0.0 collective-permute-start.8
  20.2 0.5 %collective-permute-done.3.refs_1_ = bf16[8,4096]{1,0:T(8,128)(2,1)S(1)} collective-permute-done((bf16[8,4096]{1,0:T(8,128)(2,1)S(1)}, bf16[8,4096]{1,0:T(8,128)(2,1)S(1)}, u32[]{:S(2)}, u32[]{:S(2)}) %collective-permute-start.3) | collective-permute-done | bytes 65568 | tf_op jit(solution)/shard_map/ppermute | solution.py:170
  20.7 0.0 collective-permute-start.7
  20.7 0.0 collective-permute-done.6.refs_4_
  20.7 0.0 collective-permute-done.9.refs_7_
  20.7 0.7 %collective-permute-done.8.refs_6_ = bf16[8,4096]{1,0:T(8,128)(2,1)S(1)} collective-permute-done((bf16[8,4096]{1,0:T(8,128)(2,1)S(1)}, bf16[8,4096]{1,0:T(8,128)(2,1)S(1)}, u32[]{:S(2)}, u32[]{:S(2)}) %collective-permute-start.8) | collective-permute-done | bytes 65568 | tf_op jit(solution)/shard_map/ppermute | solution.py:154
  21.5 0.5 %collective-permute-done.7.refs_5_ = bf16[8,4096]{1,0:T(8,128)(2,1)S(1)} collective-permute-done((bf16[8,4096]{1,0:T(8,128)(2,1)S(1)}, bf16[8,4096]{1,0:T(8,128)(2,1)S(1)}, u32[]{:S(2)}, u32[]{:S(2)}) %collective-permute-start.7) | collective-permute-done | bytes 65568 | tf_op jit(solution)/shard_map/ppermute | solution.py:154
  22.0 0.0 copy-done
  22.0 1.0 %scores.1 = f32[64,64]{1,0:T(8,128)} custom-call(bf16[64,4096]{1,0:T(8,128)(2,1)S(1)} %copy-done, bf16[8,4096]{1,0:T(8,128)(2,1)S(1)} %add_convert_fusion.refs_0_, bf16[8,4096]{1,0:T(8,128)(2,1)S(1)} %collective-permute-done.3.refs_1_, bf16[8,4096]{1,0:T(8,128)(2,1)S(1)} %collective-permute-done.4.refs_2_, ...), custom_call_target="tpu_custom_call" | custom-call | tf_op jit(solution)/shard_map/scores/pallas_call | solution.py:143
  (1 shorter events, 0.0 us)
Async XLA Ops:
  0.0 22.0 %copy-start = (bf16[64,4096]{1,0:T(8,128)(2,1)S(1)}, bf16[64,4096]{1,0:T(8,128)(2,1)}, u32[]{:S(2)}) copy-start(bf16[64,4096]{1,0:T(8,128)(2,1)} %query.1) | copy-start | bytes 1572868
  3.0 7.9 %collective-permute-start = (bf16[8,4096]{1,0:T(8,128)(2,1)S(1)}, bf16[8,4096]{1,0:T(8,128)(2,1)S(1)}, u32[]{:S(2)}, u32[]{:S(2)}) collective-permute-start(bf16[8,4096]{1,0:T(8,128)(2,1)S(1)} %get-tuple-element.10), channel_id=1, source_target_pairs={{0,2},{1,3},{2,0},{3,1},{4,6},{5,7},{6,4},{7,5},{8,10},{9,11},{10,... | collective-permute-start | bytes 196616 | tf_op jit(solution)/shard_map/ppermute | solution.py:154
  7.1 6.2 %collective-permute-start.1 = (bf16[8,4096]{1,0:T(8,128)(2,1)S(1)}, bf16[8,4096]{1,0:T(8,128)(2,1)S(1)}, u32[]{:S(2)}, u32[]{:S(2)}) collective-permute-start(bf16[8,4096]{1,0:T(8,128)(2,1)S(1)} %get-tuple-element.11), channel_id=1, source_target_pairs={{0,3},{1,2},{2,1},{3,0},{4,7},{5,6},{6,5},{7,4},{8,11},{9,10},{10,... | collective-permute-start | bytes 196616 | tf_op jit(solution)/shard_map/ppermute | solution.py:154
  8.4 5.0 %collective-permute-start.2 = (bf16[8,4096]{1,0:T(8,128)(2,1)S(1)}, bf16[8,4096]{1,0:T(8,128)(2,1)S(1)}, u32[]{:S(2)}, u32[]{:S(2)}) collective-permute-start(bf16[8,4096]{1,0:T(8,128)(2,1)S(1)} %get-tuple-element.12), channel_id=1, source_target_pairs={{0,1},{1,0},{2,3},{3,2},{4,5},{5,4},{6,7},{7,6},{8,9},{9,8},{10,11... | collective-permute-start | bytes 196616 | tf_op jit(solution)/shard_map/ppermute | solution.py:154
  13.4 5.2 %collective-permute-start.5 = (bf16[8,4096]{1,0:T(8,128)(2,1)S(1)}, bf16[8,4096]{1,0:T(8,128)(2,1)S(1)}, u32[]{:S(2)}, u32[]{:S(2)}) collective-permute-start(bf16[8,4096]{1,0:T(8,128)(2,1)S(1)} %add_convert_fusion.refs_0_), channel_id=1, source_target_pairs={{0,24},{4,28},{8,16},{12,20},{16,8},{20,12},{24,0},{28,4},{1,25},{... | collective-permute-start | bytes 196616 | tf_op jit(solution)/shard_map/ppermute | solution.py:154
  16.0 4.3 %collective-permute-start.4 = (bf16[8,4096]{1,0:T(8,128)(2,1)S(1)}, bf16[8,4096]{1,0:T(8,128)(2,1)S(1)}, u32[]{:S(2)}, u32[]{:S(2)}) collective-permute-start(bf16[8,4096]{1,0:T(8,128)(2,1)S(1)} %add_convert_fusion.refs_0_), channel_id=1, source_target_pairs={{0,16},{4,12},{8,24},{12,4},{16,0},{20,28},{24,8},{28,20},{1,17},{... | collective-permute-start | bytes 196616 | tf_op jit(solution)/shard_map/ppermute | solution.py:170
  16.5 4.3 %collective-permute-start.3 = (bf16[8,4096]{1,0:T(8,128)(2,1)S(1)}, bf16[8,4096]{1,0:T(8,128)(2,1)S(1)}, u32[]{:S(2)}, u32[]{:S(2)}) collective-permute-start(bf16[8,4096]{1,0:T(8,128)(2,1)S(1)} %add_convert_fusion.refs_0_), channel_id=1, source_target_pairs={{0,8},{4,20},{8,0},{12,28},{16,24},{20,4},{24,16},{28,12},{1,9},{5... | collective-permute-start | bytes 196616 | tf_op jit(solution)/shard_map/ppermute | solution.py:170
  17.0 3.7 %collective-permute-start.6 = (bf16[8,4096]{1,0:T(8,128)(2,1)S(1)}, bf16[8,4096]{1,0:T(8,128)(2,1)S(1)}, u32[]{:S(2)}, u32[]{:S(2)}) collective-permute-start(bf16[8,4096]{1,0:T(8,128)(2,1)S(1)} %add_convert_fusion.refs_0_), channel_id=1, source_target_pairs={{0,4},{4,0},{8,12},{12,8},{16,20},{20,16},{24,28},{28,24},{1,5},{5... | collective-permute-start | bytes 196616 | tf_op jit(solution)/shard_map/ppermute | solution.py:154
  18.7 2.1 %collective-permute-start.9 = (bf16[8,4096]{1,0:T(8,128)(2,1)S(1)}, bf16[8,4096]{1,0:T(8,128)(2,1)S(1)}, u32[]{:S(2)}, u32[]{:S(2)}) collective-permute-start(bf16[8,4096]{1,0:T(8,128)(2,1)S(1)} %collective-permute-done.5.refs_3_), channel_id=1, source_target_pairs={{0,4},{4,0},{8,12},{12,8},{16,20},{20,16},{24,28},{28,24},{1,5},{5... | collective-permute-start | bytes 196616 | tf_op jit(solution)/shard_map/ppermute | solution.py:154
  20.2 1.3 %collective-permute-start.8 = (bf16[8,4096]{1,0:T(8,128)(2,1)S(1)}, bf16[8,4096]{1,0:T(8,128)(2,1)S(1)}, u32[]{:S(2)}, u32[]{:S(2)}) collective-permute-start(bf16[8,4096]{1,0:T(8,128)(2,1)S(1)} %collective-permute-done.4.refs_2_), channel_id=1, source_target_pairs={{0,4},{4,0},{8,12},{12,8},{16,20},{20,16},{24,28},{28,24},{1,5},{5... | collective-permute-start | bytes 196616 | tf_op jit(solution)/shard_map/ppermute | solution.py:154
  20.7 1.3 %collective-permute-start.7 = (bf16[8,4096]{1,0:T(8,128)(2,1)S(1)}, bf16[8,4096]{1,0:T(8,128)(2,1)S(1)}, u32[]{:S(2)}, u32[]{:S(2)}) collective-permute-start(bf16[8,4096]{1,0:T(8,128)(2,1)S(1)} %collective-permute-done.3.refs_1_), channel_id=1, source_target_pairs={{0,4},{4,0},{8,12},{12,8},{16,20},{20,16},{24,28},{28,24},{1,5},{5... | collective-permute-start | bytes 196616 | tf_op jit(solution)/shard_map/ppermute | solution.py:154

commit v17 on v15

--- a/solution.py
+++ b/solution.py
@@ -31,7 +31,7 @@
     token = tok * count + token + lax.broadcasted_iota(jnp.int32, (blocks, LANES), 1)
     slot_of = jnp.zeros((blocks, LANES), jnp.int32)
     size_row = lax.broadcasted_iota(jnp.int32, (doc_dev, LANES), 0)
-    size_slots = [((tok ^ s) << shift) + size_row for s in range(tok_count)]
+    size_slots = [(lax.rem(tok + s, tok_count) << shift) + size_row for s in range(tok_count)]
     sizes = [jnp.ones((doc_dev, LANES), jnp.int32) for _ in shares]
     start = jnp.int32(0)
     for k in range(docs):
@@ -39,7 +39,8 @@
         slot_of = jnp.where(token >= start, slot, slot_of)
         sizes = [jnp.where(at == slot, length, size) for at, size in zip(size_slots, sizes)]
         start = start + length
-    share_of, row_of = (slot_of >> shift) ^ tok, slot_of & (doc_dev - 1)
+    share_of = (slot_of >> shift) - tok
+    share_of, row_of = jnp.where(share_of < 0, share_of + tok_count, share_of), slot_of & (doc_dev - 1)
 
     eye = (
         lax.broadcasted_iota(jnp.int32, (2 * width, 2 * width), 0)
@@ -157,8 +158,9 @@
     tok_count = lax.axis_size("tok")
     shares = feature_shares(proj_rows, doc_lengths, owner_map, tok_count)
     total = shares[0]
-    for shift in sorted(range(1, tok_count), key=lambda flip: (flip < 2, flip)):
-        total = total + exchange(shares[shift], "tok", shift).astype(jnp.float32)
+    for shift in sorted(range(1, tok_count), key=lambda shift: (2 * shift != tok_count, shift)):
+        pairs = [(i, (i + shift) % tok_count) for i in range(tok_count)]
+        total = total + lax.ppermute(shares[shift], "tok", pairs).astype(jnp.float32)
     features = total.astype(jnp.bfloat16)
     ex_count = lax.axis_size("ex")
     if ex_count != 8:

time: 23.1 us -> 23.3 us (level)
  starting transfers between devices: 9.25 us -> 11.5 us
  waiting for transfers between devices: 9.7 us -> 7.68 us
    ppermute x0 -> x3, starting transfers between devices: none -> 7.93 us  [body(): lax.ppermute(shares[shift], 'tok', pairs).astype(jnp.float32)]
    ppermute x8 -> x5, starting transfers between devices: 8.21 us -> 2.52 us  [exchange(): lax.ppermute(block, axis, [(i, i ^ flip) for i in range(lax.axis_size(axi...]
    ppermute x8 -> x5, waiting for transfers between devices: 7.66 us -> 2.92 us  [exchange(): lax.ppermute(block, axis, [(i, i ^ flip) for i in range(lax.axis_size(axi...]
    ppermute x0 -> x3, waiting for transfers between devices: none -> 2.72 us  [body(): lax.ppermute(shares[shift], 'tok', pairs).astype(jnp.float32)]
  transfers between devices with their start and end apart: 10 -> 10, of which waited for: 8 -> 7; matrix products, arithmetic and copies ran while one was open for 0% -> 0% of each run, Pallas kernels for 0% -> 0%
where the time goes in v17:
time: 23.3 us; the launch traced here: 23.1 us
  starting transfers between devices  11.5 us (49%)
  waiting for transfers between devices  7.68 us (33%)
  Pallas kernels  3.89 us (17%)
    ppermute x3, starting transfers between devices, body(): lax.ppermute(shares[shift], 'tok', pairs).astype(jnp.float32)  7.93 us
    ppermute x5, waiting for transfers between devices, exchange(): lax.ppermute(block, axis, [(i, i ^ flip) for i in range(lax.axis_size(axi...  2.92 us
    pallas_call x1, Pallas kernels, feature_shares(): pl.pallas_call(feature_kernel, out_shape=[jax.ShapeDtypeStruct((doc_dev,...  2.9 us
    ppermute x3, waiting for transfers between devices, body(): lax.ppermute(shares[shift], 'tok', pairs).astype(jnp.float32)  2.72 us
    ppermute x5, starting transfers between devices, exchange(): lax.ppermute(block, axis, [(i, i ^ flip) for i in range(lax.axis_size(axi...  2.52 us
    ppermute x2, waiting for transfers between devices, body(): first, second = (lax.ppermute(features, 'ex', turn) for turn in turns)  2.05 us
    ppermute x2, starting transfers between devices, body(): first, second = (lax.ppermute(features, 'ex', turn) for turn in turns)  1.04 us
    pallas_call x1, Pallas kernels, block_scores(): pl.pallas_call(score_kernel, out_shape=jax.ShapeDtypeStruct((query_featur...  0.99 us
  transfers between devices with their start and end apart: 10, of which 7 were waited for; matrix products, arithmetic and copies ran while one was open for 0% of the time, Pallas kernels for 0%

profile of v17, /device:TPU:0, one launch (start us, length us, event | category | flops | bytes accessed | tf_op | source)
XLA Modules:
  0.0 23.1 jit_solution(9732217214707469280)
XLA Ops:
  0.0 0.0 copy-start
  0.0 2.9 %features.1 = (f32[8,4096]{1,0:T(8,128)S(1)}, bf16[8,4096]{1,0:T(8,128)(2,1)S(1)}, bf16[8,4096]{1,0:T(8,128)(2,1)S(1)}, bf16[8,4096]{1,0:T(8,128)(2,1)S(1)}) custom-call(s32[1,32]{1,0:T(1,128)} %lengths_hbm.1, s32[1,32]{1,0:T(1,128)} %owners_hbm.1, bf16[2048,128]{1,0:T(8,128)(2,1)} %rows_hbm.1), custom_call_target="tpu_custom_call" | custom-call | tf_op jit(solution)/shard_map/features/pallas_call | solution.py:87
  2.9 4.1 %collective-permute-start = (bf16[8,4096]{1,0:T(8,128)(2,1)S(1)}, bf16[8,4096]{1,0:T(8,128)(2,1)S(1)}, u32[]{:S(2)}, u32[]{:S(2)}) collective-permute-start(bf16[8,4096]{1,0:T(8,128)(2,1)S(1)} %get-tuple-element.10), channel_id=1, source_target_pairs={{0,2},{1,3},{2,0},{3,1},{4,6},{5,7},{6,4},{7,5},{8,10},{9,11},{10,... | collective-permute-start | bytes 196616 | tf_op jit(solution)/shard_map/ppermute | solution.py:163
  7.0 1.6 %collective-permute-start.1 = (bf16[8,4096]{1,0:T(8,128)(2,1)S(1)}, bf16[8,4096]{1,0:T(8,128)(2,1)S(1)}, u32[]{:S(2)}, u32[]{:S(2)}) collective-permute-start(bf16[8,4096]{1,0:T(8,128)(2,1)S(1)} %get-tuple-element.11), channel_id=1, source_target_pairs={{0,1},{1,2},{2,3},{3,0},{4,5},{5,6},{6,7},{7,4},{8,9},{9,10},{10,1... | collective-permute-start | bytes 196616 | tf_op jit(solution)/shard_map/ppermute | solution.py:163
  8.6 2.3 %collective-permute-start.2 = (bf16[8,4096]{1,0:T(8,128)(2,1)S(1)}, bf16[8,4096]{1,0:T(8,128)(2,1)S(1)}, u32[]{:S(2)}, u32[]{:S(2)}) collective-permute-start(bf16[8,4096]{1,0:T(8,128)(2,1)S(1)} %get-tuple-element.12), channel_id=1, source_target_pairs={{0,3},{1,0},{2,1},{3,2},{4,7},{5,4},{6,5},{7,6},{8,11},{9,8},{10,9... | collective-permute-start | bytes 196616 | tf_op jit(solution)/shard_map/ppermute | solution.py:163
  10.8 0.0 collective-permute-done
  10.8 2.4 %collective-permute-done.1 = bf16[8,4096]{1,0:T(8,128)(2,1)S(1)} collective-permute-done((bf16[8,4096]{1,0:T(8,128)(2,1)S(1)}, bf16[8,4096]{1,0:T(8,128)(2,1)S(1)}, u32[]{:S(2)}, u32[]{:S(2)}) %collective-permute-start.1) | collective-permute-done | bytes 65568 | tf_op jit(solution)/shard_map/ppermute | solution.py:163
  13.2 0.3 %collective-permute-done.2 = bf16[8,4096]{1,0:T(8,128)(2,1)S(1)} collective-permute-done((bf16[8,4096]{1,0:T(8,128)(2,1)S(1)}, bf16[8,4096]{1,0:T(8,128)(2,1)S(1)}, u32[]{:S(2)}, u32[]{:S(2)}) %collective-permute-start.2) | collective-permute-done | bytes 65568 | tf_op jit(solution)/shard_map/ppermute | solution.py:163
  13.6 2.5 %collective-permute-start.5 = (bf16[8,4096]{1,0:T(8,128)(2,1)S(1)}, bf16[8,4096]{1,0:T(8,128)(2,1)S(1)}, u32[]{:S(2)}, u32[]{:S(2)}) collective-permute-start(bf16[8,4096]{1,0:T(8,128)(2,1)S(1)} %add_convert_fusion.refs_0_), channel_id=1, source_target_pairs={{0,24},{4,28},{8,16},{12,20},{16,8},{20,12},{24,0},{28,4},{1,25},{... | collective-permute-start | bytes 196616 | tf_op jit(solution)/shard_map/ppermute | solution.py:154
  16.1 0.5 %collective-permute-start.4 = (bf16[8,4096]{1,0:T(8,128)(2,1)S(1)}, bf16[8,4096]{1,0:T(8,128)(2,1)S(1)}, u32[]{:S(2)}, u32[]{:S(2)}) collective-permute-start(bf16[8,4096]{1,0:T(8,128)(2,1)S(1)} %add_convert_fusion.refs_0_), channel_id=1, source_target_pairs={{0,16},{4,12},{8,24},{12,4},{16,0},{20,28},{24,8},{28,20},{1,17},{... | collective-permute-start | bytes 196616 | tf_op jit(solution)/shard_map/ppermute | solution.py:171
  16.6 0.5 %collective-permute-start.3 = (bf16[8,4096]{1,0:T(8,128)(2,1)S(1)}, bf16[8,4096]{1,0:T(8,128)(2,1)S(1)}, u32[]{:S(2)}, u32[]{:S(2)}) collective-permute-start(bf16[8,4096]{1,0:T(8,128)(2,1)S(1)} %add_convert_fusion.refs_0_), channel_id=1, source_target_pairs={{0,8},{4,20},{8,0},{12,28},{16,24},{20,4},{24,16},{28,12},{1,9},{5... | collective-permute-start | bytes 196616 | tf_op jit(solution)/shard_map/ppermute | solution.py:171
  17.2 0.0 collective-permute-start.6
  17.2 1.7 %collective-permute-done.5.refs_3_ = bf16[8,4096]{1,0:T(8,128)(2,1)S(1)} collective-permute-done((bf16[8,4096]{1,0:T(8,128)(2,1)S(1)}, bf16[8,4096]{1,0:T(8,128)(2,1)S(1)}, u32[]{:S(2)}, u32[]{:S(2)}) %collective-permute-start.5) | collective-permute-done | bytes 65568 | tf_op jit(solution)/shard_map/ppermute | solution.py:154
  18.8 0.0 collective-permute-start.9
  18.8 1.5 %collective-permute-done.4.refs_2_ = bf16[8,4096]{1,0:T(8,128)(2,1)S(1)} collective-permute-done((bf16[8,4096]{1,0:T(8,128)(2,1)S(1)}, bf16[8,4096]{1,0:T(8,128)(2,1)S(1)}, u32[]{:S(2)}, u32[]{:S(2)}) %collective-permute-start.4) | collective-permute-done | bytes 65568 | tf_op jit(solution)/shard_map/ppermute | solution.py:171
  20.4 0.0 collective-permute-start.8
  20.4 0.5 %collective-permute-done.3.refs_1_ = bf16[8,4096]{1,0:T(8,128)(2,1)S(1)} collective-permute-done((bf16[8,4096]{1,0:T(8,128)(2,1)S(1)}, bf16[8,4096]{1,0:T(8,128)(2,1)S(1)}, u32[]{:S(2)}, u32[]{:S(2)}) %collective-permute-start.3) | collective-permute-done | bytes 65568 | tf_op jit(solution)/shard_map/ppermute | solution.py:171
  20.9 0.0 collective-permute-start.7
  20.9 0.0 collective-permute-done.6.refs_4_
  20.9 0.0 collective-permute-done.9.refs_7_
  20.9 0.7 %collective-permute-done.8.refs_6_ = bf16[8,4096]{1,0:T(8,128)(2,1)S(1)} collective-permute-done((bf16[8,4096]{1,0:T(8,128)(2,1)S(1)}, bf16[8,4096]{1,0:T(8,128)(2,1)S(1)}, u32[]{:S(2)}, u32[]{:S(2)}) %collective-permute-start.8) | collective-permute-done | bytes 65568 | tf_op jit(solution)/shard_map/ppermute | solution.py:154
  21.6 0.5 %collective-permute-done.7.refs_5_ = bf16[8,4096]{1,0:T(8,128)(2,1)S(1)} collective-permute-done((bf16[8,4096]{1,0:T(8,128)(2,1)S(1)}, bf16[8,4096]{1,0:T(8,128)(2,1)S(1)}, u32[]{:S(2)}, u32[]{:S(2)}) %collective-permute-start.7) | collective-permute-done | bytes 65568 | tf_op jit(solution)/shard_map/ppermute | solution.py:154
  22.1 0.0 copy-done
  22.1 1.0 %scores.1 = f32[64,64]{1,0:T(8,128)} custom-call(bf16[64,4096]{1,0:T(8,128)(2,1)S(1)} %copy-done, bf16[8,4096]{1,0:T(8,128)(2,1)S(1)} %add_convert_fusion.refs_0_, bf16[8,4096]{1,0:T(8,128)(2,1)S(1)} %collective-permute-done.3.refs_1_, bf16[8,4096]{1,0:T(8,128)(2,1)S(1)} %collective-permute-done.4.refs_2_, ...), custom_call_target="tpu_custom_call" | custom-call | tf_op jit(solution)/shard_map/scores/pallas_call | solution.py:143
  (1 shorter events, 0.0 us)
Async XLA Ops:
  0.0 22.1 %copy-start = (bf16[64,4096]{1,0:T(8,128)(2,1)S(1)}, bf16[64,4096]{1,0:T(8,128)(2,1)}, u32[]{:S(2)}) copy-start(bf16[64,4096]{1,0:T(8,128)(2,1)} %query.1) | copy-start | bytes 1572868
  2.9 7.9 %collective-permute-start = (bf16[8,4096]{1,0:T(8,128)(2,1)S(1)}, bf16[8,4096]{1,0:T(8,128)(2,1)S(1)}, u32[]{:S(2)}, u32[]{:S(2)}) collective-permute-start(bf16[8,4096]{1,0:T(8,128)(2,1)S(1)} %get-tuple-element.10), channel_id=1, source_target_pairs={{0,2},{1,3},{2,0},{3,1},{4,6},{5,7},{6,4},{7,5},{8,10},{9,11},{10,... | collective-permute-start | bytes 196616 | tf_op jit(solution)/shard_map/ppermute | solution.py:163
  7.0 6.2 %collective-permute-start.1 = (bf16[8,4096]{1,0:T(8,128)(2,1)S(1)}, bf16[8,4096]{1,0:T(8,128)(2,1)S(1)}, u32[]{:S(2)}, u32[]{:S(2)}) collective-permute-start(bf16[8,4096]{1,0:T(8,128)(2,1)S(1)} %get-tuple-element.11), channel_id=1, source_target_pairs={{0,1},{1,2},{2,3},{3,0},{4,5},{5,6},{6,7},{7,4},{8,9},{9,10},{10,1... | collective-permute-start | bytes 196616 | tf_op jit(solution)/shard_map/ppermute | solution.py:163
  8.6 5.0 %collective-permute-start.2 = (bf16[8,4096]{1,0:T(8,128)(2,1)S(1)}, bf16[8,4096]{1,0:T(8,128)(2,1)S(1)}, u32[]{:S(2)}, u32[]{:S(2)}) collective-permute-start(bf16[8,4096]{1,0:T(8,128)(2,1)S(1)} %get-tuple-element.12), channel_id=1, source_target_pairs={{0,3},{1,0},{2,1},{3,2},{4,7},{5,4},{6,5},{7,6},{8,11},{9,8},{10,9... | collective-permute-start | bytes 196616 | tf_op jit(solution)/shard_map/ppermute | solution.py:163
  13.6 5.2 %collective-permute-start.5 = (bf16[8,4096]{1,0:T(8,128)(2,1)S(1)}, bf16[8,4096]{1,0:T(8,128)(2,1)S(1)}, u32[]{:S(2)}, u32[]{:S(2)}) collective-permute-start(bf16[8,4096]{1,0:T(8,128)(2,1)S(1)} %add_convert_fusion.refs_0_), channel_id=1, source_target_pairs={{0,24},{4,28},{8,16},{12,20},{16,8},{20,12},{24,0},{28,4},{1,25},{... | collective-permute-start | bytes 196616 | tf_op jit(solution)/shard_map/ppermute | solution.py:154
  16.1 4.3 %collective-permute-start.4 = (bf16[8,4096]{1,0:T(8,128)(2,1)S(1)}, bf16[8,4096]{1,0:T(8,128)(2,1)S(1)}, u32[]{:S(2)}, u32[]{:S(2)}) collective-permute-start(bf16[8,4096]{1,0:T(8,128)(2,1)S(1)} %add_convert_fusion.refs_0_), channel_id=1, source_target_pairs={{0,16},{4,12},{8,24},{12,4},{16,0},{20,28},{24,8},{28,20},{1,17},{... | collective-permute-start | bytes 196616 | tf_op jit(solution)/shard_map/ppermute | solution.py:171
  16.6 4.3 %collective-permute-start.3 = (bf16[8,4096]{1,0:T(8,128)(2,1)S(1)}, bf16[8,4096]{1,0:T(8,128)(2,1)S(1)}, u32[]{:S(2)}, u32[]{:S(2)}) collective-permute-start(bf16[8,4096]{1,0:T(8,128)(2,1)S(1)} %add_convert_fusion.refs_0_), channel_id=1, source_target_pairs={{0,8},{4,20},{8,0},{12,28},{16,24},{20,4},{24,16},{28,12},{1,9},{5... | collective-permute-start | bytes 196616 | tf_op jit(solution)/shard_map/ppermute | solution.py:171
  17.2 3.7 %collective-permute-start.6 = (bf16[8,4096]{1,0:T(8,128)(2,1)S(1)}, bf16[8,4096]{1,0:T(8,128)(2,1)S(1)}, u32[]{:S(2)}, u32[]{:S(2)}) collective-permute-start(bf16[8,4096]{1,0:T(8,128)(2,1)S(1)} %add_convert_fusion.refs_0_), channel_id=1, source_target_pairs={{0,4},{4,0},{8,12},{12,8},{16,20},{20,16},{24,28},{28,24},{1,5},{5... | collective-permute-start | bytes 196616 | tf_op jit(solution)/shard_map/ppermute | solution.py:154
  18.8 2.1 %collective-permute-start.9 = (bf16[8,4096]{1,0:T(8,128)(2,1)S(1)}, bf16[8,4096]{1,0:T(8,128)(2,1)S(1)}, u32[]{:S(2)}, u32[]{:S(2)}) collective-permute-start(bf16[8,4096]{1,0:T(8,128)(2,1)S(1)} %collective-permute-done.5.refs_3_), channel_id=1, source_target_pairs={{0,4},{4,0},{8,12},{12,8},{16,20},{20,16},{24,28},{28,24},{1,5},{5... | collective-permute-start | bytes 196616 | tf_op jit(solution)/shard_map/ppermute | solution.py:154
  20.4 1.3 %collective-permute-start.8 = (bf16[8,4096]{1,0:T(8,128)(2,1)S(1)}, bf16[8,4096]{1,0:T(8,128)(2,1)S(1)}, u32[]{:S(2)}, u32[]{:S(2)}) collective-permute-start(bf16[8,4096]{1,0:T(8,128)(2,1)S(1)} %collective-permute-done.4.refs_2_), channel_id=1, source_target_pairs={{0,4},{4,0},{8,12},{12,8},{16,20},{20,16},{24,28},{28,24},{1,5},{5... | collective-permute-start | bytes 196616 | tf_op jit(solution)/shard_map/ppermute | solution.py:154
  20.9 1.3 %collective-permute-start.7 = (bf16[8,4096]{1,0:T(8,128)(2,1)S(1)}, bf16[8,4096]{1,0:T(8,128)(2,1)S(1)}, u32[]{:S(2)}, u32[]{:S(2)}) collective-permute-start(bf16[8,4096]{1,0:T(8,128)(2,1)S(1)} %collective-permute-done.3.refs_1_), channel_id=1, source_target_pairs={{0,4},{4,0},{8,12},{12,8},{16,20},{20,16},{24,28},{28,24},{1,5},{5... | collective-permute-start | bytes 196616 | tf_op jit(solution)/shard_map/ppermute | solution.py:154

commit v18 on v15

--- a/solution.py
+++ b/solution.py
@@ -31,7 +31,10 @@
     token = tok * count + token + lax.broadcasted_iota(jnp.int32, (blocks, LANES), 1)
     slot_of = jnp.zeros((blocks, LANES), jnp.int32)
     size_row = lax.broadcasted_iota(jnp.int32, (doc_dev, LANES), 0)
-    size_slots = [((tok ^ s) << shift) + size_row for s in range(tok_count)]
+    odd = lax.rem(lax.axis_index("ex"), 2) == 1
+    turn = tok_count - 1
+    flips = [0] + [jnp.where(odd, s, s % turn + 1) for s in range(1, tok_count)]
+    size_slots = [((tok ^ flip) << shift) + size_row for flip in flips]
     sizes = [jnp.ones((doc_dev, LANES), jnp.int32) for _ in shares]
     start = jnp.int32(0)
     for k in range(docs):
@@ -39,7 +42,10 @@
         slot_of = jnp.where(token >= start, slot, slot_of)
         sizes = [jnp.where(at == slot, length, size) for at, size in zip(size_slots, sizes)]
         start = start + length
-    share_of, row_of = (slot_of >> shift) ^ tok, slot_of & (doc_dev - 1)
+    flip_of, row_of = (slot_of >> shift) ^ tok, slot_of & (doc_dev - 1)
+    share_of = jnp.zeros_like(flip_of)
+    for s in range(1, tok_count):
+        share_of = jnp.where(flip_of == flips[s], s, share_of)
 
     eye = (
         lax.broadcasted_iota(jnp.int32, (2 * width, 2 * width), 0)
@@ -157,8 +163,13 @@
     tok_count = lax.axis_size("tok")
     shares = feature_shares(proj_rows, doc_lengths, owner_map, tok_count)
     total = shares[0]
-    for shift in sorted(range(1, tok_count), key=lambda flip: (flip < 2, flip)):
-        total = total + exchange(shares[shift], "tok", shift).astype(jnp.float32)
+    groups = range(lax.axis_size("ex"))
+    for s in range(1, tok_count):
+        flips = [s % (tok_count - 1) + 1, s]
+        pairs = [
+            (e * tok_count + i, e * tok_count + (i ^ flips[e % 2])) for e in groups for i in range(tok_count)
+        ]
+        total = total + lax.ppermute(shares[s], ("ex", "tok"), pairs).astype(jnp.float32)
     features = total.astype(jnp.bfloat16)
     ex_count = lax.axis_size("ex")
     if ex_count != 8:

time: 23.1 us -> 23.8 us (1.030)
  waiting for transfers between devices: 9.7 us -> 10.4 us
    ppermute x0 -> x3, starting transfers between devices: none -> 5.68 us  [body(): lax.ppermute(shares[s], ('ex', 'tok'), pairs).astype(jnp.float32)]
    ppermute x8 -> x5, starting transfers between devices: 8.21 us -> 2.53 us  [exchange(): lax.ppermute(block, axis, [(i, i ^ flip) for i in range(lax.axis_size(axi...]
    ppermute x0 -> x3, waiting for transfers between devices: none -> 5.44 us  [body(): lax.ppermute(shares[s], ('ex', 'tok'), pairs).astype(jnp.float32)]
    ppermute x8 -> x5, waiting for transfers between devices: 7.66 us -> 3.64 us  [exchange(): lax.ppermute(block, axis, [(i, i ^ flip) for i in range(lax.axis_size(axi...]
    ppermute x2, waiting for transfers between devices: 2.05 us -> 1.32 us  [body(): first, second = (lax.ppermute(features, 'ex', turn) for turn in turns)]
where the time goes in v18:
time: 23.8 us; the launch traced here: 23.6 us
  waiting for transfers between devices  10.4 us (44%)
  starting transfers between devices  9.25 us (39%)
  Pallas kernels  3.89 us (16%)
    ppermute x3, starting transfers between devices, body(): lax.ppermute(shares[s], ('ex', 'tok'), pairs).astype(jnp.float32)  5.68 us
    ppermute x3, waiting for transfers between devices, body(): lax.ppermute(shares[s], ('ex', 'tok'), pairs).astype(jnp.float32)  5.44 us
    ppermute x5, waiting for transfers between devices, exchange(): lax.ppermute(block, axis, [(i, i ^ flip) for i in range(lax.axis_size(axi...  3.64 us
    pallas_call x1, Pallas kernels, feature_shares(): pl.pallas_call(feature_kernel, out_shape=[jax.ShapeDtypeStruct((doc_dev,...  2.9 us
    ppermute x5, starting transfers between devices, exchange(): lax.ppermute(block, axis, [(i, i ^ flip) for i in range(lax.axis_size(axi...  2.53 us
    ppermute x2, waiting for transfers between devices, body(): first, second = (lax.ppermute(features, 'ex', turn) for turn in turns)  1.32 us
    ppermute x2, starting transfers between devices, body(): first, second = (lax.ppermute(features, 'ex', turn) for turn in turns)  1.04 us
    pallas_call x1, Pallas kernels, block_scores(): pl.pallas_call(score_kernel, out_shape=jax.ShapeDtypeStruct((query_featur...  0.99 us
  transfers between devices with their start and end apart: 10, of which 8 were waited for; matrix products, arithmetic and copies ran while one was open for 0% of the time, Pallas kernels for 0%

profile of v18, /device:TPU:0, one launch (start us, length us, event | category | flops | bytes accessed | tf_op | source)
XLA Modules:
  0.0 23.6 jit_solution(14253040794896462514)
XLA Ops:
  0.0 0.0 copy-start
  0.0 2.9 %features.1 = (f32[8,4096]{1,0:T(8,128)S(1)}, bf16[8,4096]{1,0:T(8,128)(2,1)S(1)}, bf16[8,4096]{1,0:T(8,128)(2,1)S(1)}, bf16[8,4096]{1,0:T(8,128)(2,1)S(1)}) custom-call(s32[1,32]{1,0:T(1,128)} %lengths_hbm.1, s32[1,32]{1,0:T(1,128)} %owners_hbm.1, bf16[2048,128]{1,0:T(8,128)(2,1)} %rows_hbm.1), custom_call_target="tpu_custom_call" | custom-call | tf_op jit(solution)/shard_map/features/pallas_call | solution.py:92
  2.9 4.1 %collective-permute-start = (bf16[8,4096]{1,0:T(8,128)(2,1)S(1)}, bf16[8,4096]{1,0:T(8,128)(2,1)S(1)}, u32[]{:S(2)}, u32[]{:S(2)}) collective-permute-start(bf16[8,4096]{1,0:T(8,128)(2,1)S(1)} %get-tuple-element.10), channel_id=1, source_target_pairs={{0,2},{1,3},{2,0},{3,1},{4,5},{5,4},{6,7},{7,6},{8,10},{9,11},{10,... | collective-permute-start | bytes 196616 | tf_op jit(solution)/shard_map/ppermute | solution.py:172
  7.0 1.3 %collective-permute-start.1 = (bf16[8,4096]{1,0:T(8,128)(2,1)S(1)}, bf16[8,4096]{1,0:T(8,128)(2,1)S(1)}, u32[]{:S(2)}, u32[]{:S(2)}) collective-permute-start(bf16[8,4096]{1,0:T(8,128)(2,1)S(1)} %get-tuple-element.11), channel_id=1, source_target_pairs={{0,3},{1,2},{2,1},{3,0},{4,6},{5,7},{6,4},{7,5},{8,11},{9,10},{10,... | collective-permute-start | bytes 196616 | tf_op jit(solution)/shard_map/ppermute | solution.py:172
  8.4 0.2 collective-permute-start.2
  8.6 0.9 %collective-permute-done = bf16[8,4096]{1,0:T(8,128)(2,1)S(1)} collective-permute-done((bf16[8,4096]{1,0:T(8,128)(2,1)S(1)}, bf16[8,4096]{1,0:T(8,128)(2,1)S(1)}, u32[]{:S(2)}, u32[]{:S(2)}) %collective-permute-start) | collective-permute-done | bytes 65568 | tf_op jit(solution)/shard_map/ppermute | solution.py:172
  9.5 4.3 %collective-permute-done.1 = bf16[8,4096]{1,0:T(8,128)(2,1)S(1)} collective-permute-done((bf16[8,4096]{1,0:T(8,128)(2,1)S(1)}, bf16[8,4096]{1,0:T(8,128)(2,1)S(1)}, u32[]{:S(2)}, u32[]{:S(2)}) %collective-permute-start.1) | collective-permute-done | bytes 65568 | tf_op jit(solution)/shard_map/ppermute | solution.py:172
  13.8 0.2 collective-permute-done.2
  14.1 2.5 %collective-permute-start.5 = (bf16[8,4096]{1,0:T(8,128)(2,1)S(1)}, bf16[8,4096]{1,0:T(8,128)(2,1)S(1)}, u32[]{:S(2)}, u32[]{:S(2)}) collective-permute-start(bf16[8,4096]{1,0:T(8,128)(2,1)S(1)} %add_convert_fusion.refs_0_), channel_id=1, source_target_pairs={{0,24},{4,28},{8,16},{12,20},{16,8},{20,12},{24,0},{28,4},{1,25},{... | collective-permute-start | bytes 196616 | tf_op jit(solution)/shard_map/ppermute | solution.py:159
  16.6 0.5 %collective-permute-start.4 = (bf16[8,4096]{1,0:T(8,128)(2,1)S(1)}, bf16[8,4096]{1,0:T(8,128)(2,1)S(1)}, u32[]{:S(2)}, u32[]{:S(2)}) collective-permute-start(bf16[8,4096]{1,0:T(8,128)(2,1)S(1)} %add_convert_fusion.refs_0_), channel_id=1, source_target_pairs={{0,16},{4,12},{8,24},{12,4},{16,0},{20,28},{24,8},{28,20},{1,17},{... | collective-permute-start | bytes 196616 | tf_op jit(solution)/shard_map/ppermute | solution.py:180
  17.1 0.5 %collective-permute-start.3 = (bf16[8,4096]{1,0:T(8,128)(2,1)S(1)}, bf16[8,4096]{1,0:T(8,128)(2,1)S(1)}, u32[]{:S(2)}, u32[]{:S(2)}) collective-permute-start(bf16[8,4096]{1,0:T(8,128)(2,1)S(1)} %add_convert_fusion.refs_0_), channel_id=1, source_target_pairs={{0,8},{4,20},{8,0},{12,28},{16,24},{20,4},{24,16},{28,12},{1,9},{5... | collective-permute-start | bytes 196616 | tf_op jit(solution)/shard_map/ppermute | solution.py:180
  17.6 0.0 collective-permute-start.6
  17.6 2.4 %collective-permute-done.5.refs_3_ = bf16[8,4096]{1,0:T(8,128)(2,1)S(1)} collective-permute-done((bf16[8,4096]{1,0:T(8,128)(2,1)S(1)}, bf16[8,4096]{1,0:T(8,128)(2,1)S(1)}, u32[]{:S(2)}, u32[]{:S(2)}) %collective-permute-start.5) | collective-permute-done | bytes 65568 | tf_op jit(solution)/shard_map/ppermute | solution.py:159
  20.0 0.0 collective-permute-start.9
  20.0 0.8 %collective-permute-done.4.refs_2_ = bf16[8,4096]{1,0:T(8,128)(2,1)S(1)} collective-permute-done((bf16[8,4096]{1,0:T(8,128)(2,1)S(1)}, bf16[8,4096]{1,0:T(8,128)(2,1)S(1)}, u32[]{:S(2)}, u32[]{:S(2)}) %collective-permute-start.4) | collective-permute-done | bytes 65568 | tf_op jit(solution)/shard_map/ppermute | solution.py:180
  20.9 0.0 collective-permute-start.8
  20.9 0.5 %collective-permute-done.3.refs_1_ = bf16[8,4096]{1,0:T(8,128)(2,1)S(1)} collective-permute-done((bf16[8,4096]{1,0:T(8,128)(2,1)S(1)}, bf16[8,4096]{1,0:T(8,128)(2,1)S(1)}, u32[]{:S(2)}, u32[]{:S(2)}) %collective-permute-start.3) | collective-permute-done | bytes 65568 | tf_op jit(solution)/shard_map/ppermute | solution.py:180
  21.4 0.0 collective-permute-start.7
  21.4 0.0 collective-permute-done.6.refs_4_
  21.4 0.0 collective-permute-done.9.refs_7_
  21.4 0.7 %collective-permute-done.8.refs_6_ = bf16[8,4096]{1,0:T(8,128)(2,1)S(1)} collective-permute-done((bf16[8,4096]{1,0:T(8,128)(2,1)S(1)}, bf16[8,4096]{1,0:T(8,128)(2,1)S(1)}, u32[]{:S(2)}, u32[]{:S(2)}) %collective-permute-start.8) | collective-permute-done | bytes 65568 | tf_op jit(solution)/shard_map/ppermute | solution.py:159
  22.1 0.5 %collective-permute-done.7.refs_5_ = bf16[8,4096]{1,0:T(8,128)(2,1)S(1)} collective-permute-done((bf16[8,4096]{1,0:T(8,128)(2,1)S(1)}, bf16[8,4096]{1,0:T(8,128)(2,1)S(1)}, u32[]{:S(2)}, u32[]{:S(2)}) %collective-permute-start.7) | collective-permute-done | bytes 65568 | tf_op jit(solution)/shard_map/ppermute | solution.py:159
  22.6 0.0 copy-done
  22.6 1.0 %scores.1 = f32[64,64]{1,0:T(8,128)} custom-call(bf16[64,4096]{1,0:T(8,128)(2,1)S(1)} %copy-done, bf16[8,4096]{1,0:T(8,128)(2,1)S(1)} %add_convert_fusion.refs_0_, bf16[8,4096]{1,0:T(8,128)(2,1)S(1)} %collective-permute-done.3.refs_1_, bf16[8,4096]{1,0:T(8,128)(2,1)S(1)} %collective-permute-done.4.refs_2_, ...), custom_call_target="tpu_custom_call" | custom-call | tf_op jit(solution)/shard_map/scores/pallas_call | solution.py:148
  (1 shorter events, 0.0 us)
Async XLA Ops:
  0.0 22.6 %copy-start = (bf16[64,4096]{1,0:T(8,128)(2,1)S(1)}, bf16[64,4096]{1,0:T(8,128)(2,1)}, u32[]{:S(2)}) copy-start(bf16[64,4096]{1,0:T(8,128)(2,1)} %query.1) | copy-start | bytes 1572868
  2.9 6.6 %collective-permute-start = (bf16[8,4096]{1,0:T(8,128)(2,1)S(1)}, bf16[8,4096]{1,0:T(8,128)(2,1)S(1)}, u32[]{:S(2)}, u32[]{:S(2)}) collective-permute-start(bf16[8,4096]{1,0:T(8,128)(2,1)S(1)} %get-tuple-element.10), channel_id=1, source_target_pairs={{0,2},{1,3},{2,0},{3,1},{4,5},{5,4},{6,7},{7,6},{8,10},{9,11},{10,... | collective-permute-start | bytes 196616 | tf_op jit(solution)/shard_map/ppermute | solution.py:172
  7.0 6.8 %collective-permute-start.1 = (bf16[8,4096]{1,0:T(8,128)(2,1)S(1)}, bf16[8,4096]{1,0:T(8,128)(2,1)S(1)}, u32[]{:S(2)}, u32[]{:S(2)}) collective-permute-start(bf16[8,4096]{1,0:T(8,128)(2,1)S(1)} %get-tuple-element.11), channel_id=1, source_target_pairs={{0,3},{1,2},{2,1},{3,0},{4,6},{5,7},{6,4},{7,5},{8,11},{9,10},{10,... | collective-permute-start | bytes 196616 | tf_op jit(solution)/shard_map/ppermute | solution.py:172
  8.4 5.7 %collective-permute-start.2 = (bf16[8,4096]{1,0:T(8,128)(2,1)S(1)}, bf16[8,4096]{1,0:T(8,128)(2,1)S(1)}, u32[]{:S(2)}, u32[]{:S(2)}) collective-permute-start(bf16[8,4096]{1,0:T(8,128)(2,1)S(1)} %get-tuple-element.12), channel_id=1, source_target_pairs={{0,1},{1,0},{2,3},{3,2},{4,7},{5,6},{6,5},{7,4},{8,9},{9,8},{10,11... | collective-permute-start | bytes 196616 | tf_op jit(solution)/shard_map/ppermute | solution.py:172
  14.1 6.0 %collective-permute-start.5 = (bf16[8,4096]{1,0:T(8,128)(2,1)S(1)}, bf16[8,4096]{1,0:T(8,128)(2,1)S(1)}, u32[]{:S(2)}, u32[]{:S(2)}) collective-permute-start(bf16[8,4096]{1,0:T(8,128)(2,1)S(1)} %add_convert_fusion.refs_0_), channel_id=1, source_target_pairs={{0,24},{4,28},{8,16},{12,20},{16,8},{20,12},{24,0},{28,4},{1,25},{... | collective-permute-start | bytes 196616 | tf_op jit(solution)/shard_map/ppermute | solution.py:159
  16.6 4.3 %collective-permute-start.4 = (bf16[8,4096]{1,0:T(8,128)(2,1)S(1)}, bf16[8,4096]{1,0:T(8,128)(2,1)S(1)}, u32[]{:S(2)}, u32[]{:S(2)}) collective-permute-start(bf16[8,4096]{1,0:T(8,128)(2,1)S(1)} %add_convert_fusion.refs_0_), channel_id=1, source_target_pairs={{0,16},{4,12},{8,24},{12,4},{16,0},{20,28},{24,8},{28,20},{1,17},{... | collective-permute-start | bytes 196616 | tf_op jit(solution)/shard_map/ppermute | solution.py:180
  17.1 4.3 %collective-permute-start.3 = (bf16[8,4096]{1,0:T(8,128)(2,1)S(1)}, bf16[8,4096]{1,0:T(8,128)(2,1)S(1)}, u32[]{:S(2)}, u32[]{:S(2)}) collective-permute-start(bf16[8,4096]{1,0:T(8,128)(2,1)S(1)} %add_convert_fusion.refs_0_), channel_id=1, source_target_pairs={{0,8},{4,20},{8,0},{12,28},{16,24},{20,4},{24,16},{28,12},{1,9},{5... | collective-permute-start | bytes 196616 | tf_op jit(solution)/shard_map/ppermute | solution.py:180
  17.6 3.7 %collective-permute-start.6 = (bf16[8,4096]{1,0:T(8,128)(2,1)S(1)}, bf16[8,4096]{1,0:T(8,128)(2,1)S(1)}, u32[]{:S(2)}, u32[]{:S(2)}) collective-permute-start(bf16[8,4096]{1,0:T(8,128)(2,1)S(1)} %add_convert_fusion.refs_0_), channel_id=1, source_target_pairs={{0,4},{4,0},{8,12},{12,8},{16,20},{20,16},{24,28},{28,24},{1,5},{5... | collective-permute-start | bytes 196616 | tf_op jit(solution)/shard_map/ppermute | solution.py:159
  20.0 1.3 %collective-permute-start.9 = (bf16[8,4096]{1,0:T(8,128)(2,1)S(1)}, bf16[8,4096]{1,0:T(8,128)(2,1)S(1)}, u32[]{:S(2)}, u32[]{:S(2)}) collective-permute-start(bf16[8,4096]{1,0:T(8,128)(2,1)S(1)} %collective-permute-done.5.refs_3_), channel_id=1, source_target_pairs={{0,4},{4,0},{8,12},{12,8},{16,20},{20,16},{24,28},{28,24},{1,5},{5... | collective-permute-start | bytes 196616 | tf_op jit(solution)/shard_map/ppermute | solution.py:159
  20.9 1.3 %collective-permute-start.8 = (bf16[8,4096]{1,0:T(8,128)(2,1)S(1)}, bf16[8,4096]{1,0:T(8,128)(2,1)S(1)}, u32[]{:S(2)}, u32[]{:S(2)}) collective-permute-start(bf16[8,4096]{1,0:T(8,128)(2,1)S(1)} %collective-permute-done.4.refs_2_), channel_id=1, source_target_pairs={{0,4},{4,0},{8,12},{12,8},{16,20},{20,16},{24,28},{28,24},{1,5},{5... | collective-permute-start | bytes 196616 | tf_op jit(solution)/shard_map/ppermute | solution.py:159
  21.4 1.3 %collective-permute-start.7 = (bf16[8,4096]{1,0:T(8,128)(2,1)S(1)}, bf16[8,4096]{1,0:T(8,128)(2,1)S(1)}, u32[]{:S(2)}, u32[]{:S(2)}) collective-permute-start(bf16[8,4096]{1,0:T(8,128)(2,1)S(1)} %collective-permute-done.3.refs_1_), channel_id=1, source_target_pairs={{0,4},{4,0},{8,12},{12,8},{16,20},{20,16},{24,28},{28,24},{1,5},{5... | collective-permute-start | bytes 196616 | tf_op jit(solution)/shard_map/ppermute | solution.py:159

commit v19 on v15

--- a/solution.py
+++ b/solution.py
@@ -105,16 +105,24 @@
     )(*(pltpu.with_memory_space_constraint(x, pltpu.HBM) for x in (doc_lengths, owner_map, proj_rows)))
 
 
-def score_kernel(query, *refs):
+def block_products(query, blocks):
+    features = jnp.concatenate([block[...] for block in blocks], axis=0)
+    return lax.dot_general(features, query[...], ROW_BY_ROW, preferred_element_type=jnp.float32)
+
+
+def early_kernel(query, *refs):
+    *blocks, products = refs
+    products[...] = block_products(query, blocks)
+
+
+def score_kernel(query, early, *refs):
     *blocks, scores = refs
     doc_dev = blocks[0].shape[0]
-    features = jnp.concatenate([block[...] for block in blocks], axis=0)
-    products = lax.dot_general(
-        features, query[...], ROW_BY_ROW, preferred_element_type=jnp.float32
+    late = block_products(query, blocks)
+    own, second, first, third, own_next, third_next = (
+        early[i : i + doc_dev, :] for i in range(0, early.shape[0], doc_dev)
     )
-    own, second, first, third, own_next, second_next, first_next, third_next = (
-        products[i * doc_dev : (i + 1) * doc_dev] for i in range(len(blocks))
-    )
+    second_next, first_next = late[:doc_dev], late[doc_dev:]
     ex = lax.axis_index("ex")
     odd = lax.rem(ex, 2) == 1
     parts = [
@@ -135,18 +143,29 @@
     scores[...] = jnp.concatenate(parts, axis=0).T
 
 
-def block_scores(query_features, held, held_next):
+def call_on_vmem(kernel, name, shape, *operands):
     whole = pl.BlockSpec(memory_space=pltpu.VMEM)
-    operands = (query_features, *held, *held_next)
-    docs = (len(operands) - 1) * held[0].shape[0]
+    moved = sum(x.nbytes for x in operands)
     return pl.pallas_call(
-        score_kernel,
-        out_shape=jax.ShapeDtypeStruct((query_features.shape[0], docs), jnp.float32),
+        kernel,
+        out_shape=jax.ShapeDtypeStruct(shape, jnp.float32),
         in_specs=[whole] * len(operands),
         out_specs=whole,
+        cost_estimate=pl.CostEstimate(flops=0, bytes_accessed=moved, transcendentals=0),
         compiler_params=pltpu.CompilerParams(vmem_limit_bytes=16 * 1024 * 1024),
-        name="scores",
+        name=name,
     )(*(pltpu.with_memory_space_constraint(x, pltpu.VMEM) for x in operands))
+
+
+def block_scores(query, held, held_next):
+    own_next, second_next, first_next, third_next = held_next
+    ready = (*held, own_next, third_next)
+    doc_dev, queries = held[0].shape[0], query.shape[0]
+    early = call_on_vmem(
+        early_kernel, "early_products", (len(ready) * doc_dev, queries), query, *ready
+    )
+    shape = (queries, (len(ready) + 2) * doc_dev)
+    return call_on_vmem(score_kernel, "scores", shape, query, early, second_next, first_next)
 
 
 def exchange(block, axis, flip):

time: 23.1 us -> 23 us (level)
  waiting for transfers between devices: 9.7 us -> 9.43 us
  Pallas kernels: 3.89 us -> 4.14 us
    ppermute x2, waiting for transfers between devices: 2.05 us -> 1.43 us  [body(): first, second = (lax.ppermute(features, 'ex', turn) for turn in turns)]
    ppermute x8, waiting for transfers between devices: 7.66 us -> 8 us  [exchange(): lax.ppermute(block, axis, [(i, i ^ flip) for i in range(lax.axis_size(axi...]
    pallas_call x1 -> x2, Pallas kernels: 0.99 us -> 1.24 us  [call_on_vmem(): pl.pallas_call(kernel, out_shape=jax.ShapeDtypeStruct(shape, jnp.float32)...]
  transfers between devices with their start and end apart: 10 -> 10, of which waited for: 8 -> 8; matrix products, arithmetic and copies ran while one was open for 0% -> 0% of each run, Pallas kernels for 0% -> 1%
where the time goes in v19:
time: 23 us; the launch traced here: 22.9 us
  waiting for transfers between devices  9.43 us (41%)
  starting transfers between devices  9.24 us (40%)
  Pallas kernels  4.14 us (18%)
    ppermute x8, starting transfers between devices, exchange(): lax.ppermute(block, axis, [(i, i ^ flip) for i in range(lax.axis_size(axi...  8.2 us
    ppermute x8, waiting for transfers between devices, exchange(): lax.ppermute(block, axis, [(i, i ^ flip) for i in range(lax.axis_size(axi...  8 us
    pallas_call x1, Pallas kernels, feature_shares(): pl.pallas_call(feature_kernel, out_shape=[jax.ShapeDtypeStruct((doc_dev,...  2.9 us
    ppermute x2, waiting for transfers between devices, body(): first, second = (lax.ppermute(features, 'ex', turn) for turn in turns)  1.43 us
    pallas_call x2, Pallas kernels, call_on_vmem(): pl.pallas_call(kernel, out_shape=jax.ShapeDtypeStruct(shape, jnp.float32)...  1.24 us
    ppermute x2, starting transfers between devices, body(): first, second = (lax.ppermute(features, 'ex', turn) for turn in turns)  1.04 us
  transfers between devices with their start and end apart: 10, of which 8 were waited for; matrix products, arithmetic and copies ran while one was open for 0% of the time, Pallas kernels for 1%

profile of v19, /device:TPU:0, one launch (start us, length us, event | category | flops | bytes accessed | tf_op | source)
XLA Modules:
  0.0 22.9 jit_solution(10454631220485251092)
XLA Ops:
  0.0 2.9 %features.1 = (f32[8,4096]{1,0:T(8,128)S(1)}, bf16[8,4096]{1,0:T(8,128)(2,1)S(1)}, bf16[8,4096]{1,0:T(8,128)(2,1)S(1)}, bf16[8,4096]{1,0:T(8,128)(2,1)S(1)}) custom-call(s32[1,32]{1,0:T(1,128)} %lengths_hbm.1, s32[1,32]{1,0:T(1,128)} %owners_hbm.1, bf16[2048,128]{1,0:T(8,128)(2,1)} %rows_hbm.1), custom_call_target="tpu_custom_call" | custom-call | tf_op jit(solution)/shard_map/features/pallas_call | solution.py:86
  2.9 4.1 %collective-permute-start = (bf16[8,4096]{1,0:T(8,128)(2,1)S(1)}, bf16[8,4096]{1,0:T(8,128)(2,1)S(1)}, u32[]{:S(2)}, u32[]{:S(2)}) collective-permute-start(bf16[8,4096]{1,0:T(8,128)(2,1)S(1)} %get-tuple-element.10), channel_id=1, source_target_pairs={{0,2},{1,3},{2,0},{3,1},{4,6},{5,7},{6,4},{7,5},{8,10},{9,11},{10,... | collective-permute-start | bytes 196616 | tf_op jit(solution)/shard_map/ppermute | solution.py:172
  7.0 1.3 %collective-permute-start.1 = (bf16[8,4096]{1,0:T(8,128)(2,1)S(1)}, bf16[8,4096]{1,0:T(8,128)(2,1)S(1)}, u32[]{:S(2)}, u32[]{:S(2)}) collective-permute-start(bf16[8,4096]{1,0:T(8,128)(2,1)S(1)} %get-tuple-element.11), channel_id=1, source_target_pairs={{0,3},{1,2},{2,1},{3,0},{4,7},{5,6},{6,5},{7,4},{8,11},{9,10},{10,... | collective-permute-start | bytes 196616 | tf_op jit(solution)/shard_map/ppermute | solution.py:172
  8.4 0.2 collective-permute-start.2
  8.6 2.2 %collective-permute-done = bf16[8,4096]{1,0:T(8,128)(2,1)S(1)} collective-permute-done((bf16[8,4096]{1,0:T(8,128)(2,1)S(1)}, bf16[8,4096]{1,0:T(8,128)(2,1)S(1)}, u32[]{:S(2)}, u32[]{:S(2)}) %collective-permute-start) | collective-permute-done | bytes 65568 | tf_op jit(solution)/shard_map/ppermute | solution.py:172
  10.8 2.5 %collective-permute-done.1 = bf16[8,4096]{1,0:T(8,128)(2,1)S(1)} collective-permute-done((bf16[8,4096]{1,0:T(8,128)(2,1)S(1)}, bf16[8,4096]{1,0:T(8,128)(2,1)S(1)}, u32[]{:S(2)}, u32[]{:S(2)}) %collective-permute-start.1) | collective-permute-done | bytes 65568 | tf_op jit(solution)/shard_map/ppermute | solution.py:172
  13.2 0.1 collective-permute-done.2
  13.4 2.5 %collective-permute-start.5 = (bf16[8,4096]{1,0:T(8,128)(2,1)S(1)}, bf16[8,4096]{1,0:T(8,128)(2,1)S(1)}, u32[]{:S(2)}, u32[]{:S(2)}) collective-permute-start(bf16[8,4096]{1,0:T(8,128)(2,1)S(1)} %add_convert_fusion.refs_0_), channel_id=1, source_target_pairs={{0,24},{4,28},{8,16},{12,20},{16,8},{20,12},{24,0},{28,4},{1,25},{... | collective-permute-start | bytes 196616 | tf_op jit(solution)/shard_map/ppermute | solution.py:172
  15.9 0.5 %collective-permute-start.3 = (bf16[8,4096]{1,0:T(8,128)(2,1)S(1)}, bf16[8,4096]{1,0:T(8,128)(2,1)S(1)}, u32[]{:S(2)}, u32[]{:S(2)}) collective-permute-start(bf16[8,4096]{1,0:T(8,128)(2,1)S(1)} %add_convert_fusion.refs_0_), channel_id=1, source_target_pairs={{0,8},{4,20},{8,0},{12,28},{16,24},{20,4},{24,16},{28,12},{1,9},{5... | collective-permute-start | bytes 196616 | tf_op jit(solution)/shard_map/ppermute | solution.py:188
  16.4 0.5 %collective-permute-start.4 = (bf16[8,4096]{1,0:T(8,128)(2,1)S(1)}, bf16[8,4096]{1,0:T(8,128)(2,1)S(1)}, u32[]{:S(2)}, u32[]{:S(2)}) collective-permute-start(bf16[8,4096]{1,0:T(8,128)(2,1)S(1)} %add_convert_fusion.refs_0_), channel_id=1, source_target_pairs={{0,16},{4,12},{8,24},{12,4},{16,0},{20,28},{24,8},{28,20},{1,17},{... | collective-permute-start | bytes 196616 | tf_op jit(solution)/shard_map/ppermute | solution.py:188
  16.9 0.0 collective-permute-start.6
  16.9 2.3 %collective-permute-done.5.refs_3_ = bf16[8,4096]{1,0:T(8,128)(2,1)S(1)} collective-permute-done((bf16[8,4096]{1,0:T(8,128)(2,1)S(1)}, bf16[8,4096]{1,0:T(8,128)(2,1)S(1)}, u32[]{:S(2)}, u32[]{:S(2)}) %collective-permute-start.5) | collective-permute-done | bytes 65568 | tf_op jit(solution)/shard_map/ppermute | solution.py:172
  19.2 0.0 collective-permute-start.7
  19.2 0.9 %collective-permute-done.3.refs_1_ = bf16[8,4096]{1,0:T(8,128)(2,1)S(1)} collective-permute-done((bf16[8,4096]{1,0:T(8,128)(2,1)S(1)}, bf16[8,4096]{1,0:T(8,128)(2,1)S(1)}, u32[]{:S(2)}, u32[]{:S(2)}) %collective-permute-start.3) | collective-permute-done | bytes 65568 | tf_op jit(solution)/shard_map/ppermute | solution.py:188
  20.2 0.0 collective-permute-start.8
  20.2 0.5 %collective-permute-done.4.refs_2_ = bf16[8,4096]{1,0:T(8,128)(2,1)S(1)} collective-permute-done((bf16[8,4096]{1,0:T(8,128)(2,1)S(1)}, bf16[8,4096]{1,0:T(8,128)(2,1)S(1)}, u32[]{:S(2)}, u32[]{:S(2)}) %collective-permute-start.4) | collective-permute-done | bytes 65568 | tf_op jit(solution)/shard_map/ppermute | solution.py:188
  20.7 0.0 collective-permute-start.9
  20.7 0.0 collective-permute-done.6.refs_4_
  20.7 0.0 collective-permute-done.7.refs_5_
  20.7 0.0 copy-done
  20.7 0.3 %early_products.1.early = f32[48,64]{1,0:T(8,128)S(1)} custom-call(bf16[64,4096]{1,0:T(8,128)(2,1)S(1)} %copy-done, bf16[8,4096]{1,0:T(8,128)(2,1)S(1)} %add_convert_fusion.refs_0_, bf16[8,4096]{1,0:T(8,128)(2,1)S(1)} %collective-permute-done.3.refs_1_, bf16[8,4096]{1,0:T(8,128)(2,1)S(1)} %collective-permute-done.4.refs_2_, ...), custom_call_target="tpu_custom_call" | custom-call | bytes 917504 | tf_op jit(solution)/shard_map/early_products/pallas_call | solution.py:149
  21.0 0.4 %collective-permute-done.8.refs_0_ = bf16[8,4096]{1,0:T(8,128)(2,1)S(1)} collective-permute-done((bf16[8,4096]{1,0:T(8,128)(2,1)S(1)}, bf16[8,4096]{1,0:T(8,128)(2,1)S(1)}, u32[]{:S(2)}, u32[]{:S(2)}) %collective-permute-start.8) | collective-permute-done | bytes 65568 | tf_op jit(solution)/shard_map/ppermute | solution.py:172
  21.4 0.5 %collective-permute-done.9.refs_1_ = bf16[8,4096]{1,0:T(8,128)(2,1)S(1)} collective-permute-done((bf16[8,4096]{1,0:T(8,128)(2,1)S(1)}, bf16[8,4096]{1,0:T(8,128)(2,1)S(1)}, u32[]{:S(2)}, u32[]{:S(2)}) %collective-permute-start.9) | collective-permute-done | bytes 65568 | tf_op jit(solution)/shard_map/ppermute | solution.py:172
  21.9 1.0 %scores.1 = f32[64,64]{1,0:T(8,128)} custom-call(bf16[64,4096]{1,0:T(8,128)(2,1)S(1)} %copy-done, f32[48,64]{1,0:T(8,128)S(1)} %early_products.1.early, bf16[8,4096]{1,0:T(8,128)(2,1)S(1)} %collective-permute-done.8.refs_0_, bf16[8,4096]{1,0:T(8,128)(2,1)S(1)} %collective-permute-done.9.refs_1_), custom_call_target="tpu_custom_call" | custom-call | bytes 667648 | tf_op jit(solution)/shard_map/scores/pallas_call | solution.py:149
  (2 shorter events, 0.0 us)
Async XLA Ops:
  0.0 20.7 %copy-start = (bf16[64,4096]{1,0:T(8,128)(2,1)S(1)}, bf16[64,4096]{1,0:T(8,128)(2,1)}, u32[]{:S(2)}) copy-start(bf16[64,4096]{1,0:T(8,128)(2,1)} %query.3) | copy-start | bytes 1572868
  2.9 7.9 %collective-permute-start = (bf16[8,4096]{1,0:T(8,128)(2,1)S(1)}, bf16[8,4096]{1,0:T(8,128)(2,1)S(1)}, u32[]{:S(2)}, u32[]{:S(2)}) collective-permute-start(bf16[8,4096]{1,0:T(8,128)(2,1)S(1)} %get-tuple-element.10), channel_id=1, source_target_pairs={{0,2},{1,3},{2,0},{3,1},{4,6},{5,7},{6,4},{7,5},{8,10},{9,11},{10,... | collective-permute-start | bytes 196616 | tf_op jit(solution)/shard_map/ppermute | solution.py:172
  7.0 6.2 %collective-permute-start.1 = (bf16[8,4096]{1,0:T(8,128)(2,1)S(1)}, bf16[8,4096]{1,0:T(8,128)(2,1)S(1)}, u32[]{:S(2)}, u32[]{:S(2)}) collective-permute-start(bf16[8,4096]{1,0:T(8,128)(2,1)S(1)} %get-tuple-element.11), channel_id=1, source_target_pairs={{0,3},{1,2},{2,1},{3,0},{4,7},{5,6},{6,5},{7,4},{8,11},{9,10},{10,... | collective-permute-start | bytes 196616 | tf_op jit(solution)/shard_map/ppermute | solution.py:172
  8.4 5.0 %collective-permute-start.2 = (bf16[8,4096]{1,0:T(8,128)(2,1)S(1)}, bf16[8,4096]{1,0:T(8,128)(2,1)S(1)}, u32[]{:S(2)}, u32[]{:S(2)}) collective-permute-start(bf16[8,4096]{1,0:T(8,128)(2,1)S(1)} %get-tuple-element.12), channel_id=1, source_target_pairs={{0,1},{1,0},{2,3},{3,2},{4,5},{5,4},{6,7},{7,6},{8,9},{9,8},{10,11... | collective-permute-start | bytes 196616 | tf_op jit(solution)/shard_map/ppermute | solution.py:172
  13.4 5.9 %collective-permute-start.5 = (bf16[8,4096]{1,0:T(8,128)(2,1)S(1)}, bf16[8,4096]{1,0:T(8,128)(2,1)S(1)}, u32[]{:S(2)}, u32[]{:S(2)}) collective-permute-start(bf16[8,4096]{1,0:T(8,128)(2,1)S(1)} %add_convert_fusion.refs_0_), channel_id=1, source_target_pairs={{0,24},{4,28},{8,16},{12,20},{16,8},{20,12},{24,0},{28,4},{1,25},{... | collective-permute-start | bytes 196616 | tf_op jit(solution)/shard_map/ppermute | solution.py:172
  15.9 4.3 %collective-permute-start.3 = (bf16[8,4096]{1,0:T(8,128)(2,1)S(1)}, bf16[8,4096]{1,0:T(8,128)(2,1)S(1)}, u32[]{:S(2)}, u32[]{:S(2)}) collective-permute-start(bf16[8,4096]{1,0:T(8,128)(2,1)S(1)} %add_convert_fusion.refs_0_), channel_id=1, source_target_pairs={{0,8},{4,20},{8,0},{12,28},{16,24},{20,4},{24,16},{28,12},{1,9},{5... | collective-permute-start | bytes 196616 | tf_op jit(solution)/shard_map/ppermute | solution.py:188
  16.4 4.3 %collective-permute-start.4 = (bf16[8,4096]{1,0:T(8,128)(2,1)S(1)}, bf16[8,4096]{1,0:T(8,128)(2,1)S(1)}, u32[]{:S(2)}, u32[]{:S(2)}) collective-permute-start(bf16[8,4096]{1,0:T(8,128)(2,1)S(1)} %add_convert_fusion.refs_0_), channel_id=1, source_target_pairs={{0,16},{4,12},{8,24},{12,4},{16,0},{20,28},{24,8},{28,20},{1,17},{... | collective-permute-start | bytes 196616 | tf_op jit(solution)/shard_map/ppermute | solution.py:188
  16.9 3.8 %collective-permute-start.6 = (bf16[8,4096]{1,0:T(8,128)(2,1)S(1)}, bf16[8,4096]{1,0:T(8,128)(2,1)S(1)}, u32[]{:S(2)}, u32[]{:S(2)}) collective-permute-start(bf16[8,4096]{1,0:T(8,128)(2,1)S(1)} %add_convert_fusion.refs_0_), channel_id=1, source_target_pairs={{0,4},{4,0},{8,12},{12,8},{16,20},{20,16},{24,28},{28,24},{1,5},{5... | collective-permute-start | bytes 196616 | tf_op jit(solution)/shard_map/ppermute | solution.py:172
  19.2 1.4 %collective-permute-start.7 = (bf16[8,4096]{1,0:T(8,128)(2,1)S(1)}, bf16[8,4096]{1,0:T(8,128)(2,1)S(1)}, u32[]{:S(2)}, u32[]{:S(2)}) collective-permute-start(bf16[8,4096]{1,0:T(8,128)(2,1)S(1)} %collective-permute-done.5.refs_3_), channel_id=1, source_target_pairs={{0,4},{4,0},{8,12},{12,8},{16,20},{20,16},{24,28},{28,24},{1,5},{5... | collective-permute-start | bytes 196616 | tf_op jit(solution)/shard_map/ppermute | solution.py:172
  20.2 1.3 %collective-permute-start.8 = (bf16[8,4096]{1,0:T(8,128)(2,1)S(1)}, bf16[8,4096]{1,0:T(8,128)(2,1)S(1)}, u32[]{:S(2)}, u32[]{:S(2)}) collective-permute-start(bf16[8,4096]{1,0:T(8,128)(2,1)S(1)} %collective-permute-done.3.refs_1_), channel_id=1, source_target_pairs={{0,4},{4,0},{8,12},{12,8},{16,20},{20,16},{24,28},{28,24},{1,5},{5... | collective-permute-start | bytes 196616 | tf_op jit(solution)/shard_map/ppermute | solution.py:172
  20.7 1.3 %collective-permute-start.9 = (bf16[8,4096]{1,0:T(8,128)(2,1)S(1)}, bf16[8,4096]{1,0:T(8,128)(2,1)S(1)}, u32[]{:S(2)}, u32[]{:S(2)}) collective-permute-start(bf16[8,4096]{1,0:T(8,128)(2,1)S(1)} %collective-permute-done.4.refs_2_), channel_id=1, source_target_pairs={{0,4},{4,0},{8,12},{12,8},{16,20},{20,16},{24,28},{28,24},{1,5},{5... | collective-permute-start | bytes 196616 | tf_op jit(solution)/shard_map/ppermute | solution.py:172

commit v20 on v19

--- a/solution.py
+++ b/solution.py
@@ -9,16 +9,16 @@
 ROW_BY_ROW = (((1,), (1,)), ((), ()))
 
 
-def feature_kernel(lengths_hbm, owners_hbm, rows_hbm, *refs):
-    *shares, lengths, owners, rows, grads, inputs, sums, arrived = refs
+def feature_kernel(lengths_hbm, owners_hbm, rows_hbm, query_hbm, *refs):
+    *shares, query, lengths, owners, rows, grads, inputs, sums, arrived = refs
     count, width = rows.shape[0], rows.shape[1] // 2
     copies = [
         pltpu.make_async_copy(source, target, arrived.at[i])
         for i, (source, target) in enumerate(
-            ((lengths_hbm, lengths), (owners_hbm, owners), (rows_hbm, rows))
+            ((lengths_hbm, lengths), (owners_hbm, owners), (rows_hbm, rows), (query_hbm, query))
         )
     ]
-    for copy in copies:
+    for copy in copies[:3]:
         copy.start()
     docs, tok_count = lengths.shape[1], len(shares)
     doc_dev = docs // tok_count
@@ -46,6 +46,7 @@
         == lax.broadcasted_iota(jnp.int32, (2 * width, 2 * width), 1)
     ).astype(rows.dtype)
     copies[2].wait()
+    copies[3].start()
     for b in range(blocks):
         part = slice(b * LANES, (b + 1) * LANES)
         turned = lax.dot_general(eye, rows[part, :], ROW_BY_ROW, preferred_element_type=jnp.float32)
@@ -75,9 +76,10 @@
             right = jnp.where(low_half, pltpu.roll(first, width, 1), second)
             shares[s][:, out] = (left * scales[s]).astype(shares[s].dtype)
             shares[s + 1][:, out] = (right * scales[s + 1]).astype(shares[s + 1].dtype)
-
-
-def feature_shares(proj_rows, doc_lengths, owner_map, tok_count):
+    copies[3].wait()
+
+
+def feature_shares(proj_rows, query_features, doc_lengths, owner_map, tok_count):
     count, width = proj_rows.shape[0], proj_rows.shape[1] // 2
     doc_dev = doc_lengths.shape[1] // tok_count
     feat = width * width
@@ -88,9 +90,10 @@
         out_shape=[
             jax.ShapeDtypeStruct((doc_dev, feat), jnp.bfloat16 if s else jnp.float32)
             for s in range(tok_count)
-        ],
-        in_specs=[far, far, far],
-        out_specs=[whole] * tok_count,
+        ]
+        + [jax.ShapeDtypeStruct(query_features.shape, query_features.dtype)],
+        in_specs=[far] * 4,
+        out_specs=[whole] * (tok_count + 1),
         scratch_shapes=[
             pltpu.SMEM(doc_lengths.shape, jnp.int32),
             pltpu.SMEM(owner_map.shape, jnp.int32),
@@ -98,11 +101,11 @@
             pltpu.VMEM((doc_dev * width, count), jnp.bfloat16),
             pltpu.VMEM((tok_count * width, count), jnp.bfloat16),
             pltpu.VMEM((tok_count // 2, doc_dev * width, LANES), jnp.float32),
-            pltpu.SemaphoreType.DMA((3,)),
+            pltpu.SemaphoreType.DMA((4,)),
         ],
         compiler_params=pltpu.CompilerParams(vmem_limit_bytes=32 * 1024 * 1024),
         name="features",
-    )(*(pltpu.with_memory_space_constraint(x, pltpu.HBM) for x in (doc_lengths, owner_map, proj_rows)))
+    )(*(pltpu.with_memory_space_constraint(x, pltpu.HBM) for x in (doc_lengths, owner_map, proj_rows, query_features)))
 
 
 def block_products(query, blocks):
@@ -174,7 +177,9 @@
 
 def body(proj_rows, query_features, doc_lengths, owner_map):
     tok_count = lax.axis_size("tok")
-    shares = feature_shares(proj_rows, doc_lengths, owner_map, tok_count)
+    *shares, query_features = feature_shares(
+        proj_rows, query_features, doc_lengths, owner_map, tok_count
+    )
     total = shares[0]
     for shift in sorted(range(1, tok_count), key=lambda flip: (flip < 2, flip)):
         total = total + exchange(shares[shift], "tok", shift).astype(jnp.float32)

time: 23 us -> 23 us (level)
  no operation moved by 1% of the time
where the time goes in v20:
time: 23 us; the launch traced here: 22.8 us
  waiting for transfers between devices  9.44 us (41%)
  starting transfers between devices  9.24 us (40%)
  Pallas kernels  4.09 us (18%)
    ppermute x8, starting transfers between devices, exchange(): lax.ppermute(block, axis, [(i, i ^ flip) for i in range(lax.axis_size(axi...  8.2 us
    ppermute x8, waiting for transfers between devices, exchange(): lax.ppermute(block, axis, [(i, i ^ flip) for i in range(lax.axis_size(axi...  7.99 us
    pallas_call x1, Pallas kernels, feature_shares(): pl.pallas_call(feature_kernel, out_shape=[jax.ShapeDtypeStruct((doc_dev,...  2.86 us
    ppermute x2, waiting for transfers between devices, body(): first, second = (lax.ppermute(features, 'ex', turn) for turn in turns)  1.45 us
    pallas_call x2, Pallas kernels, call_on_vmem(): pl.pallas_call(kernel, out_shape=jax.ShapeDtypeStruct(shape, jnp.float32)...  1.24 us
    ppermute x2, starting transfers between devices, body(): first, second = (lax.ppermute(features, 'ex', turn) for turn in turns)  1.04 us
  transfers between devices with their start and end apart: 10, of which 8 were waited for; matrix products, arithmetic and copies ran while one was open for 0% of the time, Pallas kernels for 1%

profile of v20, /device:TPU:0, one launch (start us, length us, event | category | flops | bytes accessed | tf_op | source)
XLA Modules:
  0.0 22.8 jit_solution(13834279713724302986)
XLA Ops:
  0.0 2.9 %features.1 = (f32[8,4096]{1,0:T(8,128)S(1)}, bf16[8,4096]{1,0:T(8,128)(2,1)S(1)}, bf16[8,4096]{1,0:T(8,128)(2,1)S(1)}, bf16[8,4096]{1,0:T(8,128)(2,1)S(1)}, bf16[64,4096]{1,0:T(8,128)(2,1)S(1)}) custom-call(s32[1,32]{1,0:T(1,128)} %lengths_hbm.1, s32[1,32]{1,0:T(1,128)} %owners_hbm.1, bf16[2048,128]{1,0:T(8,128)(2,1)} %rows_hbm.1, bf16[64,4096]{1,0:T(8,128)(2,1)} %query_hbm.1), custom_call_target="tpu_custom_call" | custom-call | tf_op jit(solution)/shard_map/features/pallas_call | solution.py:88
  2.9 4.1 %collective-permute-start = (bf16[8,4096]{1,0:T(8,128)(2,1)S(1)}, bf16[8,4096]{1,0:T(8,128)(2,1)S(1)}, u32[]{:S(2)}, u32[]{:S(2)}) collective-permute-start(bf16[8,4096]{1,0:T(8,128)(2,1)S(1)} %get-tuple-element.12), channel_id=1, source_target_pairs={{0,2},{1,3},{2,0},{3,1},{4,6},{5,7},{6,4},{7,5},{8,10},{9,11},{10,... | collective-permute-start | bytes 196616 | tf_op jit(solution)/shard_map/ppermute | solution.py:175
  7.0 1.4 %collective-permute-start.1 = (bf16[8,4096]{1,0:T(8,128)(2,1)S(1)}, bf16[8,4096]{1,0:T(8,128)(2,1)S(1)}, u32[]{:S(2)}, u32[]{:S(2)}) collective-permute-start(bf16[8,4096]{1,0:T(8,128)(2,1)S(1)} %get-tuple-element.13), channel_id=1, source_target_pairs={{0,3},{1,2},{2,1},{3,0},{4,7},{5,6},{6,5},{7,4},{8,11},{9,10},{10,... | collective-permute-start | bytes 196616 | tf_op jit(solution)/shard_map/ppermute | solution.py:175
  8.3 0.2 %collective-permute-start.2 = (bf16[8,4096]{1,0:T(8,128)(2,1)S(1)}, bf16[8,4096]{1,0:T(8,128)(2,1)S(1)}, u32[]{:S(2)}, u32[]{:S(2)}) collective-permute-start(bf16[8,4096]{1,0:T(8,128)(2,1)S(1)} %get-tuple-element.14), channel_id=1, source_target_pairs={{0,1},{1,0},{2,3},{3,2},{4,5},{5,4},{6,7},{7,6},{8,9},{9,8},{10,11... | collective-permute-start | bytes 196616 | tf_op jit(solution)/shard_map/ppermute | solution.py:175
  8.5 2.2 %collective-permute-done = bf16[8,4096]{1,0:T(8,128)(2,1)S(1)} collective-permute-done((bf16[8,4096]{1,0:T(8,128)(2,1)S(1)}, bf16[8,4096]{1,0:T(8,128)(2,1)S(1)}, u32[]{:S(2)}, u32[]{:S(2)}) %collective-permute-start) | collective-permute-done | bytes 65568 | tf_op jit(solution)/shard_map/ppermute | solution.py:175
  10.7 2.5 %collective-permute-done.1 = bf16[8,4096]{1,0:T(8,128)(2,1)S(1)} collective-permute-done((bf16[8,4096]{1,0:T(8,128)(2,1)S(1)}, bf16[8,4096]{1,0:T(8,128)(2,1)S(1)}, u32[]{:S(2)}, u32[]{:S(2)}) %collective-permute-start.1) | collective-permute-done | bytes 65568 | tf_op jit(solution)/shard_map/ppermute | solution.py:175
  13.2 0.1 collective-permute-done.2
  13.3 2.5 %collective-permute-start.5 = (bf16[8,4096]{1,0:T(8,128)(2,1)S(1)}, bf16[8,4096]{1,0:T(8,128)(2,1)S(1)}, u32[]{:S(2)}, u32[]{:S(2)}) collective-permute-start(bf16[8,4096]{1,0:T(8,128)(2,1)S(1)} %add_convert_fusion.refs_0_), channel_id=1, source_target_pairs={{0,24},{4,28},{8,16},{12,20},{16,8},{20,12},{24,0},{28,4},{1,25},{... | collective-permute-start | bytes 196616 | tf_op jit(solution)/shard_map/ppermute | solution.py:175
  15.8 0.5 %collective-permute-start.3 = (bf16[8,4096]{1,0:T(8,128)(2,1)S(1)}, bf16[8,4096]{1,0:T(8,128)(2,1)S(1)}, u32[]{:S(2)}, u32[]{:S(2)}) collective-permute-start(bf16[8,4096]{1,0:T(8,128)(2,1)S(1)} %add_convert_fusion.refs_0_), channel_id=1, source_target_pairs={{0,8},{4,20},{8,0},{12,28},{16,24},{20,4},{24,16},{28,12},{1,9},{5... | collective-permute-start | bytes 196616 | tf_op jit(solution)/shard_map/ppermute | solution.py:193
  16.4 0.5 %collective-permute-start.4 = (bf16[8,4096]{1,0:T(8,128)(2,1)S(1)}, bf16[8,4096]{1,0:T(8,128)(2,1)S(1)}, u32[]{:S(2)}, u32[]{:S(2)}) collective-permute-start(bf16[8,4096]{1,0:T(8,128)(2,1)S(1)} %add_convert_fusion.refs_0_), channel_id=1, source_target_pairs={{0,16},{4,12},{8,24},{12,4},{16,0},{20,28},{24,8},{28,20},{1,17},{... | collective-permute-start | bytes 196616 | tf_op jit(solution)/shard_map/ppermute | solution.py:193
  16.9 0.0 collective-permute-start.6
  16.9 2.3 %collective-permute-done.5.refs_3_ = bf16[8,4096]{1,0:T(8,128)(2,1)S(1)} collective-permute-done((bf16[8,4096]{1,0:T(8,128)(2,1)S(1)}, bf16[8,4096]{1,0:T(8,128)(2,1)S(1)}, u32[]{:S(2)}, u32[]{:S(2)}) %collective-permute-start.5) | collective-permute-done | bytes 65568 | tf_op jit(solution)/shard_map/ppermute | solution.py:175
  19.2 0.0 collective-permute-start.7
  19.2 0.9 %collective-permute-done.3.refs_1_ = bf16[8,4096]{1,0:T(8,128)(2,1)S(1)} collective-permute-done((bf16[8,4096]{1,0:T(8,128)(2,1)S(1)}, bf16[8,4096]{1,0:T(8,128)(2,1)S(1)}, u32[]{:S(2)}, u32[]{:S(2)}) %collective-permute-start.3) | collective-permute-done | bytes 65568 | tf_op jit(solution)/shard_map/ppermute | solution.py:193
  20.1 0.0 collective-permute-start.8
  20.1 0.5 %collective-permute-done.4.refs_2_ = bf16[8,4096]{1,0:T(8,128)(2,1)S(1)} collective-permute-done((bf16[8,4096]{1,0:T(8,128)(2,1)S(1)}, bf16[8,4096]{1,0:T(8,128)(2,1)S(1)}, u32[]{:S(2)}, u32[]{:S(2)}) %collective-permute-start.4) | collective-permute-done | bytes 65568 | tf_op jit(solution)/shard_map/ppermute | solution.py:193
  20.6 0.0 collective-permute-start.9
  20.6 0.0 collective-permute-done.6.refs_4_
  20.6 0.0 collective-permute-done.7.refs_5_
  20.7 0.3 %early_products.1.early = f32[48,64]{1,0:T(8,128)S(1)} custom-call(bf16[64,4096]{1,0:T(8,128)(2,1)S(1)} %get-tuple-element.10.query, bf16[8,4096]{1,0:T(8,128)(2,1)S(1)} %add_convert_fusion.refs_0_, bf16[8,4096]{1,0:T(8,128)(2,1)S(1)} %collective-permute-done.3.refs_1_, bf16[8,4096]{1,0:T(8,128)(2,1)S(1)} %collective-permute-done.4.refs_2_, ...), custom_call_target="tpu_custom_call" | custom-call | bytes 917504 | tf_op jit(solution)/shard_map/early_products/pallas_call | solution.py:152
  20.9 0.4 %collective-permute-done.8.refs_0_ = bf16[8,4096]{1,0:T(8,128)(2,1)S(1)} collective-permute-done((bf16[8,4096]{1,0:T(8,128)(2,1)S(1)}, bf16[8,4096]{1,0:T(8,128)(2,1)S(1)}, u32[]{:S(2)}, u32[]{:S(2)}) %collective-permute-start.8) | collective-permute-done | bytes 65568 | tf_op jit(solution)/shard_map/ppermute | solution.py:175
  21.4 0.5 %collective-permute-done.9.refs_1_ = bf16[8,4096]{1,0:T(8,128)(2,1)S(1)} collective-permute-done((bf16[8,4096]{1,0:T(8,128)(2,1)S(1)}, bf16[8,4096]{1,0:T(8,128)(2,1)S(1)}, u32[]{:S(2)}, u32[]{:S(2)}) %collective-permute-start.9) | collective-permute-done | bytes 65568 | tf_op jit(solution)/shard_map/ppermute | solution.py:175
  21.9 1.0 %scores.1 = f32[64,64]{1,0:T(8,128)} custom-call(bf16[64,4096]{1,0:T(8,128)(2,1)S(1)} %get-tuple-element.10.query, f32[48,64]{1,0:T(8,128)S(1)} %early_products.1.early, bf16[8,4096]{1,0:T(8,128)(2,1)S(1)} %collective-permute-done.8.refs_0_, bf16[8,4096]{1,0:T(8,128)(2,1)S(1)} %collective-permute-done.9.refs_1_), custom_call_target="tpu_custom_call" | custom-call | bytes 667648 | tf_op jit(solution)/shard_map/scores/pallas_call | solution.py:152
  (1 shorter events, 0.0 us)
Async XLA Ops:
  2.9 7.9 %collective-permute-start = (bf16[8,4096]{1,0:T(8,128)(2,1)S(1)}, bf16[8,4096]{1,0:T(8,128)(2,1)S(1)}, u32[]{:S(2)}, u32[]{:S(2)}) collective-permute-start(bf16[8,4096]{1,0:T(8,128)(2,1)S(1)} %get-tuple-element.12), channel_id=1, source_target_pairs={{0,2},{1,3},{2,0},{3,1},{4,6},{5,7},{6,4},{7,5},{8,10},{9,11},{10,... | collective-permute-start | bytes 196616 | tf_op jit(solution)/shard_map/ppermute | solution.py:175
  7.0 6.2 %collective-permute-start.1 = (bf16[8,4096]{1,0:T(8,128)(2,1)S(1)}, bf16[8,4096]{1,0:T(8,128)(2,1)S(1)}, u32[]{:S(2)}, u32[]{:S(2)}) collective-permute-start(bf16[8,4096]{1,0:T(8,128)(2,1)S(1)} %get-tuple-element.13), channel_id=1, source_target_pairs={{0,3},{1,2},{2,1},{3,0},{4,7},{5,6},{6,5},{7,4},{8,11},{9,10},{10,... | collective-permute-start | bytes 196616 | tf_op jit(solution)/shard_map/ppermute | solution.py:175
  8.3 5.0 %collective-permute-start.2 = (bf16[8,4096]{1,0:T(8,128)(2,1)S(1)}, bf16[8,4096]{1,0:T(8,128)(2,1)S(1)}, u32[]{:S(2)}, u32[]{:S(2)}) collective-permute-start(bf16[8,4096]{1,0:T(8,128)(2,1)S(1)} %get-tuple-element.14), channel_id=1, source_target_pairs={{0,1},{1,0},{2,3},{3,2},{4,5},{5,4},{6,7},{7,6},{8,9},{9,8},{10,11... | collective-permute-start | bytes 196616 | tf_op jit(solution)/shard_map/ppermute | solution.py:175
  13.3 5.9 %collective-permute-start.5 = (bf16[8,4096]{1,0:T(8,128)(2,1)S(1)}, bf16[8,4096]{1,0:T(8,128)(2,1)S(1)}, u32[]{:S(2)}, u32[]{:S(2)}) collective-permute-start(bf16[8,4096]{1,0:T(8,128)(2,1)S(1)} %add_convert_fusion.refs_0_), channel_id=1, source_target_pairs={{0,24},{4,28},{8,16},{12,20},{16,8},{20,12},{24,0},{28,4},{1,25},{... | collective-permute-start | bytes 196616 | tf_op jit(solution)/shard_map/ppermute | solution.py:175
  15.8 4.3 %collective-permute-start.3 = (bf16[8,4096]{1,0:T(8,128)(2,1)S(1)}, bf16[8,4096]{1,0:T(8,128)(2,1)S(1)}, u32[]{:S(2)}, u32[]{:S(2)}) collective-permute-start(bf16[8,4096]{1,0:T(8,128)(2,1)S(1)} %add_convert_fusion.refs_0_), channel_id=1, source_target_pairs={{0,8},{4,20},{8,0},{12,28},{16,24},{20,4},{24,16},{28,12},{1,9},{5... | collective-permute-start | bytes 196616 | tf_op jit(solution)/shard_map/ppermute | solution.py:193
  16.4 4.3 %collective-permute-start.4 = (bf16[8,4096]{1,0:T(8,128)(2,1)S(1)}, bf16[8,4096]{1,0:T(8,128)(2,1)S(1)}, u32[]{:S(2)}, u32[]{:S(2)}) collective-permute-start(bf16[8,4096]{1,0:T(8,128)(2,1)S(1)} %add_convert_fusion.refs_0_), channel_id=1, source_target_pairs={{0,16},{4,12},{8,24},{12,4},{16,0},{20,28},{24,8},{28,20},{1,17},{... | collective-permute-start | bytes 196616 | tf_op jit(solution)/shard_map/ppermute | solution.py:193
  16.9 3.8 %collective-permute-start.6 = (bf16[8,4096]{1,0:T(8,128)(2,1)S(1)}, bf16[8,4096]{1,0:T(8,128)(2,1)S(1)}, u32[]{:S(2)}, u32[]{:S(2)}) collective-permute-start(bf16[8,4096]{1,0:T(8,128)(2,1)S(1)} %add_convert_fusion.refs_0_), channel_id=1, source_target_pairs={{0,4},{4,0},{8,12},{12,8},{16,20},{20,16},{24,28},{28,24},{1,5},{5... | collective-permute-start | bytes 196616 | tf_op jit(solution)/shard_map/ppermute | solution.py:175
  19.2 1.5 %collective-permute-start.7 = (bf16[8,4096]{1,0:T(8,128)(2,1)S(1)}, bf16[8,4096]{1,0:T(8,128)(2,1)S(1)}, u32[]{:S(2)}, u32[]{:S(2)}) collective-permute-start(bf16[8,4096]{1,0:T(8,128)(2,1)S(1)} %collective-permute-done.5.refs_3_), channel_id=1, source_target_pairs={{0,4},{4,0},{8,12},{12,8},{16,20},{20,16},{24,28},{28,24},{1,5},{5... | collective-permute-start | bytes 196616 | tf_op jit(solution)/shard_map/ppermute | solution.py:175
  20.1 1.3 %collective-permute-start.8 = (bf16[8,4096]{1,0:T(8,128)(2,1)S(1)}, bf16[8,4096]{1,0:T(8,128)(2,1)S(1)}, u32[]{:S(2)}, u32[]{:S(2)}) collective-permute-start(bf16[8,4096]{1,0:T(8,128)(2,1)S(1)} %collective-permute-done.3.refs_1_), channel_id=1, source_target_pairs={{0,4},{4,0},{8,12},{12,8},{16,20},{20,16},{24,28},{28,24},{1,5},{5... | collective-permute-start | bytes 196616 | tf_op jit(solution)/shard_map/ppermute | solution.py:175
  20.6 1.3 %collective-permute-start.9 = (bf16[8,4096]{1,0:T(8,128)(2,1)S(1)}, bf16[8,4096]{1,0:T(8,128)(2,1)S(1)}, u32[]{:S(2)}, u32[]{:S(2)}) collective-permute-start(bf16[8,4096]{1,0:T(8,128)(2,1)S(1)} %collective-permute-done.4.refs_2_), channel_id=1, source_target_pairs={{0,4},{4,0},{8,12},{12,8},{16,20},{20,16},{24,28},{28,24},{1,5},{5... | collective-permute-start | bytes 196616 | tf_op jit(solution)/shard_map/ppermute | solution.py:175

commit v21 on v15

--- a/solution.py
+++ b/solution.py
@@ -112,7 +112,7 @@
     products = lax.dot_general(
         features, query[...], ROW_BY_ROW, preferred_element_type=jnp.float32
     )
-    own, second, first, third, own_next, second_next, first_next, third_next = (
+    own, second, third, first, own_next, second_next, third_next, first_next = (
         products[i * doc_dev : (i + 1) * doc_dev] for i in range(len(blocks))
     )
     ex = lax.axis_index("ex")
@@ -167,7 +167,7 @@
     turns = [[(i, i ^ (first if i % 2 else 6 - first)) for i in range(ex_count)] for first in (2, 4)]
     third = exchange(features, "ex", 6)
     first, second = (lax.ppermute(features, "ex", turn) for turn in turns)
-    held = (features, second, first, third)
+    held = (features, second, third, first)
     return block_scores(query_features, held, [exchange(block, "ex", 1) for block in held])
 
 

time: 23.1 us -> 23.1 us (level)
    ppermute x8, starting transfers between devices: 8.21 us -> 7.13 us  [exchange(): lax.ppermute(block, axis, [(i, i ^ flip) for i in range(lax.axis_size(axi...]
    ppermute x2, starting transfers between devices: 1.04 us -> 2.12 us  [body(): first, second = (lax.ppermute(features, 'ex', turn) for turn in turns)]
    ppermute x2, waiting for transfers between devices: 2.05 us -> 2.43 us  [body(): first, second = (lax.ppermute(features, 'ex', turn) for turn in turns)]
    ppermute x8, waiting for transfers between devices: 7.66 us -> 7.27 us  [exchange(): lax.ppermute(block, axis, [(i, i ^ flip) for i in range(lax.axis_size(axi...]
where the time goes in v21:
time: 23.1 us; the launch traced here: 22.9 us
  waiting for transfers between devices  9.7 us (42%)
  starting transfers between devices  9.24 us (40%)
  Pallas kernels  3.89 us (17%)
    ppermute x8, waiting for transfers between devices, exchange(): lax.ppermute(block, axis, [(i, i ^ flip) for i in range(lax.axis_size(axi...  7.27 us
    ppermute x8, starting transfers between devices, exchange(): lax.ppermute(block, axis, [(i, i ^ flip) for i in range(lax.axis_size(axi...  7.13 us
    pallas_call x1, Pallas kernels, feature_shares(): pl.pallas_call(feature_kernel, out_shape=[jax.ShapeDtypeStruct((doc_dev,...  2.9 us
    ppermute x2, waiting for transfers between devices, body(): first, second = (lax.ppermute(features, 'ex', turn) for turn in turns)  2.43 us
    ppermute x2, starting transfers between devices, body(): first, second = (lax.ppermute(features, 'ex', turn) for turn in turns)  2.12 us
    pallas_call x1, Pallas kernels, block_scores(): pl.pallas_call(score_kernel, out_shape=jax.ShapeDtypeStruct((query_featur...  0.99 us
  transfers between devices with their start and end apart: 10, of which 8 were waited for; matrix products, arithmetic and copies ran while one was open for 0% of the time, Pallas kernels for 0%

profile of v21, /device:TPU:0, one launch (start us, length us, event | category | flops | bytes accessed | tf_op | source)
XLA Modules:
  0.0 22.9 jit_solution(11641429406971935406)
XLA Ops:
  0.0 0.0 copy-start
  0.0 2.9 %features.1 = (f32[8,4096]{1,0:T(8,128)S(1)}, bf16[8,4096]{1,0:T(8,128)(2,1)S(1)}, bf16[8,4096]{1,0:T(8,128)(2,1)S(1)}, bf16[8,4096]{1,0:T(8,128)(2,1)S(1)}) custom-call(s32[1,32]{1,0:T(1,128)} %lengths_hbm.1, s32[1,32]{1,0:T(1,128)} %owners_hbm.1, bf16[2048,128]{1,0:T(8,128)(2,1)} %rows_hbm.1), custom_call_target="tpu_custom_call" | custom-call | tf_op jit(solution)/shard_map/features/pallas_call | solution.py:86
  2.9 4.1 %collective-permute-start = (bf16[8,4096]{1,0:T(8,128)(2,1)S(1)}, bf16[8,4096]{1,0:T(8,128)(2,1)S(1)}, u32[]{:S(2)}, u32[]{:S(2)}) collective-permute-start(bf16[8,4096]{1,0:T(8,128)(2,1)S(1)} %get-tuple-element.10), channel_id=1, source_target_pairs={{0,2},{1,3},{2,0},{3,1},{4,6},{5,7},{6,4},{7,5},{8,10},{9,11},{10,... | collective-permute-start | bytes 196616 | tf_op jit(solution)/shard_map/ppermute | solution.py:153
  7.0 1.3 %collective-permute-start.1 = (bf16[8,4096]{1,0:T(8,128)(2,1)S(1)}, bf16[8,4096]{1,0:T(8,128)(2,1)S(1)}, u32[]{:S(2)}, u32[]{:S(2)}) collective-permute-start(bf16[8,4096]{1,0:T(8,128)(2,1)S(1)} %get-tuple-element.11), channel_id=1, source_target_pairs={{0,3},{1,2},{2,1},{3,0},{4,7},{5,6},{6,5},{7,4},{8,11},{9,10},{10,... | collective-permute-start | bytes 196616 | tf_op jit(solution)/shard_map/ppermute | solution.py:153
  8.4 0.2 collective-permute-start.2
  8.6 2.2 %collective-permute-done = bf16[8,4096]{1,0:T(8,128)(2,1)S(1)} collective-permute-done((bf16[8,4096]{1,0:T(8,128)(2,1)S(1)}, bf16[8,4096]{1,0:T(8,128)(2,1)S(1)}, u32[]{:S(2)}, u32[]{:S(2)}) %collective-permute-start) | collective-permute-done | bytes 65568 | tf_op jit(solution)/shard_map/ppermute | solution.py:153
  10.8 2.5 %collective-permute-done.1 = bf16[8,4096]{1,0:T(8,128)(2,1)S(1)} collective-permute-done((bf16[8,4096]{1,0:T(8,128)(2,1)S(1)}, bf16[8,4096]{1,0:T(8,128)(2,1)S(1)}, u32[]{:S(2)}, u32[]{:S(2)}) %collective-permute-start.1) | collective-permute-done | bytes 65568 | tf_op jit(solution)/shard_map/ppermute | solution.py:153
  13.2 0.1 collective-permute-done.2
  13.4 1.6 %collective-permute-start.5 = (bf16[8,4096]{1,0:T(8,128)(2,1)S(1)}, bf16[8,4096]{1,0:T(8,128)(2,1)S(1)}, u32[]{:S(2)}, u32[]{:S(2)}) collective-permute-start(bf16[8,4096]{1,0:T(8,128)(2,1)S(1)} %add_convert_fusion.refs_0_), channel_id=1, source_target_pairs={{0,16},{4,12},{8,24},{12,4},{16,0},{20,28},{24,8},{28,20},{1,17},{... | collective-permute-start | bytes 196616 | tf_op jit(solution)/shard_map/ppermute | solution.py:169
  15.0 1.4 %collective-permute-start.4 = (bf16[8,4096]{1,0:T(8,128)(2,1)S(1)}, bf16[8,4096]{1,0:T(8,128)(2,1)S(1)}, u32[]{:S(2)}, u32[]{:S(2)}) collective-permute-start(bf16[8,4096]{1,0:T(8,128)(2,1)S(1)} %add_convert_fusion.refs_0_), channel_id=1, source_target_pairs={{0,24},{4,28},{8,16},{12,20},{16,8},{20,12},{24,0},{28,4},{1,25},{... | collective-permute-start | bytes 196616 | tf_op jit(solution)/shard_map/ppermute | solution.py:153
  16.4 0.5 %collective-permute-start.3 = (bf16[8,4096]{1,0:T(8,128)(2,1)S(1)}, bf16[8,4096]{1,0:T(8,128)(2,1)S(1)}, u32[]{:S(2)}, u32[]{:S(2)}) collective-permute-start(bf16[8,4096]{1,0:T(8,128)(2,1)S(1)} %add_convert_fusion.refs_0_), channel_id=1, source_target_pairs={{0,8},{4,20},{8,0},{12,28},{16,24},{20,4},{24,16},{28,12},{1,9},{5... | collective-permute-start | bytes 196616 | tf_op jit(solution)/shard_map/ppermute | solution.py:169
  16.9 0.0 collective-permute-start.6
  16.9 1.9 %collective-permute-done.5.refs_3_ = bf16[8,4096]{1,0:T(8,128)(2,1)S(1)} collective-permute-done((bf16[8,4096]{1,0:T(8,128)(2,1)S(1)}, bf16[8,4096]{1,0:T(8,128)(2,1)S(1)}, u32[]{:S(2)}, u32[]{:S(2)}) %collective-permute-start.5) | collective-permute-done | bytes 65568 | tf_op jit(solution)/shard_map/ppermute | solution.py:169
  18.8 0.0 collective-permute-start.9
  18.8 1.3 %collective-permute-done.4.refs_2_ = bf16[8,4096]{1,0:T(8,128)(2,1)S(1)} collective-permute-done((bf16[8,4096]{1,0:T(8,128)(2,1)S(1)}, bf16[8,4096]{1,0:T(8,128)(2,1)S(1)}, u32[]{:S(2)}, u32[]{:S(2)}) %collective-permute-start.4) | collective-permute-done | bytes 65568 | tf_op jit(solution)/shard_map/ppermute | solution.py:153
  20.1 0.0 collective-permute-start.8
  20.1 0.5 %collective-permute-done.3.refs_1_ = bf16[8,4096]{1,0:T(8,128)(2,1)S(1)} collective-permute-done((bf16[8,4096]{1,0:T(8,128)(2,1)S(1)}, bf16[8,4096]{1,0:T(8,128)(2,1)S(1)}, u32[]{:S(2)}, u32[]{:S(2)}) %collective-permute-start.3) | collective-permute-done | bytes 65568 | tf_op jit(solution)/shard_map/ppermute | solution.py:169
  20.7 0.0 collective-permute-start.7
  20.7 0.0 collective-permute-done.6.refs_4_
  20.7 0.0 collective-permute-done.9.refs_7_
  20.7 0.7 %collective-permute-done.8.refs_6_ = bf16[8,4096]{1,0:T(8,128)(2,1)S(1)} collective-permute-done((bf16[8,4096]{1,0:T(8,128)(2,1)S(1)}, bf16[8,4096]{1,0:T(8,128)(2,1)S(1)}, u32[]{:S(2)}, u32[]{:S(2)}) %collective-permute-start.8) | collective-permute-done | bytes 65568 | tf_op jit(solution)/shard_map/ppermute | solution.py:153
  21.4 0.5 %collective-permute-done.7.refs_5_ = bf16[8,4096]{1,0:T(8,128)(2,1)S(1)} collective-permute-done((bf16[8,4096]{1,0:T(8,128)(2,1)S(1)}, bf16[8,4096]{1,0:T(8,128)(2,1)S(1)}, u32[]{:S(2)}, u32[]{:S(2)}) %collective-permute-start.7) | collective-permute-done | bytes 65568 | tf_op jit(solution)/shard_map/ppermute | solution.py:153
  21.9 0.0 copy-done
  21.9 1.0 %scores.1 = f32[64,64]{1,0:T(8,128)} custom-call(bf16[64,4096]{1,0:T(8,128)(2,1)S(1)} %copy-done, bf16[8,4096]{1,0:T(8,128)(2,1)S(1)} %add_convert_fusion.refs_0_, bf16[8,4096]{1,0:T(8,128)(2,1)S(1)} %collective-permute-done.3.refs_1_, bf16[8,4096]{1,0:T(8,128)(2,1)S(1)} %collective-permute-done.4.refs_2_, ...), custom_call_target="tpu_custom_call" | custom-call | tf_op jit(solution)/shard_map/scores/pallas_call | solution.py:142
  (1 shorter events, 0.0 us)
Async XLA Ops:
  0.0 21.9 %copy-start = (bf16[64,4096]{1,0:T(8,128)(2,1)S(1)}, bf16[64,4096]{1,0:T(8,128)(2,1)}, u32[]{:S(2)}) copy-start(bf16[64,4096]{1,0:T(8,128)(2,1)} %query.1) | copy-start | bytes 1572868
  2.9 7.9 %collective-permute-start = (bf16[8,4096]{1,0:T(8,128)(2,1)S(1)}, bf16[8,4096]{1,0:T(8,128)(2,1)S(1)}, u32[]{:S(2)}, u32[]{:S(2)}) collective-permute-start(bf16[8,4096]{1,0:T(8,128)(2,1)S(1)} %get-tuple-element.10), channel_id=1, source_target_pairs={{0,2},{1,3},{2,0},{3,1},{4,6},{5,7},{6,4},{7,5},{8,10},{9,11},{10,... | collective-permute-start | bytes 196616 | tf_op jit(solution)/shard_map/ppermute | solution.py:153
  7.0 6.2 %collective-permute-start.1 = (bf16[8,4096]{1,0:T(8,128)(2,1)S(1)}, bf16[8,4096]{1,0:T(8,128)(2,1)S(1)}, u32[]{:S(2)}, u32[]{:S(2)}) collective-permute-start(bf16[8,4096]{1,0:T(8,128)(2,1)S(1)} %get-tuple-element.11), channel_id=1, source_target_pairs={{0,3},{1,2},{2,1},{3,0},{4,7},{5,6},{6,5},{7,4},{8,11},{9,10},{10,... | collective-permute-start | bytes 196616 | tf_op jit(solution)/shard_map/ppermute | solution.py:153
  8.4 5.0 %collective-permute-start.2 = (bf16[8,4096]{1,0:T(8,128)(2,1)S(1)}, bf16[8,4096]{1,0:T(8,128)(2,1)S(1)}, u32[]{:S(2)}, u32[]{:S(2)}) collective-permute-start(bf16[8,4096]{1,0:T(8,128)(2,1)S(1)} %get-tuple-element.12), channel_id=1, source_target_pairs={{0,1},{1,0},{2,3},{3,2},{4,5},{5,4},{6,7},{7,6},{8,9},{9,8},{10,11... | collective-permute-start | bytes 196616 | tf_op jit(solution)/shard_map/ppermute | solution.py:153
  13.4 5.5 %collective-permute-start.5 = (bf16[8,4096]{1,0:T(8,128)(2,1)S(1)}, bf16[8,4096]{1,0:T(8,128)(2,1)S(1)}, u32[]{:S(2)}, u32[]{:S(2)}) collective-permute-start(bf16[8,4096]{1,0:T(8,128)(2,1)S(1)} %add_convert_fusion.refs_0_), channel_id=1, source_target_pairs={{0,16},{4,12},{8,24},{12,4},{16,0},{20,28},{24,8},{28,20},{1,17},{... | collective-permute-start | bytes 196616 | tf_op jit(solution)/shard_map/ppermute | solution.py:169
  15.0 5.2 %collective-permute-start.4 = (bf16[8,4096]{1,0:T(8,128)(2,1)S(1)}, bf16[8,4096]{1,0:T(8,128)(2,1)S(1)}, u32[]{:S(2)}, u32[]{:S(2)}) collective-permute-start(bf16[8,4096]{1,0:T(8,128)(2,1)S(1)} %add_convert_fusion.refs_0_), channel_id=1, source_target_pairs={{0,24},{4,28},{8,16},{12,20},{16,8},{20,12},{24,0},{28,4},{1,25},{... | collective-permute-start | bytes 196616 | tf_op jit(solution)/shard_map/ppermute | solution.py:153
  16.4 4.3 %collective-permute-start.3 = (bf16[8,4096]{1,0:T(8,128)(2,1)S(1)}, bf16[8,4096]{1,0:T(8,128)(2,1)S(1)}, u32[]{:S(2)}, u32[]{:S(2)}) collective-permute-start(bf16[8,4096]{1,0:T(8,128)(2,1)S(1)} %add_convert_fusion.refs_0_), channel_id=1, source_target_pairs={{0,8},{4,20},{8,0},{12,28},{16,24},{20,4},{24,16},{28,12},{1,9},{5... | collective-permute-start | bytes 196616 | tf_op jit(solution)/shard_map/ppermute | solution.py:169
  16.9 3.7 %collective-permute-start.6 = (bf16[8,4096]{1,0:T(8,128)(2,1)S(1)}, bf16[8,4096]{1,0:T(8,128)(2,1)S(1)}, u32[]{:S(2)}, u32[]{:S(2)}) collective-permute-start(bf16[8,4096]{1,0:T(8,128)(2,1)S(1)} %add_convert_fusion.refs_0_), channel_id=1, source_target_pairs={{0,4},{4,0},{8,12},{12,8},{16,20},{20,16},{24,28},{28,24},{1,5},{5... | collective-permute-start | bytes 196616 | tf_op jit(solution)/shard_map/ppermute | solution.py:153
  18.8 1.8 %collective-permute-start.9 = (bf16[8,4096]{1,0:T(8,128)(2,1)S(1)}, bf16[8,4096]{1,0:T(8,128)(2,1)S(1)}, u32[]{:S(2)}, u32[]{:S(2)}) collective-permute-start(bf16[8,4096]{1,0:T(8,128)(2,1)S(1)} %collective-permute-done.5.refs_3_), channel_id=1, source_target_pairs={{0,4},{4,0},{8,12},{12,8},{16,20},{20,16},{24,28},{28,24},{1,5},{5... | collective-permute-start | bytes 196616 | tf_op jit(solution)/shard_map/ppermute | solution.py:153
  20.1 1.3 %collective-permute-start.8 = (bf16[8,4096]{1,0:T(8,128)(2,1)S(1)}, bf16[8,4096]{1,0:T(8,128)(2,1)S(1)}, u32[]{:S(2)}, u32[]{:S(2)}) collective-permute-start(bf16[8,4096]{1,0:T(8,128)(2,1)S(1)} %collective-permute-done.4.refs_2_), channel_id=1, source_target_pairs={{0,4},{4,0},{8,12},{12,8},{16,20},{20,16},{24,28},{28,24},{1,5},{5... | collective-permute-start | bytes 196616 | tf_op jit(solution)/shard_map/ppermute | solution.py:153
  20.7 1.3 %collective-permute-start.7 = (bf16[8,4096]{1,0:T(8,128)(2,1)S(1)}, bf16[8,4096]{1,0:T(8,128)(2,1)S(1)}, u32[]{:S(2)}, u32[]{:S(2)}) collective-permute-start(bf16[8,4096]{1,0:T(8,128)(2,1)S(1)} %collective-permute-done.3.refs_1_), channel_id=1, source_target_pairs={{0,4},{4,0},{8,12},{12,8},{16,20},{20,16},{24,28},{28,24},{1,5},{5... | collective-permute-start | bytes 196616 | tf_op jit(solution)/shard_map/ppermute | solution.py:153

commit v22 on v20

--- a/solution.py
+++ b/solution.py
@@ -50,15 +50,16 @@
     for b in range(blocks):
         part = slice(b * LANES, (b + 1) * LANES)
         turned = lax.dot_general(eye, rows[part, :], ROW_BY_ROW, preferred_element_type=jnp.float32)
+        turned = turned.astype(rows.dtype)
         for digits, values, target in (
             (share_of, turned[:width], inputs),
             (row_of, turned[width:], grads),
         ):
-            digit = jnp.broadcast_to(digits[b : b + 1, :], (8, LANES))[None]
-            values = values.reshape(-1, 8, LANES)
+            digit = jnp.broadcast_to(digits[b : b + 1, :], (16, LANES))
+            values = values.reshape(-1, 16, LANES)
             for at in range(target.shape[0] // width):
-                kept = jnp.where(digit == at, values, 0.0).reshape(width, LANES)
-                target[at * width : (at + 1) * width, part] = kept.astype(target.dtype)
+                mask = jnp.where(digit == at, 1.0, 0.0).astype(values.dtype)
+                target[at * width : (at + 1) * width, part] = (values * mask[None]).reshape(width, LANES)
     product = lax.dot_general(
         grads[...], inputs[...], ROW_BY_ROW, preferred_element_type=jnp.float32
     )

time: 23 us -> 23.1 us (level)
  no operation moved by 1% of the time
where the time goes in v22:
time: 23.1 us; the launch traced here: 22.9 us
  waiting for transfers between devices  9.44 us (41%)
  starting transfers between devices  9.25 us (40%)
  Pallas kernels  4.16 us (18%)
    ppermute x8, starting transfers between devices, exchange(): lax.ppermute(block, axis, [(i, i ^ flip) for i in range(lax.axis_size(axi...  8.2 us
    ppermute x8, waiting for transfers between devices, exchange(): lax.ppermute(block, axis, [(i, i ^ flip) for i in range(lax.axis_size(axi...  8 us
    pallas_call x1, Pallas kernels, feature_shares(): pl.pallas_call(feature_kernel, out_shape=[jax.ShapeDtypeStruct((doc_dev,...  2.93 us
    ppermute x2, waiting for transfers between devices, body(): first, second = (lax.ppermute(features, 'ex', turn) for turn in turns)  1.44 us
    pallas_call x2, Pallas kernels, call_on_vmem(): pl.pallas_call(kernel, out_shape=jax.ShapeDtypeStruct(shape, jnp.float32)...  1.23 us
    ppermute x2, starting transfers between devices, body(): first, second = (lax.ppermute(features, 'ex', turn) for turn in turns)  1.04 us
  transfers between devices with their start and end apart: 10, of which 8 were waited for; matrix products, arithmetic and copies ran while one was open for 0% of the time, Pallas kernels for 1%

profile of v22, /device:TPU:0, one launch (start us, length us, event | category | flops | bytes accessed | tf_op | source)
XLA Modules:
  0.0 22.9 jit_solution(1856512418348620931)
XLA Ops:
  0.0 2.9 %features.1 = (f32[8,4096]{1,0:T(8,128)S(1)}, bf16[8,4096]{1,0:T(8,128)(2,1)S(1)}, bf16[8,4096]{1,0:T(8,128)(2,1)S(1)}, bf16[8,4096]{1,0:T(8,128)(2,1)S(1)}, bf16[64,4096]{1,0:T(8,128)(2,1)S(1)}) custom-call(s32[1,32]{1,0:T(1,128)} %lengths_hbm.1, s32[1,32]{1,0:T(1,128)} %owners_hbm.1, bf16[2048,128]{1,0:T(8,128)(2,1)} %rows_hbm.1, bf16[64,4096]{1,0:T(8,128)(2,1)} %query_hbm.1), custom_call_target="tpu_custom_call" | custom-call | tf_op jit(solution)/shard_map/features/pallas_call | solution.py:89
  2.9 4.1 %collective-permute-start = (bf16[8,4096]{1,0:T(8,128)(2,1)S(1)}, bf16[8,4096]{1,0:T(8,128)(2,1)S(1)}, u32[]{:S(2)}, u32[]{:S(2)}) collective-permute-start(bf16[8,4096]{1,0:T(8,128)(2,1)S(1)} %get-tuple-element.12), channel_id=1, source_target_pairs={{0,2},{1,3},{2,0},{3,1},{4,6},{5,7},{6,4},{7,5},{8,10},{9,11},{10,... | collective-permute-start | bytes 196616 | tf_op jit(solution)/shard_map/ppermute | solution.py:176
  7.0 1.4 %collective-permute-start.1 = (bf16[8,4096]{1,0:T(8,128)(2,1)S(1)}, bf16[8,4096]{1,0:T(8,128)(2,1)S(1)}, u32[]{:S(2)}, u32[]{:S(2)}) collective-permute-start(bf16[8,4096]{1,0:T(8,128)(2,1)S(1)} %get-tuple-element.13), channel_id=1, source_target_pairs={{0,3},{1,2},{2,1},{3,0},{4,7},{5,6},{6,5},{7,4},{8,11},{9,10},{10,... | collective-permute-start | bytes 196616 | tf_op jit(solution)/shard_map/ppermute | solution.py:176
  8.4 0.2 collective-permute-start.2
  8.6 2.2 %collective-permute-done = bf16[8,4096]{1,0:T(8,128)(2,1)S(1)} collective-permute-done((bf16[8,4096]{1,0:T(8,128)(2,1)S(1)}, bf16[8,4096]{1,0:T(8,128)(2,1)S(1)}, u32[]{:S(2)}, u32[]{:S(2)}) %collective-permute-start) | collective-permute-done | bytes 65568 | tf_op jit(solution)/shard_map/ppermute | solution.py:176
  10.8 2.5 %collective-permute-done.1 = bf16[8,4096]{1,0:T(8,128)(2,1)S(1)} collective-permute-done((bf16[8,4096]{1,0:T(8,128)(2,1)S(1)}, bf16[8,4096]{1,0:T(8,128)(2,1)S(1)}, u32[]{:S(2)}, u32[]{:S(2)}) %collective-permute-start.1) | collective-permute-done | bytes 65568 | tf_op jit(solution)/shard_map/ppermute | solution.py:176
  13.3 0.1 collective-permute-done.2
  13.4 2.5 %collective-permute-start.5 = (bf16[8,4096]{1,0:T(8,128)(2,1)S(1)}, bf16[8,4096]{1,0:T(8,128)(2,1)S(1)}, u32[]{:S(2)}, u32[]{:S(2)}) collective-permute-start(bf16[8,4096]{1,0:T(8,128)(2,1)S(1)} %add_convert_fusion.refs_0_), channel_id=1, source_target_pairs={{0,24},{4,28},{8,16},{12,20},{16,8},{20,12},{24,0},{28,4},{1,25},{... | collective-permute-start | bytes 196616 | tf_op jit(solution)/shard_map/ppermute | solution.py:176
  15.9 0.5 %collective-permute-start.3 = (bf16[8,4096]{1,0:T(8,128)(2,1)S(1)}, bf16[8,4096]{1,0:T(8,128)(2,1)S(1)}, u32[]{:S(2)}, u32[]{:S(2)}) collective-permute-start(bf16[8,4096]{1,0:T(8,128)(2,1)S(1)} %add_convert_fusion.refs_0_), channel_id=1, source_target_pairs={{0,8},{4,20},{8,0},{12,28},{16,24},{20,4},{24,16},{28,12},{1,9},{5... | collective-permute-start | bytes 196616 | tf_op jit(solution)/shard_map/ppermute | solution.py:194
  16.4 0.5 %collective-permute-start.4 = (bf16[8,4096]{1,0:T(8,128)(2,1)S(1)}, bf16[8,4096]{1,0:T(8,128)(2,1)S(1)}, u32[]{:S(2)}, u32[]{:S(2)}) collective-permute-start(bf16[8,4096]{1,0:T(8,128)(2,1)S(1)} %add_convert_fusion.refs_0_), channel_id=1, source_target_pairs={{0,16},{4,12},{8,24},{12,4},{16,0},{20,28},{24,8},{28,20},{1,17},{... | collective-permute-start | bytes 196616 | tf_op jit(solution)/shard_map/ppermute | solution.py:194
  17.0 0.0 collective-permute-start.6
  17.0 2.3 %collective-permute-done.5.refs_3_ = bf16[8,4096]{1,0:T(8,128)(2,1)S(1)} collective-permute-done((bf16[8,4096]{1,0:T(8,128)(2,1)S(1)}, bf16[8,4096]{1,0:T(8,128)(2,1)S(1)}, u32[]{:S(2)}, u32[]{:S(2)}) %collective-permute-start.5) | collective-permute-done | bytes 65568 | tf_op jit(solution)/shard_map/ppermute | solution.py:176
  19.3 0.0 collective-permute-start.7
  19.3 0.9 %collective-permute-done.3.refs_1_ = bf16[8,4096]{1,0:T(8,128)(2,1)S(1)} collective-permute-done((bf16[8,4096]{1,0:T(8,128)(2,1)S(1)}, bf16[8,4096]{1,0:T(8,128)(2,1)S(1)}, u32[]{:S(2)}, u32[]{:S(2)}) %collective-permute-start.3) | collective-permute-done | bytes 65568 | tf_op jit(solution)/shard_map/ppermute | solution.py:194
  20.2 0.0 collective-permute-start.8
  20.2 0.5 %collective-permute-done.4.refs_2_ = bf16[8,4096]{1,0:T(8,128)(2,1)S(1)} collective-permute-done((bf16[8,4096]{1,0:T(8,128)(2,1)S(1)}, bf16[8,4096]{1,0:T(8,128)(2,1)S(1)}, u32[]{:S(2)}, u32[]{:S(2)}) %collective-permute-start.4) | collective-permute-done | bytes 65568 | tf_op jit(solution)/shard_map/ppermute | solution.py:194
  20.7 0.0 collective-permute-start.9
  20.7 0.0 collective-permute-done.6.refs_4_
  20.7 0.0 collective-permute-done.7.refs_5_
  20.7 0.3 %early_products.1.early = f32[48,64]{1,0:T(8,128)S(1)} custom-call(bf16[64,4096]{1,0:T(8,128)(2,1)S(1)} %get-tuple-element.10.query, bf16[8,4096]{1,0:T(8,128)(2,1)S(1)} %add_convert_fusion.refs_0_, bf16[8,4096]{1,0:T(8,128)(2,1)S(1)} %collective-permute-done.3.refs_1_, bf16[8,4096]{1,0:T(8,128)(2,1)S(1)} %collective-permute-done.4.refs_2_, ...), custom_call_target="tpu_custom_call" | custom-call | bytes 917504 | tf_op jit(solution)/shard_map/early_products/pallas_call | solution.py:153
  21.0 0.4 %collective-permute-done.8.refs_0_ = bf16[8,4096]{1,0:T(8,128)(2,1)S(1)} collective-permute-done((bf16[8,4096]{1,0:T(8,128)(2,1)S(1)}, bf16[8,4096]{1,0:T(8,128)(2,1)S(1)}, u32[]{:S(2)}, u32[]{:S(2)}) %collective-permute-start.8) | collective-permute-done | bytes 65568 | tf_op jit(solution)/shard_map/ppermute | solution.py:176
  21.4 0.5 %collective-permute-done.9.refs_1_ = bf16[8,4096]{1,0:T(8,128)(2,1)S(1)} collective-permute-done((bf16[8,4096]{1,0:T(8,128)(2,1)S(1)}, bf16[8,4096]{1,0:T(8,128)(2,1)S(1)}, u32[]{:S(2)}, u32[]{:S(2)}) %collective-permute-start.9) | collective-permute-done | bytes 65568 | tf_op jit(solution)/shard_map/ppermute | solution.py:176
  22.0 1.0 %scores.1 = f32[64,64]{1,0:T(8,128)} custom-call(bf16[64,4096]{1,0:T(8,128)(2,1)S(1)} %get-tuple-element.10.query, f32[48,64]{1,0:T(8,128)S(1)} %early_products.1.early, bf16[8,4096]{1,0:T(8,128)(2,1)S(1)} %collective-permute-done.8.refs_0_, bf16[8,4096]{1,0:T(8,128)(2,1)S(1)} %collective-permute-done.9.refs_1_), custom_call_target="tpu_custom_call" | custom-call | bytes 667648 | tf_op jit(solution)/shard_map/scores/pallas_call | solution.py:153
  (1 shorter events, 0.0 us)
Async XLA Ops:
  2.9 7.9 %collective-permute-start = (bf16[8,4096]{1,0:T(8,128)(2,1)S(1)}, bf16[8,4096]{1,0:T(8,128)(2,1)S(1)}, u32[]{:S(2)}, u32[]{:S(2)}) collective-permute-start(bf16[8,4096]{1,0:T(8,128)(2,1)S(1)} %get-tuple-element.12), channel_id=1, source_target_pairs={{0,2},{1,3},{2,0},{3,1},{4,6},{5,7},{6,4},{7,5},{8,10},{9,11},{10,... | collective-permute-start | bytes 196616 | tf_op jit(solution)/shard_map/ppermute | solution.py:176
  7.0 6.2 %collective-permute-start.1 = (bf16[8,4096]{1,0:T(8,128)(2,1)S(1)}, bf16[8,4096]{1,0:T(8,128)(2,1)S(1)}, u32[]{:S(2)}, u32[]{:S(2)}) collective-permute-start(bf16[8,4096]{1,0:T(8,128)(2,1)S(1)} %get-tuple-element.13), channel_id=1, source_target_pairs={{0,3},{1,2},{2,1},{3,0},{4,7},{5,6},{6,5},{7,4},{8,11},{9,10},{10,... | collective-permute-start | bytes 196616 | tf_op jit(solution)/shard_map/ppermute | solution.py:176
  8.4 5.0 %collective-permute-start.2 = (bf16[8,4096]{1,0:T(8,128)(2,1)S(1)}, bf16[8,4096]{1,0:T(8,128)(2,1)S(1)}, u32[]{:S(2)}, u32[]{:S(2)}) collective-permute-start(bf16[8,4096]{1,0:T(8,128)(2,1)S(1)} %get-tuple-element.14), channel_id=1, source_target_pairs={{0,1},{1,0},{2,3},{3,2},{4,5},{5,4},{6,7},{7,6},{8,9},{9,8},{10,11... | collective-permute-start | bytes 196616 | tf_op jit(solution)/shard_map/ppermute | solution.py:176
  13.4 5.9 %collective-permute-start.5 = (bf16[8,4096]{1,0:T(8,128)(2,1)S(1)}, bf16[8,4096]{1,0:T(8,128)(2,1)S(1)}, u32[]{:S(2)}, u32[]{:S(2)}) collective-permute-start(bf16[8,4096]{1,0:T(8,128)(2,1)S(1)} %add_convert_fusion.refs_0_), channel_id=1, source_target_pairs={{0,24},{4,28},{8,16},{12,20},{16,8},{20,12},{24,0},{28,4},{1,25},{... | collective-permute-start | bytes 196616 | tf_op jit(solution)/shard_map/ppermute | solution.py:176
  15.9 4.3 %collective-permute-start.3 = (bf16[8,4096]{1,0:T(8,128)(2,1)S(1)}, bf16[8,4096]{1,0:T(8,128)(2,1)S(1)}, u32[]{:S(2)}, u32[]{:S(2)}) collective-permute-start(bf16[8,4096]{1,0:T(8,128)(2,1)S(1)} %add_convert_fusion.refs_0_), channel_id=1, source_target_pairs={{0,8},{4,20},{8,0},{12,28},{16,24},{20,4},{24,16},{28,12},{1,9},{5... | collective-permute-start | bytes 196616 | tf_op jit(solution)/shard_map/ppermute | solution.py:194
  16.4 4.3 %collective-permute-start.4 = (bf16[8,4096]{1,0:T(8,128)(2,1)S(1)}, bf16[8,4096]{1,0:T(8,128)(2,1)S(1)}, u32[]{:S(2)}, u32[]{:S(2)}) collective-permute-start(bf16[8,4096]{1,0:T(8,128)(2,1)S(1)} %add_convert_fusion.refs_0_), channel_id=1, source_target_pairs={{0,16},{4,12},{8,24},{12,4},{16,0},{20,28},{24,8},{28,20},{1,17},{... | collective-permute-start | bytes 196616 | tf_op jit(solution)/shard_map/ppermute | solution.py:194
  17.0 3.8 %collective-permute-start.6 = (bf16[8,4096]{1,0:T(8,128)(2,1)S(1)}, bf16[8,4096]{1,0:T(8,128)(2,1)S(1)}, u32[]{:S(2)}, u32[]{:S(2)}) collective-permute-start(bf16[8,4096]{1,0:T(8,128)(2,1)S(1)} %add_convert_fusion.refs_0_), channel_id=1, source_target_pairs={{0,4},{4,0},{8,12},{12,8},{16,20},{20,16},{24,28},{28,24},{1,5},{5... | collective-permute-start | bytes 196616 | tf_op jit(solution)/shard_map/ppermute | solution.py:176
  19.3 1.5 %collective-permute-start.7 = (bf16[8,4096]{1,0:T(8,128)(2,1)S(1)}, bf16[8,4096]{1,0:T(8,128)(2,1)S(1)}, u32[]{:S(2)}, u32[]{:S(2)}) collective-permute-start(bf16[8,4096]{1,0:T(8,128)(2,1)S(1)} %collective-permute-done.5.refs_3_), channel_id=1, source_target_pairs={{0,4},{4,0},{8,12},{12,8},{16,20},{20,16},{24,28},{28,24},{1,5},{5... | collective-permute-start | bytes 196616 | tf_op jit(solution)/shard_map/ppermute | solution.py:176
  20.2 1.3 %collective-permute-start.8 = (bf16[8,4096]{1,0:T(8,128)(2,1)S(1)}, bf16[8,4096]{1,0:T(8,128)(2,1)S(1)}, u32[]{:S(2)}, u32[]{:S(2)}) collective-permute-start(bf16[8,4096]{1,0:T(8,128)(2,1)S(1)} %collective-permute-done.3.refs_1_), channel_id=1, source_target_pairs={{0,4},{4,0},{8,12},{12,8},{16,20},{20,16},{24,28},{28,24},{1,5},{5... | collective-permute-start | bytes 196616 | tf_op jit(solution)/shard_map/ppermute | solution.py:176
  20.7 1.3 %collective-permute-start.9 = (bf16[8,4096]{1,0:T(8,128)(2,1)S(1)}, bf16[8,4096]{1,0:T(8,128)(2,1)S(1)}, u32[]{:S(2)}, u32[]{:S(2)}) collective-permute-start(bf16[8,4096]{1,0:T(8,128)(2,1)S(1)} %collective-permute-done.4.refs_2_), channel_id=1, source_target_pairs={{0,4},{4,0},{8,12},{12,8},{16,20},{20,16},{24,28},{28,24},{1,5},{5... | collective-permute-start | bytes 196616 | tf_op jit(solution)/shard_map/ppermute | solution.py:176

commit v23 on v22

--- a/solution.py
+++ b/solution.py
@@ -126,7 +126,7 @@
     own, second, first, third, own_next, third_next = (
         early[i : i + doc_dev, :] for i in range(0, early.shape[0], doc_dev)
     )
-    second_next, first_next = late[:doc_dev], late[doc_dev:]
+    first_next, second_next = late[:doc_dev], late[doc_dev:]
     ex = lax.axis_index("ex")
     odd = lax.rem(ex, 2) == 1
     parts = [
@@ -169,7 +169,7 @@
         early_kernel, "early_products", (len(ready) * doc_dev, queries), query, *ready
     )
     shape = (queries, (len(ready) + 2) * doc_dev)
-    return call_on_vmem(score_kernel, "scores", shape, query, early, second_next, first_next)
+    return call_on_vmem(score_kernel, "scores", shape, query, early, first_next, second_next)
 
 
 def exchange(block, axis, flip):

time: 23.1 us -> 23 us (level)
    ppermute x8, waiting for transfers between devices: 8 us -> 7.37 us  [exchange(): lax.ppermute(block, axis, [(i, i ^ flip) for i in range(lax.axis_size(axi...]
    ppermute x2, waiting for transfers between devices: 1.44 us -> 2.05 us  [body(): first, second = (lax.ppermute(features, 'ex', turn) for turn in turns)]
where the time goes in v23:
time: 23 us; the launch traced here: 22.9 us
  waiting for transfers between devices  9.41 us (41%)
  starting transfers between devices  9.25 us (40%)
  Pallas kernels  4.16 us (18%)
    ppermute x8, starting transfers between devices, exchange(): lax.ppermute(block, axis, [(i, i ^ flip) for i in range(lax.axis_size(axi...  8.21 us
    ppermute x8, waiting for transfers between devices, exchange(): lax.ppermute(block, axis, [(i, i ^ flip) for i in range(lax.axis_size(axi...  7.37 us
    pallas_call x1, Pallas kernels, feature_shares(): pl.pallas_call(feature_kernel, out_shape=[jax.ShapeDtypeStruct((doc_dev,...  2.93 us
    ppermute x2, waiting for transfers between devices, body(): first, second = (lax.ppermute(features, 'ex', turn) for turn in turns)  2.05 us
    pallas_call x2, Pallas kernels, call_on_vmem(): pl.pallas_call(kernel, out_shape=jax.ShapeDtypeStruct(shape, jnp.float32)...  1.23 us
    ppermute x2, starting transfers between devices, body(): first, second = (lax.ppermute(features, 'ex', turn) for turn in turns)  1.04 us
  transfers between devices with their start and end apart: 10, of which 8 were waited for; matrix products, arithmetic and copies ran while one was open for 0% of the time, Pallas kernels for 1%

profile of v23, /device:TPU:0, one launch (start us, length us, event | category | flops | bytes accessed | tf_op | source)
XLA Modules:
  0.0 22.9 jit_solution(15205258179691793739)
XLA Ops:
  0.0 2.9 %features.1 = (f32[8,4096]{1,0:T(8,128)S(1)}, bf16[8,4096]{1,0:T(8,128)(2,1)S(1)}, bf16[8,4096]{1,0:T(8,128)(2,1)S(1)}, bf16[8,4096]{1,0:T(8,128)(2,1)S(1)}, bf16[64,4096]{1,0:T(8,128)(2,1)S(1)}) custom-call(s32[1,32]{1,0:T(1,128)} %lengths_hbm.1, s32[1,32]{1,0:T(1,128)} %owners_hbm.1, bf16[2048,128]{1,0:T(8,128)(2,1)} %rows_hbm.1, bf16[64,4096]{1,0:T(8,128)(2,1)} %query_hbm.1), custom_call_target="tpu_custom_call" | custom-call | tf_op jit(solution)/shard_map/features/pallas_call | solution.py:89
  2.9 4.1 %collective-permute-start = (bf16[8,4096]{1,0:T(8,128)(2,1)S(1)}, bf16[8,4096]{1,0:T(8,128)(2,1)S(1)}, u32[]{:S(2)}, u32[]{:S(2)}) collective-permute-start(bf16[8,4096]{1,0:T(8,128)(2,1)S(1)} %get-tuple-element.12), channel_id=1, source_target_pairs={{0,2},{1,3},{2,0},{3,1},{4,6},{5,7},{6,4},{7,5},{8,10},{9,11},{10,... | collective-permute-start | bytes 196616 | tf_op jit(solution)/shard_map/ppermute | solution.py:176
  7.0 1.4 %collective-permute-start.1 = (bf16[8,4096]{1,0:T(8,128)(2,1)S(1)}, bf16[8,4096]{1,0:T(8,128)(2,1)S(1)}, u32[]{:S(2)}, u32[]{:S(2)}) collective-permute-start(bf16[8,4096]{1,0:T(8,128)(2,1)S(1)} %get-tuple-element.13), channel_id=1, source_target_pairs={{0,3},{1,2},{2,1},{3,0},{4,7},{5,6},{6,5},{7,4},{8,11},{9,10},{10,... | collective-permute-start | bytes 196616 | tf_op jit(solution)/shard_map/ppermute | solution.py:176
  8.4 0.2 collective-permute-start.2
  8.6 2.2 %collective-permute-done = bf16[8,4096]{1,0:T(8,128)(2,1)S(1)} collective-permute-done((bf16[8,4096]{1,0:T(8,128)(2,1)S(1)}, bf16[8,4096]{1,0:T(8,128)(2,1)S(1)}, u32[]{:S(2)}, u32[]{:S(2)}) %collective-permute-start) | collective-permute-done | bytes 65568 | tf_op jit(solution)/shard_map/ppermute | solution.py:176
  10.8 2.5 %collective-permute-done.1 = bf16[8,4096]{1,0:T(8,128)(2,1)S(1)} collective-permute-done((bf16[8,4096]{1,0:T(8,128)(2,1)S(1)}, bf16[8,4096]{1,0:T(8,128)(2,1)S(1)}, u32[]{:S(2)}, u32[]{:S(2)}) %collective-permute-start.1) | collective-permute-done | bytes 65568 | tf_op jit(solution)/shard_map/ppermute | solution.py:176
  13.3 0.1 collective-permute-done.2
  13.4 2.5 %collective-permute-start.5 = (bf16[8,4096]{1,0:T(8,128)(2,1)S(1)}, bf16[8,4096]{1,0:T(8,128)(2,1)S(1)}, u32[]{:S(2)}, u32[]{:S(2)}) collective-permute-start(bf16[8,4096]{1,0:T(8,128)(2,1)S(1)} %add_convert_fusion.refs_0_), channel_id=1, source_target_pairs={{0,24},{4,28},{8,16},{12,20},{16,8},{20,12},{24,0},{28,4},{1,25},{... | collective-permute-start | bytes 196616 | tf_op jit(solution)/shard_map/ppermute | solution.py:176
  15.9 0.5 %collective-permute-start.4 = (bf16[8,4096]{1,0:T(8,128)(2,1)S(1)}, bf16[8,4096]{1,0:T(8,128)(2,1)S(1)}, u32[]{:S(2)}, u32[]{:S(2)}) collective-permute-start(bf16[8,4096]{1,0:T(8,128)(2,1)S(1)} %add_convert_fusion.refs_0_), channel_id=1, source_target_pairs={{0,16},{4,12},{8,24},{12,4},{16,0},{20,28},{24,8},{28,20},{1,17},{... | collective-permute-start | bytes 196616 | tf_op jit(solution)/shard_map/ppermute | solution.py:194
  16.4 0.5 %collective-permute-start.3 = (bf16[8,4096]{1,0:T(8,128)(2,1)S(1)}, bf16[8,4096]{1,0:T(8,128)(2,1)S(1)}, u32[]{:S(2)}, u32[]{:S(2)}) collective-permute-start(bf16[8,4096]{1,0:T(8,128)(2,1)S(1)} %add_convert_fusion.refs_0_), channel_id=1, source_target_pairs={{0,8},{4,20},{8,0},{12,28},{16,24},{20,4},{24,16},{28,12},{1,9},{5... | collective-permute-start | bytes 196616 | tf_op jit(solution)/shard_map/ppermute | solution.py:194
  17.0 0.0 collective-permute-start.6
  17.0 1.7 %collective-permute-done.5.refs_3_ = bf16[8,4096]{1,0:T(8,128)(2,1)S(1)} collective-permute-done((bf16[8,4096]{1,0:T(8,128)(2,1)S(1)}, bf16[8,4096]{1,0:T(8,128)(2,1)S(1)}, u32[]{:S(2)}, u32[]{:S(2)}) %collective-permute-start.5) | collective-permute-done | bytes 65568 | tf_op jit(solution)/shard_map/ppermute | solution.py:176
  18.6 0.0 collective-permute-start.7
  18.6 1.5 %collective-permute-done.4.refs_2_ = bf16[8,4096]{1,0:T(8,128)(2,1)S(1)} collective-permute-done((bf16[8,4096]{1,0:T(8,128)(2,1)S(1)}, bf16[8,4096]{1,0:T(8,128)(2,1)S(1)}, u32[]{:S(2)}, u32[]{:S(2)}) %collective-permute-start.4) | collective-permute-done | bytes 65568 | tf_op jit(solution)/shard_map/ppermute | solution.py:194
  20.2 0.0 collective-permute-start.8
  20.2 0.5 %collective-permute-done.3.refs_1_ = bf16[8,4096]{1,0:T(8,128)(2,1)S(1)} collective-permute-done((bf16[8,4096]{1,0:T(8,128)(2,1)S(1)}, bf16[8,4096]{1,0:T(8,128)(2,1)S(1)}, u32[]{:S(2)}, u32[]{:S(2)}) %collective-permute-start.3) | collective-permute-done | bytes 65568 | tf_op jit(solution)/shard_map/ppermute | solution.py:194
  20.7 0.0 collective-permute-start.9
  20.7 0.0 collective-permute-done.6.refs_4_
  20.7 0.0 collective-permute-done.7.refs_5_
  20.7 0.3 %early_products.1.early = f32[48,64]{1,0:T(8,128)S(1)} custom-call(bf16[64,4096]{1,0:T(8,128)(2,1)S(1)} %get-tuple-element.10.query, bf16[8,4096]{1,0:T(8,128)(2,1)S(1)} %add_convert_fusion.refs_0_, bf16[8,4096]{1,0:T(8,128)(2,1)S(1)} %collective-permute-done.3.refs_1_, bf16[8,4096]{1,0:T(8,128)(2,1)S(1)} %collective-permute-done.4.refs_2_, ...), custom_call_target="tpu_custom_call" | custom-call | bytes 917504 | tf_op jit(solution)/shard_map/early_products/pallas_call | solution.py:153
  21.0 0.4 %collective-permute-done.8.refs_0_ = bf16[8,4096]{1,0:T(8,128)(2,1)S(1)} collective-permute-done((bf16[8,4096]{1,0:T(8,128)(2,1)S(1)}, bf16[8,4096]{1,0:T(8,128)(2,1)S(1)}, u32[]{:S(2)}, u32[]{:S(2)}) %collective-permute-start.8) | collective-permute-done | bytes 65568 | tf_op jit(solution)/shard_map/ppermute | solution.py:176
  21.4 0.5 %collective-permute-done.9.refs_1_ = bf16[8,4096]{1,0:T(8,128)(2,1)S(1)} collective-permute-done((bf16[8,4096]{1,0:T(8,128)(2,1)S(1)}, bf16[8,4096]{1,0:T(8,128)(2,1)S(1)}, u32[]{:S(2)}, u32[]{:S(2)}) %collective-permute-start.9) | collective-permute-done | bytes 65568 | tf_op jit(solution)/shard_map/ppermute | solution.py:176
  21.9 1.0 %scores.1 = f32[64,64]{1,0:T(8,128)} custom-call(bf16[64,4096]{1,0:T(8,128)(2,1)S(1)} %get-tuple-element.10.query, f32[48,64]{1,0:T(8,128)S(1)} %early_products.1.early, bf16[8,4096]{1,0:T(8,128)(2,1)S(1)} %collective-permute-done.8.refs_0_, bf16[8,4096]{1,0:T(8,128)(2,1)S(1)} %collective-permute-done.9.refs_1_), custom_call_target="tpu_custom_call" | custom-call | bytes 667648 | tf_op jit(solution)/shard_map/scores/pallas_call | solution.py:153
  (1 shorter events, 0.0 us)
Async XLA Ops:
  2.9 7.9 %collective-permute-start = (bf16[8,4096]{1,0:T(8,128)(2,1)S(1)}, bf16[8,4096]{1,0:T(8,128)(2,1)S(1)}, u32[]{:S(2)}, u32[]{:S(2)}) collective-permute-start(bf16[8,4096]{1,0:T(8,128)(2,1)S(1)} %get-tuple-element.12), channel_id=1, source_target_pairs={{0,2},{1,3},{2,0},{3,1},{4,6},{5,7},{6,4},{7,5},{8,10},{9,11},{10,... | collective-permute-start | bytes 196616 | tf_op jit(solution)/shard_map/ppermute | solution.py:176
  7.0 6.2 %collective-permute-start.1 = (bf16[8,4096]{1,0:T(8,128)(2,1)S(1)}, bf16[8,4096]{1,0:T(8,128)(2,1)S(1)}, u32[]{:S(2)}, u32[]{:S(2)}) collective-permute-start(bf16[8,4096]{1,0:T(8,128)(2,1)S(1)} %get-tuple-element.13), channel_id=1, source_target_pairs={{0,3},{1,2},{2,1},{3,0},{4,7},{5,6},{6,5},{7,4},{8,11},{9,10},{10,... | collective-permute-start | bytes 196616 | tf_op jit(solution)/shard_map/ppermute | solution.py:176
  8.4 5.0 %collective-permute-start.2 = (bf16[8,4096]{1,0:T(8,128)(2,1)S(1)}, bf16[8,4096]{1,0:T(8,128)(2,1)S(1)}, u32[]{:S(2)}, u32[]{:S(2)}) collective-permute-start(bf16[8,4096]{1,0:T(8,128)(2,1)S(1)} %get-tuple-element.14), channel_id=1, source_target_pairs={{0,1},{1,0},{2,3},{3,2},{4,5},{5,4},{6,7},{7,6},{8,9},{9,8},{10,11... | collective-permute-start | bytes 196616 | tf_op jit(solution)/shard_map/ppermute | solution.py:176
  13.4 5.2 %collective-permute-start.5 = (bf16[8,4096]{1,0:T(8,128)(2,1)S(1)}, bf16[8,4096]{1,0:T(8,128)(2,1)S(1)}, u32[]{:S(2)}, u32[]{:S(2)}) collective-permute-start(bf16[8,4096]{1,0:T(8,128)(2,1)S(1)} %add_convert_fusion.refs_0_), channel_id=1, source_target_pairs={{0,24},{4,28},{8,16},{12,20},{16,8},{20,12},{24,0},{28,4},{1,25},{... | collective-permute-start | bytes 196616 | tf_op jit(solution)/shard_map/ppermute | solution.py:176
  15.9 4.3 %collective-permute-start.4 = (bf16[8,4096]{1,0:T(8,128)(2,1)S(1)}, bf16[8,4096]{1,0:T(8,128)(2,1)S(1)}, u32[]{:S(2)}, u32[]{:S(2)}) collective-permute-start(bf16[8,4096]{1,0:T(8,128)(2,1)S(1)} %add_convert_fusion.refs_0_), channel_id=1, source_target_pairs={{0,16},{4,12},{8,24},{12,4},{16,0},{20,28},{24,8},{28,20},{1,17},{... | collective-permute-start | bytes 196616 | tf_op jit(solution)/shard_map/ppermute | solution.py:194
  16.4 4.3 %collective-permute-start.3 = (bf16[8,4096]{1,0:T(8,128)(2,1)S(1)}, bf16[8,4096]{1,0:T(8,128)(2,1)S(1)}, u32[]{:S(2)}, u32[]{:S(2)}) collective-permute-start(bf16[8,4096]{1,0:T(8,128)(2,1)S(1)} %add_convert_fusion.refs_0_), channel_id=1, source_target_pairs={{0,8},{4,20},{8,0},{12,28},{16,24},{20,4},{24,16},{28,12},{1,9},{5... | collective-permute-start | bytes 196616 | tf_op jit(solution)/shard_map/ppermute | solution.py:194
  17.0 3.7 %collective-permute-start.6 = (bf16[8,4096]{1,0:T(8,128)(2,1)S(1)}, bf16[8,4096]{1,0:T(8,128)(2,1)S(1)}, u32[]{:S(2)}, u32[]{:S(2)}) collective-permute-start(bf16[8,4096]{1,0:T(8,128)(2,1)S(1)} %add_convert_fusion.refs_0_), channel_id=1, source_target_pairs={{0,4},{4,0},{8,12},{12,8},{16,20},{20,16},{24,28},{28,24},{1,5},{5... | collective-permute-start | bytes 196616 | tf_op jit(solution)/shard_map/ppermute | solution.py:176
  18.6 2.1 %collective-permute-start.7 = (bf16[8,4096]{1,0:T(8,128)(2,1)S(1)}, bf16[8,4096]{1,0:T(8,128)(2,1)S(1)}, u32[]{:S(2)}, u32[]{:S(2)}) collective-permute-start(bf16[8,4096]{1,0:T(8,128)(2,1)S(1)} %collective-permute-done.5.refs_3_), channel_id=1, source_target_pairs={{0,4},{4,0},{8,12},{12,8},{16,20},{20,16},{24,28},{28,24},{1,5},{5... | collective-permute-start | bytes 196616 | tf_op jit(solution)/shard_map/ppermute | solution.py:176
  20.2 1.3 %collective-permute-start.8 = (bf16[8,4096]{1,0:T(8,128)(2,1)S(1)}, bf16[8,4096]{1,0:T(8,128)(2,1)S(1)}, u32[]{:S(2)}, u32[]{:S(2)}) collective-permute-start(bf16[8,4096]{1,0:T(8,128)(2,1)S(1)} %collective-permute-done.4.refs_2_), channel_id=1, source_target_pairs={{0,4},{4,0},{8,12},{12,8},{16,20},{20,16},{24,28},{28,24},{1,5},{5... | collective-permute-start | bytes 196616 | tf_op jit(solution)/shard_map/ppermute | solution.py:176
  20.7 1.3 %collective-permute-start.9 = (bf16[8,4096]{1,0:T(8,128)(2,1)S(1)}, bf16[8,4096]{1,0:T(8,128)(2,1)S(1)}, u32[]{:S(2)}, u32[]{:S(2)}) collective-permute-start(bf16[8,4096]{1,0:T(8,128)(2,1)S(1)} %collective-permute-done.3.refs_1_), channel_id=1, source_target_pairs={{0,4},{4,0},{8,12},{12,8},{16,20},{20,16},{24,28},{28,24},{1,5},{5... | collective-permute-start | bytes 196616 | tf_op jit(solution)/shard_map/ppermute | solution.py:176
